TPU v7x, 32 devices: a whole 2x2x4 slice. The times are simulated.
32 devices in a mesh: srv: 2 (over y), head: 4 (over x, core), wsh: 4 (over z).
Axes of the slice: x: 2, y: 2, z: 4, core: 2. Of those that a mesh axis runs over, the one named last changes fastest.
Arguments:
- queries: bfloat16 [1536, 8192], P(('srv', 'wsh'), 'head'), may hold values from -4.5 to 4.5
- keys: bfloat16 [1536, 1024], P(('srv', 'wsh'), 'head'), may hold values from -4.5 to 4.5
- values: bfloat16 [1536, 1024], P(('srv', 'wsh'), 'head'), may hold values from -6 to 6
- doc_ids: int32 [1536], replicated, may hold values from 0 to 2, never falling along the last dimension, each value on 1 to 1152 neighbouring positions
- block_mask: int32 [8, 4], replicated, may hold values from 0 to 1, as said below
- out_weight: bfloat16 [8192, 8192], P(('head', 'wsh')), may hold values from -0.0625 to 0.0625
Outputs:
- projected: bfloat16 [1536, 8192], P(('srv', 'head', 'wsh'))
Inputs may be any that keep to these rules, and one draw needn't show every extreme that they name: `block_mask`: column 0 is 1 in every row; other entries are 0 or 1.
All inputs are finite; a program needn't handle non-finite values.
Results may differ from a plain program's by a relative error of at most 0.017.
Values may be sent and summed in bfloat16 or wider, within the bound.
No kernel may reach another device: no remote copies, remote signals or barrier semaphores. Data moves between devices by JAX's collectives and lax.ppermute only.
A program may use at most 128 MiB of HBM per device.

v0:
```python
from functools import partial
import math

import jax
import jax.numpy as jnp
from jax import lax
from jax.sharding import PartitionSpec as P

QUERY_HEAD_COUNT = 64
KEY_VALUE_HEADS = 8
HEAD_SIZE = 128
SLAB_REACH = 4


floor_score = -1e30


def shifted(block, axis, distance):
    devices = range(lax.axis_size(axis))
    route = [(i - distance, i) for i in devices if i - distance in devices]
    return lax.ppermute(block, axis, route)


def tile_update(carried, query_heads, key_block, value_block, docs_query, docs_key, causal):
    running_max, running_sum, weighted = carried
    row_count = query_heads.shape[0]
    key_heads = key_block.reshape(row_count, -1, HEAD_SIZE)
    value_heads = value_block.reshape(row_count, -1, HEAD_SIZE)
    scores = jnp.einsum(
        "qhgd,khd->hgqk", query_heads, key_heads, preferred_element_type=jnp.float32
    ) * (1.0 / math.sqrt(HEAD_SIZE))
    visible = docs_query[:, None] == docs_key[None, :]
    if causal:
        query_pos = lax.broadcasted_iota(jnp.int32, (row_count, row_count), 0)
        key_pos = lax.broadcasted_iota(jnp.int32, (row_count, row_count), 1)
        visible = visible & (key_pos <= query_pos)
    masked = jnp.where(visible, scores, floor_score)
    freshest = jnp.maximum(running_max, jnp.max(masked, axis=-1))
    softmax_terms = jnp.where(visible, jnp.exp(masked - freshest[..., None]), 0.0)
    rescale = jnp.exp(running_max - freshest)
    running_sum = running_sum * rescale + jnp.sum(softmax_terms, axis=-1)
    update = jnp.einsum(
        "hgqk,khd->qhgd",
        softmax_terms.astype(jnp.bfloat16),
        value_heads,
        preferred_element_type=jnp.float32,
    )
    weighted = weighted * jnp.transpose(rescale, (2, 0, 1))[..., None] + update
    return (freshest, running_sum, weighted)


def on_device(queries, keys, values, doc_ids, block_mask, out_weight):
    row_count = queries.shape[0]
    kv_local = keys.shape[1] // HEAD_SIZE
    query_group_width = QUERY_HEAD_COUNT // KEY_VALUE_HEADS
    query_heads = queries.reshape(row_count, kv_local, query_group_width, HEAD_SIZE)
    current_slab = lax.axis_index(("srv", "wsh"))
    docs_query = lax.dynamic_slice_in_dim(doc_ids, current_slab * row_count, row_count)
    mask_row = lax.dynamic_index_in_dim(block_mask, current_slab, 0, keepdims=False)
    carried = (
        jnp.full((kv_local, query_group_width, row_count), floor_score, jnp.float32),
        jnp.zeros((kv_local, query_group_width, row_count), jnp.float32),
        jnp.zeros((row_count, kv_local, query_group_width, HEAD_SIZE), jnp.float32),
    )
    for offset in range(SLAB_REACH):
        if offset == 0:
            key_block, value_block = (keys, values)
        else:
            key_block, value_block = shifted((keys, values), ("srv", "wsh"), offset)
        source = current_slab - offset
        docs_key = lax.dynamic_slice_in_dim(doc_ids, jnp.maximum(source, 0) * row_count, row_count)
        live = (mask_row[offset] > 0) & (source >= 0)
        update_tile = partial(
            tile_update,
            query_heads=query_heads,
            key_block=key_block,
            value_block=value_block,
            docs_query=docs_query,
            docs_key=docs_key,
            causal=offset == 0,
        )
        carried = lax.cond(live, update_tile, lambda running: running, carried)
    running_max, running_sum, weighted = carried
    normalizer = jnp.transpose(running_sum, (2, 0, 1))[..., None]
    attention = (weighted / normalizer).reshape(row_count, -1).astype(jnp.bfloat16)
    spread = lax.all_to_all(attention, "wsh", split_axis=1, concat_axis=0, tiled=True)
    return lax.psum_scatter(
        jnp.dot(spread, out_weight, preferred_element_type=jnp.float32).astype(jnp.bfloat16),
        ("head", "wsh"),
        scatter_dimension=0,
        tiled=True,
    )


def solution(mesh):
    in_specs = (
        P(("srv", "wsh"), "head"),
        P(("srv", "wsh"), "head"),
        P(("srv", "wsh"), "head"),
        P(),
        P(),
        P(("head", "wsh"), None),
    )
    out_specs = P(("srv", "head", "wsh"), None)
    return jax.shard_map(
        on_device, mesh=mesh, in_specs=in_specs, out_specs=out_specs, check_vma=False
    )
```

profile of v0, /device:TPU:0, one launch (start us, length us, event | category | flops | bytes accessed | tf_op | source)
XLA Modules:
  0.0 231.5 jit_solution(13649710990811896044)
XLA Ops:
  6.5 0.0 copy-start
  6.5 0.0 reduce-scatter.2.cloned.1.call-start
  6.5 5.1 %collective-permute-start = (bf16[192,256]{1,0:T(8,128)(2,1)}, bf16[192,256]{1,0:T(8,128)(2,1)S(1)}, u32[]{:S(2)}, u32[]{:S(2)}) collective-permute-start(bf16[192,256]{1,0:T(8,128)(2,1)} %param.15), channel_id=1, source_target_pairs={{0,1},{1,2},{2,3},{3,16},{16,17},{17,18},{18,19},{4,5},{5,6},{6,7}... | collective-permute-start | bytes 294920 | tf_op jit(solution)/shard_map/ppermute | solution.py:21
  11.6 5.1 %collective-permute-start.4 = (bf16[192,256]{1,0:T(8,128)(2,1)}, bf16[192,256]{1,0:T(8,128)(2,1)S(1)}, u32[]{:S(2)}, u32[]{:S(2)}) collective-permute-start(bf16[192,256]{1,0:T(8,128)(2,1)} %param.15), channel_id=1, source_target_pairs={{0,3},{1,16},{2,17},{3,18},{16,19},{4,7},{5,20},{6,21},{7,22},{20,... | collective-permute-start | bytes 294920 | tf_op jit(solution)/shard_map/ppermute | solution.py:21
  16.7 2.7 %collective-permute-start.2 = (bf16[192,256]{1,0:T(8,128)(2,1)}, bf16[192,256]{1,0:T(8,128)(2,1)S(1)}, u32[]{:S(2)}, u32[]{:S(2)}) collective-permute-start(bf16[192,256]{1,0:T(8,128)(2,1)} %param.15), channel_id=1, source_target_pairs={{0,2},{1,3},{2,16},{3,17},{16,18},{17,19},{4,6},{5,7},{6,20},{7,21... | collective-permute-start | bytes 294920 | tf_op jit(solution)/shard_map/ppermute | solution.py:21
  19.4 3.5 %collective-permute-start.1 = (bf16[192,256]{1,0:T(8,128)(2,1)}, bf16[192,256]{1,0:T(8,128)(2,1)S(1)}, u32[]{:S(2)}, u32[]{:S(2)}) collective-permute-start(bf16[192,256]{1,0:T(8,128)(2,1)} %param.16), channel_id=1, source_target_pairs={{0,1},{1,2},{2,3},{3,16},{16,17},{17,18},{18,19},{4,5},{5,6},{6,7}... | collective-permute-start | bytes 294920 | tf_op jit(solution)/shard_map/ppermute | solution.py:21
  22.9 3.1 %collective-permute-start.5 = (bf16[192,256]{1,0:T(8,128)(2,1)}, bf16[192,256]{1,0:T(8,128)(2,1)S(1)}, u32[]{:S(2)}, u32[]{:S(2)}) collective-permute-start(bf16[192,256]{1,0:T(8,128)(2,1)} %param.16), channel_id=1, source_target_pairs={{0,3},{1,16},{2,17},{3,18},{16,19},{4,7},{5,20},{6,21},{7,22},{20,... | collective-permute-start | bytes 294920 | tf_op jit(solution)/shard_map/ppermute | solution.py:21
  26.0 0.0 copy-done
  26.1 0.1 constant_dynamic-slice_fusion
  26.1 0.6 fusion.83
  29.3 1.3 copy.83
  30.6 0.0 collective-permute-done
  30.6 1.3 collective-permute-start.3
  31.9 0.9 fusion.82
  32.8 7.7 %conditional.4 = (f32[2,8,192]{2,1,0:T(8,128)}, f32[2,8,192]{2,1,0:T(8,128)S(1)}, f32[192,2,8,128]{3,0,2,1:T(8,128)S(1)}) conditional(s32[]{:T(128)} %convert_element_type.39, () %tuple.38, (s32[192]{0:T(256)S(1)}, s32[192]{0:T(256)S(1)}, bf16[192,256]{1,0:T(8,128)(2,1)}, bf16[192,2,8,128]{3,2,1,0:T(8,128)(2,1)S(1)}, bf16[192,256]{1,0:T(8,128)(2,1)}) %tuple.81), branch_computations={%region_0.1_spmd, %region_1.4_spmd} | conditional | flops 310173696 | bytes 10311192 | solution.py:82
  32.8 0.1 fusion.14
  32.9 0.9 reshape.64
  33.8 0.9 reshape.63
  34.7 0.8 fusion
  35.5 0.6 fusion.17
  36.2 1.5 fusion.2
  37.7 2.1 bitcast_add_fusion
  39.8 0.7 fusion.18
  40.5 0.0 collective-permute-done.1
  40.5 0.0 collective-permute-done.2
  40.5 0.0 collective-permute-done.3
  40.6 0.0 collective-permute-done.4
  40.6 0.0 collective-permute-done.5
  40.6 0.2 conditional.7
  40.8 0.5 divide_convert_fusion
  41.3 0.5 copy.53
  41.8 0.3 convert_element_type.41
  42.1 0.1 copy.54
  42.2 27.1 %all_to_all.16 = bf16[192,4,512]{2,0,1:T(8,128)(2,1)S(1)} all-to-all(bf16[192,4,512]{2,0,1:T(8,128)(2,1)S(1)} %copy.54), channel_id=1, replica_groups=mesh['srv'=2,'head'=4,'wsh'=4] {'wsh'}, dimensions={1} | all-to-all | bytes 1572864 | tf_op jit(solution)/shard_map/all_to_all | solution.py:86
  69.3 13.1 %convolution_convert_fusion = bf16[768,8192]{1,0:T(8,128)(2,1)} fusion(bf16[768,512]{1,0:T(8,128)(2,1)S(1)} %bitcast.96, bf16[512,8192]{1,0:T(8,128)(2,1)} %param.19), kind=kOutput, calls=%fused_computation.94 | convolution fusion | flops 6448742400 | bytes 21757952 | tf_op jit(solution)/shard_map/dot_general | solution.py:88
  82.4 0.0 reduce-scatter.2.cloned.1.call-update
  82.5 142.2 %reduce-scatter.2.cloned.1.call-done = bf16[48,8192]{1,0:T(8,128)(2,1)} async-done(((bf16[768,8192]{1,0:T(8,128)(2,1)}), bf16[48,8192]{1,0:T(8,128)(2,1)}) %reduce-scatter.2.cloned.1.call-update) | async-done | bytes 786448 | tf_op jit(solution)/shard_map/reduce_scatter | solution.py:87
  (2 shorter events, 0.0 us)
Async XLA Ops:
  6.5 19.5 %copy-start = (s32[8,4]{0,1:T(4,128)S(1)}, s32[8,4]{0,1:T(4,128)}, u32[]{:S(2)}) copy-start(s32[8,4]{0,1:T(4,128)} %param.18) | copy-start | bytes 388
  6.5 218.1 %reduce-scatter.2.cloned.1.call-start = ((), (), s32[]{:S(2)}) async-start(), calls=%async_computation.2 | async-start | bytes 13369344 | tf_op jit(solution)/shard_map/reduce_scatter | solution.py:87
  6.5 24.0 %collective-permute-start = (bf16[192,256]{1,0:T(8,128)(2,1)}, bf16[192,256]{1,0:T(8,128)(2,1)S(1)}, u32[]{:S(2)}, u32[]{:S(2)}) collective-permute-start(bf16[192,256]{1,0:T(8,128)(2,1)} %param.15), channel_id=1, source_target_pairs={{0,1},{1,2},{2,3},{3,16},{16,17},{17,18},{18,19},{4,5},{5,6},{6,7}... | collective-permute-start | bytes 294920 | tf_op jit(solution)/shard_map/ppermute | solution.py:21
  11.6 29.0 %collective-permute-start.4 = (bf16[192,256]{1,0:T(8,128)(2,1)}, bf16[192,256]{1,0:T(8,128)(2,1)S(1)}, u32[]{:S(2)}, u32[]{:S(2)}) collective-permute-start(bf16[192,256]{1,0:T(8,128)(2,1)} %param.15), channel_id=1, source_target_pairs={{0,3},{1,16},{2,17},{3,18},{16,19},{4,7},{5,20},{6,21},{7,22},{20,... | collective-permute-start | bytes 294920 | tf_op jit(solution)/shard_map/ppermute | solution.py:21
  16.7 23.8 %collective-permute-start.2 = (bf16[192,256]{1,0:T(8,128)(2,1)}, bf16[192,256]{1,0:T(8,128)(2,1)S(1)}, u32[]{:S(2)}, u32[]{:S(2)}) collective-permute-start(bf16[192,256]{1,0:T(8,128)(2,1)} %param.15), channel_id=1, source_target_pairs={{0,2},{1,3},{2,16},{3,17},{16,18},{17,19},{4,6},{5,7},{6,20},{7,21... | collective-permute-start | bytes 294920 | tf_op jit(solution)/shard_map/ppermute | solution.py:21
  19.4 21.1 %collective-permute-start.1 = (bf16[192,256]{1,0:T(8,128)(2,1)}, bf16[192,256]{1,0:T(8,128)(2,1)S(1)}, u32[]{:S(2)}, u32[]{:S(2)}) collective-permute-start(bf16[192,256]{1,0:T(8,128)(2,1)} %param.16), channel_id=1, source_target_pairs={{0,1},{1,2},{2,3},{3,16},{16,17},{17,18},{18,19},{4,5},{5,6},{6,7}... | collective-permute-start | bytes 294920 | tf_op jit(solution)/shard_map/ppermute | solution.py:21
  22.9 17.7 %collective-permute-start.5 = (bf16[192,256]{1,0:T(8,128)(2,1)}, bf16[192,256]{1,0:T(8,128)(2,1)S(1)}, u32[]{:S(2)}, u32[]{:S(2)}) collective-permute-start(bf16[192,256]{1,0:T(8,128)(2,1)} %param.16), channel_id=1, source_target_pairs={{0,3},{1,16},{2,17},{3,18},{16,19},{4,7},{5,20},{6,21},{7,22},{20,... | collective-permute-start | bytes 294920 | tf_op jit(solution)/shard_map/ppermute | solution.py:21
  30.6 10.0 %collective-permute-start.3 = (bf16[192,256]{1,0:T(8,128)(2,1)}, bf16[192,256]{1,0:T(8,128)(2,1)S(1)}, u32[]{:S(2)}, u32[]{:S(2)}) collective-permute-start(bf16[192,256]{1,0:T(8,128)(2,1)} %param.16), channel_id=1, source_target_pairs={{0,2},{1,3},{2,16},{3,17},{16,18},{17,19},{4,6},{5,7},{6,20},{7,21... | collective-permute-start | bytes 294920 | tf_op jit(solution)/shard_map/ppermute | solution.py:21
Sparse Core Ops, SparseCore 0:
  82.6 142.0 reduce-scatter.1
where the time goes:
time: 232 us
  waiting for transfers between devices  142 us (61%)
  blocking collectives  27.1 us (12%)
  starting transfers between devices  20.7 us (9%)
  between operations  16.1 us (7%)
  matrix products  16 us (7%)
  local copies, waits for them, and re-layouts  5.67 us (2%)
  other arithmetic  3.44 us (1%)
    reduce_scatter x1, waiting for transfers between devices, on_device(): lax.psum_scatter(jnp.dot(spread, out_weight, preferred_element_type=jnp.f...  142 us
    all_to_all x1, blocking collectives, on_device(): lax.all_to_all(attention, 'wsh', split_axis=1, concat_axis=0, tiled=True)  27.1 us
    ppermute x6, starting transfers between devices, shifted(): return lax.ppermute(block, axis, route)  20.7 us
    dot_general x1, matrix products, on_device(): jnp.dot(spread, out_weight, preferred_element_type=jnp.float32)  13.1 us
  transfers between devices with their start and end apart: 7, of which 1 were waited for; matrix products, arithmetic and copies ran while one was open for 5% of the time, Pallas kernels for 0%

commit v1 on v0

v1 whole, which is shorter than its diff:
```python
from functools import partial
import math

import jax
import jax.numpy as jnp
import numpy as np
from jax import lax
from jax.experimental import pallas as pl
from jax.experimental.pallas import tpu as pltpu
from jax.sharding import PartitionSpec as P

QUERY_HEAD_COUNT = 64
KEY_VALUE_HEADS = 8
HEAD_SIZE = 128
SLAB_REACH = 4

MASKED = -1e30
NEVER = 1 << 30
F32 = jnp.float32
BF16 = jnp.bfloat16


def destination_order(count):
    table = []
    for z in range(count):
        due = {d: (count - 1 - d + z if d > z else count - 1 - z + d) for d in range(count)}
        due[z] = count
        table.append(sorted(range(count), key=lambda d: (due[d], -d if z < count // 2 else d)))
    return np.array(table, np.int32)


def attend_kernel(place, kv_now, kv_before, key_doc, key_pos, query_doc, query_pos, *refs, slabs, heads, spread):
    queries, (keep, send, key_rows, value_rows) = refs[:slabs], refs[slabs:]
    scale = math.log2(math.e) / math.sqrt(HEAD_SIZE)
    block = kv_now.shape[1]
    for k in range(slabs):
        slab = place[k, 0]
        for o in range(SLAB_REACH):
            rows = slice((SLAB_REACH - 1 - o) * block, (SLAB_REACH - o) * block)
            held = (k + o) % slabs

            def fill(source):
                key_rows[rows, :] = source[held, :, :HEAD_SIZE]
                value_rows[rows, :] = source[held, :, HEAD_SIZE:]

            if o == 0:
                fill(kv_now)
            else:
                pl.when(slab >= o)(partial(fill, kv_now))
                pl.when(slab < o)(partial(fill, kv_before))
        visible = (query_doc[k] == key_doc[k]) & (key_pos[k] <= query_pos[k])
        columns = []
        for h in range(heads):
            scores = lax.dot_general(
                queries[k][:, h * HEAD_SIZE : (h + 1) * HEAD_SIZE],
                key_rows[...],
                (((1,), (1,)), ((), ())),
                preferred_element_type=F32,
            )
            scores = jnp.where(visible, scores, MASKED)
            largest = jnp.max(scores, axis=-1, keepdims=True)
            terms = jnp.exp2((scores - largest) * scale)
            normalizer = jnp.sum(terms, axis=-1, keepdims=True)
            weighted = jnp.dot(terms.astype(BF16), value_rows[...], preferred_element_type=F32)
            columns.append((weighted / normalizer).astype(BF16))
        result = jnp.concatenate(columns, axis=1)
        slot = place[k, 2]

        @pl.when(place[k, 1] == 1)
        def _():
            keep[slot] = result

        @pl.when(place[k, 1] == 0)
        def _():
            send[slot] = result


def attend(place, kv_now, kv_before, key_info, query_info, queries):
    slabs, block, _ = kv_now.shape
    rows, width = queries[0].shape
    out = jax.ShapeDtypeStruct((slabs // 2, rows, width), BF16)
    vmem = pl.BlockSpec(memory_space=pltpu.VMEM)
    terms = slabs * rows * SLAB_REACH * block * (width // HEAD_SIZE)
    return pl.pallas_call(
        partial(attend_kernel, slabs=slabs, heads=width // HEAD_SIZE, spread=None),
        out_shape=(out, out),
        in_specs=[pl.BlockSpec(memory_space=pltpu.SMEM)] + [vmem] * (6 + slabs),
        out_specs=(vmem, vmem),
        scratch_shapes=[pltpu.VMEM((SLAB_REACH * block, HEAD_SIZE), BF16)] * 2,
        compiler_params=pltpu.CompilerParams(vmem_limit_bytes=40 << 20),
        cost_estimate=pl.CostEstimate(
            flops=4 * terms * HEAD_SIZE, bytes_accessed=4 * slabs * rows * width * 2, transcendentals=terms
        ),
    )(place, kv_now, kv_before, *key_info, *query_info, *queries)


def project_kernel(mine, theirs, weight_mine, weight_theirs, *outs, rows):
    total = jnp.dot(mine[...], weight_mine[...], preferred_element_type=F32)
    total = total + jnp.dot(theirs[...], weight_theirs[...], preferred_element_type=F32)
    for n, out in enumerate(outs):
        out[...] = total[n * rows : (n + 1) * rows].astype(BF16)


def project(mine, theirs, weight_mine, weight_theirs, rows):
    count, depth = mine.shape
    width = weight_mine.shape[1]
    tile = 1024 if width % 1024 == 0 else width
    whole = pl.BlockSpec((count, depth), lambda n: (0, 0))
    strip = pl.BlockSpec((depth, tile), lambda n: (0, n))
    pieces = count // rows
    return pl.pallas_call(
        partial(project_kernel, rows=rows),
        grid=(width // tile,),
        out_shape=[jax.ShapeDtypeStruct((rows, width), BF16)] * pieces,
        in_specs=[whole, whole, strip, strip],
        out_specs=[pl.BlockSpec((rows, tile), lambda n: (0, n))] * pieces,
        compiler_params=pltpu.CompilerParams(vmem_limit_bytes=40 << 20),
        cost_estimate=pl.CostEstimate(
            flops=4 * count * depth * width,
            bytes_accessed=4 * depth * width + 2 * count * width,
            transcendentals=0,
        ),
    )(mine, theirs, weight_mine, weight_theirs)


def on_device(queries, keys, values, doc_ids, block_mask, out_weight, *, order):
    groups, head_shards, slabs = (lax.axis_size(a) for a in ("srv", "head", "wsh"))
    srv, head, z = (lax.axis_index(a) for a in ("srv", "head", "wsh"))
    core, x, columns_x = head % 2, head // 2, head_shards // 2
    block = queries.shape[0]
    kv_local = keys.shape[1] // HEAD_SIZE
    width = queries.shape[1] // slabs
    share = block // head_shards
    per_shard = slabs // head_shards
    table = jnp.asarray(order)
    staged = per_shard == 1

    def kv_for(target):
        first = (target * kv_local // slabs) * HEAD_SIZE
        cut = lambda a: lax.dynamic_slice(a, (0, first), (block, HEAD_SIZE))
        return jnp.concatenate([cut(keys), cut(values)], axis=1)

    def around(k):
        return [(i, (i + k) % slabs) for i in range(slabs)]

    def query_rows(target, stage):
        strip = lax.dynamic_slice(queries, (0, target * width), (block, width))
        if not staged:
            return strip
        pieces = [
            lax.dynamic_slice(queries, (table[target, i] * share, target * width), (share, width)) for i in stage
        ]
        return pieces[0] if len(pieces) == 1 else jnp.concatenate(pieces, axis=0)

    stages = [[0], list(range(1, slabs))] if staged else [list(range(slabs))]

    held = [kv_for(z)] + [lax.ppermute(kv_for((z + k) % slabs), "wsh", around(k)) for k in range(1, slabs)]
    kv_now = jnp.stack(held)
    kv_before = lax.ppermute(kv_now, "srv", [(g, g + 1) for g in range(groups - 1)])
    stage_queries = [
        [query_rows(z, stage)]
        + [lax.ppermute(query_rows((z + k) % slabs, stage), "wsh", around(k)) for k in range(1, slabs)]
        for stage in stages
    ]
    siblings = [(h, h ^ 1) for h in range(head_shards)]
    weight_sibling = lax.ppermute(out_weight, "head", siblings)

    slab_of = (z - jnp.arange(slabs, dtype=jnp.int32)) % slabs
    offsets = jnp.arange(SLAB_REACH - 1, -1, -1, dtype=jnp.int32)
    global_slab = srv * slabs + slab_of
    source = global_slab[:, None] - offsets[None, :]
    docs = doc_ids.reshape(-1, block)
    open_pair = jnp.take_along_axis(
        block_mask[global_slab], jnp.broadcast_to(offsets[None, :], source.shape), axis=1
    )
    live = (open_pair > 0) & (source >= 0)
    within = jnp.arange(block, dtype=jnp.int32)
    key_doc = docs[jnp.maximum(source, 0)].reshape(slabs, 1, -1)
    key_pos = jnp.where(live[..., None], source[..., None] * block + within, NEVER).reshape(slabs, 1, -1)
    target = slab_of // per_shard
    place = jnp.stack(
        [slab_of, (target % 2 == core).astype(jnp.int32), ((target // 2 - x) % columns_x) * per_shard + slab_of % per_shard],
        axis=1,
    ).astype(jnp.int32)

    partials = []
    for stage, blocks in zip(stages, stage_queries):
        if staged:
            rows = jnp.concatenate([table[z, i] * share + jnp.arange(share, dtype=jnp.int32) for i in stage])
        else:
            rows = within
        query_doc = docs[global_slab][:, rows][..., None]
        query_pos = (global_slab[:, None] * block + rows[None, :])[..., None]
        keep, send = attend(place, kv_now, kv_before, (key_doc, key_pos), (query_doc, query_pos), blocks)
        if not staged:
            keep, send = (
                jnp.concatenate(
                    [
                        lax.dynamic_slice_in_dim(a.reshape(columns_x, -1, width), table[z, i] * share, share, 1)
                        for i in stage
                    ],
                    axis=1,
                )
                for a in (keep, send)
            )
        theirs = lax.ppermute(send, "head", siblings)
        results = project(
            keep.reshape(-1, width), theirs.reshape(-1, width), out_weight, weight_sibling, share
        )
        count = len(stage)
        for n in range(count):
            partials.append([results[k * count + n] for k in range(columns_x)])

    sums = []
    for own, *others in partials:
        total = own.astype(F32)
        for k, other in enumerate(others, 1):
            route = [(h, (h + 2 * k) % head_shards) for h in range(head_shards)]
            total = total + lax.ppermute(other, "head", route).astype(F32)
        sums.append(total.astype(BF16))

    position = np.argsort(order, axis=1)

    def along(direction):
        arrived = None
        for t in range(slabs - 1):
            which = np.zeros(slabs, np.int32)
            route = []
            for i in range(slabs):
                step = i if direction > 0 else slabs - 1 - i
                if step <= t:
                    d = slabs - 1 - t + step
                    d = d if direction > 0 else slabs - 1 - d
                    which[i] = position[i, d]
                    route.append((i, i + direction))
            message = sums[which[0 if direction > 0 else slabs - 1]]
            for i in range(slabs):
                if any(i == r[0] for r in route) and sums[which[i]] is not message:
                    message = jnp.where(z == i, sums[which[i]], message)
            if arrived is not None:
                message = (message.astype(F32) + arrived.astype(F32)).astype(BF16)
            arrived = lax.ppermute(message, "wsh", route)
        return arrived

    total = sums[-1].astype(F32)
    if slabs > 1:
        total = total + along(1).astype(F32) + along(-1).astype(F32)
    return total.astype(BF16)


def solution(mesh):
    in_specs = (
        P(("srv", "wsh"), "head"),
        P(("srv", "wsh"), "head"),
        P(("srv", "wsh"), "head"),
        P(),
        P(),
        P(("head", "wsh"), None),
    )
    out_specs = P(("srv", "head", "wsh"), None)
    return jax.shard_map(
        partial(on_device, order=destination_order(mesh.shape["wsh"])),
        mesh=mesh,
        in_specs=in_specs,
        out_specs=out_specs,
        check_vma=False,
    )
```

time: 232 us -> 154 us (0.66)
  waiting for transfers between devices: 142 us -> 49.4 us
  Pallas kernels: 0 us -> 31.6 us
  blocking collectives: 27.1 us -> 0 us
  starting transfers between devices: 20.7 us -> 40.9 us
  matrix products: 16 us -> 0 us
  local copies, waits for them, and re-layouts: 5.67 us -> 14.7 us
  between operations: 16.1 us -> 10.4 us
  other arithmetic: 3.44 us -> 6.17 us
    reduce_scatter x1 -> x0, waiting for transfers between devices: 142 us -> none  [on_device(): lax.psum_scatter(jnp.dot(spread, out_weight, preferred_element_type=jnp.f...]
    ppermute x6 -> x23, waiting for transfers between devices: 0.02 us -> 49.4 us  [the longest x6 27.5 us: along(): arrived = lax.ppermute(message, 'wsh', route)]
    pallas_call x0 -> x4, Pallas kernels: none -> 31.6 us  [the longest x2 18.2 us: project(): pl.pallas_call(partial(project_kernel, rows=rows), grid=(width // tile,),...]
    all_to_all x1 -> x0, blocking collectives: 27.1 us -> none  [on_device(): lax.all_to_all(attention, 'wsh', split_axis=1, concat_axis=0, tiled=True)]
    ppermute x6 -> x23, starting transfers between devices: 20.7 us -> 40.9 us  [the longest x6 16.8 us: along(): arrived = lax.ppermute(message, 'wsh', route)]
    dot_general x3 -> x0, matrix products: 16 us -> none  [the longest x1 13.1 us: on_device(): jnp.dot(spread, out_weight, preferred_element_type=jnp.float32)]
    unnamed x3 -> x15, local copies, waits for them, and re-layouts: 1.29 us -> 6.87 us
    convert_element_type x1 -> x6, other arithmetic: 0.48 us -> 5.14 us  [the longest x3 2.79 us: along(): message = (message.astype(F32) + arrived.astype(F32)).astype(BF16)]
  transfers between devices with their start and end apart: 7 -> 23, of which waited for: 1 -> 9; matrix products, arithmetic and copies ran while one was open for 5% -> 8% of each run, Pallas kernels for 0% -> 21%
where the time goes in v1:
time: 154 us; the launch traced here: 153 us
  waiting for transfers between devices  49.4 us (32%)
  starting transfers between devices  40.9 us (27%)
  Pallas kernels  31.6 us (21%)
  local copies, waits for them, and re-layouts  14.7 us (10%)
  between operations  10.4 us (7%)
  other arithmetic  6.17 us (4%)
    ppermute x6, waiting for transfers between devices, along(): arrived = lax.ppermute(message, 'wsh', route)  27.5 us
    ppermute x4, waiting for transfers between devices, on_device(): total = total + lax.ppermute(other, 'head', route).astype(F32)  19 us
    pallas_call x2, Pallas kernels, project(): pl.pallas_call(partial(project_kernel, rows=rows), grid=(width // tile,),...  18.2 us
    ppermute x6, starting transfers between devices, along(): arrived = lax.ppermute(message, 'wsh', route)  16.8 us
    pallas_call x2, Pallas kernels, attend(): pl.pallas_call(partial(attend_kernel, slabs=slabs, heads=width // HEAD_SI...  13.4 us
    ppermute x6, starting transfers between devices, on_device(): lax.ppermute(query_rows((z + k) % slabs, stage), 'wsh', around(k))  8.03 us
    ppermute x3, starting transfers between devices, on_device(): lax.ppermute(kv_for((z + k) % slabs), 'wsh', around(k))  6.87 us
    unnamed x15, local copies, waits for them, and re-layouts  6.87 us
  transfers between devices with their start and end apart: 23, of which 9 were waited for; matrix products, arithmetic and copies ran while one was open for 8% of the time, Pallas kernels for 21%

profile of v1, /device:TPU:0, one launch (start us, length us, event | category | flops | bytes accessed | tf_op | source)
XLA Modules:
  0.0 153.2 jit_solution(14987498703763371822)
XLA Ops:
  0.0 0.5 collective-permute-start.8
  0.5 1.0 constant_dynamic-slice_fusion.10
  1.5 2.8 %collective-permute-start = (bf16[192,256]{1,0:T(8,128)(2,1)S(1)}, bf16[192,256]{1,0:T(8,128)(2,1)S(1)}, u32[]{:S(2)}, u32[]{:S(2)}) collective-permute-start(bf16[192,256]{1,0:T(8,128)(2,1)S(1)} %pad_maximum_fusion.5), channel_id=1, source_target_pairs={{0,1},{1,2},{2,3},{3,0},{4,5},{5,6},{6,7},{7,4},{8,9},{9,10},{10,1... | collective-permute-start | bytes 294920 | tf_op jit(solution)/shard_map/ppermute | solution.py:157
  4.4 2.7 %collective-permute-start.1 = (bf16[192,256]{1,0:T(8,128)(2,1)S(1)}, bf16[192,256]{1,0:T(8,128)(2,1)S(1)}, u32[]{:S(2)}, u32[]{:S(2)}) collective-permute-start(bf16[192,256]{1,0:T(8,128)(2,1)S(1)} %pad_maximum_fusion.6), channel_id=1, source_target_pairs={{0,2},{1,3},{2,0},{3,1},{4,6},{5,7},{6,4},{7,5},{8,10},{9,11},{10,... | collective-permute-start | bytes 294920 | tf_op jit(solution)/shard_map/ppermute | solution.py:157
  7.0 1.4 collective-permute-start.2
  8.4 0.7 constant_dynamic-slice_fusion.16
  19.8 0.6 gather_fusion.1
  20.4 0.7 gather_fusion.5
  22.4 3.0 %collective-permute-start.14 = (bf16[48,512]{1,0:T(8,128)(2,1)S(1)}, bf16[48,512]{1,0:T(8,128)(2,1)S(1)}, u32[]{:S(2)}, u32[]{:S(2)}) collective-permute-start(bf16[48,512]{1,0:T(8,128)(2,1)S(1)} %get-tuple-element.49), channel_id=1, source_target_pairs={{0,3},{1,0},{2,1},{3,2},{4,7},{5,4},{6,5},{7,6},{8,11},{9,8},{10,9... | collective-permute-start | bytes 147464 | tf_op jit(solution)/shard_map/ppermute | solution.py:162
  25.5 3.4 %collective-permute-start.3 = (bf16[4,192,256]{2,1,0:T(8,128)(2,1)S(1)}, bf16[4,192,256]{2,1,0:T(8,128)(2,1)S(1)}, u32[]{:S(2)}, u32[]{:S(2)}) collective-permute-start(bf16[4,192,256]{2,1,0:T(8,128)(2,1)S(1)} %pad_maximum_fusion.kv_now), channel_id=1, source_target_pairs={{0,16},{1,17},{2,18},{3,19},{4,20},{5,21},{6,22},{7,23},{8,24},{9,... | collective-permute-start | bytes 1179656 | tf_op jit(solution)/shard_map/ppermute | solution.py:159
  29.3 0.6 gather_fusion.2
  30.0 0.7 gather_fusion.3
  30.6 1.0 copy.17.query_doc
  31.6 0.6 gather_fusion
  32.3 0.6 gather_fusion.4
  32.9 0.4 copy.20.query_doc
  33.3 0.6 collective-permute-start.4
  33.9 3.9 %collective-permute-start.5 = (bf16[144,512]{1,0:T(8,128)(2,1)S(1)}, bf16[144,512]{1,0:T(8,128)(2,1)S(1)}, u32[]{:S(2)}, u32[]{:S(2)}) collective-permute-start(bf16[144,512]{1,0:T(8,128)(2,1)S(1)} %pad_maximum_fusion.3), channel_id=1, source_target_pairs={{0,2},{1,3},{2,0},{3,1},{4,6},{5,7},{6,4},{7,5},{8,10},{9,11},{10,... | collective-permute-start | bytes 442376 | tf_op jit(solution)/shard_map/ppermute | solution.py:162
  37.7 0.5 collective-permute-start.6
  38.2 6.3 %shard_map.75 = (bf16[2,48,512]{2,1,0:T(8,128)(2,1)S(1)}, bf16[2,48,512]{2,1,0:T(8,128)(2,1)S(1)}) custom-call(s32[4,3]{1,0:T(4,128)S(1)} %pad_add_fusion.place, bf16[4,192,256]{2,1,0:T(8,128)(2,1)S(1)} %pad_maximum_fusion.kv_now, bf16[4,192,256]{2,1,0:T(8,128)(2,1)S(1)} %collective-permute-done.3.kv_before, s32[4,1,768]{2,1,0:T(1,128)S(1)} %reshape.657.key_doc, ...), custom_call_target="tpu_custom_call" | custom-call | flops 301989888 | bytes 786432 | tf_op jit(solution)/shard_map/pallas_call | solution.py:84
  44.6 1.3 collective-permute-done.15
  45.9 3.4 %copy-done = bf16[512,8192]{1,0:T(8,128)(2,1)S(1)} copy-done((bf16[512,8192]{1,0:T(8,128)(2,1)S(1)}, bf16[512,8192]{1,0:T(8,128)(2,1)}, u32[]{:S(2)}) %copy-start) | copy-done | bytes 8388632
  49.3 8.0 %shard_map.76 = (bf16[48,8192]{1,0:T(8,128)(2,1)S(1)}, bf16[48,8192]{1,0:T(8,128)(2,1)S(1)}) custom-call(bf16[96,512]{1,0:T(8,128)(2,1)S(1)} %bitcast.44, bf16[96,512]{1,0:T(8,128)(2,1)S(1)} %bitcast.45, bf16[512,8192]{1,0:T(8,128)(2,1)S(1)} %copy-done, bf16[512,8192]{1,0:T(8,128)(2,1)} %collective-permute-done.8.weight_theirs), custom_call_target="tpu_custom_call" | custom-call | flops 1610612736 | bytes 18350080 | tf_op jit(solution)/shard_map/pallas_call | solution.py:111
  57.2 1.6 %collective-permute-start.16 = (bf16[48,8192]{1,0:T(8,128)(2,1)S(1)}, bf16[48,8192]{1,0:T(8,128)(2,1)S(1)}, u32[]{:S(2)}, u32[]{:S(2)}) collective-permute-start(bf16[48,8192]{1,0:T(8,128)(2,1)S(1)} %get-tuple-element.28), channel_id=1, source_target_pairs={{0,8},{4,12},{8,0},{12,4},{1,9},{5,13},{9,1},{13,5},{2,10},{6,14},... | collective-permute-start | bytes 2359304 | tf_op jit(solution)/shard_map/ppermute | solution.py:219
  58.8 7.1 %shard_map.73 = (bf16[2,144,512]{2,1,0:T(8,128)(2,1)S(1)}, bf16[2,144,512]{2,1,0:T(8,128)(2,1)S(1)}) custom-call(s32[4,3]{1,0:T(4,128)S(1)} %pad_add_fusion.place, bf16[4,192,256]{2,1,0:T(8,128)(2,1)S(1)} %pad_maximum_fusion.kv_now, bf16[4,192,256]{2,1,0:T(8,128)(2,1)S(1)} %collective-permute-done.3.kv_before, s32[4,1,768]{2,1,0:T(1,128)S(1)} %reshape.657.key_doc, ...), custom_call_target="tpu_custom_call" | custom-call | flops 905969664 | bytes 2359296 | tf_op jit(solution)/shard_map/pallas_call | solution.py:84
  66.0 1.6 %collective-permute-done.7 = bf16[2,144,512]{2,1,0:T(8,128)(2,1)S(1)} collective-permute-done((bf16[2,144,512]{2,1,0:T(8,128)(2,1)S(1)}, bf16[2,144,512]{2,1,0:T(8,128)(2,1)S(1)}, u32[]{:S(2)}, u32[]{:S(2)}) %collective-permute-start.7) | collective-permute-done | bytes 294944 | tf_op jit(solution)/shard_map/ppermute | solution.py:206
  67.5 3.4 %copy-done.1 = bf16[512,8192]{1,0:T(8,128)(2,1)S(1)} copy-done((bf16[512,8192]{1,0:T(8,128)(2,1)S(1)}, bf16[512,8192]{1,0:T(8,128)(2,1)}, u32[]{:S(2)}) %copy-start.1) | copy-done | bytes 8388632
  70.9 10.2 %shard_map.74 = (bf16[48,8192]{1,0:T(8,128)(2,1)S(1)}, bf16[48,8192]{1,0:T(8,128)(2,1)S(1)}, bf16[48,8192]{1,0:T(8,128)(2,1)S(1)}, bf16[48,8192]{1,0:T(8,128)(2,...) custom-call(bf16[288,512]{1,0:T(8,128)(2,1)S(1)} %bitcast.47, bf16[288,512]{1,0:T(8,128)(2,1)S(1)} %bitcast.46, ...), custom_call_target="tpu_custom_call" | custom-call | flops 4831838208 | bytes 21495808 | tf_op jit(solution)/shard_map/pallas_call | solution.py:111
  81.1 0.5 collective-permute-start.11
  81.7 1.1 add_convert_fusion.5
  82.7 4.4 %collective-permute-start.17 = (bf16[48,8192]{1,0:T(8,128)(2,1)}, bf16[48,8192]{1,0:T(8,128)(2,1)}, u32[]{:S(2)}, u32[]{:S(2)}) collective-permute-start(bf16[48,8192]{1,0:T(8,128)(2,1)} %add_convert_fusion.5), channel_id=1, source_target_pairs={{0,1},{4,5},{8,9},{12,13},{16,17},{20,21},{24,25},{28,29}} | collective-permute-start | bytes 2359304 | tf_op jit(solution)/shard_map/ppermute | solution.py:242
  87.1 1.5 collective-permute-start.10
  88.6 0.7 collective-permute-start.20
  89.3 12.5 %collective-permute-done.11 = bf16[48,8192]{1,0:T(8,128)(2,1)} collective-permute-done((bf16[48,8192]{1,0:T(8,128)(2,1)}, bf16[48,8192]{1,0:T(8,128)(2,1)}, u32[]{:S(2)}, u32[]{:S(2)}) %collective-permute-start.11) | collective-permute-done | bytes 786464 | tf_op jit(solution)/shard_map/ppermute | solution.py:219
  101.8 1.5 collective-permute-done.17
  103.3 1.8 %add_convert_fusion.4 = (bf16[48,8192]{1,0:T(8,128)(2,1)S(1)}, bf16[48,8192]{1,0:T(8,128)(2,1)S(1)}) fusion(bf16[48,8192]{1,0:T(8,128)(2,1)} %collective-permute-done.17, bf16[48,8192]{1,0:T(8,128)(2,1)} %add_convert_fusion.5, pred[]{:T(512)S(6)} %eq.45, bf16[48,8192]{1,0:T(8,128)(2,1)} %collective-permute-done.11, bf16[48,8192]{1,0:T(8,128)(2,1)S(1)} %get-tuple-element.23), kind=kLoop, calls=%fused_computation.10 | loop fusion | flops 3538944 | bytes 4718593 | tf_op jit(solution)/shard_map/convert_element_type | solution.py:241
  105.5 0.7 collective-permute-start.21
  106.2 5.3 %collective-permute-start.18 = (bf16[48,8192]{1,0:T(8,128)(2,1)S(1)}, bf16[48,8192]{1,0:T(8,128)(2,1)S(1)}, u32[]{:S(2)}, u32[]{:S(2)}) collective-permute-start(bf16[48,8192]{1,0:T(8,128)(2,1)S(1)} %get-tuple-element.29), channel_id=1, source_target_pairs={{0,1},{1,2},{4,5},{5,6},{8,9},{9,10},{12,13},{13,14},{16,17},{17,1... | collective-permute-start | bytes 2359304 | tf_op jit(solution)/shard_map/ppermute | solution.py:242
  111.5 1.6 %collective-permute-start.9 = (bf16[48,8192]{1,0:T(8,128)(2,1)S(1)}, bf16[48,8192]{1,0:T(8,128)(2,1)S(1)}, u32[]{:S(2)}, u32[]{:S(2)}) collective-permute-start(bf16[48,8192]{1,0:T(8,128)(2,1)S(1)} %get-tuple-element.20), channel_id=1, source_target_pairs={{0,8},{4,12},{8,0},{12,4},{1,9},{5,13},{9,1},{13,5},{2,10},{6,14},... | collective-permute-start | bytes 2359304 | tf_op jit(solution)/shard_map/ppermute | solution.py:219
  113.0 5.6 %collective-permute-done.10 = bf16[48,8192]{1,0:T(8,128)(2,1)S(1)} collective-permute-done((bf16[48,8192]{1,0:T(8,128)(2,1)}, bf16[48,8192]{1,0:T(8,128)(2,1)S(1)}, u32[]{:S(2)}, u32[]{:S(2)}) %collective-permute-start.10) | collective-permute-done | bytes 786464 | tf_op jit(solution)/shard_map/ppermute | solution.py:219
  118.6 8.8 %collective-permute-done.18 = bf16[48,8192]{1,0:T(8,128)(2,1)S(1)} collective-permute-done((bf16[48,8192]{1,0:T(8,128)(2,1)S(1)}, bf16[48,8192]{1,0:T(8,128)(2,1)S(1)}, u32[]{:S(2)}, u32[]{:S(2)}) %collective-permute-start.18) | collective-permute-done | bytes 786464 | tf_op jit(solution)/shard_map/ppermute | solution.py:242
  127.4 0.7 add_convert_fusion.3
  128.0 4.4 %collective-permute-start.19 = (bf16[48,8192]{1,0:T(8,128)(2,1)S(1)}, bf16[48,8192]{1,0:T(8,128)(2,1)S(1)}, u32[]{:S(2)}, u32[]{:S(2)}) collective-permute-start(bf16[48,8192]{1,0:T(8,128)(2,1)S(1)} %get-tuple-element.33), channel_id=1, source_target_pairs={{0,1},{1,2},{2,3},{4,5},{5,6},{6,7},{8,9},{9,10},{10,11},{12,13},{... | collective-permute-start | bytes 2359304 | tf_op jit(solution)/shard_map/ppermute | solution.py:242
  132.5 1.3 collective-permute-start.22
  133.8 0.9 collective-permute-done.9
  134.6 12.8 %collective-permute-done.19 = bf16[48,8192]{1,0:T(8,128)(2,1)S(1)} collective-permute-done((bf16[48,8192]{1,0:T(8,128)(2,1)S(1)}, bf16[48,8192]{1,0:T(8,128)(2,1)S(1)}, u32[]{:S(2)}, u32[]{:S(2)}) %collective-permute-start.19) | collective-permute-done | bytes 786464 | tf_op jit(solution)/shard_map/ppermute | solution.py:242
  147.4 4.5 %collective-permute-done.22 = bf16[48,8192]{1,0:T(8,128)(2,1)S(1)} collective-permute-done((bf16[48,8192]{1,0:T(8,128)(2,1)S(1)}, bf16[48,8192]{1,0:T(8,128)(2,1)S(1)}, u32[]{:S(2)}, u32[]{:S(2)}) %collective-permute-start.22) | collective-permute-done | bytes 786464 | tf_op jit(solution)/shard_map/ppermute | solution.py:242
  151.9 1.3 add_convert_fusion
  (80 shorter events, 3.0 us)
Async XLA Ops:
  0.0 8.4 %copy-start.4 = (s32[4,4]{1,0:T(4,128)S(1)}, s32[4,4]{1,0:T(4,128)}, u32[]{:S(2)}) copy-start(s32[4,4]{1,0:T(4,128)} %constant.204.clone) | copy-start | bytes 196
  0.0 10.4 %copy-start.3 = (bf16[192,2048]{1,0:T(8,128)(2,1)S(1)}, bf16[192,2048]{1,0:T(8,128)(2,1)}, u32[]{:S(2)}) copy-start(bf16[192,2048]{1,0:T(8,128)(2,1)} %param.7) | copy-start | bytes 2359300
  0.0 19.6 %copy-start.6 = (s32[8,4]{0,1:T(4,128)S(1)}, s32[8,4]{0,1:T(4,128)}, u32[]{:S(2)}) copy-start(s32[8,4]{0,1:T(4,128)} %param.11) | copy-start | bytes 388
  0.0 45.9 %collective-permute-start.8 = (bf16[512,8192]{1,0:T(8,128)(2,1)}, bf16[512,8192]{1,0:T(8,128)(2,1)}, u32[]{:S(2)}, u32[]{:S(2)}) collective-permute-start(bf16[512,8192]{1,0:T(8,128)(2,1)} %weight_mine.3), channel_id=1, source_target_pairs={{0,4},{4,0},{8,12},{12,8},{1,5},{5,1},{9,13},{13,9},{2,6},{6,2},{1... | collective-permute-start | bytes 25165832 | tf_op jit(solution)/shard_map/ppermute | solution.py:166
  1.5 20.9 %collective-permute-start = (bf16[192,256]{1,0:T(8,128)(2,1)S(1)}, bf16[192,256]{1,0:T(8,128)(2,1)S(1)}, u32[]{:S(2)}, u32[]{:S(2)}) collective-permute-start(bf16[192,256]{1,0:T(8,128)(2,1)S(1)} %pad_maximum_fusion.5), channel_id=1, source_target_pairs={{0,1},{1,2},{2,3},{3,0},{4,5},{5,6},{6,7},{7,4},{8,9},{9,10},{10,1... | collective-permute-start | bytes 294920 | tf_op jit(solution)/shard_map/ppermute | solution.py:157
  4.4 21.0 %collective-permute-start.1 = (bf16[192,256]{1,0:T(8,128)(2,1)S(1)}, bf16[192,256]{1,0:T(8,128)(2,1)S(1)}, u32[]{:S(2)}, u32[]{:S(2)}) collective-permute-start(bf16[192,256]{1,0:T(8,128)(2,1)S(1)} %pad_maximum_fusion.6), channel_id=1, source_target_pairs={{0,2},{1,3},{2,0},{3,1},{4,6},{5,7},{6,4},{7,5},{8,10},{9,11},{10,... | collective-permute-start | bytes 294920 | tf_op jit(solution)/shard_map/ppermute | solution.py:157
  7.0 18.4 %collective-permute-start.2 = (bf16[192,256]{1,0:T(8,128)(2,1)S(1)}, bf16[192,256]{1,0:T(8,128)(2,1)S(1)}, u32[]{:S(2)}, u32[]{:S(2)}) collective-permute-start(bf16[192,256]{1,0:T(8,128)(2,1)S(1)} %pad_maximum_fusion.7), channel_id=1, source_target_pairs={{0,3},{1,0},{2,1},{3,2},{4,7},{5,4},{6,5},{7,6},{8,11},{9,8},{10,9... | collective-permute-start | bytes 294920 | tf_op jit(solution)/shard_map/ppermute | solution.py:157
  10.5 22.9 %collective-permute-start.13 = (bf16[48,512]{1,0:T(8,128)(2,1)S(1)}, bf16[48,512]{1,0:T(8,128)(2,1)S(1)}, u32[]{:S(2)}, u32[]{:S(2)}) collective-permute-start(bf16[48,512]{1,0:T(8,128)(2,1)S(1)} %get-tuple-element.50), channel_id=1, source_target_pairs={{0,2},{1,3},{2,0},{3,1},{4,6},{5,7},{6,4},{7,5},{8,10},{9,11},{10,... | collective-permute-start | bytes 147464 | tf_op jit(solution)/shard_map/ppermute | solution.py:162
  22.1 7.1 %copy-start.5 = (s32[1536]{0:T(1024)S(1)}, s32[1536]{0:T(1024)}, u32[]{:S(2)}) copy-start(s32[1536]{0:T(1024)} %param.10) | copy-start | bytes 18436
  22.4 11.4 %collective-permute-start.14 = (bf16[48,512]{1,0:T(8,128)(2,1)S(1)}, bf16[48,512]{1,0:T(8,128)(2,1)S(1)}, u32[]{:S(2)}, u32[]{:S(2)}) collective-permute-start(bf16[48,512]{1,0:T(8,128)(2,1)S(1)} %get-tuple-element.49), channel_id=1, source_target_pairs={{0,3},{1,0},{2,1},{3,2},{4,7},{5,4},{6,5},{7,6},{8,11},{9,8},{10,9... | collective-permute-start | bytes 147464 | tf_op jit(solution)/shard_map/ppermute | solution.py:162
  25.4 12.3 %collective-permute-start.12 = (bf16[48,512]{1,0:T(8,128)(2,1)S(1)}, bf16[48,512]{1,0:T(8,128)(2,1)S(1)}, u32[]{:S(2)}, u32[]{:S(2)}) collective-permute-start(bf16[48,512]{1,0:T(8,128)(2,1)S(1)} %get-tuple-element.36), channel_id=1, source_target_pairs={{0,1},{1,2},{2,3},{3,0},{4,5},{5,6},{6,7},{7,4},{8,9},{9,10},{10,1... | collective-permute-start | bytes 147464 | tf_op jit(solution)/shard_map/ppermute | solution.py:162
  25.5 12.7 %collective-permute-start.3 = (bf16[4,192,256]{2,1,0:T(8,128)(2,1)S(1)}, bf16[4,192,256]{2,1,0:T(8,128)(2,1)S(1)}, u32[]{:S(2)}, u32[]{:S(2)}) collective-permute-start(bf16[4,192,256]{2,1,0:T(8,128)(2,1)S(1)} %pad_maximum_fusion.kv_now), channel_id=1, source_target_pairs={{0,16},{1,17},{2,18},{3,19},{4,20},{5,21},{6,22},{7,23},{8,24},{9,... | collective-permute-start | bytes 1179656 | tf_op jit(solution)/shard_map/ppermute | solution.py:159
  33.3 25.5 %collective-permute-start.4 = (bf16[144,512]{1,0:T(8,128)(2,1)S(1)}, bf16[144,512]{1,0:T(8,128)(2,1)S(1)}, u32[]{:S(2)}, u32[]{:S(2)}) collective-permute-start(bf16[144,512]{1,0:T(8,128)(2,1)S(1)} %pad_maximum_fusion.2), channel_id=1, source_target_pairs={{0,1},{1,2},{2,3},{3,0},{4,5},{5,6},{6,7},{7,4},{8,9},{9,10},{10,1... | collective-permute-start | bytes 442376 | tf_op jit(solution)/shard_map/ppermute | solution.py:162
  33.9 24.9 %collective-permute-start.5 = (bf16[144,512]{1,0:T(8,128)(2,1)S(1)}, bf16[144,512]{1,0:T(8,128)(2,1)S(1)}, u32[]{:S(2)}, u32[]{:S(2)}) collective-permute-start(bf16[144,512]{1,0:T(8,128)(2,1)S(1)} %pad_maximum_fusion.3), channel_id=1, source_target_pairs={{0,2},{1,3},{2,0},{3,1},{4,6},{5,7},{6,4},{7,5},{8,10},{9,11},{10,... | collective-permute-start | bytes 442376 | tf_op jit(solution)/shard_map/ppermute | solution.py:162
  37.7 21.0 %collective-permute-start.6 = (bf16[144,512]{1,0:T(8,128)(2,1)S(1)}, bf16[144,512]{1,0:T(8,128)(2,1)S(1)}, u32[]{:S(2)}, u32[]{:S(2)}) collective-permute-start(bf16[144,512]{1,0:T(8,128)(2,1)S(1)} %pad_maximum_fusion.4), channel_id=1, source_target_pairs={{0,3},{1,0},{2,1},{3,2},{4,7},{5,4},{6,5},{7,6},{8,11},{9,8},{10,9... | collective-permute-start | bytes 442376 | tf_op jit(solution)/shard_map/ppermute | solution.py:162
  44.5 1.4 collective-permute-start.15
  45.9 3.4 %copy-start = (bf16[512,8192]{1,0:T(8,128)(2,1)S(1)}, bf16[512,8192]{1,0:T(8,128)(2,1)}, u32[]{:S(2)}) copy-start(bf16[512,8192]{1,0:T(8,128)(2,1)} %weight_mine.3) | copy-start | bytes 25165828
  57.2 24.5 %collective-permute-start.16 = (bf16[48,8192]{1,0:T(8,128)(2,1)S(1)}, bf16[48,8192]{1,0:T(8,128)(2,1)S(1)}, u32[]{:S(2)}, u32[]{:S(2)}) collective-permute-start(bf16[48,8192]{1,0:T(8,128)(2,1)S(1)} %get-tuple-element.28), channel_id=1, source_target_pairs={{0,8},{4,12},{8,0},{12,4},{1,9},{5,13},{9,1},{13,5},{2,10},{6,14},... | collective-permute-start | bytes 2359304 | tf_op jit(solution)/shard_map/ppermute | solution.py:219
  65.9 1.6 %collective-permute-start.7 = (bf16[2,144,512]{2,1,0:T(8,128)(2,1)S(1)}, bf16[2,144,512]{2,1,0:T(8,128)(2,1)S(1)}, u32[]{:S(2)}, u32[]{:S(2)}) collective-permute-start(bf16[2,144,512]{2,1,0:T(8,128)(2,1)S(1)} %get-tuple-element.18), channel_id=1, source_target_pairs={{0,4},{4,0},{8,12},{12,8},{1,5},{5,1},{9,13},{13,9},{2,6},{6,2},{1... | collective-permute-start | bytes 884744 | tf_op jit(solution)/shard_map/ppermute | solution.py:206
  67.5 3.4 %copy-start.1 = (bf16[512,8192]{1,0:T(8,128)(2,1)S(1)}, bf16[512,8192]{1,0:T(8,128)(2,1)}, u32[]{:S(2)}) copy-start(bf16[512,8192]{1,0:T(8,128)(2,1)} %weight_mine.3) | copy-start | bytes 25165828
  81.1 1.6 %copy-start.2 = (bf16[48,8192]{1,0:T(8,128)(2,1)}, bf16[48,8192]{1,0:T(8,128)(2,1)S(1)}, u32[]{:S(2)}) copy-start(bf16[48,8192]{1,0:T(8,128)(2,1)S(1)} %get-tuple-element.22) | copy-start | bytes 2359300
  81.1 20.7 %collective-permute-start.11 = (bf16[48,8192]{1,0:T(8,128)(2,1)}, bf16[48,8192]{1,0:T(8,128)(2,1)}, u32[]{:S(2)}, u32[]{:S(2)}) collective-permute-start(bf16[48,8192]{1,0:T(8,128)(2,1)} %get-tuple-element.24), channel_id=1, source_target_pairs={{0,8},{4,12},{8,0},{12,4},{1,9},{5,13},{9,1},{13,5},{2,10},{6,14},... | collective-permute-start | bytes 2359304 | tf_op jit(solution)/shard_map/ppermute | solution.py:219
  82.7 20.6 %collective-permute-start.17 = (bf16[48,8192]{1,0:T(8,128)(2,1)}, bf16[48,8192]{1,0:T(8,128)(2,1)}, u32[]{:S(2)}, u32[]{:S(2)}) collective-permute-start(bf16[48,8192]{1,0:T(8,128)(2,1)} %add_convert_fusion.5), channel_id=1, source_target_pairs={{0,1},{4,5},{8,9},{12,13},{16,17},{20,21},{24,25},{28,29}} | collective-permute-start | bytes 2359304 | tf_op jit(solution)/shard_map/ppermute | solution.py:242
  87.1 31.5 %collective-permute-start.10 = (bf16[48,8192]{1,0:T(8,128)(2,1)}, bf16[48,8192]{1,0:T(8,128)(2,1)S(1)}, u32[]{:S(2)}, u32[]{:S(2)}) collective-permute-start(bf16[48,8192]{1,0:T(8,128)(2,1)} %copy-done.2), channel_id=1, source_target_pairs={{0,8},{4,12},{8,0},{12,4},{1,9},{5,13},{9,1},{13,5},{2,10},{6,14},... | collective-permute-start | bytes 2359304 | tf_op jit(solution)/shard_map/ppermute | solution.py:219
  88.6 16.5 %collective-permute-start.20 = (bf16[48,8192]{1,0:T(8,128)(2,1)}, bf16[48,8192]{1,0:T(8,128)(2,1)S(1)}, u32[]{:S(2)}, u32[]{:S(2)}) collective-permute-start(bf16[48,8192]{1,0:T(8,128)(2,1)} %add_convert_fusion.5), channel_id=1, source_target_pairs={{3,2},{7,6},{11,10},{15,14},{19,18},{23,22},{27,26},{31,30}} | collective-permute-start | bytes 2359304 | tf_op jit(solution)/shard_map/ppermute | solution.py:242
  105.5 13.1 %collective-permute-start.21 = (bf16[48,8192]{1,0:T(8,128)(2,1)S(1)}, bf16[48,8192]{1,0:T(8,128)(2,1)S(1)}, u32[]{:S(2)}, u32[]{:S(2)}) collective-permute-start(bf16[48,8192]{1,0:T(8,128)(2,1)S(1)} %add_convert_fusion.2), channel_id=1, source_target_pairs={{2,1},{3,2},{6,5},{7,6},{10,9},{11,10},{14,13},{15,14},{18,17},{19... | collective-permute-start | bytes 2359304 | tf_op jit(solution)/shard_map/ppermute | solution.py:242
  106.2 21.1 %collective-permute-start.18 = (bf16[48,8192]{1,0:T(8,128)(2,1)S(1)}, bf16[48,8192]{1,0:T(8,128)(2,1)S(1)}, u32[]{:S(2)}, u32[]{:S(2)}) collective-permute-start(bf16[48,8192]{1,0:T(8,128)(2,1)S(1)} %get-tuple-element.29), channel_id=1, source_target_pairs={{0,1},{1,2},{4,5},{5,6},{8,9},{9,10},{12,13},{13,14},{16,17},{17,1... | collective-permute-start | bytes 2359304 | tf_op jit(solution)/shard_map/ppermute | solution.py:242
  111.5 23.2 %collective-permute-start.9 = (bf16[48,8192]{1,0:T(8,128)(2,1)S(1)}, bf16[48,8192]{1,0:T(8,128)(2,1)S(1)}, u32[]{:S(2)}, u32[]{:S(2)}) collective-permute-start(bf16[48,8192]{1,0:T(8,128)(2,1)S(1)} %get-tuple-element.20), channel_id=1, source_target_pairs={{0,8},{4,12},{8,0},{12,4},{1,9},{5,13},{9,1},{13,5},{2,10},{6,14},... | collective-permute-start | bytes 2359304 | tf_op jit(solution)/shard_map/ppermute | solution.py:219
  128.0 19.4 %collective-permute-start.19 = (bf16[48,8192]{1,0:T(8,128)(2,1)S(1)}, bf16[48,8192]{1,0:T(8,128)(2,1)S(1)}, u32[]{:S(2)}, u32[]{:S(2)}) collective-permute-start(bf16[48,8192]{1,0:T(8,128)(2,1)S(1)} %get-tuple-element.33), channel_id=1, source_target_pairs={{0,1},{1,2},{2,3},{4,5},{5,6},{6,7},{8,9},{9,10},{10,11},{12,13},{... | collective-permute-start | bytes 2359304 | tf_op jit(solution)/shard_map/ppermute | solution.py:242
  132.5 19.4 %collective-permute-start.22 = (bf16[48,8192]{1,0:T(8,128)(2,1)S(1)}, bf16[48,8192]{1,0:T(8,128)(2,1)S(1)}, u32[]{:S(2)}, u32[]{:S(2)}) collective-permute-start(bf16[48,8192]{1,0:T(8,128)(2,1)S(1)} %get-tuple-element.34), channel_id=1, source_target_pairs={{1,0},{2,1},{3,2},{5,4},{6,5},{7,6},{9,8},{10,9},{11,10},{13,12},{... | collective-permute-start | bytes 2359304 | tf_op jit(solution)/shard_map/ppermute | solution.py:242

commit v2 on v0

v2 whole, which is shorter than its diff:
```python
from functools import partial
import math

import jax
import jax.numpy as jnp
import numpy as np
from jax import lax
from jax.experimental import pallas as pl
from jax.experimental.pallas import tpu as pltpu
from jax.sharding import PartitionSpec as P

QUERY_HEAD_COUNT = 64
KEY_VALUE_HEADS = 8
HEAD_SIZE = 128
SLAB_REACH = 4

MASKED = -1e30
F32 = jnp.float32
BF16 = jnp.bfloat16
VMEM = pl.BlockSpec(memory_space=pltpu.VMEM)
SMEM = pl.BlockSpec(memory_space=pltpu.SMEM)
HBM = pl.BlockSpec(memory_space=pl.ANY)
LIMIT = pltpu.CompilerParams(vmem_limit_bytes=28 << 20)
TILE = 1024


def destination_order(count):
    table = []
    for z in range(count):
        due = {d: (count - 1 - d + z if d > z else count - 1 - z + d) for d in range(count)}
        due[z] = count
        table.append(sorted(range(count), key=lambda d: (due[d], -d if z < count // 2 else d)))
    return np.array(table, np.int32)


def in_vmem(array):
    return pltpu.with_memory_space_constraint(array, pltpu.VMEM)


def joined(parts):
    return parts[0] if len(parts) == 1 else jnp.concatenate(parts, axis=0)


def attend_kernel(info, key_doc, doc_col, *refs, slabs, heads, share, pieces, offset, columns_x, per_shard, fetched):
    refs = list(refs)
    take = lambda n: [refs.pop(0) for _ in range(n)]
    now, before, queries, weights = take(slabs), take(slabs), take(slabs), take(fetched)
    (keep, send), copied = take(2), take(fetched)
    key_rows, value_rows = take(2)
    copies = [pltpu.make_async_copy(w, c, refs[0].at[n]) for n, (w, c) in enumerate(zip(weights, copied))]
    for copy in copies:
        copy.start()
    scale = math.log2(math.e) / math.sqrt(HEAD_SIZE)
    block = doc_col.shape[1]
    span = SLAB_REACH * block
    rows = share * pieces
    z, core, x = info[0], info[1], info[2]
    starts = [pl.multiple_of(info[3 + n], 16) for n in range(pieces)]
    column = lax.broadcasted_iota(jnp.int32, (share, span), 1) - (SLAB_REACH - 1) * block
    row = lax.broadcasted_iota(jnp.int32, (share, span), 0)
    causal = joined([column - row <= start for start in starts])
    for k in range(slabs):
        slab = lax.rem(z - k + slabs, slabs)
        for o in range(SLAB_REACH):
            place = slice((SLAB_REACH - 1 - o) * block, (SLAB_REACH - o) * block)
            held = (k + o) % slabs

            def fill(source):
                key_rows[place, :] = source[:block, :]
                value_rows[place, :] = source[block : 2 * block, :]

            if o == 0:
                fill(now[held])
            else:
                pl.when(slab >= o)(partial(fill, now[held]))
                pl.when(slab < o)(partial(fill, before[held]))
        query_doc = joined([doc_col[slab, pl.ds(start, share), :] for start in starts])
        visible = causal & (query_doc == key_doc[slab])
        scores = lax.dot_general(
            queries[k][offset : offset + heads * rows, :],
            key_rows[...],
            (((1,), (1,)), ((), ())),
            preferred_element_type=F32,
        ).reshape(heads, rows, span)
        scores = jnp.where(visible[None], scores, MASKED)
        largest = jnp.max(scores, axis=-1, keepdims=True)
        terms = jnp.exp2((scores - largest) * scale)
        normalizer = jnp.sum(terms, axis=-1, keepdims=True)
        weighted = jnp.dot(
            terms.reshape(heads * rows, span).astype(BF16), value_rows[...], preferred_element_type=F32
        ).reshape(heads, rows, HEAD_SIZE)
        result = (weighted / normalizer).astype(BF16)
        result = jnp.concatenate([result[h] for h in range(heads)], axis=1)
        target = lax.div(slab, per_shard)
        slot = lax.rem(lax.div(target, 2) - x + columns_x, columns_x) * per_shard + lax.rem(slab, per_shard)

        @pl.when(lax.rem(target, 2) == core)
        def _():
            keep[slot] = result

        @pl.when(lax.rem(target, 2) != core)
        def _():
            send[slot] = result

    for copy in copies:
        copy.wait()


def attend(info, docs, now, before, queries, weights, *, heads, share, pieces, offset, columns_x, per_shard):
    slabs, block = docs[1].shape[:2]
    rows = share * pieces
    out = jax.ShapeDtypeStruct((slabs // 2, rows, heads * HEAD_SIZE), BF16)
    terms = slabs * rows * SLAB_REACH * block * heads
    fetched = len(weights)
    return pl.pallas_call(
        partial(
            attend_kernel,
            slabs=slabs,
            heads=heads,
            share=share,
            pieces=pieces,
            offset=offset,
            columns_x=columns_x,
            per_shard=per_shard,
            fetched=fetched,
        ),
        out_shape=[out, out] + [pltpu.VMEM(w.shape, w.dtype) for w in weights],
        in_specs=[SMEM] + [VMEM] * (2 + 3 * slabs) + [HBM] * fetched,
        out_specs=[VMEM] * (2 + fetched),
        scratch_shapes=[pltpu.VMEM((SLAB_REACH * block, HEAD_SIZE), BF16)] * 2
        + [pltpu.SemaphoreType.DMA((fetched,))] * (fetched > 0),
        compiler_params=LIMIT,
        cost_estimate=pl.CostEstimate(
            flops=4 * terms * HEAD_SIZE, bytes_accessed=sum(w.size * 2 for w in weights), transcendentals=terms
        ),
        name="attend",
    )(info, *docs, *now, *before, *queries, *weights)


def first_half_kernel(rows_here, weight, fetch, total, fetched, semaphore):
    copy = pltpu.make_async_copy(fetch, fetched, semaphore)
    copy.start()
    for n in range(0, total.shape[1], TILE):
        total[:, n : n + TILE] = jnp.dot(rows_here[...], weight[:, n : n + TILE], preferred_element_type=F32)
    copy.wait()


def first_half(rows_here, weight, fetch):
    count, depth = rows_here.shape
    width = weight.shape[1]
    return pl.pallas_call(
        first_half_kernel,
        out_shape=[pltpu.VMEM((count, width), F32), pltpu.VMEM(fetch.shape, fetch.dtype)],
        in_specs=[VMEM, VMEM, HBM],
        out_specs=[VMEM, VMEM],
        scratch_shapes=[pltpu.SemaphoreType.DMA],
        compiler_params=LIMIT,
        cost_estimate=pl.CostEstimate(
            flops=2 * count * depth * width, bytes_accessed=2 * depth * width, transcendentals=0
        ),
        name="first_half",
    )(rows_here, in_vmem(weight), fetch)


def project_kernel(*refs, terms, begun, share, halves):
    lhs, rhs, (*start, ) = refs[:terms], refs[terms : 2 * terms], refs[2 * terms : 2 * terms + begun]
    outs = refs[2 * terms + begun :]
    half = outs[0].shape[1]
    for n in range(0, half * halves, TILE):
        total = sum(
            jnp.dot(a[...], w[:, n : n + TILE], preferred_element_type=F32) for a, w in zip(lhs, rhs)
        )
        for s in start:
            total = total + s[:, n : n + TILE]
        for m in range(total.shape[0] // share):
            outs[m * halves + n // half][:, n % half : n % half + TILE] = total[m * share : (m + 1) * share].astype(BF16)


def project(lhs, rhs, start, share, halves):
    count, depth = lhs[0].shape
    width = rhs[0].shape[1]
    return pl.pallas_call(
        partial(project_kernel, terms=len(lhs), begun=len(start), share=share, halves=halves),
        out_shape=[jax.ShapeDtypeStruct((share, width // halves), BF16)] * (count // share * halves),
        in_specs=[VMEM] * (2 * len(lhs) + len(start)),
        out_specs=[VMEM] * (count // share * halves),
        compiler_params=LIMIT,
        cost_estimate=pl.CostEstimate(
            flops=2 * len(lhs) * count * depth * width, bytes_accessed=2 * count * width, transcendentals=0
        ),
        name="project",
    )(*lhs, *[in_vmem(w) for w in rhs], *[in_vmem(s) for s in start])


def on_device(queries, keys, values, doc_ids, block_mask, out_weight, *, order):
    groups, head_shards, slabs = (lax.axis_size(a) for a in ("srv", "head", "wsh"))
    srv, head, z = (lax.axis_index(a) for a in ("srv", "head", "wsh"))
    core, x, columns_x = head % 2, head // 2, head_shards // 2
    block = queries.shape[0]
    kv_local = keys.shape[1] // HEAD_SIZE
    heads = queries.shape[1] // HEAD_SIZE // slabs
    share = block // head_shards
    per_shard = slabs // head_shards
    table = jnp.asarray(order)
    staged = per_shard == 1
    stages = [[0], list(range(1, slabs))] if staged else [list(range(slabs))]
    halves = 2

    def kv_for(target):
        first = (target * kv_local // slabs) * HEAD_SIZE
        return [lax.dynamic_slice(a, (0, first), (block, HEAD_SIZE)) for a in (keys, values)]

    def query_rows(target, stage):
        pieces = [(table[target, i] * share, share) for i in stage] if staged else [(0, block)]
        return [
            lax.dynamic_slice(queries, (start, (target * heads + h) * HEAD_SIZE), (count, HEAD_SIZE))
            for h in range(heads)
            for start, count in pieces
        ]

    def around(array, k):
        return lax.ppermute(array, "wsh", [(i, (i + k) % slabs) for i in range(slabs)])

    siblings = [(h, h ^ 1) for h in range(head_shards)]

    def load(k):
        target = (z + k) % slabs
        return jnp.concatenate(kv_for(target) + query_rows(target, stages[0]), axis=0)

    loads = [load(0)] + [around(load(k), k) for k in range(1, slabs)]
    before = [
        lax.ppermute(a[: 2 * block], "srv", [(g, g + 1) for g in range(groups - 1)]) for a in loads
    ]
    weight_sibling = lax.ppermute(out_weight, "head", siblings)
    stage_queries = [loads]
    for stage in stages[1:]:
        rest = [jnp.concatenate(query_rows((z + k) % slabs, stage), axis=0) for k in range(slabs)]
        rest, loads = lax.optimization_barrier((rest, loads))
        stage_queries.append([rest[0]] + [around(rest[k], k) for k in range(1, slabs)])

    own_docs = lax.dynamic_slice(doc_ids, (srv * slabs * block,), (slabs * block,)).reshape(slabs, block)
    reach = SLAB_REACH - 1
    padded = jnp.concatenate([jnp.full((reach * block,), -1, jnp.int32), doc_ids])
    window = lax.dynamic_slice(padded, (srv * slabs * block,), ((slabs + reach) * block,)).reshape(-1, block)
    opened = lax.dynamic_slice(block_mask, (srv * slabs, 0), (slabs, SLAB_REACH))
    key_doc = jnp.stack(
        [
            jnp.where(opened[:, reach - j, None] > 0, window[j : j + slabs], -1)
            for j in range(SLAB_REACH)
        ],
        axis=1,
    ).reshape(slabs, 1, SLAB_REACH * block)
    docs = (key_doc, own_docs[..., None])

    partials = []
    weight_near = None
    for n, (stage, arrived) in enumerate(zip(stages, stage_queries)):
        if staged:
            starts = [table[z, i] * share for i in stage]
            sizes = dict(share=share, pieces=len(stage))
        else:
            starts = [jnp.int32(0)]
            sizes = dict(share=block, pieces=1)
        info = jnp.stack([z, core, x] + starts).astype(jnp.int32)
        fetch = [] if n else [out_weight] if staged else [out_weight, weight_sibling]
        keep, send, *fetched = attend(
            info,
            docs,
            loads,
            before,
            arrived,
            fetch,
            heads=heads,
            offset=2 * block if n == 0 else 0,
            columns_x=columns_x,
            per_shard=per_shard,
            **sizes,
        )
        if not staged:
            keep, send = (
                jnp.concatenate(
                    [
                        lax.dynamic_slice_in_dim(a.reshape(columns_x, -1, a.shape[-1]), table[z, i] * share, share, 1)
                        for i in stage
                    ],
                    axis=1,
                )
                for a in (keep, send)
            )
        theirs = lax.ppermute(send, "head", siblings)
        keep, theirs = (a.reshape(-1, a.shape[-1]) for a in (keep, theirs))
        if n == 0 and staged:
            weight_near = fetched[0]
            begun, weight_far = first_half(keep, weight_near, weight_sibling)
            results = project([theirs], [weight_far], [begun], share, halves)
        else:
            if fetched:
                weight_near, weight_far = fetched
            results = project([keep, theirs], [weight_near, weight_far], [], share, halves)
        for m in range(len(stage)):
            partials.append(
                [
                    [results[(k * len(stage) + m) * halves + half] for half in range(halves)]
                    for k in range(columns_x)
                ]
            )

    sums = [[] for _ in range(halves)]
    for piece in partials:
        for half in range(halves):
            total = piece[0][half].astype(F32)
            for k in range(1, columns_x):
                route = [(h, (h + 2 * k) % head_shards) for h in range(head_shards)]
                total = total + lax.ppermute(piece[k][half], "head", route).astype(F32)
            sums[half].append(total.astype(BF16))

    position = np.argsort(order, axis=1)

    def senders(direction, t):
        found = {}
        for i in range(slabs):
            step = i if direction > 0 else slabs - 1 - i
            if step <= t:
                d = slabs - 1 - t + step
                found[i] = int(position[i, d if direction > 0 else slabs - 1 - d])
        return found

    def message(which, own, arrived):
        picked = None
        for i, piece in which.items():
            picked = own[piece] if picked is None else jnp.where(z == i, own[piece], picked)
        if arrived is None:
            return picked
        return (picked.astype(F32) + arrived.astype(F32)).astype(BF16)

    arrived = [{1: None, -1: None} for _ in range(halves)]
    for t in range(slabs - 1):
        for half in range(halves):
            last = arrived[half]
            found = {direction: senders(direction, t) for direction in (1, -1)}
            routes = {direction: [(i, i + direction) for i in found[direction]] for direction in found}
            for direction in found:
                last[direction] = lax.ppermute(
                    message(found[direction], sums[half], last[direction]), "wsh", routes[direction]
                )
    outs = []
    for half in range(halves):
        total = sums[half][-1].astype(F32)
        if slabs > 1:
            total = total + arrived[half][1].astype(F32) + arrived[half][-1].astype(F32)
        outs.append(total.astype(BF16))
    return jnp.concatenate(outs, axis=1)


def solution(mesh):
    in_specs = (
        P(("srv", "wsh"), "head"),
        P(("srv", "wsh"), "head"),
        P(("srv", "wsh"), "head"),
        P(),
        P(),
        P(("head", "wsh"), None),
    )
    out_specs = P(("srv", "head", "wsh"), None)
    return jax.shard_map(
        partial(on_device, order=destination_order(mesh.shape["wsh"])),
        mesh=mesh,
        in_specs=in_specs,
        out_specs=out_specs,
        check_vma=False,
    )
```

time: 232 us -> 215 us (0.927)
  waiting for transfers between devices: 142 us -> 79.4 us
  starting transfers between devices: 20.7 us -> 62 us
  local copies, waits for them, and re-layouts: 5.67 us -> 35.5 us
  blocking collectives: 27.1 us -> 0 us
  Pallas kernels: 0 us -> 19.8 us
  matrix products: 16 us -> 0 us
  between operations: 16.1 us -> 13.3 us
    reduce_scatter x1 -> x0, waiting for transfers between devices: 142 us -> none  [on_device(): lax.psum_scatter(jnp.dot(spread, out_weight, preferred_element_type=jnp.f...]
    ppermute x6 -> x33, waiting for transfers between devices: 0.02 us -> 79.4 us  [the longest x8 39.8 us: on_device(): total = total + lax.ppermute(piece[k][half], 'head', route).astype(F32)]
    ppermute x6 -> x33, starting transfers between devices: 20.7 us -> 62 us  [the longest x12 35.8 us: on_device(): lax.ppermute(message(found[direction], sums[half], last[direction]), 'wsh...]
    unnamed x3 -> x31, local copies, waits for them, and re-layouts: 1.29 us -> 30.7 us
    all_to_all x1 -> x0, blocking collectives: 27.1 us -> none  [on_device(): lax.all_to_all(attention, 'wsh', split_axis=1, concat_axis=0, tiled=True)]
    pallas_call x0 -> x5, Pallas kernels: none -> 19.8 us  [the longest x2 9.83 us: attend(): pl.pallas_call(partial(attend_kernel, slabs=slabs, heads=heads, share=sha...]
    dot_general x3 -> x0, matrix products: 16 us -> none  [the longest x1 13.1 us: on_device(): jnp.dot(spread, out_weight, preferred_element_type=jnp.float32)]
  transfers between devices with their start and end apart: 7 -> 33, of which waited for: 1 -> 12; matrix products, arithmetic and copies ran while one was open for 5% -> 10% of each run, Pallas kernels for 0% -> 9%
where the time goes in v2:
time: 215 us; the launch traced here: 213 us
  waiting for transfers between devices  79.4 us (37%)
  starting transfers between devices  62 us (29%)
  local copies, waits for them, and re-layouts  35.5 us (17%)
  Pallas kernels  19.8 us (9%)
  between operations  13.3 us (6%)
  other arithmetic  3.18 us (1%)
    ppermute x8, waiting for transfers between devices, on_device(): total = total + lax.ppermute(piece[k][half], 'head', route).astype(F32)  39.8 us
    ppermute x12, starting transfers between devices, on_device(): lax.ppermute(message(found[direction], sums[half], last[direction]), 'wsh...  35.8 us
    unnamed x31, local copies, waits for them, and re-layouts  30.7 us
    ppermute x12, waiting for transfers between devices, on_device(): lax.ppermute(message(found[direction], sums[half], last[direction]), 'wsh...  26.3 us
    ppermute x6, waiting for transfers between devices, around(): lax.ppermute(array, 'wsh', [(i, (i + k) % slabs) for i in range(slabs)])  11.6 us
    pallas_call x2, Pallas kernels, attend(): pl.pallas_call(partial(attend_kernel, slabs=slabs, heads=heads, share=sha...  9.83 us
    ppermute x4, starting transfers between devices, on_device(): lax.ppermute(a[:2 * block], 'srv', [(g, g + 1) for g in range(groups - 1)])  9.02 us
    ppermute x6, starting transfers between devices, around(): lax.ppermute(array, 'wsh', [(i, (i + k) % slabs) for i in range(slabs)])  8.78 us
  transfers between devices with their start and end apart: 33, of which 12 were waited for; matrix products, arithmetic and copies ran while one was open for 10% of the time, Pallas kernels for 9%

profile of v2, /device:TPU:0, one launch (start us, length us, event | category | flops | bytes accessed | tf_op | source)
XLA Modules:
  0.0 213.2 jit_solution(5190131436088851554)
XLA Ops:
  0.5 0.9 constant_dynamic-update-slice_fusion.71
  1.4 0.9 constant_dynamic-update-slice_fusion.70
  2.3 4.6 %collective-permute-start.3 = (bf16[384,128]{1,0:T(8,128)(2,1)S(1)}, bf16[384,128]{1,0:T(8,128)(2,1)S(1)}, u32[]{:S(2)}, u32[]{:S(2)}) collective-permute-start(bf16[384,128]{1,0:T(8,128)(2,1)S(1)} %pad_maximum_fusion.1), channel_id=1, source_target_pairs={{0,16},{1,17},{2,18},{3,19},{4,20},{5,21},{6,22},{7,23},{8,24},{9,... | collective-permute-start | bytes 294920 | tf_op jit(solution)/shard_map/ppermute | solution.py:232
  7.0 2.2 %constant_dynamic-slice_fusion.12 = (s32[1,1]{1,0:T(1,128)}, s32[1,1]{1,0:T(1,128)}, s32[1,1]{1,0:T(1,128)}, s32[1,1]{1,0:T(1,128)}, s32[1,1]{1,0:T(1,128)}, /*i...) fusion(s32[4,4]{1,0:T(4,128)} %constant.147.clone, ...), kind=kLoop, calls=%fused_computation.121 | loop fusion | bytes 180 | tf_op jit(solution)/shard_map/dynamic_slice | solution.py:259
  29.2 0.8 constant_dynamic-update-slice_fusion.68
  30.1 0.8 constant_dynamic-update-slice_fusion.67
  30.9 0.8 constant_dynamic-update-slice_fusion.66
  31.8 3.7 %collective-permute-start.2 = (bf16[576,128]{1,0:T(8,128)(2,1)S(1)}, bf16[576,128]{1,0:T(8,128)(2,1)S(1)}, u32[]{:S(2)}, u32[]{:S(2)}) collective-permute-start(bf16[576,128]{1,0:T(8,128)(2,1)S(1)} %get-tuple-element.79), channel_id=1, source_target_pairs={{0,3},{1,0},{2,1},{3,2},{4,7},{5,4},{6,5},{7,6},{8,11},{9,8},{10,9... | collective-permute-start | bytes 442376 | tf_op jit(solution)/shard_map/ppermute | solution.py:222
  35.4 1.0 collective-permute-start
  36.5 1.0 fusion
  37.7 2.1 collective-permute-done.2.refs_3_.refs_11_
  39.7 1.3 collective-permute-start.6
  41.3 6.9 %collective-permute-done.1.refs_2_.refs_10_ = bf16[576,128]{1,0:T(8,128)(2,1)S(1)} collective-permute-done((bf16[576,128]{1,0:T(8,128)(2,1)S(1)}, bf16[576,128]{1,0:T(8,128)(2,1)S(1)}, u32[]{:S(2)}, u32[]{:S(2)}) %collective-permute-start.1) | collective-permute-done | bytes 147488 | tf_op jit(solution)/shard_map/ppermute | solution.py:222
  48.2 1.6 collective-permute-start.5
  49.9 1.8 collective-permute-start.8
  51.7 2.2 %collective-permute-start.9 = (bf16[576,128]{1,0:T(8,128)(2,1)S(1)}, bf16[576,128]{1,0:T(8,128)(2,1)S(1)}, u32[]{:S(2)}, u32[]{:S(2)}) collective-permute-start(bf16[576,128]{1,0:T(8,128)(2,1)S(1)} %get-tuple-element.43), channel_id=1, source_target_pairs={{0,3},{1,0},{2,1},{3,2},{4,7},{5,4},{6,5},{7,6},{8,11},{9,8},{10,9... | collective-permute-start | bytes 442376 | tf_op jit(solution)/shard_map/ppermute | solution.py:222
  56.6 1.6 collective-permute-start.4
  58.7 1.7 collective-permute-done.4.refs_5_
  60.4 2.7 %collective-permute-done.8.refs_10_ = bf16[576,128]{1,0:T(8,128)(2,1)S(1)} collective-permute-done((bf16[576,128]{1,0:T(8,128)(2,1)S(1)}, bf16[576,128]{1,0:T(8,128)(2,1)S(1)}, u32[]{:S(2)}, u32[]{:S(2)}) %collective-permute-start.8) | collective-permute-done | bytes 147488 | tf_op jit(solution)/shard_map/ppermute | solution.py:222
  63.1 6.1 %attend.2 = (bf16[2,144,512]{2,1,0:T(8,128)(2,1)S(1)}, bf16[2,144,512]{2,1,0:T(8,128)(2,1)S(1)}) custom-call(s32[6]{0:T(128)S(1)} %stack.43.info, s32[4,1,768]{2,1,0:T(1,128)S(1)} %reshape.232.key_doc, s32[4,192,1]{2,1,0:T(8,128)S(1)} %broadcast_in_dim_reshape.4.doc_col, bf16[576,128]{1,0:T(8,128)(2,1)S(1)} %get-tuple-element.36.refs_0_.refs_8_, ...), custom_call_target="tpu_custom_call" | custom-call | flops 905969664 | tf_op jit(solution)/shard_map/attend/pallas_call | solution.py:115
  69.3 3.4 %copy-done.1 = bf16[512,8192]{1,0:T(8,128)(2,1)S(1)} copy-done((bf16[512,8192]{1,0:T(8,128)(2,1)S(1)}, bf16[512,8192]{1,0:T(8,128)(2,1)}, u32[]{:S(2)}) %copy-start.1) | copy-done | bytes 8388632
  72.7 3.7 %attend.3 = (bf16[2,48,512]{2,1,0:T(8,128)(2,1)S(1)}, bf16[2,48,512]{2,1,0:T(8,128)(2,1)S(1)}, bf16[512,8192]{1,0:T(8,128)(2,1)S(1)}) custom-call(s32[4]{0:T(128)S(1)} %pad_add_fusion.1.info, s32[4,1,768]{2,1,0:T(1,128)S(1)} %reshape.232.key_doc, s32[4,192,1]{2,1,0:T(8,128)S(1)} %broadcast_in_dim_reshape.4.doc_col, ...), custom_call_target="tpu_custom_call" | custom-call | flops 301989888 | bytes 8388608 | tf_op jit(solution)/shard_map/attend/pallas_call | solution.py:115
  76.5 3.3 %copy-done.2 = bf16[512,8192]{1,0:T(8,128)(2,1)} copy-done((bf16[512,8192]{1,0:T(8,128)(2,1)}, bf16[512,8192]{1,0:T(8,128)(2,1)S(1)}, u32[]{:S(2)}) %copy-start.2) | copy-done | bytes 8388632
  80.2 3.4 %copy-done.3 = bf16[512,8192]{1,0:T(8,128)(2,1)S(1)} copy-done((bf16[512,8192]{1,0:T(8,128)(2,1)S(1)}, bf16[512,8192]{1,0:T(8,128)(2,1)}, u32[]{:S(2)}) %copy-start.3) | copy-done | bytes 8388632
  83.6 3.4 %first_half.1 = (f32[96,8192]{1,0:T(8,128)S(1)}, bf16[512,8192]{1,0:T(8,128)(2,1)S(1)}) custom-call(bf16[96,512]{1,0:T(8,128)(2,1)S(1)} %bitcast.35, bf16[512,8192]{1,0:T(8,128)(2,1)S(1)} %copy-done.3, bf16[512,8192]{1,0:T(8,128)(2,1)} %collective-permute-done.11.fetch), custom_call_target="tpu_custom_call" | custom-call | flops 805306368 | bytes 8388608 | tf_op jit(solution)/shard_map/first_half/pallas_call | solution.py:151
  87.0 1.6 project.3
  88.6 3.7 %copy-done.5 = bf16[512,8192]{1,0:T(8,128)(2,1)} copy-done((bf16[512,8192]{1,0:T(8,128)(2,1)}, bf16[512,8192]{1,0:T(8,128)(2,1)S(1)}, u32[]{:S(2)}) %copy-start.5) | copy-done | bytes 8388632
  92.3 1.5 collective-permute-start.16
  93.8 3.4 %copy-done.6 = bf16[512,8192]{1,0:T(8,128)(2,1)S(1)} copy-done((bf16[512,8192]{1,0:T(8,128)(2,1)S(1)}, bf16[512,8192]{1,0:T(8,128)(2,1)}, u32[]{:S(2)}) %copy-start.6) | copy-done | bytes 8388632
  97.2 5.0 %project.2 = (bf16[48,4096]{1,0:T(8,128)(2,1)S(1)}, bf16[48,4096]{1,0:T(8,128)(2,1)S(1)}, bf16[48,4096]{1,0:T(8,128)(2,1)S(1)}, bf16[48,4096]{1,0:T(8,128)(2,1)S...) custom-call(bf16[288,512]{1,0:T(8,128)(2,1)S(1)} %bitcast.38, ...), custom_call_target="tpu_custom_call" | custom-call | flops 4831838208 | bytes 4718592 | tf_op jit(solution)/shard_map/project/pallas_call | solution.py:182
  102.9 1.5 collective-permute-start.13
  104.9 1.5 collective-permute-start.23
  107.0 39.7 %collective-permute-done.26 = bf16[48,4096]{1,0:T(8,128)(2,1)S(1)} collective-permute-done((bf16[48,4096]{1,0:T(8,128)(2,1)S(1)}, bf16[48,4096]{1,0:T(8,128)(2,1)S(1)}, u32[]{:S(2)}, u32[]{:S(2)}) %collective-permute-start.26) | collective-permute-done | bytes 393248 | tf_op jit(solution)/shard_map/ppermute | solution.py:314
  146.8 4.7 %collective-permute-start.17 = (bf16[48,4096]{1,0:T(8,128)(2,1)S(1)}, bf16[48,4096]{1,0:T(8,128)(2,1)S(1)}, u32[]{:S(2)}, u32[]{:S(2)}) collective-permute-start(bf16[48,4096]{1,0:T(8,128)(2,1)S(1)} %add_convert_fusion.14), channel_id=1, source_target_pairs={{0,1},{4,5},{8,9},{12,13},{16,17},{20,21},{24,25},{28,29}} | collective-permute-start | bytes 1179656 | tf_op jit(solution)/shard_map/ppermute | solution.py:343
  152.2 6.6 %collective-permute-done.17 = bf16[48,4096]{1,0:T(8,128)(2,1)S(1)} collective-permute-done((bf16[48,4096]{1,0:T(8,128)(2,1)S(1)}, bf16[48,4096]{1,0:T(8,128)(2,1)S(1)}, u32[]{:S(2)}, u32[]{:S(2)}) %collective-permute-start.17) | collective-permute-done | bytes 393248 | tf_op jit(solution)/shard_map/ppermute | solution.py:343
  158.8 4.4 %collective-permute-start.27 = (bf16[48,4096]{1,0:T(8,128)(2,1)S(1)}, bf16[48,4096]{1,0:T(8,128)(2,1)S(1)}, u32[]{:S(2)}, u32[]{:S(2)}) collective-permute-start(bf16[48,4096]{1,0:T(8,128)(2,1)S(1)} %add_convert_fusion.5), channel_id=1, source_target_pairs={{0,1},{4,5},{8,9},{12,13},{16,17},{20,21},{24,25},{28,29}} | collective-permute-start | bytes 1179656 | tf_op jit(solution)/shard_map/ppermute | solution.py:343
  164.2 5.5 %collective-permute-done.27 = bf16[48,4096]{1,0:T(8,128)(2,1)S(1)} collective-permute-done((bf16[48,4096]{1,0:T(8,128)(2,1)S(1)}, bf16[48,4096]{1,0:T(8,128)(2,1)S(1)}, u32[]{:S(2)}, u32[]{:S(2)}) %collective-permute-start.27) | collective-permute-done | bytes 393248 | tf_op jit(solution)/shard_map/ppermute | solution.py:343
  170.6 4.4 %collective-permute-start.18 = (bf16[48,4096]{1,0:T(8,128)(2,1)S(1)}, bf16[48,4096]{1,0:T(8,128)(2,1)S(1)}, u32[]{:S(2)}, u32[]{:S(2)}) collective-permute-start(bf16[48,4096]{1,0:T(8,128)(2,1)S(1)} %get-tuple-element.67), channel_id=1, source_target_pairs={{0,1},{1,2},{4,5},{5,6},{8,9},{9,10},{12,13},{13,14},{16,17},{17,1... | collective-permute-start | bytes 1179656 | tf_op jit(solution)/shard_map/ppermute | solution.py:343
  176.6 3.9 %collective-permute-done.18 = bf16[48,4096]{1,0:T(8,128)(2,1)S(1)} collective-permute-done((bf16[48,4096]{1,0:T(8,128)(2,1)S(1)}, bf16[48,4096]{1,0:T(8,128)(2,1)S(1)}, u32[]{:S(2)}, u32[]{:S(2)}) %collective-permute-start.18) | collective-permute-done | bytes 393248 | tf_op jit(solution)/shard_map/ppermute | solution.py:343
  180.5 4.4 %collective-permute-start.28 = (bf16[48,4096]{1,0:T(8,128)(2,1)S(1)}, bf16[48,4096]{1,0:T(8,128)(2,1)S(1)}, u32[]{:S(2)}, u32[]{:S(2)}) collective-permute-start(bf16[48,4096]{1,0:T(8,128)(2,1)S(1)} %get-tuple-element.69), channel_id=1, source_target_pairs={{0,1},{1,2},{4,5},{5,6},{8,9},{9,10},{12,13},{13,14},{16,17},{17,1... | collective-permute-start | bytes 1179656 | tf_op jit(solution)/shard_map/ppermute | solution.py:343
  186.0 4.9 %collective-permute-start.19 = (bf16[48,4096]{1,0:T(8,128)(2,1)S(1)}, bf16[48,4096]{1,0:T(8,128)(2,1)S(1)}, u32[]{:S(2)}, u32[]{:S(2)}) collective-permute-start(bf16[48,4096]{1,0:T(8,128)(2,1)S(1)} %get-tuple-element.75), channel_id=1, source_target_pairs={{0,1},{1,2},{2,3},{4,5},{5,6},{6,7},{8,9},{9,10},{10,11},{12,13},{... | collective-permute-start | bytes 1179656 | tf_op jit(solution)/shard_map/ppermute | solution.py:343
  190.9 2.1 collective-permute-done.28
  193.0 1.3 collective-permute-start.22
  194.6 7.7 %collective-permute-start.29 = (bf16[48,4096]{1,0:T(8,128)(2,1)S(1)}, bf16[48,4096]{1,0:T(8,128)(2,1)S(1)}, u32[]{:S(2)}, u32[]{:S(2)}) collective-permute-start(bf16[48,4096]{1,0:T(8,128)(2,1)S(1)} %get-tuple-element.77), channel_id=1, source_target_pairs={{0,1},{1,2},{2,3},{4,5},{5,6},{6,7},{8,9},{9,10},{10,11},{12,13},{... | collective-permute-start | bytes 1179656 | tf_op jit(solution)/shard_map/ppermute | solution.py:343
  202.4 1.3 collective-permute-start.32
  203.7 3.6 %collective-permute-done.22 = bf16[48,4096]{1,0:T(8,128)(2,1)S(1)} collective-permute-done((bf16[48,4096]{1,0:T(8,128)(2,1)S(1)}, bf16[48,4096]{1,0:T(8,128)(2,1)S(1)}, u32[]{:S(2)}, u32[]{:S(2)}) %collective-permute-start.22) | collective-permute-done | bytes 393248 | tf_op jit(solution)/shard_map/ppermute | solution.py:343
  207.6 4.4 %collective-permute-done.32 = bf16[48,4096]{1,0:T(8,128)(2,1)S(1)} collective-permute-done((bf16[48,4096]{1,0:T(8,128)(2,1)S(1)}, bf16[48,4096]{1,0:T(8,128)(2,1)S(1)}, u32[]{:S(2)}, u32[]{:S(2)}) %collective-permute-start.32) | collective-permute-done | bytes 393248 | tf_op jit(solution)/shard_map/ppermute | solution.py:343
  212.2 0.9 pad_maximum_fusion
  (85 shorter events, 20.0 us)
Async XLA Ops:
  0.0 37.6 %copy-start = (s32[8,4]{0,1:T(4,128)S(1)}, s32[8,4]{0,1:T(4,128)}, u32[]{:S(2)}) copy-start(s32[8,4]{0,1:T(4,128)} %param.11) | copy-start | bytes 388
  0.0 80.2 %collective-permute-start.11 = (bf16[512,8192]{1,0:T(8,128)(2,1)}, bf16[512,8192]{1,0:T(8,128)(2,1)}, u32[]{:S(2)}, u32[]{:S(2)}) collective-permute-start(bf16[512,8192]{1,0:T(8,128)(2,1)} %refs_12_.1), channel_id=1, source_target_pairs={{0,4},{4,0},{8,12},{12,8},{1,5},{5,1},{9,13},{13,9},{2,6},{6,2},{1... | collective-permute-start | bytes 25165832 | tf_op jit(solution)/shard_map/ppermute | solution.py:234
  2.3 47.5 %collective-permute-start.3 = (bf16[384,128]{1,0:T(8,128)(2,1)S(1)}, bf16[384,128]{1,0:T(8,128)(2,1)S(1)}, u32[]{:S(2)}, u32[]{:S(2)}) collective-permute-start(bf16[384,128]{1,0:T(8,128)(2,1)S(1)} %pad_maximum_fusion.1), channel_id=1, source_target_pairs={{0,16},{1,17},{2,18},{3,19},{4,20},{5,21},{6,22},{7,23},{8,24},{9,... | collective-permute-start | bytes 294920 | tf_op jit(solution)/shard_map/ppermute | solution.py:232
  31.8 8.0 %collective-permute-start.2 = (bf16[576,128]{1,0:T(8,128)(2,1)S(1)}, bf16[576,128]{1,0:T(8,128)(2,1)S(1)}, u32[]{:S(2)}, u32[]{:S(2)}) collective-permute-start(bf16[576,128]{1,0:T(8,128)(2,1)S(1)} %get-tuple-element.79), channel_id=1, source_target_pairs={{0,3},{1,0},{2,1},{3,2},{4,7},{5,4},{6,5},{7,6},{8,11},{9,8},{10,9... | collective-permute-start | bytes 442376 | tf_op jit(solution)/shard_map/ppermute | solution.py:222
  35.4 12.8 %collective-permute-start.1 = (bf16[576,128]{1,0:T(8,128)(2,1)S(1)}, bf16[576,128]{1,0:T(8,128)(2,1)S(1)}, u32[]{:S(2)}, u32[]{:S(2)}) collective-permute-start(bf16[576,128]{1,0:T(8,128)(2,1)S(1)} %get-tuple-element.80), channel_id=1, source_target_pairs={{0,2},{1,3},{2,0},{3,1},{4,6},{5,7},{6,4},{7,5},{8,10},{9,11},{10,... | collective-permute-start | bytes 442376 | tf_op jit(solution)/shard_map/ppermute | solution.py:222
  35.4 14.3 %collective-permute-start = (bf16[576,128]{1,0:T(8,128)(2,1)S(1)}, bf16[576,128]{1,0:T(8,128)(2,1)S(1)}, u32[]{:S(2)}, u32[]{:S(2)}) collective-permute-start(bf16[576,128]{1,0:T(8,128)(2,1)S(1)} %get-tuple-element.81), channel_id=1, source_target_pairs={{0,1},{1,2},{2,3},{3,0},{4,5},{5,6},{6,7},{7,4},{8,9},{9,10},{10,1... | collective-permute-start | bytes 442376 | tf_op jit(solution)/shard_map/ppermute | solution.py:222
  39.7 12.0 %collective-permute-start.6 = (bf16[384,128]{1,0:T(8,128)(2,1)S(1)}, bf16[384,128]{1,0:T(8,128)(2,1)S(1)}, u32[]{:S(2)}, u32[]{:S(2)}) collective-permute-start(bf16[384,128]{1,0:T(8,128)(2,1)S(1)} %slice.96), channel_id=1, source_target_pairs={{0,16},{1,17},{2,18},{3,19},{4,20},{5,21},{6,22},{7,23},{8,24},{9,... | collective-permute-start | bytes 294920 | tf_op jit(solution)/shard_map/ppermute | solution.py:232
  48.2 8.4 %collective-permute-start.5 = (bf16[384,128]{1,0:T(8,128)(2,1)S(1)}, bf16[384,128]{1,0:T(8,128)(2,1)S(1)}, u32[]{:S(2)}, u32[]{:S(2)}) collective-permute-start(bf16[384,128]{1,0:T(8,128)(2,1)S(1)} %slice.95), channel_id=1, source_target_pairs={{0,16},{1,17},{2,18},{3,19},{4,20},{5,21},{6,22},{7,23},{8,24},{9,... | collective-permute-start | bytes 294920 | tf_op jit(solution)/shard_map/ppermute | solution.py:232
  49.8 10.6 %collective-permute-start.7 = (bf16[576,128]{1,0:T(8,128)(2,1)S(1)}, bf16[576,128]{1,0:T(8,128)(2,1)S(1)}, u32[]{:S(2)}, u32[]{:S(2)}) collective-permute-start(bf16[576,128]{1,0:T(8,128)(2,1)S(1)} %get-tuple-element.41), channel_id=1, source_target_pairs={{0,1},{1,2},{2,3},{3,0},{4,5},{5,6},{6,7},{7,4},{8,9},{9,10},{10,1... | collective-permute-start | bytes 442376 | tf_op jit(solution)/shard_map/ppermute | solution.py:222
  49.9 13.2 %collective-permute-start.8 = (bf16[576,128]{1,0:T(8,128)(2,1)S(1)}, bf16[576,128]{1,0:T(8,128)(2,1)S(1)}, u32[]{:S(2)}, u32[]{:S(2)}) collective-permute-start(bf16[576,128]{1,0:T(8,128)(2,1)S(1)} %get-tuple-element.42), channel_id=1, source_target_pairs={{0,2},{1,3},{2,0},{3,1},{4,6},{5,7},{6,4},{7,5},{8,10},{9,11},{10,... | collective-permute-start | bytes 442376 | tf_op jit(solution)/shard_map/ppermute | solution.py:222
  51.7 11.4 %collective-permute-start.9 = (bf16[576,128]{1,0:T(8,128)(2,1)S(1)}, bf16[576,128]{1,0:T(8,128)(2,1)S(1)}, u32[]{:S(2)}, u32[]{:S(2)}) collective-permute-start(bf16[576,128]{1,0:T(8,128)(2,1)S(1)} %get-tuple-element.43), channel_id=1, source_target_pairs={{0,3},{1,0},{2,1},{3,2},{4,7},{5,4},{6,5},{7,6},{8,11},{9,8},{10,9... | collective-permute-start | bytes 442376 | tf_op jit(solution)/shard_map/ppermute | solution.py:222
  56.6 3.8 %collective-permute-start.4 = (bf16[384,128]{1,0:T(8,128)(2,1)S(1)}, bf16[384,128]{1,0:T(8,128)(2,1)S(1)}, u32[]{:S(2)}, u32[]{:S(2)}) collective-permute-start(bf16[384,128]{1,0:T(8,128)(2,1)S(1)} %slice.94), channel_id=1, source_target_pairs={{0,16},{1,17},{2,18},{3,19},{4,20},{5,21},{6,22},{7,23},{8,24},{9,... | collective-permute-start | bytes 294920 | tf_op jit(solution)/shard_map/ppermute | solution.py:232
  69.2 24.7 %collective-permute-start.10 = (bf16[2,144,512]{2,1,0:T(8,128)(2,1)S(1)}, bf16[2,144,512]{2,1,0:T(8,128)(2,1)S(1)}, u32[]{:S(2)}, u32[]{:S(2)}) collective-permute-start(bf16[2,144,512]{2,1,0:T(8,128)(2,1)S(1)} %get-tuple-element.45), channel_id=1, source_target_pairs={{0,4},{4,0},{8,12},{12,8},{1,5},{5,1},{9,13},{13,9},{2,6},{6,2},{1... | collective-permute-start | bytes 884744 | tf_op jit(solution)/shard_map/ppermute | solution.py:290
  69.3 3.4 %copy-start.1 = (bf16[512,8192]{1,0:T(8,128)(2,1)S(1)}, bf16[512,8192]{1,0:T(8,128)(2,1)}, u32[]{:S(2)}) copy-start(bf16[512,8192]{1,0:T(8,128)(2,1)} %refs_12_.1) | copy-start | bytes 25165828
  76.5 3.3 %copy-start.2 = (bf16[512,8192]{1,0:T(8,128)(2,1)}, bf16[512,8192]{1,0:T(8,128)(2,1)S(1)}, u32[]{:S(2)}) copy-start(bf16[512,8192]{1,0:T(8,128)(2,1)S(1)} %get-tuple-element.46.weight.refs_2_) | copy-start | bytes 25165828
  79.7 7.3 %collective-permute-start.15 = (bf16[2,48,512]{2,1,0:T(8,128)(2,1)S(1)}, bf16[2,48,512]{2,1,0:T(8,128)(2,1)S(1)}, u32[]{:S(2)}, u32[]{:S(2)}) collective-permute-start(bf16[2,48,512]{2,1,0:T(8,128)(2,1)S(1)} %get-tuple-element.55), channel_id=1, source_target_pairs={{0,4},{4,0},{8,12},{12,8},{1,5},{5,1},{9,13},{13,9},{2,6},{6,2},{1... | collective-permute-start | bytes 294920 | tf_op jit(solution)/shard_map/ppermute | solution.py:290
  80.2 3.4 %copy-start.3 = (bf16[512,8192]{1,0:T(8,128)(2,1)S(1)}, bf16[512,8192]{1,0:T(8,128)(2,1)}, u32[]{:S(2)}) copy-start(bf16[512,8192]{1,0:T(8,128)(2,1)} %copy-done.2) | copy-start | bytes 25165828
  87.0 6.8 %copy-start.4 = (bf16[512,8192]{1,0:T(8,128)(2,1)S(1)}, bf16[512,8192]{1,0:T(8,128)(2,1)}, u32[]{:S(2)}) copy-start(bf16[512,8192]{1,0:T(8,128)(2,1)} %copy-done.2) | copy-start | bytes 25165828
  88.6 3.7 %copy-start.5 = (bf16[512,8192]{1,0:T(8,128)(2,1)}, bf16[512,8192]{1,0:T(8,128)(2,1)S(1)}, u32[]{:S(2)}) copy-start(bf16[512,8192]{1,0:T(8,128)(2,1)S(1)} %get-tuple-element.48.refs_3_.refs_1_) | copy-start | bytes 25165828
  92.3 14.0 %collective-permute-start.16 = (bf16[48,4096]{1,0:T(8,128)(2,1)S(1)}, bf16[48,4096]{1,0:T(8,128)(2,1)S(1)}, u32[]{:S(2)}, u32[]{:S(2)}) collective-permute-start(bf16[48,4096]{1,0:T(8,128)(2,1)S(1)} %get-tuple-element.58), channel_id=1, source_target_pairs={{0,8},{4,12},{8,0},{12,4},{1,9},{5,13},{9,1},{13,5},{2,10},{6,14},... | collective-permute-start | bytes 1179656 | tf_op jit(solution)/shard_map/ppermute | solution.py:314
  93.8 3.4 %copy-start.6 = (bf16[512,8192]{1,0:T(8,128)(2,1)S(1)}, bf16[512,8192]{1,0:T(8,128)(2,1)}, u32[]{:S(2)}) copy-start(bf16[512,8192]{1,0:T(8,128)(2,1)} %copy-done.5) | copy-start | bytes 25165828
  102.3 100.1 %collective-permute-start.12 = (bf16[48,4096]{1,0:T(8,128)(2,1)S(1)}, bf16[48,4096]{1,0:T(8,128)(2,1)S(1)}, u32[]{:S(2)}, u32[]{:S(2)}) collective-permute-start(bf16[48,4096]{1,0:T(8,128)(2,1)S(1)} %get-tuple-element.50), channel_id=1, source_target_pairs={{0,8},{4,12},{8,0},{12,4},{1,9},{5,13},{9,1},{13,5},{2,10},{6,14},... | collective-permute-start | bytes 1179656 | tf_op jit(solution)/shard_map/ppermute | solution.py:314
  102.9 73.1 %collective-permute-start.13 = (bf16[48,4096]{1,0:T(8,128)(2,1)S(1)}, bf16[48,4096]{1,0:T(8,128)(2,1)S(1)}, u32[]{:S(2)}, u32[]{:S(2)}) collective-permute-start(bf16[48,4096]{1,0:T(8,128)(2,1)S(1)} %get-tuple-element.52), channel_id=1, source_target_pairs={{0,8},{4,12},{8,0},{12,4},{1,9},{5,13},{9,1},{13,5},{2,10},{6,14},... | collective-permute-start | bytes 1179656 | tf_op jit(solution)/shard_map/ppermute | solution.py:314
  104.4 47.2 %collective-permute-start.14 = (bf16[48,4096]{1,0:T(8,128)(2,1)S(1)}, bf16[48,4096]{1,0:T(8,128)(2,1)S(1)}, u32[]{:S(2)}, u32[]{:S(2)}) collective-permute-start(bf16[48,4096]{1,0:T(8,128)(2,1)S(1)} %get-tuple-element.54), channel_id=1, source_target_pairs={{0,8},{4,12},{8,0},{12,4},{1,9},{5,13},{9,1},{13,5},{2,10},{6,14},... | collective-permute-start | bytes 1179656 | tf_op jit(solution)/shard_map/ppermute | solution.py:314
  104.9 102.5 %collective-permute-start.23 = (bf16[48,4096]{1,0:T(8,128)(2,1)S(1)}, bf16[48,4096]{1,0:T(8,128)(2,1)S(1)}, u32[]{:S(2)}, u32[]{:S(2)}) collective-permute-start(bf16[48,4096]{1,0:T(8,128)(2,1)S(1)} %get-tuple-element.60), channel_id=1, source_target_pairs={{0,8},{4,12},{8,0},{12,4},{1,9},{5,13},{9,1},{13,5},{2,10},{6,14},... | collective-permute-start | bytes 1179656 | tf_op jit(solution)/shard_map/ppermute | solution.py:314
  106.4 40.4 %collective-permute-start.26 = (bf16[48,4096]{1,0:T(8,128)(2,1)S(1)}, bf16[48,4096]{1,0:T(8,128)(2,1)S(1)}, u32[]{:S(2)}, u32[]{:S(2)}) collective-permute-start(bf16[48,4096]{1,0:T(8,128)(2,1)S(1)} %get-tuple-element.66), channel_id=1, source_target_pairs={{0,8},{4,12},{8,0},{12,4},{1,9},{5,13},{9,1},{13,5},{2,10},{6,14},... | collective-permute-start | bytes 1179656 | tf_op jit(solution)/shard_map/ppermute | solution.py:314
  146.8 12.0 %collective-permute-start.17 = (bf16[48,4096]{1,0:T(8,128)(2,1)S(1)}, bf16[48,4096]{1,0:T(8,128)(2,1)S(1)}, u32[]{:S(2)}, u32[]{:S(2)}) collective-permute-start(bf16[48,4096]{1,0:T(8,128)(2,1)S(1)} %add_convert_fusion.14), channel_id=1, source_target_pairs={{0,1},{4,5},{8,9},{12,13},{16,17},{20,21},{24,25},{28,29}} | collective-permute-start | bytes 1179656 | tf_op jit(solution)/shard_map/ppermute | solution.py:343
  151.6 11.9 %collective-permute-start.25 = (bf16[48,4096]{1,0:T(8,128)(2,1)S(1)}, bf16[48,4096]{1,0:T(8,128)(2,1)S(1)}, u32[]{:S(2)}, u32[]{:S(2)}) collective-permute-start(bf16[48,4096]{1,0:T(8,128)(2,1)S(1)} %get-tuple-element.64), channel_id=1, source_target_pairs={{0,8},{4,12},{8,0},{12,4},{1,9},{5,13},{9,1},{13,5},{2,10},{6,14},... | collective-permute-start | bytes 1179656 | tf_op jit(solution)/shard_map/ppermute | solution.py:314
  158.8 10.8 %collective-permute-start.27 = (bf16[48,4096]{1,0:T(8,128)(2,1)S(1)}, bf16[48,4096]{1,0:T(8,128)(2,1)S(1)}, u32[]{:S(2)}, u32[]{:S(2)}) collective-permute-start(bf16[48,4096]{1,0:T(8,128)(2,1)S(1)} %add_convert_fusion.5), channel_id=1, source_target_pairs={{0,1},{4,5},{8,9},{12,13},{16,17},{20,21},{24,25},{28,29}} | collective-permute-start | bytes 1179656 | tf_op jit(solution)/shard_map/ppermute | solution.py:343
  163.5 7.1 %collective-permute-start.20 = (bf16[48,4096]{1,0:T(8,128)(2,1)S(1)}, bf16[48,4096]{1,0:T(8,128)(2,1)S(1)}, u32[]{:S(2)}, u32[]{:S(2)}) collective-permute-start(bf16[48,4096]{1,0:T(8,128)(2,1)S(1)} %add_convert_fusion.14), channel_id=1, source_target_pairs={{3,2},{7,6},{11,10},{15,14},{19,18},{23,22},{27,26},{31,30}} | collective-permute-start | bytes 1179656 | tf_op jit(solution)/shard_map/ppermute | solution.py:343
  169.7 5.5 %collective-permute-start.30 = (bf16[48,4096]{1,0:T(8,128)(2,1)S(1)}, bf16[48,4096]{1,0:T(8,128)(2,1)S(1)}, u32[]{:S(2)}, u32[]{:S(2)}) collective-permute-start(bf16[48,4096]{1,0:T(8,128)(2,1)S(1)} %add_convert_fusion.5), channel_id=1, source_target_pairs={{3,2},{7,6},{11,10},{15,14},{19,18},{23,22},{27,26},{31,30}} | collective-permute-start | bytes 1179656 | tf_op jit(solution)/shard_map/ppermute | solution.py:343
  170.6 9.9 %collective-permute-start.18 = (bf16[48,4096]{1,0:T(8,128)(2,1)S(1)}, bf16[48,4096]{1,0:T(8,128)(2,1)S(1)}, u32[]{:S(2)}, u32[]{:S(2)}) collective-permute-start(bf16[48,4096]{1,0:T(8,128)(2,1)S(1)} %get-tuple-element.67), channel_id=1, source_target_pairs={{0,1},{1,2},{4,5},{5,6},{8,9},{9,10},{12,13},{13,14},{16,17},{17,1... | collective-permute-start | bytes 1179656 | tf_op jit(solution)/shard_map/ppermute | solution.py:343
  175.2 9.8 %collective-permute-start.21 = (bf16[48,4096]{1,0:T(8,128)(2,1)S(1)}, bf16[48,4096]{1,0:T(8,128)(2,1)S(1)}, u32[]{:S(2)}, u32[]{:S(2)}) collective-permute-start(bf16[48,4096]{1,0:T(8,128)(2,1)S(1)} %add_convert_fusion.11), channel_id=1, source_target_pairs={{2,1},{3,2},{6,5},{7,6},{10,9},{11,10},{14,13},{15,14},{18,17},{19... | collective-permute-start | bytes 1179656 | tf_op jit(solution)/shard_map/ppermute | solution.py:343
  176.0 9.9 %collective-permute-start.24 = (bf16[48,4096]{1,0:T(8,128)(2,1)S(1)}, bf16[48,4096]{1,0:T(8,128)(2,1)S(1)}, u32[]{:S(2)}, u32[]{:S(2)}) collective-permute-start(bf16[48,4096]{1,0:T(8,128)(2,1)S(1)} %get-tuple-element.62), channel_id=1, source_target_pairs={{0,8},{4,12},{8,0},{12,4},{1,9},{5,13},{9,1},{13,5},{2,10},{6,14},... | collective-permute-start | bytes 1179656 | tf_op jit(solution)/shard_map/ppermute | solution.py:314
  180.5 12.5 %collective-permute-start.28 = (bf16[48,4096]{1,0:T(8,128)(2,1)S(1)}, bf16[48,4096]{1,0:T(8,128)(2,1)S(1)}, u32[]{:S(2)}, u32[]{:S(2)}) collective-permute-start(bf16[48,4096]{1,0:T(8,128)(2,1)S(1)} %get-tuple-element.69), channel_id=1, source_target_pairs={{0,1},{1,2},{4,5},{5,6},{8,9},{9,10},{12,13},{13,14},{16,17},{17,1... | collective-permute-start | bytes 1179656 | tf_op jit(solution)/shard_map/ppermute | solution.py:343
  184.9 9.3 %collective-permute-start.31 = (bf16[48,4096]{1,0:T(8,128)(2,1)S(1)}, bf16[48,4096]{1,0:T(8,128)(2,1)S(1)}, u32[]{:S(2)}, u32[]{:S(2)}) collective-permute-start(bf16[48,4096]{1,0:T(8,128)(2,1)S(1)} %add_convert_fusion.2), channel_id=1, source_target_pairs={{2,1},{3,2},{6,5},{7,6},{10,9},{11,10},{14,13},{15,14},{18,17},{19... | collective-permute-start | bytes 1179656 | tf_op jit(solution)/shard_map/ppermute | solution.py:343
  186.0 17.7 %collective-permute-start.19 = (bf16[48,4096]{1,0:T(8,128)(2,1)S(1)}, bf16[48,4096]{1,0:T(8,128)(2,1)S(1)}, u32[]{:S(2)}, u32[]{:S(2)}) collective-permute-start(bf16[48,4096]{1,0:T(8,128)(2,1)S(1)} %get-tuple-element.75), channel_id=1, source_target_pairs={{0,1},{1,2},{2,3},{4,5},{5,6},{6,7},{8,9},{9,10},{10,11},{12,13},{... | collective-permute-start | bytes 1179656 | tf_op jit(solution)/shard_map/ppermute | solution.py:343
  193.0 14.3 %collective-permute-start.22 = (bf16[48,4096]{1,0:T(8,128)(2,1)S(1)}, bf16[48,4096]{1,0:T(8,128)(2,1)S(1)}, u32[]{:S(2)}, u32[]{:S(2)}) collective-permute-start(bf16[48,4096]{1,0:T(8,128)(2,1)S(1)} %get-tuple-element.76), channel_id=1, source_target_pairs={{1,0},{2,1},{3,2},{5,4},{6,5},{7,6},{9,8},{10,9},{11,10},{13,12},{... | collective-permute-start | bytes 1179656 | tf_op jit(solution)/shard_map/ppermute | solution.py:343
  194.6 13.0 %collective-permute-start.29 = (bf16[48,4096]{1,0:T(8,128)(2,1)S(1)}, bf16[48,4096]{1,0:T(8,128)(2,1)S(1)}, u32[]{:S(2)}, u32[]{:S(2)}) collective-permute-start(bf16[48,4096]{1,0:T(8,128)(2,1)S(1)} %get-tuple-element.77), channel_id=1, source_target_pairs={{0,1},{1,2},{2,3},{4,5},{5,6},{6,7},{8,9},{9,10},{10,11},{12,13},{... | collective-permute-start | bytes 1179656 | tf_op jit(solution)/shard_map/ppermute | solution.py:343
  202.4 9.7 %collective-permute-start.32 = (bf16[48,4096]{1,0:T(8,128)(2,1)S(1)}, bf16[48,4096]{1,0:T(8,128)(2,1)S(1)}, u32[]{:S(2)}, u32[]{:S(2)}) collective-permute-start(bf16[48,4096]{1,0:T(8,128)(2,1)S(1)} %get-tuple-element.78), channel_id=1, source_target_pairs={{1,0},{2,1},{3,2},{5,4},{6,5},{7,6},{9,8},{10,9},{11,10},{13,12},{... | collective-permute-start | bytes 1179656 | tf_op jit(solution)/shard_map/ppermute | solution.py:343

commit v3 on v2

v3 whole, which is shorter than its diff:
```python
from functools import partial
import math

import jax
import jax.numpy as jnp
import numpy as np
from jax import lax
from jax.experimental import pallas as pl
from jax.experimental.pallas import tpu as pltpu
from jax.sharding import PartitionSpec as P

QUERY_HEAD_COUNT = 64
KEY_VALUE_HEADS = 8
HEAD_SIZE = 128
SLAB_REACH = 4

MASKED = -1e30
F32 = jnp.float32
BF16 = jnp.bfloat16
VMEM = pl.BlockSpec(memory_space=pltpu.VMEM)
SMEM = pl.BlockSpec(memory_space=pltpu.SMEM)
HBM = pl.BlockSpec(memory_space=pltpu.HBM)
LIMIT = pltpu.CompilerParams(vmem_limit_bytes=20 << 20)
TILE = 1024


def destination_order(count):
    table = []
    for z in range(count):
        due = {d: (count - 1 - d + z if d > z else count - 1 - z + d) for d in range(count)}
        due[z] = count
        table.append(sorted(range(count), key=lambda d: (due[d], -d if z < count // 2 else d)))
    return np.array(table, np.int32)


def in_vmem(array):
    return pltpu.with_memory_space_constraint(array, pltpu.VMEM)


def in_hbm(array):
    return pltpu.with_memory_space_constraint(array, pltpu.HBM)


def after(value, *others):
    return lax.optimization_barrier((value, others))[0]


def chosen(table, z, i):
    picked = jnp.int32(int(table[0, i]))
    for n in range(1, table.shape[0]):
        picked = jnp.where(z == n, jnp.int32(int(table[n, i])), picked)
    return picked


def joined(parts):
    return parts[0] if len(parts) == 1 else jnp.concatenate(parts, axis=0)


def pack_kernel(queries, keys, values, *outs, slabs, heads, kv_local, order, share, stages):
    z = lax.axis_index("wsh")
    block = queries.shape[0]
    for k in range(slabs):
        target = lax.rem(z + k, slabs)
        first = pl.multiple_of(lax.div(target * kv_local, slabs) * HEAD_SIZE, HEAD_SIZE)
        load = outs[k]
        load[:block, :] = keys[:, pl.ds(first, HEAD_SIZE)]
        load[block : 2 * block, :] = values[:, pl.ds(first, HEAD_SIZE)]
        for n, stage in enumerate(stages):
            out, place = outs[n * slabs + k], 2 * block if n == 0 else 0
            for h in range(heads):
                column = pl.multiple_of((target * heads + h) * HEAD_SIZE, HEAD_SIZE)
                for i in stage:
                    if share == block:
                        rows, count = slice(None), block
                    else:
                        rows, count = pl.ds(pl.multiple_of(chosen(order, target, i) * share, 16), share), share
                    out[place : place + count, :] = queries[rows, pl.ds(column, HEAD_SIZE)]
                    place += count


def pack(queries, keys, values, *, slabs, heads, kv_local, order, share, stages):
    block = queries.shape[0]
    counts = [heads * share * len(stage) + (2 * block if n == 0 else 0) for n, stage in enumerate(stages)]
    return pl.pallas_call(
        partial(
            pack_kernel, slabs=slabs, heads=heads, kv_local=kv_local, order=order, share=share, stages=stages
        ),
        out_shape=[jax.ShapeDtypeStruct((count, HEAD_SIZE), BF16) for count in counts for _ in range(slabs)],
        in_specs=[VMEM] * 3,
        out_specs=[VMEM] * (slabs * len(stages)),
        compiler_params=LIMIT,
        cost_estimate=pl.CostEstimate(flops=0, bytes_accessed=4 * queries.size, transcendentals=0),
        name="pack",
    )(queries, keys, values)


def attend_kernel(key_doc, *refs, slabs, heads, share, stage, order, offset, columns_x, per_shard, fetched):
    refs = list(refs)
    take = lambda n: [refs.pop(0) for _ in range(n)]
    now, before, queries, weights = take(slabs), take(slabs), take(slabs), take(fetched)
    (keep, send), copied = take(2), take(fetched)
    key_rows, value_rows = take(2)
    copies = [pltpu.make_async_copy(w, c, refs[0].at[n]) for n, (w, c) in enumerate(zip(weights, copied))]
    for copy in copies:
        copy.start()
    scale = math.log2(math.e) / math.sqrt(HEAD_SIZE)
    span = key_doc.shape[2]
    block = span // SLAB_REACH
    rows = share * len(stage)
    srv, head, z = (lax.axis_index(a) for a in ("srv", "head", "wsh"))
    core, x = lax.rem(head, 2), lax.div(head, 2)
    column = lax.broadcasted_iota(jnp.int32, (share, span), 1) - (SLAB_REACH - 1) * block
    row = lax.broadcasted_iota(jnp.int32, (share, span), 0)
    behind = [column - row - (0 if share == block else chosen(order, z, i) * share) for i in stage]
    causal = joined([b <= 0 for b in behind])
    for k in range(slabs):
        slab = lax.rem(z - k + slabs, slabs)
        for o in range(SLAB_REACH):
            place = slice((SLAB_REACH - 1 - o) * block, (SLAB_REACH - o) * block)
            held = (k + o) % slabs

            def fill(source):
                key_rows[place, :] = source[:block, :]
                value_rows[place, :] = source[block : 2 * block, :]

            if o == 0:
                fill(now[held])
            else:
                pl.when(slab >= o)(partial(fill, now[held]))
                pl.when(slab < o)(partial(fill, before[held]))
        docs = key_doc[srv * slabs + slab]
        query_doc = joined([jnp.max(jnp.where(b == 0, docs, -2.0), axis=1, keepdims=True) for b in behind])
        visible = causal & (query_doc == docs)
        scores = lax.dot_general(
            queries[k][offset : offset + heads * rows, :],
            key_rows[...],
            (((1,), (1,)), ((), ())),
            preferred_element_type=F32,
        ).reshape(heads, rows, span)
        scores = jnp.where(visible[None], scores, MASKED)
        largest = jnp.max(scores, axis=-1, keepdims=True)
        terms = jnp.exp2((scores - largest) * scale)
        normalizer = jnp.sum(terms, axis=-1, keepdims=True)
        weighted = jnp.dot(
            terms.reshape(heads * rows, span).astype(BF16), value_rows[...], preferred_element_type=F32
        ).reshape(heads, rows, HEAD_SIZE)
        result = (weighted / normalizer).astype(BF16)
        result = jnp.concatenate([result[h] for h in range(heads)], axis=1)
        target = lax.div(slab, per_shard)
        slot = lax.rem(lax.div(target, 2) - x + columns_x, columns_x) * per_shard + lax.rem(slab, per_shard)

        @pl.when(lax.rem(target, 2) == core)
        def _():
            keep[slot] = result

        @pl.when(lax.rem(target, 2) != core)
        def _():
            send[slot] = result

    for copy in copies:
        copy.wait()


def attend(key_doc, now, before, queries, weights, *, slabs, heads, share, stage, **rest):
    span = key_doc.shape[2]
    rows = share * len(stage)
    out = jax.ShapeDtypeStruct((slabs // 2, rows, heads * HEAD_SIZE), BF16)
    terms = slabs * rows * span * heads
    fetched = len(weights)
    return pl.pallas_call(
        partial(
            attend_kernel, slabs=slabs, heads=heads, share=share, stage=stage, fetched=fetched, **rest
        ),
        out_shape=[out, out] + [pltpu.VMEM(w.shape, w.dtype) for w in weights],
        in_specs=[VMEM] * (1 + 3 * slabs) + [HBM] * fetched,
        out_specs=[VMEM] * (2 + fetched),
        scratch_shapes=[pltpu.VMEM((span, HEAD_SIZE), BF16)] * 2
        + [pltpu.SemaphoreType.DMA((fetched,))] * (fetched > 0),
        compiler_params=LIMIT,
        cost_estimate=pl.CostEstimate(
            flops=4 * terms * HEAD_SIZE, bytes_accessed=sum(w.size * 2 for w in weights), transcendentals=terms
        ),
        name="attend",
    )(key_doc, *now, *before, *queries, *[in_hbm(w) for w in weights])


def first_half_kernel(rows_here, weight, total):
    for n in range(0, total.shape[1], TILE):
        total[:, n : n + TILE] = jnp.dot(rows_here[...], weight[:, n : n + TILE], preferred_element_type=F32)


def first_half(rows_here, weight):
    count, depth = rows_here.shape
    width = weight.shape[1]
    return pl.pallas_call(
        first_half_kernel,
        out_shape=pltpu.VMEM((count, width), F32),
        in_specs=[VMEM, VMEM],
        out_specs=VMEM,
        compiler_params=LIMIT,
        cost_estimate=pl.CostEstimate(flops=2 * count * depth * width, bytes_accessed=0, transcendentals=0),
        name="first_half",
    )(rows_here, in_vmem(weight))


def project_kernel(*refs, terms, begun, share, halves):
    lhs, rhs, start = refs[:terms], refs[terms : 2 * terms], refs[2 * terms : 2 * terms + begun]
    outs = refs[2 * terms + begun :]
    half = outs[0].shape[1]
    for n in range(0, half * halves, TILE):
        total = sum(
            jnp.dot(a[...], w[:, n : n + TILE], preferred_element_type=F32) for a, w in zip(lhs, rhs)
        )
        for s in start:
            total = total + s[:, n : n + TILE]
        for m in range(total.shape[0] // share):
            outs[m * halves + n // half][:, n % half : n % half + TILE] = total[m * share : (m + 1) * share].astype(BF16)


def project(lhs, rhs, start, share, halves):
    count, depth = lhs[0].shape
    width = rhs[0].shape[1]
    return pl.pallas_call(
        partial(project_kernel, terms=len(lhs), begun=len(start), share=share, halves=halves),
        out_shape=[jax.ShapeDtypeStruct((share, width // halves), BF16)] * (count // share * halves),
        in_specs=[VMEM] * (2 * len(lhs) + len(start)),
        out_specs=[VMEM] * (count // share * halves),
        compiler_params=LIMIT,
        cost_estimate=pl.CostEstimate(
            flops=2 * len(lhs) * count * depth * width, bytes_accessed=2 * count * width, transcendentals=0
        ),
        name="project",
    )(*lhs, *[in_vmem(w) for w in rhs], *[in_vmem(s) for s in start])


def on_device(queries, keys, values, doc_ids, block_mask, out_weight, *, order):
    groups, head_shards, slabs = (lax.axis_size(a) for a in ("srv", "head", "wsh"))
    z = lax.axis_index("wsh")
    columns_x = head_shards // 2
    block = queries.shape[0]
    heads = queries.shape[1] // HEAD_SIZE // slabs
    share = block // head_shards
    per_shard = slabs // head_shards
    staged = per_shard == 1
    stages = [[0], list(range(1, slabs))] if staged else [[0]]
    rows_at_once = share if staged else block
    halves = 2
    siblings = [(h, h ^ 1) for h in range(head_shards)]

    def around(array, k):
        return lax.ppermute(array, "wsh", [(i, (i + k) % slabs) for i in range(slabs)])

    packed = pack(
        queries,
        keys,
        values,
        slabs=slabs,
        heads=heads,
        kv_local=keys.shape[1] // HEAD_SIZE,
        order=order,
        share=rows_at_once,
        stages=stages,
    )
    loads = [packed[0]] + [around(packed[k], k) for k in range(1, slabs)]
    before = [
        lax.ppermute(a[: 2 * block], "srv", [(g, g + 1) for g in range(groups - 1)]) for a in loads
    ]
    weight_sibling = lax.ppermute(out_weight, "head", siblings)
    stage_queries = [loads]
    for n in range(1, len(stages)):
        rest = packed[n * slabs : (n + 1) * slabs]
        stage_queries.append([rest[0]] + [around(after(rest[k], *loads), k) for k in range(1, slabs)])

    reach = SLAB_REACH - 1
    padded = jnp.concatenate([jnp.full((reach, block), -1.0, F32), doc_ids.reshape(-1, block).astype(F32)])
    count = padded.shape[0] - reach
    key_doc = jnp.stack(
        [jnp.where(block_mask[:, reach - j, None] > 0, padded[j : j + count], -1.0) for j in range(SLAB_REACH)],
        axis=1,
    ).reshape(count, 1, SLAB_REACH * block)

    partials = []
    results = weight_near = None
    for n, (stage, arrived) in enumerate(zip(stages, stage_queries)):
        if n:
            arrived = after(arrived, *results)
        fetch = [] if n else [out_weight]
        keep, send, *fetched = attend(
            key_doc,
            loads,
            before,
            arrived,
            fetch,
            slabs=slabs,
            heads=heads,
            share=rows_at_once,
            stage=stage,
            order=order,
            offset=2 * block if n == 0 else 0,
            columns_x=columns_x,
            per_shard=per_shard,
        )
        pieces = stage
        if not staged:
            pieces = range(slabs)
            keep, send = (
                jnp.concatenate(
                    [
                        lax.dynamic_slice_in_dim(
                            a.reshape(columns_x, -1, a.shape[-1]), chosen(order, z, i) * share, share, 1
                        )
                        for i in pieces
                    ],
                    axis=1,
                )
                for a in (keep, send)
            )
        theirs = lax.ppermute(send, "head", siblings)
        keep, theirs = (a.reshape(-1, a.shape[-1]) for a in (keep, theirs))
        if n == 0 and staged:
            weight_near = fetched[0]
            begun = first_half(keep, weight_near)
            results = project([theirs], [weight_sibling], [begun], share, halves)
        else:
            if fetched:
                weight_near = fetched[0]
            results = project([keep, theirs], [weight_near, weight_sibling], [], share, halves)
        for m in range(len(pieces)):
            partials.append(
                [
                    [results[(k * len(pieces) + m) * halves + half] for half in range(halves)]
                    for k in range(columns_x)
                ]
            )

    position = np.argsort(order, axis=1)

    def senders(direction, t):
        found = {}
        for i in range(slabs):
            step = i if direction > 0 else slabs - 1 - i
            if step <= t:
                d = slabs - 1 - t + step
                found[i] = int(position[i, d if direction > 0 else slabs - 1 - d])
        return found

    def message(which, own, arrived):
        picked = None
        for i, piece in which.items():
            picked = own[piece] if picked is None else jnp.where(z == i, own[piece], picked)
        if arrived is None:
            return picked
        return (picked.astype(F32) + arrived.astype(F32)).astype(BF16)

    sums = [[] for _ in range(halves)]
    messages = [[] for _ in range(halves)]
    arrived = [{1: None, -1: None} for _ in range(halves)]
    for t in range(slabs):
        for half in range(halves):
            total = partials[t][0][half].astype(F32)
            for k in range(1, columns_x):
                route = [(h, (h + 2 * k) % head_shards) for h in range(head_shards)]
                piece = partials[t][k][half]
                if t >= 2:
                    piece = after(piece, *messages[half][t - 2])
                total = total + lax.ppermute(piece, "head", route).astype(F32)
            sums[half].append(total.astype(BF16))
            if t == slabs - 1:
                continue
            up, down = senders(1, t), senders(-1, t)
            if t + 1 < slabs - 2 - t:
                sent = message({**up, **down}, sums[half], arrived[half][1])
                both = lax.ppermute(sent, "wsh", [(i, i + 1) for i in up] + [(i, i - 1) for i in down])
                arrived[half] = {1: both, -1: both}
                messages[half].append([sent])
            else:
                sent = {
                    direction: message(found, sums[half], arrived[half][direction])
                    for direction, found in ((1, up), (-1, down))
                }
                for direction, found in ((1, up), (-1, down)):
                    arrived[half][direction] = lax.ppermute(
                        sent[direction], "wsh", [(i, i + direction) for i in found]
                    )
                messages[half].append(list(sent.values()))
    outs = []
    for half in range(halves):
        total = sums[half][-1].astype(F32)
        if slabs > 1:
            total = total + arrived[half][1].astype(F32) + arrived[half][-1].astype(F32)
        outs.append(total.astype(BF16))
    return jnp.concatenate(outs, axis=1)


def solution(mesh):
    in_specs = (
        P(("srv", "wsh"), "head"),
        P(("srv", "wsh"), "head"),
        P(("srv", "wsh"), "head"),
        P(),
        P(),
        P(("head", "wsh"), None),
    )
    out_specs = P(("srv", "head", "wsh"), None)
    return jax.shard_map(
        partial(on_device, order=destination_order(mesh.shape["wsh"])),
        mesh=mesh,
        in_specs=in_specs,
        out_specs=out_specs,
        check_vma=False,
    )
```

time: 215 us -> 134 us (0.62)
  waiting for transfers between devices: 79.4 us -> 32.3 us
  local copies, waits for them, and re-layouts: 35.5 us -> 6.62 us
  between operations: 13.3 us -> 0.4 us
  Pallas kernels: 19.8 us -> 24.2 us
  starting transfers between devices: 62 us -> 64.9 us
    ppermute x20 -> x18, waiting for transfers between devices: 66.1 us -> 23.2 us  [the longest x8 12.5 us: on_device(): lax.ppermute(sent[direction], 'wsh', [(i, i + direction) for i in found])]
    unnamed x31 -> x10, local copies, waits for them, and re-layouts: 30.7 us -> 6.3 us
    pallas_call x2, Pallas kernels: 6.59 us -> 13.3 us  [project(): pl.pallas_call(partial(project_kernel, terms=len(lhs), begun=len(start),...]
    ppermute x6, waiting for transfers between devices: 11.6 us -> 6.24 us  [around(): lax.ppermute(array, 'wsh', [(i, (i + k) % slabs) for i in range(slabs)])]
    dynamic_slice x3 -> x0, local copies, waits for them, and re-layouts: 3.19 us -> none  [the longest x1 2.15 us: on_device(): starts = [table[z, i] * share for i in stage]]
    ppermute x6, starting transfers between devices: 8.78 us -> 11.8 us  [around(): lax.ppermute(array, 'wsh', [(i, (i + k) % slabs) for i in range(slabs)])]
    ppermute x20 -> x18, starting transfers between devices: 43.1 us -> 43 us  [the longest x8 25.3 us: on_device(): lax.ppermute(sent[direction], 'wsh', [(i, i + direction) for i in found])]
  transfers between devices with their start and end apart: 33 -> 31, of which waited for: 12 -> 13; matrix products, arithmetic and copies ran while one was open for 10% -> 3% of each run, Pallas kernels for 9% -> 14%
where the time goes in v3:
time: 134 us; the launch traced here: 133 us
  starting transfers between devices  64.9 us (48%)
  waiting for transfers between devices  32.3 us (24%)
  Pallas kernels  24.2 us (18%)
  local copies, waits for them, and re-layouts  6.62 us (5%)
  other arithmetic  4.63 us (3%)
    ppermute x8, starting transfers between devices, on_device(): lax.ppermute(sent[direction], 'wsh', [(i, i + direction) for i in found])  25.3 us
    pallas_call x2, Pallas kernels, project(): pl.pallas_call(partial(project_kernel, terms=len(lhs), begun=len(start),...  13.3 us
    ppermute x8, waiting for transfers between devices, on_device(): lax.ppermute(sent[direction], 'wsh', [(i, i + direction) for i in found])  12.5 us
    ppermute x6, starting transfers between devices, around(): lax.ppermute(array, 'wsh', [(i, (i + k) % slabs) for i in range(slabs)])  11.8 us
    ppermute x8, waiting for transfers between devices, on_device(): total = total + lax.ppermute(piece, 'head', route).astype(F32)  9.83 us
    ppermute x4, starting transfers between devices, on_device(): lax.ppermute(a[:2 * block], 'srv', [(g, g + 1) for g in range(groups - 1)])  9.44 us
    ppermute x8, starting transfers between devices, on_device(): total = total + lax.ppermute(piece, 'head', route).astype(F32)  9.32 us
    pallas_call x2, Pallas kernels, attend(): pl.pallas_call(partial(attend_kernel, slabs=slabs, heads=heads, share=sha...  9.23 us
  transfers between devices with their start and end apart: 31, of which 13 were waited for; matrix products, arithmetic and copies ran while one was open for 3% of the time, Pallas kernels for 14%

profile of v3, /device:TPU:0, one launch (start us, length us, event | category | flops | bytes accessed | tf_op | source)
XLA Modules:
  0.0 133.0 jit_solution(11065714399098346030)
XLA Ops:
  0.5 1.1 copy-done.2
  1.6 0.9 copy-done.3
  2.5 0.9 copy-done.4
  3.7 2.6 %collective-permute-start = (bf16[576,128]{1,0:T(8,128)(2,1)S(1)}, bf16[576,128]{1,0:T(8,128)(2,1)S(1)}, u32[]{:S(2)}, u32[]{:S(2)}) collective-permute-start(bf16[576,128]{1,0:T(8,128)(2,1)S(1)} %get-tuple-element.46), channel_id=1, source_target_pairs={{0,1},{1,2},{2,3},{3,0},{4,5},{5,6},{6,7},{7,4},{8,9},{9,10},{10,1... | collective-permute-start | bytes 442376 | tf_op jit(solution)/shard_map/ppermute | solution.py:251
  6.3 2.6 %collective-permute-start.1 = (bf16[576,128]{1,0:T(8,128)(2,1)S(1)}, bf16[576,128]{1,0:T(8,128)(2,1)S(1)}, u32[]{:S(2)}, u32[]{:S(2)}) collective-permute-start(bf16[576,128]{1,0:T(8,128)(2,1)S(1)} %get-tuple-element.47), channel_id=1, source_target_pairs={{0,2},{1,3},{2,0},{3,1},{4,6},{5,7},{6,4},{7,5},{8,10},{9,11},{10,... | collective-permute-start | bytes 442376 | tf_op jit(solution)/shard_map/ppermute | solution.py:251
  8.9 1.3 %collective-permute-start.2 = (bf16[576,128]{1,0:T(8,128)(2,1)S(1)}, bf16[576,128]{1,0:T(8,128)(2,1)S(1)}, u32[]{:S(2)}, u32[]{:S(2)}) collective-permute-start(bf16[576,128]{1,0:T(8,128)(2,1)S(1)} %get-tuple-element.48), channel_id=1, source_target_pairs={{0,3},{1,0},{2,1},{3,2},{4,7},{5,4},{6,5},{7,6},{8,11},{9,8},{10,9... | collective-permute-start | bytes 442376 | tf_op jit(solution)/shard_map/ppermute | solution.py:251
  10.2 3.4 %collective-permute-start.3 = (bf16[384,128]{1,0:T(8,128)(2,1)S(1)}, bf16[384,128]{1,0:T(8,128)(2,1)S(1)}, u32[]{:S(2)}, u32[]{:S(2)}) collective-permute-start(bf16[384,128]{1,0:T(8,128)(2,1)S(1)} %slice.40), channel_id=1, source_target_pairs={{0,16},{1,17},{2,18},{3,19},{4,20},{5,21},{6,22},{7,23},{8,24},{9,... | collective-permute-start | bytes 294920 | tf_op jit(solution)/shard_map/ppermute | solution.py:266
  13.7 0.7 convert_element_type.180
  14.5 0.8 compare_bitcast_fusion.3
  15.6 1.3 collective-permute-start.4
  16.9 2.3 %collective-permute-done.1.refs_2_.refs_10_ = bf16[576,128]{1,0:T(8,128)(2,1)S(1)} collective-permute-done((bf16[576,128]{1,0:T(8,128)(2,1)S(1)}, bf16[576,128]{1,0:T(8,128)(2,1)S(1)}, u32[]{:S(2)}, u32[]{:S(2)}) %collective-permute-start.1) | collective-permute-done | bytes 147488 | tf_op jit(solution)/shard_map/ppermute | solution.py:251
  19.2 3.4 %collective-permute-start.5 = (bf16[384,128]{1,0:T(8,128)(2,1)S(1)}, bf16[384,128]{1,0:T(8,128)(2,1)S(1)}, u32[]{:S(2)}, u32[]{:S(2)}) collective-permute-start(bf16[384,128]{1,0:T(8,128)(2,1)S(1)} %slice.45), channel_id=1, source_target_pairs={{0,16},{1,17},{2,18},{3,19},{4,20},{5,21},{6,22},{7,23},{8,24},{9,... | collective-permute-start | bytes 294920 | tf_op jit(solution)/shard_map/ppermute | solution.py:266
  22.7 1.3 collective-permute-start.6
  24.2 1.4 %collective-permute-done.5.refs_6_ = bf16[384,128]{1,0:T(8,128)(2,1)S(1)} collective-permute-done((bf16[384,128]{1,0:T(8,128)(2,1)S(1)}, bf16[384,128]{1,0:T(8,128)(2,1)S(1)}, u32[]{:S(2)}, u32[]{:S(2)}) %collective-permute-start.5) | collective-permute-done | bytes 98336 | tf_op jit(solution)/shard_map/ppermute | solution.py:266
  25.6 1.3 %collective-permute-done.6.refs_7_ = bf16[384,128]{1,0:T(8,128)(2,1)S(1)} collective-permute-done((bf16[384,128]{1,0:T(8,128)(2,1)S(1)}, bf16[384,128]{1,0:T(8,128)(2,1)S(1)}, u32[]{:S(2)}, u32[]{:S(2)}) %collective-permute-start.6) | collective-permute-done | bytes 98336 | tf_op jit(solution)/shard_map/ppermute | solution.py:266
  27.0 3.4 %attend.2 = (bf16[2,48,512]{2,1,0:T(8,128)(2,1)S(1)}, bf16[2,48,512]{2,1,0:T(8,128)(2,1)S(1)}, bf16[512,8192]{1,0:T(8,128)(2,1)S(1)}) custom-call(f32[8,1,768]{2,1,0:T(1,128)S(1)} %reshape.55.key_doc, bf16[576,128]{1,0:T(8,128)(2,1)S(1)} %get-tuple-element.45.refs_0_.refs_8_, bf16[576,128]{1,0:T(8,128)(2,1)S(1)} %collective-permute-done.refs_1_.refs_9_, ...), custom_call_target="tpu_custom_call" | custom-call | flops 301989888 | bytes 8388608 | tf_op jit(solution)/shard_map/attend/pallas_call | solution.py:170
  30.4 1.9 %collective-permute-start.7 = (bf16[576,128]{1,0:T(8,128)(2,1)S(1)}, bf16[576,128]{1,0:T(8,128)(2,1)S(1)}, u32[]{:S(2)}, u32[]{:S(2)}) collective-permute-start(bf16[576,128]{1,0:T(8,128)(2,1)S(1)} %get-tuple-element.51), channel_id=1, source_target_pairs={{0,1},{1,2},{2,3},{3,0},{4,5},{5,6},{6,7},{7,4},{8,9},{9,10},{10,1... | collective-permute-start | bytes 442376 | tf_op jit(solution)/shard_map/ppermute | solution.py:251
  32.3 3.4 %collective-permute-start.8 = (bf16[576,128]{1,0:T(8,128)(2,1)S(1)}, bf16[576,128]{1,0:T(8,128)(2,1)S(1)}, u32[]{:S(2)}, u32[]{:S(2)}) collective-permute-start(bf16[576,128]{1,0:T(8,128)(2,1)S(1)} %get-tuple-element.53), channel_id=1, source_target_pairs={{0,2},{1,3},{2,0},{3,1},{4,6},{5,7},{6,4},{7,5},{8,10},{9,11},{10,... | collective-permute-start | bytes 442376 | tf_op jit(solution)/shard_map/ppermute | solution.py:251
  35.7 1.5 %first_half.1.refs_2_ = f32[96,8192]{1,0:T(8,128)S(1)} custom-call(bf16[96,512]{1,0:T(8,128)(2,1)S(1)} %bitcast.17, bf16[512,8192]{1,0:T(8,128)(2,1)S(1)} %get-tuple-element.58.weight.refs_2_), custom_call_target="tpu_custom_call" | custom-call | flops 805306368 | tf_op jit(solution)/shard_map/first_half/pallas_call | solution.py:195
  37.2 4.8 %project.2 = (bf16[48,4096]{1,0:T(8,128)(2,1)S(1)}, bf16[48,4096]{1,0:T(8,128)(2,1)S(1)}, bf16[48,4096]{1,0:T(8,128)(2,1)S(1)}, bf16[48,4096]{1,0:T(8,128)(2,1)S(1)}) custom-call(bf16[96,512]{1,0:T(8,128)(2,1)S(1)} %bitcast.16, bf16[512,8192]{1,0:T(8,128)(2,1)} %collective-permute-done.11.refs_1_.refs_3_, f32[96,8192]{1,0:T(8,128)S(1)} %first_half.1.refs_2_), custom_call_target="tpu_custom_call" | custom-call | flops 805306368 | bytes 1572864 | tf_op jit(solution)/shard_map/project/pallas_call | solution.py:223
  42.1 3.9 %collective-permute-done.8.refs_10_ = bf16[576,128]{1,0:T(8,128)(2,1)S(1)} collective-permute-done((bf16[576,128]{1,0:T(8,128)(2,1)S(1)}, bf16[576,128]{1,0:T(8,128)(2,1)S(1)}, u32[]{:S(2)}, u32[]{:S(2)}) %collective-permute-start.8) | collective-permute-done | bytes 147488 | tf_op jit(solution)/shard_map/ppermute | solution.py:251
  46.0 5.8 %attend.3 = (bf16[2,144,512]{2,1,0:T(8,128)(2,1)S(1)}, bf16[2,144,512]{2,1,0:T(8,128)(2,1)S(1)}) custom-call(f32[8,1,768]{2,1,0:T(1,128)S(1)} %reshape.55.key_doc, bf16[576,128]{1,0:T(8,128)(2,1)S(1)} %get-tuple-element.45.refs_0_.refs_8_, bf16[576,128]{1,0:T(8,128)(2,1)S(1)} %collective-permute-done.refs_1_.refs_9_, ...), custom_call_target="tpu_custom_call" | custom-call | flops 905969664 | tf_op jit(solution)/shard_map/attend/pallas_call | solution.py:170
  51.9 1.6 %collective-permute-start.13 = (bf16[48,4096]{1,0:T(8,128)(2,1)S(1)}, bf16[48,4096]{1,0:T(8,128)(2,1)S(1)}, u32[]{:S(2)}, u32[]{:S(2)}) collective-permute-start(bf16[48,4096]{1,0:T(8,128)(2,1)S(1)} %get-tuple-element.61), channel_id=1, source_target_pairs={{0,8},{4,12},{8,0},{12,4},{1,9},{5,13},{9,1},{13,5},{2,10},{6,14},... | collective-permute-start | bytes 1179656 | tf_op jit(solution)/shard_map/ppermute | solution.py:366
  54.0 3.4 %copy-done.1 = bf16[512,8192]{1,0:T(8,128)(2,1)S(1)} copy-done((bf16[512,8192]{1,0:T(8,128)(2,1)S(1)}, bf16[512,8192]{1,0:T(8,128)(2,1)}, u32[]{:S(2)}) %copy-start.1) | copy-done | bytes 8388632
  57.4 8.4 %project.3 = (bf16[48,4096]{1,0:T(8,128)(2,1)S(1)}, bf16[48,4096]{1,0:T(8,128)(2,1)S(1)}, bf16[48,4096]{1,0:T(8,128)(2,1)S(1)}, bf16[48,4096]{1,0:T(8,128)(2,1)S...) custom-call(bf16[288,512]{1,0:T(8,128)(2,1)S(1)} %bitcast.19, ...), custom_call_target="tpu_custom_call" | custom-call | flops 4831838208 | bytes 4718592 | tf_op jit(solution)/shard_map/project/pallas_call | solution.py:223
  65.8 1.6 %collective-permute-start.14 = (bf16[48,4096]{1,0:T(8,128)(2,1)S(1)}, bf16[48,4096]{1,0:T(8,128)(2,1)S(1)}, u32[]{:S(2)}, u32[]{:S(2)}) collective-permute-start(bf16[48,4096]{1,0:T(8,128)(2,1)S(1)} %get-tuple-element.72), channel_id=1, source_target_pairs={{0,8},{4,12},{8,0},{12,4},{1,9},{5,13},{9,1},{13,5},{2,10},{6,14},... | collective-permute-start | bytes 1179656 | tf_op jit(solution)/shard_map/ppermute | solution.py:366
  68.0 5.6 %collective-permute-start.15 = (bf16[48,4096]{1,0:T(8,128)(2,1)S(1)}, bf16[48,4096]{1,0:T(8,128)(2,1)S(1)}, u32[]{:S(2)}, u32[]{:S(2)}) collective-permute-start(bf16[48,4096]{1,0:T(8,128)(2,1)S(1)} %add_convert_fusion.13), channel_id=1, source_target_pairs={{0,1},{3,2},{4,5},{7,6},{8,9},{11,10},{12,13},{15,14},{16,17},{19,... | collective-permute-start | bytes 1179656 | tf_op jit(solution)/shard_map/ppermute | solution.py:373
  73.6 1.6 %collective-permute-start.17 = (bf16[48,4096]{1,0:T(8,128)(2,1)S(1)}, bf16[48,4096]{1,0:T(8,128)(2,1)S(1)}, u32[]{:S(2)}, u32[]{:S(2)}) collective-permute-start(bf16[48,4096]{1,0:T(8,128)(2,1)S(1)} %get-tuple-element.76), channel_id=1, source_target_pairs={{0,8},{4,12},{8,0},{12,4},{1,9},{5,13},{9,1},{13,5},{2,10},{6,14},... | collective-permute-start | bytes 1179656 | tf_op jit(solution)/shard_map/ppermute | solution.py:366
  75.3 2.8 %collective-permute-start.24 = (bf16[48,4096]{1,0:T(8,128)(2,1)S(1)}, bf16[48,4096]{1,0:T(8,128)(2,1)S(1)}, u32[]{:S(2)}, u32[]{:S(2)}) collective-permute-start(bf16[48,4096]{1,0:T(8,128)(2,1)S(1)} %add_convert_fusion.6), channel_id=1, source_target_pairs={{0,1},{3,2},{4,5},{7,6},{8,9},{11,10},{12,13},{15,14},{16,17},{19,... | collective-permute-start | bytes 1179656 | tf_op jit(solution)/shard_map/ppermute | solution.py:373
  78.0 2.7 %collective-permute-done.14 = bf16[48,4096]{1,0:T(8,128)(2,1)S(1)} collective-permute-done((bf16[48,4096]{1,0:T(8,128)(2,1)S(1)}, bf16[48,4096]{1,0:T(8,128)(2,1)S(1)}, u32[]{:S(2)}, u32[]{:S(2)}) %collective-permute-start.14) | collective-permute-done | bytes 393248 | tf_op jit(solution)/shard_map/ppermute | solution.py:366
  80.8 1.5 %collective-permute-start.26 = (bf16[48,4096]{1,0:T(8,128)(2,1)S(1)}, bf16[48,4096]{1,0:T(8,128)(2,1)S(1)}, u32[]{:S(2)}, u32[]{:S(2)}) collective-permute-start(bf16[48,4096]{1,0:T(8,128)(2,1)S(1)} %get-tuple-element.84), channel_id=1, source_target_pairs={{0,8},{4,12},{8,0},{12,4},{1,9},{5,13},{9,1},{13,5},{2,10},{6,14},... | collective-permute-start | bytes 1179656 | tf_op jit(solution)/shard_map/ppermute | solution.py:366
  82.2 0.9 collective-permute-done.15
  83.5 0.7 collective-permute-start.20
  84.2 5.0 %collective-permute-done.23 = bf16[48,4096]{1,0:T(8,128)(2,1)S(1)} collective-permute-done((bf16[48,4096]{1,0:T(8,128)(2,1)S(1)}, bf16[48,4096]{1,0:T(8,128)(2,1)S(1)}, u32[]{:S(2)}, u32[]{:S(2)}) %collective-permute-start.23) | collective-permute-done | bytes 393248 | tf_op jit(solution)/shard_map/ppermute | solution.py:366
  89.2 5.6 %collective-permute-start.18 = (bf16[48,4096]{1,0:T(8,128)(2,1)S(1)}, bf16[48,4096]{1,0:T(8,128)(2,1)S(1)}, u32[]{:S(2)}, u32[]{:S(2)}) collective-permute-start(bf16[48,4096]{1,0:T(8,128)(2,1)S(1)} %get-tuple-element.85), channel_id=1, source_target_pairs={{0,1},{1,2},{4,5},{5,6},{8,9},{9,10},{12,13},{13,14},{16,17},{17,1... | collective-permute-start | bytes 1179656 | tf_op jit(solution)/shard_map/ppermute | solution.py:382
  95.2 0.7 collective-permute-start.29
  95.9 1.7 %collective-permute-done.17 = bf16[48,4096]{1,0:T(8,128)(2,1)S(1)} collective-permute-done((bf16[48,4096]{1,0:T(8,128)(2,1)S(1)}, bf16[48,4096]{1,0:T(8,128)(2,1)S(1)}, u32[]{:S(2)}, u32[]{:S(2)}) %collective-permute-start.17) | collective-permute-done | bytes 393248 | tf_op jit(solution)/shard_map/ppermute | solution.py:366
  97.6 5.6 %collective-permute-start.27 = (bf16[48,4096]{1,0:T(8,128)(2,1)S(1)}, bf16[48,4096]{1,0:T(8,128)(2,1)S(1)}, u32[]{:S(2)}, u32[]{:S(2)}) collective-permute-start(bf16[48,4096]{1,0:T(8,128)(2,1)S(1)} %get-tuple-element.87), channel_id=1, source_target_pairs={{0,1},{1,2},{4,5},{5,6},{8,9},{9,10},{12,13},{13,14},{16,17},{17,1... | collective-permute-start | bytes 1179656 | tf_op jit(solution)/shard_map/ppermute | solution.py:382
  103.2 1.6 %collective-permute-start.16 = (bf16[48,4096]{1,0:T(8,128)(2,1)S(1)}, bf16[48,4096]{1,0:T(8,128)(2,1)S(1)}, u32[]{:S(2)}, u32[]{:S(2)}) collective-permute-start(bf16[48,4096]{1,0:T(8,128)(2,1)S(1)} %get-tuple-element.73), channel_id=1, source_target_pairs={{0,8},{4,12},{8,0},{12,4},{1,9},{5,13},{9,1},{13,5},{2,10},{6,14},... | collective-permute-start | bytes 1179656 | tf_op jit(solution)/shard_map/ppermute | solution.py:366
  106.0 5.6 %collective-permute-start.19 = (bf16[48,4096]{1,0:T(8,128)(2,1)S(1)}, bf16[48,4096]{1,0:T(8,128)(2,1)S(1)}, u32[]{:S(2)}, u32[]{:S(2)}) collective-permute-start(bf16[48,4096]{1,0:T(8,128)(2,1)S(1)} %get-tuple-element.89), channel_id=1, source_target_pairs={{0,1},{1,2},{2,3},{4,5},{5,6},{6,7},{8,9},{9,10},{10,11},{12,13},{... | collective-permute-start | bytes 1179656 | tf_op jit(solution)/shard_map/ppermute | solution.py:382
  111.6 1.3 collective-permute-start.21
  113.3 4.6 %collective-permute-start.28 = (bf16[48,4096]{1,0:T(8,128)(2,1)S(1)}, bf16[48,4096]{1,0:T(8,128)(2,1)S(1)}, u32[]{:S(2)}, u32[]{:S(2)}) collective-permute-start(bf16[48,4096]{1,0:T(8,128)(2,1)S(1)} %get-tuple-element.91), channel_id=1, source_target_pairs={{0,1},{1,2},{2,3},{4,5},{5,6},{6,7},{8,9},{9,10},{10,11},{12,13},{... | collective-permute-start | bytes 1179656 | tf_op jit(solution)/shard_map/ppermute | solution.py:382
  117.9 1.3 collective-permute-start.30
  119.2 2.0 %collective-permute-done.19 = bf16[48,4096]{1,0:T(8,128)(2,1)S(1)} collective-permute-done((bf16[48,4096]{1,0:T(8,128)(2,1)S(1)}, bf16[48,4096]{1,0:T(8,128)(2,1)S(1)}, u32[]{:S(2)}, u32[]{:S(2)}) %collective-permute-start.19) | collective-permute-done | bytes 393248 | tf_op jit(solution)/shard_map/ppermute | solution.py:382
  121.2 4.4 %collective-permute-done.21 = bf16[48,4096]{1,0:T(8,128)(2,1)S(1)} collective-permute-done((bf16[48,4096]{1,0:T(8,128)(2,1)S(1)}, bf16[48,4096]{1,0:T(8,128)(2,1)S(1)}, u32[]{:S(2)}, u32[]{:S(2)}) %collective-permute-start.21) | collective-permute-done | bytes 393248 | tf_op jit(solution)/shard_map/ppermute | solution.py:382
  125.8 1.9 %collective-permute-done.28 = bf16[48,4096]{1,0:T(8,128)(2,1)S(1)} collective-permute-done((bf16[48,4096]{1,0:T(8,128)(2,1)S(1)}, bf16[48,4096]{1,0:T(8,128)(2,1)S(1)}, u32[]{:S(2)}, u32[]{:S(2)}) %collective-permute-start.28) | collective-permute-done | bytes 393248 | tf_op jit(solution)/shard_map/ppermute | solution.py:382
  127.7 4.1 %collective-permute-done.30 = bf16[48,4096]{1,0:T(8,128)(2,1)S(1)} collective-permute-done((bf16[48,4096]{1,0:T(8,128)(2,1)S(1)}, bf16[48,4096]{1,0:T(8,128)(2,1)S(1)}, u32[]{:S(2)}, u32[]{:S(2)}) %collective-permute-start.30) | collective-permute-done | bytes 393248 | tf_op jit(solution)/shard_map/ppermute | solution.py:382
  132.1 0.9 pad_maximum_fusion
  (56 shorter events, 5.4 us)
Async XLA Ops:
  0.0 37.2 %collective-permute-start.11 = (bf16[512,8192]{1,0:T(8,128)(2,1)}, bf16[512,8192]{1,0:T(8,128)(2,1)}, u32[]{:S(2)}, u32[]{:S(2)}) collective-permute-start(bf16[512,8192]{1,0:T(8,128)(2,1)} %refs_12_.1), channel_id=1, source_target_pairs={{0,4},{4,0},{8,12},{12,8},{1,5},{5,1},{9,13},{13,9},{2,6},{6,2},{1... | collective-permute-start | bytes 25165832 | tf_op jit(solution)/shard_map/ppermute | solution.py:268
  0.5 1.1 copy-start.2
  1.6 0.9 copy-start.3
  2.5 0.9 copy-start.4
  3.7 11.9 %collective-permute-start = (bf16[576,128]{1,0:T(8,128)(2,1)S(1)}, bf16[576,128]{1,0:T(8,128)(2,1)S(1)}, u32[]{:S(2)}, u32[]{:S(2)}) collective-permute-start(bf16[576,128]{1,0:T(8,128)(2,1)S(1)} %get-tuple-element.46), channel_id=1, source_target_pairs={{0,1},{1,2},{2,3},{3,0},{4,5},{5,6},{6,7},{7,4},{8,9},{9,10},{10,1... | collective-permute-start | bytes 442376 | tf_op jit(solution)/shard_map/ppermute | solution.py:251
  6.3 12.9 %collective-permute-start.1 = (bf16[576,128]{1,0:T(8,128)(2,1)S(1)}, bf16[576,128]{1,0:T(8,128)(2,1)S(1)}, u32[]{:S(2)}, u32[]{:S(2)}) collective-permute-start(bf16[576,128]{1,0:T(8,128)(2,1)S(1)} %get-tuple-element.47), channel_id=1, source_target_pairs={{0,2},{1,3},{2,0},{3,1},{4,6},{5,7},{6,4},{7,5},{8,10},{9,11},{10,... | collective-permute-start | bytes 442376 | tf_op jit(solution)/shard_map/ppermute | solution.py:251
  8.9 13.8 %collective-permute-start.2 = (bf16[576,128]{1,0:T(8,128)(2,1)S(1)}, bf16[576,128]{1,0:T(8,128)(2,1)S(1)}, u32[]{:S(2)}, u32[]{:S(2)}) collective-permute-start(bf16[576,128]{1,0:T(8,128)(2,1)S(1)} %get-tuple-element.48), channel_id=1, source_target_pairs={{0,3},{1,0},{2,1},{3,2},{4,7},{5,4},{6,5},{7,6},{8,11},{9,8},{10,9... | collective-permute-start | bytes 442376 | tf_op jit(solution)/shard_map/ppermute | solution.py:251
  10.2 13.9 %collective-permute-start.3 = (bf16[384,128]{1,0:T(8,128)(2,1)S(1)}, bf16[384,128]{1,0:T(8,128)(2,1)S(1)}, u32[]{:S(2)}, u32[]{:S(2)}) collective-permute-start(bf16[384,128]{1,0:T(8,128)(2,1)S(1)} %slice.40), channel_id=1, source_target_pairs={{0,16},{1,17},{2,18},{3,19},{4,20},{5,21},{6,22},{7,23},{8,24},{9,... | collective-permute-start | bytes 294920 | tf_op jit(solution)/shard_map/ppermute | solution.py:266
  15.6 8.6 %collective-permute-start.4 = (bf16[384,128]{1,0:T(8,128)(2,1)S(1)}, bf16[384,128]{1,0:T(8,128)(2,1)S(1)}, u32[]{:S(2)}, u32[]{:S(2)}) collective-permute-start(bf16[384,128]{1,0:T(8,128)(2,1)S(1)} %slice.44), channel_id=1, source_target_pairs={{0,16},{1,17},{2,18},{3,19},{4,20},{5,21},{6,22},{7,23},{8,24},{9,... | collective-permute-start | bytes 294920 | tf_op jit(solution)/shard_map/ppermute | solution.py:266
  19.2 6.4 %collective-permute-start.5 = (bf16[384,128]{1,0:T(8,128)(2,1)S(1)}, bf16[384,128]{1,0:T(8,128)(2,1)S(1)}, u32[]{:S(2)}, u32[]{:S(2)}) collective-permute-start(bf16[384,128]{1,0:T(8,128)(2,1)S(1)} %slice.45), channel_id=1, source_target_pairs={{0,16},{1,17},{2,18},{3,19},{4,20},{5,21},{6,22},{7,23},{8,24},{9,... | collective-permute-start | bytes 294920 | tf_op jit(solution)/shard_map/ppermute | solution.py:266
  22.7 4.3 %collective-permute-start.6 = (bf16[384,128]{1,0:T(8,128)(2,1)S(1)}, bf16[384,128]{1,0:T(8,128)(2,1)S(1)}, u32[]{:S(2)}, u32[]{:S(2)}) collective-permute-start(bf16[384,128]{1,0:T(8,128)(2,1)S(1)} %slice.46), channel_id=1, source_target_pairs={{0,16},{1,17},{2,18},{3,19},{4,20},{5,21},{6,22},{7,23},{8,24},{9,... | collective-permute-start | bytes 294920 | tf_op jit(solution)/shard_map/ppermute | solution.py:266
  30.4 6.8 %copy-start = (bf16[512,8192]{1,0:T(8,128)(2,1)}, bf16[512,8192]{1,0:T(8,128)(2,1)S(1)}, u32[]{:S(2)}) copy-start(bf16[512,8192]{1,0:T(8,128)(2,1)S(1)} %get-tuple-element.58.weight.refs_2_) | copy-start | bytes 25165828
  30.4 6.8 %collective-permute-start.10 = (bf16[2,48,512]{2,1,0:T(8,128)(2,1)S(1)}, bf16[2,48,512]{2,1,0:T(8,128)(2,1)S(1)}, u32[]{:S(2)}, u32[]{:S(2)}) collective-permute-start(bf16[2,48,512]{2,1,0:T(8,128)(2,1)S(1)} %get-tuple-element.56), channel_id=1, source_target_pairs={{0,4},{4,0},{8,12},{12,8},{1,5},{5,1},{9,13},{13,9},{2,6},{6,2},{1... | collective-permute-start | bytes 294920 | tf_op jit(solution)/shard_map/ppermute | solution.py:318
  30.4 11.6 %collective-permute-start.7 = (bf16[576,128]{1,0:T(8,128)(2,1)S(1)}, bf16[576,128]{1,0:T(8,128)(2,1)S(1)}, u32[]{:S(2)}, u32[]{:S(2)}) collective-permute-start(bf16[576,128]{1,0:T(8,128)(2,1)S(1)} %get-tuple-element.51), channel_id=1, source_target_pairs={{0,1},{1,2},{2,3},{3,0},{4,5},{5,6},{6,7},{7,4},{8,9},{9,10},{10,1... | collective-permute-start | bytes 442376 | tf_op jit(solution)/shard_map/ppermute | solution.py:251
  32.3 13.6 %collective-permute-start.8 = (bf16[576,128]{1,0:T(8,128)(2,1)S(1)}, bf16[576,128]{1,0:T(8,128)(2,1)S(1)}, u32[]{:S(2)}, u32[]{:S(2)}) collective-permute-start(bf16[576,128]{1,0:T(8,128)(2,1)S(1)} %get-tuple-element.53), channel_id=1, source_target_pairs={{0,2},{1,3},{2,0},{3,1},{4,6},{5,7},{6,4},{7,5},{8,10},{9,11},{10,... | collective-permute-start | bytes 442376 | tf_op jit(solution)/shard_map/ppermute | solution.py:251
  35.7 10.3 %collective-permute-start.9 = (bf16[576,128]{1,0:T(8,128)(2,1)S(1)}, bf16[576,128]{1,0:T(8,128)(2,1)S(1)}, u32[]{:S(2)}, u32[]{:S(2)}) collective-permute-start(bf16[576,128]{1,0:T(8,128)(2,1)S(1)} %get-tuple-element.55), channel_id=1, source_target_pairs={{0,3},{1,0},{2,1},{3,2},{4,7},{5,4},{6,5},{7,6},{8,11},{9,8},{10,9... | collective-permute-start | bytes 442376 | tf_op jit(solution)/shard_map/ppermute | solution.py:251
  51.8 2.2 %collective-permute-start.12 = (bf16[2,144,512]{2,1,0:T(8,128)(2,1)S(1)}, bf16[2,144,512]{2,1,0:T(8,128)(2,1)S(1)}, u32[]{:S(2)}, u32[]{:S(2)}) collective-permute-start(bf16[2,144,512]{2,1,0:T(8,128)(2,1)S(1)} %get-tuple-element.68), channel_id=1, source_target_pairs={{0,4},{4,0},{8,12},{12,8},{1,5},{5,1},{9,13},{13,9},{2,6},{6,2},{1... | collective-permute-start | bytes 884744 | tf_op jit(solution)/shard_map/ppermute | solution.py:318
  51.9 16.0 %collective-permute-start.13 = (bf16[48,4096]{1,0:T(8,128)(2,1)S(1)}, bf16[48,4096]{1,0:T(8,128)(2,1)S(1)}, u32[]{:S(2)}, u32[]{:S(2)}) collective-permute-start(bf16[48,4096]{1,0:T(8,128)(2,1)S(1)} %get-tuple-element.61), channel_id=1, source_target_pairs={{0,8},{4,12},{8,0},{12,4},{1,9},{5,13},{9,1},{13,5},{2,10},{6,14},... | collective-permute-start | bytes 1179656 | tf_op jit(solution)/shard_map/ppermute | solution.py:366
  53.5 21.7 %collective-permute-start.22 = (bf16[48,4096]{1,0:T(8,128)(2,1)S(1)}, bf16[48,4096]{1,0:T(8,128)(2,1)S(1)}, u32[]{:S(2)}, u32[]{:S(2)}) collective-permute-start(bf16[48,4096]{1,0:T(8,128)(2,1)S(1)} %get-tuple-element.62), channel_id=1, source_target_pairs={{0,8},{4,12},{8,0},{12,4},{1,9},{5,13},{9,1},{13,5},{2,10},{6,14},... | collective-permute-start | bytes 1179656 | tf_op jit(solution)/shard_map/ppermute | solution.py:366
  54.0 3.4 %copy-start.1 = (bf16[512,8192]{1,0:T(8,128)(2,1)S(1)}, bf16[512,8192]{1,0:T(8,128)(2,1)}, u32[]{:S(2)}) copy-start(bf16[512,8192]{1,0:T(8,128)(2,1)} %copy-done) | copy-start | bytes 25165828
  65.8 14.9 %collective-permute-start.14 = (bf16[48,4096]{1,0:T(8,128)(2,1)S(1)}, bf16[48,4096]{1,0:T(8,128)(2,1)S(1)}, u32[]{:S(2)}, u32[]{:S(2)}) collective-permute-start(bf16[48,4096]{1,0:T(8,128)(2,1)S(1)} %get-tuple-element.72), channel_id=1, source_target_pairs={{0,8},{4,12},{8,0},{12,4},{1,9},{5,13},{9,1},{13,5},{2,10},{6,14},... | collective-permute-start | bytes 1179656 | tf_op jit(solution)/shard_map/ppermute | solution.py:366
  67.4 21.8 %collective-permute-start.23 = (bf16[48,4096]{1,0:T(8,128)(2,1)S(1)}, bf16[48,4096]{1,0:T(8,128)(2,1)S(1)}, u32[]{:S(2)}, u32[]{:S(2)}) collective-permute-start(bf16[48,4096]{1,0:T(8,128)(2,1)S(1)} %get-tuple-element.80), channel_id=1, source_target_pairs={{0,8},{4,12},{8,0},{12,4},{1,9},{5,13},{9,1},{13,5},{2,10},{6,14},... | collective-permute-start | bytes 1179656 | tf_op jit(solution)/shard_map/ppermute | solution.py:366
  68.0 15.1 %collective-permute-start.15 = (bf16[48,4096]{1,0:T(8,128)(2,1)S(1)}, bf16[48,4096]{1,0:T(8,128)(2,1)S(1)}, u32[]{:S(2)}, u32[]{:S(2)}) collective-permute-start(bf16[48,4096]{1,0:T(8,128)(2,1)S(1)} %add_convert_fusion.13), channel_id=1, source_target_pairs={{0,1},{3,2},{4,5},{7,6},{8,9},{11,10},{12,13},{15,14},{16,17},{19,... | collective-permute-start | bytes 1179656 | tf_op jit(solution)/shard_map/ppermute | solution.py:373
  73.6 24.0 %collective-permute-start.17 = (bf16[48,4096]{1,0:T(8,128)(2,1)S(1)}, bf16[48,4096]{1,0:T(8,128)(2,1)S(1)}, u32[]{:S(2)}, u32[]{:S(2)}) collective-permute-start(bf16[48,4096]{1,0:T(8,128)(2,1)S(1)} %get-tuple-element.76), channel_id=1, source_target_pairs={{0,8},{4,12},{8,0},{12,4},{1,9},{5,13},{9,1},{13,5},{2,10},{6,14},... | collective-permute-start | bytes 1179656 | tf_op jit(solution)/shard_map/ppermute | solution.py:366
  75.3 19.5 %collective-permute-start.24 = (bf16[48,4096]{1,0:T(8,128)(2,1)S(1)}, bf16[48,4096]{1,0:T(8,128)(2,1)S(1)}, u32[]{:S(2)}, u32[]{:S(2)}) collective-permute-start(bf16[48,4096]{1,0:T(8,128)(2,1)S(1)} %add_convert_fusion.6), channel_id=1, source_target_pairs={{0,1},{3,2},{4,5},{7,6},{8,9},{11,10},{12,13},{15,14},{16,17},{19,... | collective-permute-start | bytes 1179656 | tf_op jit(solution)/shard_map/ppermute | solution.py:373
  80.8 25.3 %collective-permute-start.26 = (bf16[48,4096]{1,0:T(8,128)(2,1)S(1)}, bf16[48,4096]{1,0:T(8,128)(2,1)S(1)}, u32[]{:S(2)}, u32[]{:S(2)}) collective-permute-start(bf16[48,4096]{1,0:T(8,128)(2,1)S(1)} %get-tuple-element.84), channel_id=1, source_target_pairs={{0,8},{4,12},{8,0},{12,4},{1,9},{5,13},{9,1},{13,5},{2,10},{6,14},... | collective-permute-start | bytes 1179656 | tf_op jit(solution)/shard_map/ppermute | solution.py:366
  83.5 19.7 %collective-permute-start.20 = (bf16[48,4096]{1,0:T(8,128)(2,1)S(1)}, bf16[48,4096]{1,0:T(8,128)(2,1)S(1)}, u32[]{:S(2)}, u32[]{:S(2)}) collective-permute-start(bf16[48,4096]{1,0:T(8,128)(2,1)S(1)} %fusion.1), channel_id=1, source_target_pairs={{2,1},{3,2},{6,5},{7,6},{10,9},{11,10},{14,13},{15,14},{18,17},{19... | collective-permute-start | bytes 1179656 | tf_op jit(solution)/shard_map/ppermute | solution.py:382
  89.2 15.6 %collective-permute-start.18 = (bf16[48,4096]{1,0:T(8,128)(2,1)S(1)}, bf16[48,4096]{1,0:T(8,128)(2,1)S(1)}, u32[]{:S(2)}, u32[]{:S(2)}) collective-permute-start(bf16[48,4096]{1,0:T(8,128)(2,1)S(1)} %get-tuple-element.85), channel_id=1, source_target_pairs={{0,1},{1,2},{4,5},{5,6},{8,9},{9,10},{12,13},{13,14},{16,17},{17,1... | collective-permute-start | bytes 1179656 | tf_op jit(solution)/shard_map/ppermute | solution.py:382
  95.2 16.5 %collective-permute-start.29 = (bf16[48,4096]{1,0:T(8,128)(2,1)S(1)}, bf16[48,4096]{1,0:T(8,128)(2,1)S(1)}, u32[]{:S(2)}, u32[]{:S(2)}) collective-permute-start(bf16[48,4096]{1,0:T(8,128)(2,1)S(1)} %fusion.3), channel_id=1, source_target_pairs={{2,1},{3,2},{6,5},{7,6},{10,9},{11,10},{14,13},{15,14},{18,17},{19... | collective-permute-start | bytes 1179656 | tf_op jit(solution)/shard_map/ppermute | solution.py:382
  97.6 15.3 %collective-permute-start.27 = (bf16[48,4096]{1,0:T(8,128)(2,1)S(1)}, bf16[48,4096]{1,0:T(8,128)(2,1)S(1)}, u32[]{:S(2)}, u32[]{:S(2)}) collective-permute-start(bf16[48,4096]{1,0:T(8,128)(2,1)S(1)} %get-tuple-element.87), channel_id=1, source_target_pairs={{0,1},{1,2},{4,5},{5,6},{8,9},{9,10},{12,13},{13,14},{16,17},{17,1... | collective-permute-start | bytes 1179656 | tf_op jit(solution)/shard_map/ppermute | solution.py:382
  103.2 14.7 %collective-permute-start.16 = (bf16[48,4096]{1,0:T(8,128)(2,1)S(1)}, bf16[48,4096]{1,0:T(8,128)(2,1)S(1)}, u32[]{:S(2)}, u32[]{:S(2)}) collective-permute-start(bf16[48,4096]{1,0:T(8,128)(2,1)S(1)} %get-tuple-element.73), channel_id=1, source_target_pairs={{0,8},{4,12},{8,0},{12,4},{1,9},{5,13},{9,1},{13,5},{2,10},{6,14},... | collective-permute-start | bytes 1179656 | tf_op jit(solution)/shard_map/ppermute | solution.py:366
  104.8 21.0 %collective-permute-start.25 = (bf16[48,4096]{1,0:T(8,128)(2,1)S(1)}, bf16[48,4096]{1,0:T(8,128)(2,1)S(1)}, u32[]{:S(2)}, u32[]{:S(2)}) collective-permute-start(bf16[48,4096]{1,0:T(8,128)(2,1)S(1)} %get-tuple-element.81), channel_id=1, source_target_pairs={{0,8},{4,12},{8,0},{12,4},{1,9},{5,13},{9,1},{13,5},{2,10},{6,14},... | collective-permute-start | bytes 1179656 | tf_op jit(solution)/shard_map/ppermute | solution.py:366
  106.0 15.1 %collective-permute-start.19 = (bf16[48,4096]{1,0:T(8,128)(2,1)S(1)}, bf16[48,4096]{1,0:T(8,128)(2,1)S(1)}, u32[]{:S(2)}, u32[]{:S(2)}) collective-permute-start(bf16[48,4096]{1,0:T(8,128)(2,1)S(1)} %get-tuple-element.89), channel_id=1, source_target_pairs={{0,1},{1,2},{2,3},{4,5},{5,6},{6,7},{8,9},{9,10},{10,11},{12,13},{... | collective-permute-start | bytes 1179656 | tf_op jit(solution)/shard_map/ppermute | solution.py:382
  111.6 13.9 %collective-permute-start.21 = (bf16[48,4096]{1,0:T(8,128)(2,1)S(1)}, bf16[48,4096]{1,0:T(8,128)(2,1)S(1)}, u32[]{:S(2)}, u32[]{:S(2)}) collective-permute-start(bf16[48,4096]{1,0:T(8,128)(2,1)S(1)} %get-tuple-element.90), channel_id=1, source_target_pairs={{1,0},{2,1},{3,2},{5,4},{6,5},{7,6},{9,8},{10,9},{11,10},{13,12},{... | collective-permute-start | bytes 1179656 | tf_op jit(solution)/shard_map/ppermute | solution.py:382
  113.3 14.4 %collective-permute-start.28 = (bf16[48,4096]{1,0:T(8,128)(2,1)S(1)}, bf16[48,4096]{1,0:T(8,128)(2,1)S(1)}, u32[]{:S(2)}, u32[]{:S(2)}) collective-permute-start(bf16[48,4096]{1,0:T(8,128)(2,1)S(1)} %get-tuple-element.91), channel_id=1, source_target_pairs={{0,1},{1,2},{2,3},{4,5},{5,6},{6,7},{8,9},{9,10},{10,11},{12,13},{... | collective-permute-start | bytes 1179656 | tf_op jit(solution)/shard_map/ppermute | solution.py:382
  117.9 14.0 %collective-permute-start.30 = (bf16[48,4096]{1,0:T(8,128)(2,1)S(1)}, bf16[48,4096]{1,0:T(8,128)(2,1)S(1)}, u32[]{:S(2)}, u32[]{:S(2)}) collective-permute-start(bf16[48,4096]{1,0:T(8,128)(2,1)S(1)} %get-tuple-element.92), channel_id=1, source_target_pairs={{1,0},{2,1},{3,2},{5,4},{6,5},{7,6},{9,8},{10,9},{11,10},{13,12},{... | collective-permute-start | bytes 1179656 | tf_op jit(solution)/shard_map/ppermute | solution.py:382

commit v4 on v3

--- a/solution.py
+++ b/solution.py
@@ -22,6 +22,7 @@
 HBM = pl.BlockSpec(memory_space=pltpu.HBM)
 LIMIT = pltpu.CompilerParams(vmem_limit_bytes=20 << 20)
 TILE = 1024
+FREE = pl.CostEstimate(flops=0, bytes_accessed=0, transcendentals=0)
 
 
 def destination_order(count):
@@ -89,7 +90,7 @@
         in_specs=[VMEM] * 3,
         out_specs=[VMEM] * (slabs * len(stages)),
         compiler_params=LIMIT,
-        cost_estimate=pl.CostEstimate(flops=0, bytes_accessed=4 * queries.size, transcendentals=0),
+        cost_estimate=FREE,
         name="pack",
     )(queries, keys, values)
 
@@ -177,30 +178,30 @@
         scratch_shapes=[pltpu.VMEM((span, HEAD_SIZE), BF16)] * 2
         + [pltpu.SemaphoreType.DMA((fetched,))] * (fetched > 0),
         compiler_params=LIMIT,
-        cost_estimate=pl.CostEstimate(
-            flops=4 * terms * HEAD_SIZE, bytes_accessed=sum(w.size * 2 for w in weights), transcendentals=terms
-        ),
+        cost_estimate=FREE,
         name="attend",
     )(key_doc, *now, *before, *queries, *[in_hbm(w) for w in weights])
 
 
-def first_half_kernel(rows_here, weight, total):
+def first_half_kernel(rows_here, weight, fetch, total, fetched, semaphore):
+    copy = pltpu.make_async_copy(fetch, fetched, semaphore)
+    copy.start()
     for n in range(0, total.shape[1], TILE):
         total[:, n : n + TILE] = jnp.dot(rows_here[...], weight[:, n : n + TILE], preferred_element_type=F32)
-
-
-def first_half(rows_here, weight):
-    count, depth = rows_here.shape
-    width = weight.shape[1]
+    copy.wait()
+
+
+def first_half(rows_here, weight, fetch):
     return pl.pallas_call(
         first_half_kernel,
-        out_shape=pltpu.VMEM((count, width), F32),
-        in_specs=[VMEM, VMEM],
-        out_specs=VMEM,
+        out_shape=[pltpu.VMEM((rows_here.shape[0], weight.shape[1]), F32), pltpu.VMEM(fetch.shape, fetch.dtype)],
+        in_specs=[VMEM, VMEM, HBM],
+        out_specs=[VMEM, VMEM],
+        scratch_shapes=[pltpu.SemaphoreType.DMA],
         compiler_params=LIMIT,
-        cost_estimate=pl.CostEstimate(flops=2 * count * depth * width, bytes_accessed=0, transcendentals=0),
+        cost_estimate=FREE,
         name="first_half",
-    )(rows_here, in_vmem(weight))
+    )(rows_here, in_vmem(weight), in_hbm(fetch))
 
 
 def project_kernel(*refs, terms, begun, share, halves):
@@ -226,9 +227,7 @@
         in_specs=[VMEM] * (2 * len(lhs) + len(start)),
         out_specs=[VMEM] * (count // share * halves),
         compiler_params=LIMIT,
-        cost_estimate=pl.CostEstimate(
-            flops=2 * len(lhs) * count * depth * width, bytes_accessed=2 * count * width, transcendentals=0
-        ),
+        cost_estimate=FREE,
         name="project",
     )(*lhs, *[in_vmem(w) for w in rhs], *[in_vmem(s) for s in start])
 
@@ -319,7 +318,7 @@
         keep, theirs = (a.reshape(-1, a.shape[-1]) for a in (keep, theirs))
         if n == 0 and staged:
             weight_near = fetched[0]
-            begun = first_half(keep, weight_near)
+            begun, weight_sibling = first_half(keep, weight_near, weight_sibling)
             results = project([theirs], [weight_sibling], [begun], share, halves)
         else:
             if fetched:

time: 134 us -> 130 us (0.970)
  local copies, waits for them, and re-layouts: 6.62 us -> 13.2 us
  Pallas kernels: 24.2 us -> 19.4 us
  starting transfers between devices: 64.9 us -> 60.8 us
  waiting for transfers between devices: 32.3 us -> 29.1 us
    ppermute x8, waiting for transfers between devices: 9.83 us -> 0.27 us  [on_device(): total = total + lax.ppermute(piece, 'head', route).astype(F32)]
    ppermute x2, waiting for transfers between devices: 0.9 us -> 7.81 us  [on_device(): lax.ppermute(sent, 'wsh', [(i, i + 1) for i in up] + [(i, i - 1) for i in...]
    pallas_call x2, Pallas kernels: 13.3 us -> 6.5 us  [project(): pl.pallas_call(partial(project_kernel, terms=len(lhs), begun=len(start),...]
    unnamed x10 -> x14, local copies, waits for them, and re-layouts: 6.3 us -> 12.9 us
    ppermute x8, starting transfers between devices: 25.3 us -> 21.7 us  [on_device(): lax.ppermute(sent[direction], 'wsh', [(i, i + direction) for i in found])]
    ppermute x6, waiting for transfers between devices: 6.24 us -> 2.95 us  [around(): lax.ppermute(array, 'wsh', [(i, (i + k) % slabs) for i in range(slabs)])]
    ppermute x8, waiting for transfers between devices: 12.5 us -> 15.3 us  [on_device(): lax.ppermute(sent[direction], 'wsh', [(i, i + direction) for i in found])]
    pallas_call x1, Pallas kernels: 1.46 us -> 3.39 us  [first_half(): pl.pallas_call(first_half_kernel, out_shape=[pltpu.VMEM((rows_here.shape[...]
  transfers between devices with their start and end apart: 31 -> 31, of which waited for: 13 -> 12; matrix products, arithmetic and copies ran while one was open for 3% -> 4% of each run, Pallas kernels for 14% -> 15%
where the time goes in v4:
time: 130 us; the launch traced here: 129 us
  starting transfers between devices  60.8 us (47%)
  waiting for transfers between devices  29.1 us (22%)
  Pallas kernels  19.4 us (15%)
  local copies, waits for them, and re-layouts  13.2 us (10%)
  other arithmetic  5.62 us (4%)
    ppermute x8, starting transfers between devices, on_device(): lax.ppermute(sent[direction], 'wsh', [(i, i + direction) for i in found])  21.7 us
    ppermute x8, waiting for transfers between devices, on_device(): lax.ppermute(sent[direction], 'wsh', [(i, i + direction) for i in found])  15.3 us
    unnamed x14, local copies, waits for them, and re-layouts  12.9 us
    ppermute x6, starting transfers between devices, around(): lax.ppermute(array, 'wsh', [(i, (i + k) % slabs) for i in range(slabs)])  11.8 us
    ppermute x8, starting transfers between devices, on_device(): total = total + lax.ppermute(piece, 'head', route).astype(F32)  10.1 us
    ppermute x4, starting transfers between devices, on_device(): lax.ppermute(a[:2 * block], 'srv', [(g, g + 1) for g in range(groups - 1)])  9.44 us
    pallas_call x2, Pallas kernels, attend(): pl.pallas_call(partial(attend_kernel, slabs=slabs, heads=heads, share=sha...  9.24 us
    ppermute x2, waiting for transfers between devices, on_device(): lax.ppermute(sent, 'wsh', [(i, i + 1) for i in up] + [(i, i - 1) for i in...  7.81 us
  transfers between devices with their start and end apart: 31, of which 12 were waited for; matrix products, arithmetic and copies ran while one was open for 4% of the time, Pallas kernels for 15%

profile of v4, /device:TPU:0, one launch (start us, length us, event | category | flops | bytes accessed | tf_op | source)
XLA Modules:
  0.0 128.6 jit_solution(3410942006105278785)
XLA Ops:
  0.5 1.1 copy-done.4
  1.6 0.9 copy-done.5
  2.5 0.9 copy-done.6
  3.7 2.6 %collective-permute-start = (bf16[576,128]{1,0:T(8,128)(2,1)S(1)}, bf16[576,128]{1,0:T(8,128)(2,1)S(1)}, u32[]{:S(2)}, u32[]{:S(2)}) collective-permute-start(bf16[576,128]{1,0:T(8,128)(2,1)S(1)} %get-tuple-element.48), channel_id=1, source_target_pairs={{0,1},{1,2},{2,3},{3,0},{4,5},{5,6},{6,7},{7,4},{8,9},{9,10},{10,1... | collective-permute-start | bytes 442376 | tf_op jit(solution)/shard_map/ppermute | solution.py:250
  6.3 2.6 %collective-permute-start.1 = (bf16[576,128]{1,0:T(8,128)(2,1)S(1)}, bf16[576,128]{1,0:T(8,128)(2,1)S(1)}, u32[]{:S(2)}, u32[]{:S(2)}) collective-permute-start(bf16[576,128]{1,0:T(8,128)(2,1)S(1)} %get-tuple-element.49), channel_id=1, source_target_pairs={{0,2},{1,3},{2,0},{3,1},{4,6},{5,7},{6,4},{7,5},{8,10},{9,11},{10,... | collective-permute-start | bytes 442376 | tf_op jit(solution)/shard_map/ppermute | solution.py:250
  8.9 1.3 %collective-permute-start.2 = (bf16[576,128]{1,0:T(8,128)(2,1)S(1)}, bf16[576,128]{1,0:T(8,128)(2,1)S(1)}, u32[]{:S(2)}, u32[]{:S(2)}) collective-permute-start(bf16[576,128]{1,0:T(8,128)(2,1)S(1)} %get-tuple-element.50), channel_id=1, source_target_pairs={{0,3},{1,0},{2,1},{3,2},{4,7},{5,4},{6,5},{7,6},{8,11},{9,8},{10,9... | collective-permute-start | bytes 442376 | tf_op jit(solution)/shard_map/ppermute | solution.py:250
  10.2 3.4 %collective-permute-start.3 = (bf16[384,128]{1,0:T(8,128)(2,1)S(1)}, bf16[384,128]{1,0:T(8,128)(2,1)S(1)}, u32[]{:S(2)}, u32[]{:S(2)}) collective-permute-start(bf16[384,128]{1,0:T(8,128)(2,1)S(1)} %slice.40), channel_id=1, source_target_pairs={{0,16},{1,17},{2,18},{3,19},{4,20},{5,21},{6,22},{7,23},{8,24},{9,... | collective-permute-start | bytes 294920 | tf_op jit(solution)/shard_map/ppermute | solution.py:265
  13.7 0.7 convert_element_type.180
  14.5 0.8 compare_bitcast_fusion.3
  15.6 1.3 %collective-permute-start.4 = (bf16[384,128]{1,0:T(8,128)(2,1)S(1)}, bf16[384,128]{1,0:T(8,128)(2,1)S(1)}, u32[]{:S(2)}, u32[]{:S(2)}) collective-permute-start(bf16[384,128]{1,0:T(8,128)(2,1)S(1)} %slice.44), channel_id=1, source_target_pairs={{0,16},{1,17},{2,18},{3,19},{4,20},{5,21},{6,22},{7,23},{8,24},{9,... | collective-permute-start | bytes 294920 | tf_op jit(solution)/shard_map/ppermute | solution.py:265
  16.9 2.3 %collective-permute-done.1.refs_2_.refs_10_ = bf16[576,128]{1,0:T(8,128)(2,1)S(1)} collective-permute-done((bf16[576,128]{1,0:T(8,128)(2,1)S(1)}, bf16[576,128]{1,0:T(8,128)(2,1)S(1)}, u32[]{:S(2)}, u32[]{:S(2)}) %collective-permute-start.1) | collective-permute-done | bytes 147488 | tf_op jit(solution)/shard_map/ppermute | solution.py:250
  19.2 3.4 %collective-permute-start.5 = (bf16[384,128]{1,0:T(8,128)(2,1)S(1)}, bf16[384,128]{1,0:T(8,128)(2,1)S(1)}, u32[]{:S(2)}, u32[]{:S(2)}) collective-permute-start(bf16[384,128]{1,0:T(8,128)(2,1)S(1)} %slice.45), channel_id=1, source_target_pairs={{0,16},{1,17},{2,18},{3,19},{4,20},{5,21},{6,22},{7,23},{8,24},{9,... | collective-permute-start | bytes 294920 | tf_op jit(solution)/shard_map/ppermute | solution.py:265
  22.7 1.3 %collective-permute-start.6 = (bf16[384,128]{1,0:T(8,128)(2,1)S(1)}, bf16[384,128]{1,0:T(8,128)(2,1)S(1)}, u32[]{:S(2)}, u32[]{:S(2)}) collective-permute-start(bf16[384,128]{1,0:T(8,128)(2,1)S(1)} %slice.46), channel_id=1, source_target_pairs={{0,16},{1,17},{2,18},{3,19},{4,20},{5,21},{6,22},{7,23},{8,24},{9,... | collective-permute-start | bytes 294920 | tf_op jit(solution)/shard_map/ppermute | solution.py:265
  24.2 1.4 %collective-permute-done.5.refs_6_ = bf16[384,128]{1,0:T(8,128)(2,1)S(1)} collective-permute-done((bf16[384,128]{1,0:T(8,128)(2,1)S(1)}, bf16[384,128]{1,0:T(8,128)(2,1)S(1)}, u32[]{:S(2)}, u32[]{:S(2)}) %collective-permute-start.5) | collective-permute-done | bytes 98336 | tf_op jit(solution)/shard_map/ppermute | solution.py:265
  25.6 1.3 %collective-permute-done.6.refs_7_ = bf16[384,128]{1,0:T(8,128)(2,1)S(1)} collective-permute-done((bf16[384,128]{1,0:T(8,128)(2,1)S(1)}, bf16[384,128]{1,0:T(8,128)(2,1)S(1)}, u32[]{:S(2)}, u32[]{:S(2)}) %collective-permute-start.6) | collective-permute-done | bytes 98336 | tf_op jit(solution)/shard_map/ppermute | solution.py:265
  27.0 3.4 %attend.2 = (bf16[2,48,512]{2,1,0:T(8,128)(2,1)S(1)}, bf16[2,48,512]{2,1,0:T(8,128)(2,1)S(1)}, bf16[512,8192]{1,0:T(8,128)(2,1)S(1)}) custom-call(f32[8,1,768]{2,1,0:T(1,128)S(1)} %reshape.55.key_doc, bf16[576,128]{1,0:T(8,128)(2,1)S(1)} %get-tuple-element.47.refs_0_.refs_8_, bf16[576,128]{1,0:T(8,128)(2,1)S(1)} %collective-permute-done.refs_1_.refs_9_, ...), custom_call_target="tpu_custom_call" | custom-call | tf_op jit(solution)/shard_map/attend/pallas_call | solution.py:171
  30.4 1.9 %collective-permute-start.7 = (bf16[576,128]{1,0:T(8,128)(2,1)S(1)}, bf16[576,128]{1,0:T(8,128)(2,1)S(1)}, u32[]{:S(2)}, u32[]{:S(2)}) collective-permute-start(bf16[576,128]{1,0:T(8,128)(2,1)S(1)} %get-tuple-element.53), channel_id=1, source_target_pairs={{0,1},{1,2},{2,3},{3,0},{4,5},{5,6},{6,7},{7,4},{8,9},{9,10},{10,1... | collective-permute-start | bytes 442376 | tf_op jit(solution)/shard_map/ppermute | solution.py:250
  32.3 3.4 %collective-permute-start.8 = (bf16[576,128]{1,0:T(8,128)(2,1)S(1)}, bf16[576,128]{1,0:T(8,128)(2,1)S(1)}, u32[]{:S(2)}, u32[]{:S(2)}) collective-permute-start(bf16[576,128]{1,0:T(8,128)(2,1)S(1)} %get-tuple-element.55), channel_id=1, source_target_pairs={{0,2},{1,3},{2,0},{3,1},{4,6},{5,7},{6,4},{7,5},{8,10},{9,11},{10,... | collective-permute-start | bytes 442376 | tf_op jit(solution)/shard_map/ppermute | solution.py:250
  35.7 3.4 %first_half.1 = (f32[96,8192]{1,0:T(8,128)S(1)}, bf16[512,8192]{1,0:T(8,128)(2,1)S(1)}) custom-call(bf16[96,512]{1,0:T(8,128)(2,1)S(1)} %bitcast.19, bf16[512,8192]{1,0:T(8,128)(2,1)S(1)} %get-tuple-element.60.weight.refs_2_, bf16[512,8192]{1,0:T(8,128)(2,1)} %collective-permute-done.11.fetch), custom_call_target="tpu_custom_call" | custom-call | tf_op jit(solution)/shard_map/first_half/pallas_call | solution.py:195
  39.1 1.5 %project.2 = (bf16[48,4096]{1,0:T(8,128)(2,1)S(1)}, bf16[48,4096]{1,0:T(8,128)(2,1)S(1)}, bf16[48,4096]{1,0:T(8,128)(2,1)S(1)}, bf16[48,4096]{1,0:T(8,128)(2,1)S(1)}) custom-call(bf16[96,512]{1,0:T(8,128)(2,1)S(1)} %bitcast.18, bf16[512,8192]{1,0:T(8,128)(2,1)S(1)} %get-tuple-element.61.refs_1_.refs_3_, f32[96,8192]{1,0:T(8,128)S(1)} %get-tuple-element.62.refs_2_), custom_call_target="tpu_custom_call" | custom-call | tf_op jit(solution)/shard_map/project/pallas_call | solution.py:224
  40.6 3.2 %copy-done.2 = bf16[512,8192]{1,0:T(8,128)(2,1)} copy-done((bf16[512,8192]{1,0:T(8,128)(2,1)}, bf16[512,8192]{1,0:T(8,128)(2,1)S(1)}, u32[]{:S(2)}) %copy-start.2) | copy-done | bytes 8388632
  43.9 1.5 %collective-permute-start.22 = (bf16[48,4096]{1,0:T(8,128)(2,1)S(1)}, bf16[48,4096]{1,0:T(8,128)(2,1)}, u32[]{:S(2)}, u32[]{:S(2)}) collective-permute-start(bf16[48,4096]{1,0:T(8,128)(2,1)S(1)} %get-tuple-element.66), channel_id=1, source_target_pairs={{0,8},{4,12},{8,0},{12,4},{1,9},{5,13},{9,1},{13,5},{2,10},{6,14},... | collective-permute-start | bytes 1179656 | tf_op jit(solution)/shard_map/ppermute | solution.py:365
  46.0 5.9 %attend.3 = (bf16[2,144,512]{2,1,0:T(8,128)(2,1)S(1)}, bf16[2,144,512]{2,1,0:T(8,128)(2,1)S(1)}) custom-call(f32[8,1,768]{2,1,0:T(1,128)S(1)} %reshape.55.key_doc, bf16[576,128]{1,0:T(8,128)(2,1)S(1)} %get-tuple-element.47.refs_0_.refs_8_, bf16[576,128]{1,0:T(8,128)(2,1)S(1)} %collective-permute-done.refs_1_.refs_9_, ...), custom_call_target="tpu_custom_call" | custom-call | tf_op jit(solution)/shard_map/attend/pallas_call | solution.py:171
  51.9 1.6 %collective-permute-start.13 = (bf16[48,4096]{1,0:T(8,128)(2,1)S(1)}, bf16[48,4096]{1,0:T(8,128)(2,1)S(1)}, u32[]{:S(2)}, u32[]{:S(2)}) collective-permute-start(bf16[48,4096]{1,0:T(8,128)(2,1)S(1)} %get-tuple-element.65), channel_id=1, source_target_pairs={{0,8},{4,12},{8,0},{12,4},{1,9},{5,13},{9,1},{13,5},{2,10},{6,14},... | collective-permute-start | bytes 1179656 | tf_op jit(solution)/shard_map/ppermute | solution.py:365
  53.5 3.4 %copy-done.1 = bf16[512,8192]{1,0:T(8,128)(2,1)S(1)} copy-done((bf16[512,8192]{1,0:T(8,128)(2,1)S(1)}, bf16[512,8192]{1,0:T(8,128)(2,1)}, u32[]{:S(2)}) %copy-start.1) | copy-done | bytes 8388632
  56.9 3.4 %copy-done.3 = bf16[512,8192]{1,0:T(8,128)(2,1)S(1)} copy-done((bf16[512,8192]{1,0:T(8,128)(2,1)S(1)}, bf16[512,8192]{1,0:T(8,128)(2,1)}, u32[]{:S(2)}) %copy-start.3) | copy-done | bytes 8388632
  60.3 5.0 %project.3 = (bf16[48,4096]{1,0:T(8,128)(2,1)S(1)}, bf16[48,4096]{1,0:T(8,128)(2,1)S(1)}, bf16[48,4096]{1,0:T(8,128)(2,1)S(1)}, bf16[48,4096]{1,0:T(8,128)(2,1)S...) custom-call(bf16[288,512]{1,0:T(8,128)(2,1)S(1)} %bitcast.16, ...), custom_call_target="tpu_custom_call" | custom-call | tf_op jit(solution)/shard_map/project/pallas_call | solution.py:224
  65.3 1.6 %collective-permute-start.23 = (bf16[48,4096]{1,0:T(8,128)(2,1)S(1)}, bf16[48,4096]{1,0:T(8,128)(2,1)S(1)}, u32[]{:S(2)}, u32[]{:S(2)}) collective-permute-start(bf16[48,4096]{1,0:T(8,128)(2,1)S(1)} %get-tuple-element.84), channel_id=1, source_target_pairs={{0,8},{4,12},{8,0},{12,4},{1,9},{5,13},{9,1},{13,5},{2,10},{6,14},... | collective-permute-start | bytes 1179656 | tf_op jit(solution)/shard_map/ppermute | solution.py:365
  67.4 1.1 add_convert_fusion.6
  68.5 5.7 %collective-permute-start.24 = (bf16[48,4096]{1,0:T(8,128)(2,1)S(1)}, bf16[48,4096]{1,0:T(8,128)(2,1)S(1)}, u32[]{:S(2)}, u32[]{:S(2)}) collective-permute-start(bf16[48,4096]{1,0:T(8,128)(2,1)S(1)} %add_convert_fusion.6), channel_id=1, source_target_pairs={{0,1},{3,2},{4,5},{7,6},{8,9},{11,10},{12,13},{15,14},{16,17},{19,... | collective-permute-start | bytes 1179656 | tf_op jit(solution)/shard_map/ppermute | solution.py:372
  74.2 1.5 %collective-permute-start.26 = (bf16[48,4096]{1,0:T(8,128)(2,1)S(1)}, bf16[48,4096]{1,0:T(8,128)(2,1)S(1)}, u32[]{:S(2)}, u32[]{:S(2)}) collective-permute-start(bf16[48,4096]{1,0:T(8,128)(2,1)S(1)} %get-tuple-element.88), channel_id=1, source_target_pairs={{0,8},{4,12},{8,0},{12,4},{1,9},{5,13},{9,1},{13,5},{2,10},{6,14},... | collective-permute-start | bytes 1179656 | tf_op jit(solution)/shard_map/ppermute | solution.py:365
  75.7 1.3 %collective-permute-start.15 = (bf16[48,4096]{1,0:T(8,128)(2,1)S(1)}, bf16[48,4096]{1,0:T(8,128)(2,1)S(1)}, u32[]{:S(2)}, u32[]{:S(2)}) collective-permute-start(bf16[48,4096]{1,0:T(8,128)(2,1)S(1)} %add_convert_fusion.13), channel_id=1, source_target_pairs={{0,1},{3,2},{4,5},{7,6},{8,9},{11,10},{12,13},{15,14},{16,17},{19,... | collective-permute-start | bytes 1179656 | tf_op jit(solution)/shard_map/ppermute | solution.py:372
  77.3 1.5 %collective-permute-start.17 = (bf16[48,4096]{1,0:T(8,128)(2,1)S(1)}, bf16[48,4096]{1,0:T(8,128)(2,1)S(1)}, u32[]{:S(2)}, u32[]{:S(2)}) collective-permute-start(bf16[48,4096]{1,0:T(8,128)(2,1)S(1)} %get-tuple-element.80), channel_id=1, source_target_pairs={{0,8},{4,12},{8,0},{12,4},{1,9},{5,13},{9,1},{13,5},{2,10},{6,14},... | collective-permute-start | bytes 1179656 | tf_op jit(solution)/shard_map/ppermute | solution.py:365
  78.8 4.9 %collective-permute-done.24 = bf16[48,4096]{1,0:T(8,128)(2,1)S(1)} collective-permute-done((bf16[48,4096]{1,0:T(8,128)(2,1)S(1)}, bf16[48,4096]{1,0:T(8,128)(2,1)S(1)}, u32[]{:S(2)}, u32[]{:S(2)}) %collective-permute-start.24) | collective-permute-done | bytes 393248 | tf_op jit(solution)/shard_map/ppermute | solution.py:372
  83.9 4.4 %collective-permute-start.27 = (bf16[48,4096]{1,0:T(8,128)(2,1)S(1)}, bf16[48,4096]{1,0:T(8,128)(2,1)S(1)}, u32[]{:S(2)}, u32[]{:S(2)}) collective-permute-start(bf16[48,4096]{1,0:T(8,128)(2,1)S(1)} %get-tuple-element.91), channel_id=1, source_target_pairs={{0,1},{1,2},{4,5},{5,6},{8,9},{9,10},{12,13},{13,14},{16,17},{17,1... | collective-permute-start | bytes 1179656 | tf_op jit(solution)/shard_map/ppermute | solution.py:381
  89.2 2.9 %collective-permute-done.15 = bf16[48,4096]{1,0:T(8,128)(2,1)S(1)} collective-permute-done((bf16[48,4096]{1,0:T(8,128)(2,1)S(1)}, bf16[48,4096]{1,0:T(8,128)(2,1)S(1)}, u32[]{:S(2)}, u32[]{:S(2)}) %collective-permute-start.15) | collective-permute-done | bytes 393248 | tf_op jit(solution)/shard_map/ppermute | solution.py:372
  92.3 4.4 %collective-permute-start.18 = (bf16[48,4096]{1,0:T(8,128)(2,1)S(1)}, bf16[48,4096]{1,0:T(8,128)(2,1)S(1)}, u32[]{:S(2)}, u32[]{:S(2)}) collective-permute-start(bf16[48,4096]{1,0:T(8,128)(2,1)S(1)} %get-tuple-element.89), channel_id=1, source_target_pairs={{0,1},{1,2},{4,5},{5,6},{8,9},{9,10},{12,13},{13,14},{16,17},{17,1... | collective-permute-start | bytes 1179656 | tf_op jit(solution)/shard_map/ppermute | solution.py:381
  97.6 2.9 %collective-permute-done.27 = bf16[48,4096]{1,0:T(8,128)(2,1)S(1)} collective-permute-done((bf16[48,4096]{1,0:T(8,128)(2,1)S(1)}, bf16[48,4096]{1,0:T(8,128)(2,1)S(1)}, u32[]{:S(2)}, u32[]{:S(2)}) %collective-permute-start.27) | collective-permute-done | bytes 393248 | tf_op jit(solution)/shard_map/ppermute | solution.py:381
  100.5 1.4 %collective-permute-start.25 = (bf16[48,4096]{1,0:T(8,128)(2,1)S(1)}, bf16[48,4096]{1,0:T(8,128)(2,1)S(1)}, u32[]{:S(2)}, u32[]{:S(2)}) collective-permute-start(bf16[48,4096]{1,0:T(8,128)(2,1)S(1)} %get-tuple-element.85), channel_id=1, source_target_pairs={{0,8},{4,12},{8,0},{12,4},{1,9},{5,13},{9,1},{13,5},{2,10},{6,14},... | collective-permute-start | bytes 1179656 | tf_op jit(solution)/shard_map/ppermute | solution.py:365
  102.9 1.3 %collective-permute-start.30 = (bf16[48,4096]{1,0:T(8,128)(2,1)S(1)}, bf16[48,4096]{1,0:T(8,128)(2,1)S(1)}, u32[]{:S(2)}, u32[]{:S(2)}) collective-permute-start(bf16[48,4096]{1,0:T(8,128)(2,1)S(1)} %get-tuple-element.96), channel_id=1, source_target_pairs={{1,0},{2,1},{3,2},{5,4},{6,5},{7,6},{9,8},{10,9},{11,10},{13,12},{... | collective-permute-start | bytes 1179656 | tf_op jit(solution)/shard_map/ppermute | solution.py:381
  104.2 3.3 %collective-permute-done.18 = bf16[48,4096]{1,0:T(8,128)(2,1)S(1)} collective-permute-done((bf16[48,4096]{1,0:T(8,128)(2,1)S(1)}, bf16[48,4096]{1,0:T(8,128)(2,1)S(1)}, u32[]{:S(2)}, u32[]{:S(2)}) %collective-permute-start.18) | collective-permute-done | bytes 393248 | tf_op jit(solution)/shard_map/ppermute | solution.py:381
  107.5 4.4 %collective-permute-start.28 = (bf16[48,4096]{1,0:T(8,128)(2,1)S(1)}, bf16[48,4096]{1,0:T(8,128)(2,1)S(1)}, u32[]{:S(2)}, u32[]{:S(2)}) collective-permute-start(bf16[48,4096]{1,0:T(8,128)(2,1)S(1)} %get-tuple-element.95), channel_id=1, source_target_pairs={{0,1},{1,2},{2,3},{4,5},{5,6},{6,7},{8,9},{9,10},{10,11},{12,13},{... | collective-permute-start | bytes 1179656 | tf_op jit(solution)/shard_map/ppermute | solution.py:381
  112.3 1.3 %collective-permute-start.21 = (bf16[48,4096]{1,0:T(8,128)(2,1)S(1)}, bf16[48,4096]{1,0:T(8,128)(2,1)S(1)}, u32[]{:S(2)}, u32[]{:S(2)}) collective-permute-start(bf16[48,4096]{1,0:T(8,128)(2,1)S(1)} %get-tuple-element.94), channel_id=1, source_target_pairs={{1,0},{2,1},{3,2},{5,4},{6,5},{7,6},{9,8},{10,9},{11,10},{13,12},{... | collective-permute-start | bytes 1179656 | tf_op jit(solution)/shard_map/ppermute | solution.py:381
  113.6 4.6 %collective-permute-start.19 = (bf16[48,4096]{1,0:T(8,128)(2,1)S(1)}, bf16[48,4096]{1,0:T(8,128)(2,1)S(1)}, u32[]{:S(2)}, u32[]{:S(2)}) collective-permute-start(bf16[48,4096]{1,0:T(8,128)(2,1)S(1)} %get-tuple-element.93), channel_id=1, source_target_pairs={{0,1},{1,2},{2,3},{4,5},{5,6},{6,7},{8,9},{9,10},{10,11},{12,13},{... | collective-permute-start | bytes 1179656 | tf_op jit(solution)/shard_map/ppermute | solution.py:381
  118.2 3.3 %collective-permute-done.28 = bf16[48,4096]{1,0:T(8,128)(2,1)S(1)} collective-permute-done((bf16[48,4096]{1,0:T(8,128)(2,1)S(1)}, bf16[48,4096]{1,0:T(8,128)(2,1)S(1)}, u32[]{:S(2)}, u32[]{:S(2)}) %collective-permute-start.28) | collective-permute-done | bytes 393248 | tf_op jit(solution)/shard_map/ppermute | solution.py:381
  121.6 2.7 %collective-permute-done.21 = bf16[48,4096]{1,0:T(8,128)(2,1)S(1)} collective-permute-done((bf16[48,4096]{1,0:T(8,128)(2,1)S(1)}, bf16[48,4096]{1,0:T(8,128)(2,1)S(1)}, u32[]{:S(2)}, u32[]{:S(2)}) %collective-permute-start.21) | collective-permute-done | bytes 393248 | tf_op jit(solution)/shard_map/ppermute | solution.py:381
  124.4 3.1 %collective-permute-done.19 = bf16[48,4096]{1,0:T(8,128)(2,1)S(1)} collective-permute-done((bf16[48,4096]{1,0:T(8,128)(2,1)S(1)}, bf16[48,4096]{1,0:T(8,128)(2,1)S(1)}, u32[]{:S(2)}, u32[]{:S(2)}) %collective-permute-start.19) | collective-permute-done | bytes 393248 | tf_op jit(solution)/shard_map/ppermute | solution.py:381
  127.7 0.9 pad_maximum_fusion
  (60 shorter events, 6.7 us)
Async XLA Ops:
  0.0 35.7 %collective-permute-start.11 = (bf16[512,8192]{1,0:T(8,128)(2,1)}, bf16[512,8192]{1,0:T(8,128)(2,1)}, u32[]{:S(2)}, u32[]{:S(2)}) collective-permute-start(bf16[512,8192]{1,0:T(8,128)(2,1)} %refs_12_.1), channel_id=1, source_target_pairs={{0,4},{4,0},{8,12},{12,8},{1,5},{5,1},{9,13},{13,9},{2,6},{6,2},{1... | collective-permute-start | bytes 25165832 | tf_op jit(solution)/shard_map/ppermute | solution.py:267
  0.5 1.1 copy-start.4
  1.6 0.9 copy-start.5
  2.5 0.9 copy-start.6
  3.7 11.9 %collective-permute-start = (bf16[576,128]{1,0:T(8,128)(2,1)S(1)}, bf16[576,128]{1,0:T(8,128)(2,1)S(1)}, u32[]{:S(2)}, u32[]{:S(2)}) collective-permute-start(bf16[576,128]{1,0:T(8,128)(2,1)S(1)} %get-tuple-element.48), channel_id=1, source_target_pairs={{0,1},{1,2},{2,3},{3,0},{4,5},{5,6},{6,7},{7,4},{8,9},{9,10},{10,1... | collective-permute-start | bytes 442376 | tf_op jit(solution)/shard_map/ppermute | solution.py:250
  6.3 12.9 %collective-permute-start.1 = (bf16[576,128]{1,0:T(8,128)(2,1)S(1)}, bf16[576,128]{1,0:T(8,128)(2,1)S(1)}, u32[]{:S(2)}, u32[]{:S(2)}) collective-permute-start(bf16[576,128]{1,0:T(8,128)(2,1)S(1)} %get-tuple-element.49), channel_id=1, source_target_pairs={{0,2},{1,3},{2,0},{3,1},{4,6},{5,7},{6,4},{7,5},{8,10},{9,11},{10,... | collective-permute-start | bytes 442376 | tf_op jit(solution)/shard_map/ppermute | solution.py:250
  8.9 13.8 %collective-permute-start.2 = (bf16[576,128]{1,0:T(8,128)(2,1)S(1)}, bf16[576,128]{1,0:T(8,128)(2,1)S(1)}, u32[]{:S(2)}, u32[]{:S(2)}) collective-permute-start(bf16[576,128]{1,0:T(8,128)(2,1)S(1)} %get-tuple-element.50), channel_id=1, source_target_pairs={{0,3},{1,0},{2,1},{3,2},{4,7},{5,4},{6,5},{7,6},{8,11},{9,8},{10,9... | collective-permute-start | bytes 442376 | tf_op jit(solution)/shard_map/ppermute | solution.py:250
  10.2 13.9 %collective-permute-start.3 = (bf16[384,128]{1,0:T(8,128)(2,1)S(1)}, bf16[384,128]{1,0:T(8,128)(2,1)S(1)}, u32[]{:S(2)}, u32[]{:S(2)}) collective-permute-start(bf16[384,128]{1,0:T(8,128)(2,1)S(1)} %slice.40), channel_id=1, source_target_pairs={{0,16},{1,17},{2,18},{3,19},{4,20},{5,21},{6,22},{7,23},{8,24},{9,... | collective-permute-start | bytes 294920 | tf_op jit(solution)/shard_map/ppermute | solution.py:265
  15.6 8.6 %collective-permute-start.4 = (bf16[384,128]{1,0:T(8,128)(2,1)S(1)}, bf16[384,128]{1,0:T(8,128)(2,1)S(1)}, u32[]{:S(2)}, u32[]{:S(2)}) collective-permute-start(bf16[384,128]{1,0:T(8,128)(2,1)S(1)} %slice.44), channel_id=1, source_target_pairs={{0,16},{1,17},{2,18},{3,19},{4,20},{5,21},{6,22},{7,23},{8,24},{9,... | collective-permute-start | bytes 294920 | tf_op jit(solution)/shard_map/ppermute | solution.py:265
  19.2 6.4 %collective-permute-start.5 = (bf16[384,128]{1,0:T(8,128)(2,1)S(1)}, bf16[384,128]{1,0:T(8,128)(2,1)S(1)}, u32[]{:S(2)}, u32[]{:S(2)}) collective-permute-start(bf16[384,128]{1,0:T(8,128)(2,1)S(1)} %slice.45), channel_id=1, source_target_pairs={{0,16},{1,17},{2,18},{3,19},{4,20},{5,21},{6,22},{7,23},{8,24},{9,... | collective-permute-start | bytes 294920 | tf_op jit(solution)/shard_map/ppermute | solution.py:265
  22.7 4.3 %collective-permute-start.6 = (bf16[384,128]{1,0:T(8,128)(2,1)S(1)}, bf16[384,128]{1,0:T(8,128)(2,1)S(1)}, u32[]{:S(2)}, u32[]{:S(2)}) collective-permute-start(bf16[384,128]{1,0:T(8,128)(2,1)S(1)} %slice.46), channel_id=1, source_target_pairs={{0,16},{1,17},{2,18},{3,19},{4,20},{5,21},{6,22},{7,23},{8,24},{9,... | collective-permute-start | bytes 294920 | tf_op jit(solution)/shard_map/ppermute | solution.py:265
  30.4 8.8 %copy-start = (bf16[512,8192]{1,0:T(8,128)(2,1)}, bf16[512,8192]{1,0:T(8,128)(2,1)S(1)}, u32[]{:S(2)}) copy-start(bf16[512,8192]{1,0:T(8,128)(2,1)S(1)} %get-tuple-element.60.weight.refs_2_) | copy-start | bytes 25165828
  30.4 8.8 %collective-permute-start.10 = (bf16[2,48,512]{2,1,0:T(8,128)(2,1)S(1)}, bf16[2,48,512]{2,1,0:T(8,128)(2,1)S(1)}, u32[]{:S(2)}, u32[]{:S(2)}) collective-permute-start(bf16[2,48,512]{2,1,0:T(8,128)(2,1)S(1)} %get-tuple-element.58), channel_id=1, source_target_pairs={{0,4},{4,0},{8,12},{12,8},{1,5},{5,1},{9,13},{13,9},{2,6},{6,2},{1... | collective-permute-start | bytes 294920 | tf_op jit(solution)/shard_map/ppermute | solution.py:317
  30.4 14.9 %collective-permute-start.7 = (bf16[576,128]{1,0:T(8,128)(2,1)S(1)}, bf16[576,128]{1,0:T(8,128)(2,1)S(1)}, u32[]{:S(2)}, u32[]{:S(2)}) collective-permute-start(bf16[576,128]{1,0:T(8,128)(2,1)S(1)} %get-tuple-element.53), channel_id=1, source_target_pairs={{0,1},{1,2},{2,3},{3,0},{4,5},{5,6},{6,7},{7,4},{8,9},{9,10},{10,1... | collective-permute-start | bytes 442376 | tf_op jit(solution)/shard_map/ppermute | solution.py:250
  32.3 13.6 %collective-permute-start.8 = (bf16[576,128]{1,0:T(8,128)(2,1)S(1)}, bf16[576,128]{1,0:T(8,128)(2,1)S(1)}, u32[]{:S(2)}, u32[]{:S(2)}) collective-permute-start(bf16[576,128]{1,0:T(8,128)(2,1)S(1)} %get-tuple-element.55), channel_id=1, source_target_pairs={{0,2},{1,3},{2,0},{3,1},{4,6},{5,7},{6,4},{7,5},{8,10},{9,11},{10,... | collective-permute-start | bytes 442376 | tf_op jit(solution)/shard_map/ppermute | solution.py:250
  35.7 10.3 %collective-permute-start.9 = (bf16[576,128]{1,0:T(8,128)(2,1)S(1)}, bf16[576,128]{1,0:T(8,128)(2,1)S(1)}, u32[]{:S(2)}, u32[]{:S(2)}) collective-permute-start(bf16[576,128]{1,0:T(8,128)(2,1)S(1)} %get-tuple-element.57), channel_id=1, source_target_pairs={{0,3},{1,0},{2,1},{3,2},{4,7},{5,4},{6,5},{7,6},{8,11},{9,8},{10,9... | collective-permute-start | bytes 442376 | tf_op jit(solution)/shard_map/ppermute | solution.py:250
  40.6 3.3 %copy-start.2 = (bf16[512,8192]{1,0:T(8,128)(2,1)}, bf16[512,8192]{1,0:T(8,128)(2,1)S(1)}, u32[]{:S(2)}) copy-start(bf16[512,8192]{1,0:T(8,128)(2,1)S(1)} %get-tuple-element.61.refs_1_.refs_3_) | copy-start | bytes 25165828
  43.9 23.5 %collective-permute-start.22 = (bf16[48,4096]{1,0:T(8,128)(2,1)S(1)}, bf16[48,4096]{1,0:T(8,128)(2,1)}, u32[]{:S(2)}, u32[]{:S(2)}) collective-permute-start(bf16[48,4096]{1,0:T(8,128)(2,1)S(1)} %get-tuple-element.66), channel_id=1, source_target_pairs={{0,8},{4,12},{8,0},{12,4},{1,9},{5,13},{9,1},{13,5},{2,10},{6,14},... | collective-permute-start | bytes 1179656 | tf_op jit(solution)/shard_map/ppermute | solution.py:365
  51.8 1.6 %collective-permute-start.12 = (bf16[2,144,512]{2,1,0:T(8,128)(2,1)S(1)}, bf16[2,144,512]{2,1,0:T(8,128)(2,1)S(1)}, u32[]{:S(2)}, u32[]{:S(2)}) collective-permute-start(bf16[2,144,512]{2,1,0:T(8,128)(2,1)S(1)} %get-tuple-element.72), channel_id=1, source_target_pairs={{0,4},{4,0},{8,12},{12,8},{1,5},{5,1},{9,13},{13,9},{2,6},{6,2},{1... | collective-permute-start | bytes 884744 | tf_op jit(solution)/shard_map/ppermute | solution.py:317
  51.9 23.7 %collective-permute-start.13 = (bf16[48,4096]{1,0:T(8,128)(2,1)S(1)}, bf16[48,4096]{1,0:T(8,128)(2,1)S(1)}, u32[]{:S(2)}, u32[]{:S(2)}) collective-permute-start(bf16[48,4096]{1,0:T(8,128)(2,1)S(1)} %get-tuple-element.65), channel_id=1, source_target_pairs={{0,8},{4,12},{8,0},{12,4},{1,9},{5,13},{9,1},{13,5},{2,10},{6,14},... | collective-permute-start | bytes 1179656 | tf_op jit(solution)/shard_map/ppermute | solution.py:365
  53.5 3.4 %copy-start.1 = (bf16[512,8192]{1,0:T(8,128)(2,1)S(1)}, bf16[512,8192]{1,0:T(8,128)(2,1)}, u32[]{:S(2)}) copy-start(bf16[512,8192]{1,0:T(8,128)(2,1)} %copy-done) | copy-start | bytes 25165828
  56.9 3.4 %copy-start.3 = (bf16[512,8192]{1,0:T(8,128)(2,1)S(1)}, bf16[512,8192]{1,0:T(8,128)(2,1)}, u32[]{:S(2)}) copy-start(bf16[512,8192]{1,0:T(8,128)(2,1)} %copy-done.2) | copy-start | bytes 25165828
  65.3 12.0 %collective-permute-start.23 = (bf16[48,4096]{1,0:T(8,128)(2,1)S(1)}, bf16[48,4096]{1,0:T(8,128)(2,1)S(1)}, u32[]{:S(2)}, u32[]{:S(2)}) collective-permute-start(bf16[48,4096]{1,0:T(8,128)(2,1)S(1)} %get-tuple-element.84), channel_id=1, source_target_pairs={{0,8},{4,12},{8,0},{12,4},{1,9},{5,13},{9,1},{13,5},{2,10},{6,14},... | collective-permute-start | bytes 1179656 | tf_op jit(solution)/shard_map/ppermute | solution.py:365
  66.9 21.6 %collective-permute-start.14 = (bf16[48,4096]{1,0:T(8,128)(2,1)S(1)}, bf16[48,4096]{1,0:T(8,128)(2,1)S(1)}, u32[]{:S(2)}, u32[]{:S(2)}) collective-permute-start(bf16[48,4096]{1,0:T(8,128)(2,1)S(1)} %get-tuple-element.76), channel_id=1, source_target_pairs={{0,8},{4,12},{8,0},{12,4},{1,9},{5,13},{9,1},{13,5},{2,10},{6,14},... | collective-permute-start | bytes 1179656 | tf_op jit(solution)/shard_map/ppermute | solution.py:365
  68.5 15.2 %collective-permute-start.24 = (bf16[48,4096]{1,0:T(8,128)(2,1)S(1)}, bf16[48,4096]{1,0:T(8,128)(2,1)S(1)}, u32[]{:S(2)}, u32[]{:S(2)}) collective-permute-start(bf16[48,4096]{1,0:T(8,128)(2,1)S(1)} %add_convert_fusion.6), channel_id=1, source_target_pairs={{0,1},{3,2},{4,5},{7,6},{8,9},{11,10},{12,13},{15,14},{16,17},{19,... | collective-permute-start | bytes 1179656 | tf_op jit(solution)/shard_map/ppermute | solution.py:372
  74.2 22.7 %collective-permute-start.26 = (bf16[48,4096]{1,0:T(8,128)(2,1)S(1)}, bf16[48,4096]{1,0:T(8,128)(2,1)S(1)}, u32[]{:S(2)}, u32[]{:S(2)}) collective-permute-start(bf16[48,4096]{1,0:T(8,128)(2,1)S(1)} %get-tuple-element.88), channel_id=1, source_target_pairs={{0,8},{4,12},{8,0},{12,4},{1,9},{5,13},{9,1},{13,5},{2,10},{6,14},... | collective-permute-start | bytes 1179656 | tf_op jit(solution)/shard_map/ppermute | solution.py:365
  75.7 16.4 %collective-permute-start.15 = (bf16[48,4096]{1,0:T(8,128)(2,1)S(1)}, bf16[48,4096]{1,0:T(8,128)(2,1)S(1)}, u32[]{:S(2)}, u32[]{:S(2)}) collective-permute-start(bf16[48,4096]{1,0:T(8,128)(2,1)S(1)} %add_convert_fusion.13), channel_id=1, source_target_pairs={{0,1},{3,2},{4,5},{7,6},{8,9},{11,10},{12,13},{15,14},{16,17},{19,... | collective-permute-start | bytes 1179656 | tf_op jit(solution)/shard_map/ppermute | solution.py:372
  77.3 25.6 %collective-permute-start.17 = (bf16[48,4096]{1,0:T(8,128)(2,1)S(1)}, bf16[48,4096]{1,0:T(8,128)(2,1)S(1)}, u32[]{:S(2)}, u32[]{:S(2)}) collective-permute-start(bf16[48,4096]{1,0:T(8,128)(2,1)S(1)} %get-tuple-element.80), channel_id=1, source_target_pairs={{0,8},{4,12},{8,0},{12,4},{1,9},{5,13},{9,1},{13,5},{2,10},{6,14},... | collective-permute-start | bytes 1179656 | tf_op jit(solution)/shard_map/ppermute | solution.py:365
  83.9 16.6 %collective-permute-start.27 = (bf16[48,4096]{1,0:T(8,128)(2,1)S(1)}, bf16[48,4096]{1,0:T(8,128)(2,1)S(1)}, u32[]{:S(2)}, u32[]{:S(2)}) collective-permute-start(bf16[48,4096]{1,0:T(8,128)(2,1)S(1)} %get-tuple-element.91), channel_id=1, source_target_pairs={{0,1},{1,2},{4,5},{5,6},{8,9},{9,10},{12,13},{13,14},{16,17},{17,1... | collective-permute-start | bytes 1179656 | tf_op jit(solution)/shard_map/ppermute | solution.py:381
  88.5 13.5 %collective-permute-start.29 = (bf16[48,4096]{1,0:T(8,128)(2,1)S(1)}, bf16[48,4096]{1,0:T(8,128)(2,1)S(1)}, u32[]{:S(2)}, u32[]{:S(2)}) collective-permute-start(bf16[48,4096]{1,0:T(8,128)(2,1)S(1)} %fusion.3), channel_id=1, source_target_pairs={{2,1},{3,2},{6,5},{7,6},{10,9},{11,10},{14,13},{15,14},{18,17},{19... | collective-permute-start | bytes 1179656 | tf_op jit(solution)/shard_map/ppermute | solution.py:381
  92.3 15.2 %collective-permute-start.18 = (bf16[48,4096]{1,0:T(8,128)(2,1)S(1)}, bf16[48,4096]{1,0:T(8,128)(2,1)S(1)}, u32[]{:S(2)}, u32[]{:S(2)}) collective-permute-start(bf16[48,4096]{1,0:T(8,128)(2,1)S(1)} %get-tuple-element.89), channel_id=1, source_target_pairs={{0,1},{1,2},{4,5},{5,6},{8,9},{9,10},{12,13},{13,14},{16,17},{17,1... | collective-permute-start | bytes 1179656 | tf_op jit(solution)/shard_map/ppermute | solution.py:381
  96.9 15.0 %collective-permute-start.20 = (bf16[48,4096]{1,0:T(8,128)(2,1)S(1)}, bf16[48,4096]{1,0:T(8,128)(2,1)S(1)}, u32[]{:S(2)}, u32[]{:S(2)}) collective-permute-start(bf16[48,4096]{1,0:T(8,128)(2,1)S(1)} %fusion.1), channel_id=1, source_target_pairs={{2,1},{3,2},{6,5},{7,6},{10,9},{11,10},{14,13},{15,14},{18,17},{19... | collective-permute-start | bytes 1179656 | tf_op jit(solution)/shard_map/ppermute | solution.py:381
  100.5 13.0 %collective-permute-start.25 = (bf16[48,4096]{1,0:T(8,128)(2,1)S(1)}, bf16[48,4096]{1,0:T(8,128)(2,1)S(1)}, u32[]{:S(2)}, u32[]{:S(2)}) collective-permute-start(bf16[48,4096]{1,0:T(8,128)(2,1)S(1)} %get-tuple-element.85), channel_id=1, source_target_pairs={{0,8},{4,12},{8,0},{12,4},{1,9},{5,13},{9,1},{13,5},{2,10},{6,14},... | collective-permute-start | bytes 1179656 | tf_op jit(solution)/shard_map/ppermute | solution.py:365
  102.0 19.7 %collective-permute-start.16 = (bf16[48,4096]{1,0:T(8,128)(2,1)S(1)}, bf16[48,4096]{1,0:T(8,128)(2,1)S(1)}, u32[]{:S(2)}, u32[]{:S(2)}) collective-permute-start(bf16[48,4096]{1,0:T(8,128)(2,1)S(1)} %get-tuple-element.77), channel_id=1, source_target_pairs={{0,8},{4,12},{8,0},{12,4},{1,9},{5,13},{9,1},{13,5},{2,10},{6,14},... | collective-permute-start | bytes 1179656 | tf_op jit(solution)/shard_map/ppermute | solution.py:365
  102.9 15.2 %collective-permute-start.30 = (bf16[48,4096]{1,0:T(8,128)(2,1)S(1)}, bf16[48,4096]{1,0:T(8,128)(2,1)S(1)}, u32[]{:S(2)}, u32[]{:S(2)}) collective-permute-start(bf16[48,4096]{1,0:T(8,128)(2,1)S(1)} %get-tuple-element.96), channel_id=1, source_target_pairs={{1,0},{2,1},{3,2},{5,4},{6,5},{7,6},{9,8},{10,9},{11,10},{13,12},{... | collective-permute-start | bytes 1179656 | tf_op jit(solution)/shard_map/ppermute | solution.py:381
  107.5 13.9 %collective-permute-start.28 = (bf16[48,4096]{1,0:T(8,128)(2,1)S(1)}, bf16[48,4096]{1,0:T(8,128)(2,1)S(1)}, u32[]{:S(2)}, u32[]{:S(2)}) collective-permute-start(bf16[48,4096]{1,0:T(8,128)(2,1)S(1)} %get-tuple-element.95), channel_id=1, source_target_pairs={{0,1},{1,2},{2,3},{4,5},{5,6},{6,7},{8,9},{9,10},{10,11},{12,13},{... | collective-permute-start | bytes 1179656 | tf_op jit(solution)/shard_map/ppermute | solution.py:381
  112.3 12.1 %collective-permute-start.21 = (bf16[48,4096]{1,0:T(8,128)(2,1)S(1)}, bf16[48,4096]{1,0:T(8,128)(2,1)S(1)}, u32[]{:S(2)}, u32[]{:S(2)}) collective-permute-start(bf16[48,4096]{1,0:T(8,128)(2,1)S(1)} %get-tuple-element.94), channel_id=1, source_target_pairs={{1,0},{2,1},{3,2},{5,4},{6,5},{7,6},{9,8},{10,9},{11,10},{13,12},{... | collective-permute-start | bytes 1179656 | tf_op jit(solution)/shard_map/ppermute | solution.py:381
  113.6 13.9 %collective-permute-start.19 = (bf16[48,4096]{1,0:T(8,128)(2,1)S(1)}, bf16[48,4096]{1,0:T(8,128)(2,1)S(1)}, u32[]{:S(2)}, u32[]{:S(2)}) collective-permute-start(bf16[48,4096]{1,0:T(8,128)(2,1)S(1)} %get-tuple-element.93), channel_id=1, source_target_pairs={{0,1},{1,2},{2,3},{4,5},{5,6},{6,7},{8,9},{9,10},{10,11},{12,13},{... | collective-permute-start | bytes 1179656 | tf_op jit(solution)/shard_map/ppermute | solution.py:381

commit v5 on v4

--- a/solution.py
+++ b/solution.py
@@ -57,17 +57,24 @@
     return parts[0] if len(parts) == 1 else jnp.concatenate(parts, axis=0)
 
 
-def pack_kernel(queries, keys, values, *outs, slabs, heads, kv_local, order, share, stages):
+def pack_kernel(queries, keys, values, *refs, slabs, heads, kv_local, order, share, stages):
+    *outs, all_queries, all_keys, all_values, semaphores = refs
     z = lax.axis_index("wsh")
+    pairs = ((keys, all_keys), (values, all_values), (queries, all_queries))
+    copies = [pltpu.make_async_copy(a, b, semaphores.at[n]) for n, (a, b) in enumerate(pairs)]
+    for copy in copies:
+        copy.start()
     block = queries.shape[0]
-    for k in range(slabs):
-        target = lax.rem(z + k, slabs)
-        first = pl.multiple_of(lax.div(target * kv_local, slabs) * HEAD_SIZE, HEAD_SIZE)
-        load = outs[k]
-        load[:block, :] = keys[:, pl.ds(first, HEAD_SIZE)]
-        load[block : 2 * block, :] = values[:, pl.ds(first, HEAD_SIZE)]
-        for n, stage in enumerate(stages):
-            out, place = outs[n * slabs + k], 2 * block if n == 0 else 0
+    targets = [lax.rem(z + k, slabs) for k in range(slabs)]
+    for n in range(2):
+        copies[n].wait()
+        for k, target in enumerate(targets):
+            first = pl.multiple_of(lax.div(target * kv_local, slabs) * HEAD_SIZE, HEAD_SIZE)
+            outs[k][n * block : (n + 1) * block, :] = pairs[n][1][:, pl.ds(first, HEAD_SIZE)]
+    copies[2].wait()
+    for n, stage in enumerate(stages, 1):
+        for k, target in enumerate(targets):
+            place = 0
             for h in range(heads):
                 column = pl.multiple_of((target * heads + h) * HEAD_SIZE, HEAD_SIZE)
                 for i in stage:
@@ -75,27 +82,29 @@
                         rows, count = slice(None), block
                     else:
                         rows, count = pl.ds(pl.multiple_of(chosen(order, target, i) * share, 16), share), share
-                    out[place : place + count, :] = queries[rows, pl.ds(column, HEAD_SIZE)]
+                    outs[n * slabs + k][place : place + count, :] = all_queries[rows, pl.ds(column, HEAD_SIZE)]
                     place += count
 
 
 def pack(queries, keys, values, *, slabs, heads, kv_local, order, share, stages):
     block = queries.shape[0]
-    counts = [heads * share * len(stage) + (2 * block if n == 0 else 0) for n, stage in enumerate(stages)]
+    counts = [2 * block] + [heads * share * len(stage) for stage in stages]
     return pl.pallas_call(
         partial(
             pack_kernel, slabs=slabs, heads=heads, kv_local=kv_local, order=order, share=share, stages=stages
         ),
         out_shape=[jax.ShapeDtypeStruct((count, HEAD_SIZE), BF16) for count in counts for _ in range(slabs)],
-        in_specs=[VMEM] * 3,
-        out_specs=[VMEM] * (slabs * len(stages)),
+        in_specs=[HBM] * 3,
+        out_specs=[VMEM] * (slabs * len(counts)),
+        scratch_shapes=[pltpu.VMEM(a.shape, BF16) for a in (queries, keys, values)]
+        + [pltpu.SemaphoreType.DMA((3,))],
         compiler_params=LIMIT,
         cost_estimate=FREE,
         name="pack",
-    )(queries, keys, values)
-
-
-def attend_kernel(key_doc, *refs, slabs, heads, share, stage, order, offset, columns_x, per_shard, fetched):
+    )(in_hbm(queries), in_hbm(keys), in_hbm(values))
+
+
+def attend_kernel(key_doc, *refs, slabs, heads, share, stage, order, columns_x, per_shard, fetched):
     refs = list(refs)
     take = lambda n: [refs.pop(0) for _ in range(n)]
     now, before, queries, weights = take(slabs), take(slabs), take(slabs), take(fetched)
@@ -133,7 +142,7 @@
         query_doc = joined([jnp.max(jnp.where(b == 0, docs, -2.0), axis=1, keepdims=True) for b in behind])
         visible = causal & (query_doc == docs)
         scores = lax.dot_general(
-            queries[k][offset : offset + heads * rows, :],
+            queries[k][...],
             key_rows[...],
             (((1,), (1,)), ((), ())),
             preferred_element_type=F32,
@@ -178,7 +187,7 @@
         scratch_shapes=[pltpu.VMEM((span, HEAD_SIZE), BF16)] * 2
         + [pltpu.SemaphoreType.DMA((fetched,))] * (fetched > 0),
         compiler_params=LIMIT,
-        cost_estimate=FREE,
+        cost_estimate=pl.CostEstimate(flops=4 * terms * HEAD_SIZE, bytes_accessed=0, transcendentals=terms),
         name="attend",
     )(key_doc, *now, *before, *queries, *[in_hbm(w) for w in weights])
 
@@ -262,13 +271,15 @@
     )
     loads = [packed[0]] + [around(packed[k], k) for k in range(1, slabs)]
     before = [
-        lax.ppermute(a[: 2 * block], "srv", [(g, g + 1) for g in range(groups - 1)]) for a in loads
+        lax.ppermute(a, "srv", [(g, g + 1) for g in range(groups - 1)]) for a in loads
     ]
     weight_sibling = lax.ppermute(out_weight, "head", siblings)
-    stage_queries = [loads]
-    for n in range(1, len(stages)):
-        rest = packed[n * slabs : (n + 1) * slabs]
-        stage_queries.append([rest[0]] + [around(after(rest[k], *loads), k) for k in range(1, slabs)])
+    stage_queries = []
+    for n in range(len(stages)):
+        sent = packed[(n + 1) * slabs : (n + 2) * slabs]
+        if n:
+            sent = [after(a, *loads) for a in sent]
+        stage_queries.append([sent[0]] + [around(sent[k], k) for k in range(1, slabs)])
 
     reach = SLAB_REACH - 1
     padded = jnp.concatenate([jnp.full((reach, block), -1.0, F32), doc_ids.reshape(-1, block).astype(F32)])
@@ -279,11 +290,11 @@
     ).reshape(count, 1, SLAB_REACH * block)
 
     partials = []
-    results = weight_near = None
+    results = None
     for n, (stage, arrived) in enumerate(zip(stages, stage_queries)):
         if n:
             arrived = after(arrived, *results)
-        fetch = [] if n else [out_weight]
+        fetch = [out_weight] if n == 0 else [out_weight, weight_sibling]
         keep, send, *fetched = attend(
             key_doc,
             loads,
@@ -295,7 +306,6 @@
             share=rows_at_once,
             stage=stage,
             order=order,
-            offset=2 * block if n == 0 else 0,
             columns_x=columns_x,
             per_shard=per_shard,
         )
@@ -317,13 +327,11 @@
         theirs = lax.ppermute(send, "head", siblings)
         keep, theirs = (a.reshape(-1, a.shape[-1]) for a in (keep, theirs))
         if n == 0 and staged:
-            weight_near = fetched[0]
-            begun, weight_sibling = first_half(keep, weight_near, weight_sibling)
-            results = project([theirs], [weight_sibling], [begun], share, halves)
+            begun, far = first_half(keep, fetched[0], weight_sibling)
+            results = project([theirs], [far], [begun], share, halves)
         else:
-            if fetched:
-                weight_near = fetched[0]
-            results = project([keep, theirs], [weight_near, weight_sibling], [], share, halves)
+            weights = fetched if n else [fetched[0], weight_sibling]
+            results = project([keep, theirs], weights, [], share, halves)
         for m in range(len(pieces)):
             partials.append(
                 [

time: 130 us -> 136 us (1.046)
  waiting for transfers between devices: 29.1 us -> 38 us
  starting transfers between devices: 60.8 us -> 55.7 us
  Pallas kernels: 19.4 us -> 22 us
    ppermute x8, waiting for transfers between devices: 0.27 us -> 11.6 us  [on_device(): total = total + lax.ppermute(piece, 'head', route).astype(F32)]
    ppermute x6 -> x9, waiting for transfers between devices: 2.95 us -> 8.69 us  [around(): lax.ppermute(array, 'wsh', [(i, (i + k) % slabs) for i in range(slabs)])]
    ppermute x8, waiting for transfers between devices: 15.3 us -> 10.5 us  [on_device(): lax.ppermute(sent[direction], 'wsh', [(i, i + direction) for i in found])]
    ppermute x2, starting transfers between devices: 7 us -> 3.29 us  [on_device(): lax.ppermute(sent, 'wsh', [(i, i + 1) for i in up] + [(i, i - 1) for i in...]
    ppermute x2, waiting for transfers between devices: 7.81 us -> 4.12 us  [on_device(): lax.ppermute(sent, 'wsh', [(i, i + 1) for i in up] + [(i, i - 1) for i in...]
    ppermute x6 -> x9, starting transfers between devices: 11.8 us -> 15.1 us  [around(): lax.ppermute(array, 'wsh', [(i, (i + k) % slabs) for i in range(slabs)])]
    ppermute x8, starting transfers between devices: 10.1 us -> 7.34 us  [on_device(): total = total + lax.ppermute(piece, 'head', route).astype(F32)]
    pallas_call x1, Pallas kernels: 0.29 us -> 2.13 us  [pack(): pl.pallas_call(partial(pack_kernel, slabs=slabs, heads=heads, kv_local=kv...]
  transfers between devices with their start and end apart: 31 -> 34, of which waited for: 12 -> 18; matrix products, arithmetic and copies ran while one was open for 4% -> 4% of each run, Pallas kernels for 15% -> 16%
where the time goes in v5:
time: 136 us; the launch traced here: 135 us
  starting transfers between devices  55.7 us (41%)
  waiting for transfers between devices  38 us (28%)
  Pallas kernels  22 us (16%)
  local copies, waits for them, and re-layouts  13.6 us (10%)
  other arithmetic  5.61 us (4%)
    ppermute x8, starting transfers between devices, on_device(): lax.ppermute(sent[direction], 'wsh', [(i, i + direction) for i in found])  21 us
    ppermute x9, starting transfers between devices, around(): lax.ppermute(array, 'wsh', [(i, (i + k) % slabs) for i in range(slabs)])  15.1 us
    unnamed x8, local copies, waits for them, and re-layouts  13.3 us
    ppermute x8, waiting for transfers between devices, on_device(): total = total + lax.ppermute(piece, 'head', route).astype(F32)  11.6 us
    ppermute x8, waiting for transfers between devices, on_device(): lax.ppermute(sent[direction], 'wsh', [(i, i + direction) for i in found])  10.5 us
    pallas_call x2, Pallas kernels, attend(): pl.pallas_call(partial(attend_kernel, slabs=slabs, heads=heads, share=sha...  10 us
    ppermute x9, waiting for transfers between devices, around(): lax.ppermute(array, 'wsh', [(i, (i + k) % slabs) for i in range(slabs)])  8.69 us
    ppermute x4, starting transfers between devices, on_device(): lax.ppermute(a, 'srv', [(g, g + 1) for g in range(groups - 1)])  8.23 us
  transfers between devices with their start and end apart: 34, of which 18 were waited for; matrix products, arithmetic and copies ran while one was open for 4% of the time, Pallas kernels for 16%

profile of v5, /device:TPU:0, one launch (start us, length us, event | category | flops | bytes accessed | tf_op | source)
XLA Modules:
  0.0 135.2 jit_solution(5169990145905120762)
XLA Ops:
  0.5 2.1 %pack.1 = (bf16[384,128]{1,0:T(8,128)(2,1)S(1)}, bf16[384,128]{1,0:T(8,128)(2,1)S(1)}, bf16[384,128]{1,0:T(8,128)(2,1)S(1)}, bf16[384,128]{1,0:T(8,128)(2,1)S(1)...) custom-call(bf16[192,2048]{1,0:T(8,128)(2,1)} %queries.1, ...), custom_call_target="tpu_custom_call" | custom-call | tf_op jit(solution)/shard_map/pack/pallas_call | solution.py:92
  2.6 2.6 %collective-permute-start = (bf16[384,128]{1,0:T(8,128)(2,1)S(1)}, bf16[384,128]{1,0:T(8,128)(2,1)S(1)}, u32[]{:S(2)}, u32[]{:S(2)}) collective-permute-start(bf16[384,128]{1,0:T(8,128)(2,1)S(1)} %get-tuple-element.55), channel_id=1, source_target_pairs={{0,1},{1,2},{2,3},{3,0},{4,5},{5,6},{6,7},{7,4},{8,9},{9,10},{10,1... | collective-permute-start | bytes 294920 | tf_op jit(solution)/shard_map/ppermute | solution.py:259
  5.2 2.6 %collective-permute-start.1 = (bf16[384,128]{1,0:T(8,128)(2,1)S(1)}, bf16[384,128]{1,0:T(8,128)(2,1)S(1)}, u32[]{:S(2)}, u32[]{:S(2)}) collective-permute-start(bf16[384,128]{1,0:T(8,128)(2,1)S(1)} %get-tuple-element.56), channel_id=1, source_target_pairs={{0,2},{1,3},{2,0},{3,1},{4,6},{5,7},{6,4},{7,5},{8,10},{9,11},{10,... | collective-permute-start | bytes 294920 | tf_op jit(solution)/shard_map/ppermute | solution.py:259
  7.8 1.3 collective-permute-start.2
  11.4 4.7 %collective-permute-done.10.refs_9_ = bf16[192,128]{1,0:T(8,128)(2,1)S(1)} collective-permute-done((bf16[192,128]{1,0:T(8,128)(2,1)S(1)}, bf16[192,128]{1,0:T(8,128)(2,1)S(1)}, u32[]{:S(2)}, u32[]{:S(2)}) %collective-permute-start.10) | collective-permute-done | bytes 49184 | tf_op jit(solution)/shard_map/ppermute | solution.py:259
  16.1 2.7 %collective-permute-start.11 = (bf16[192,128]{1,0:T(8,128)(2,1)S(1)}, bf16[192,128]{1,0:T(8,128)(2,1)S(1)}, u32[]{:S(2)}, u32[]{:S(2)}) collective-permute-start(bf16[192,128]{1,0:T(8,128)(2,1)S(1)} %get-tuple-element.68), channel_id=1, source_target_pairs={{0,2},{1,3},{2,0},{3,1},{4,6},{5,7},{6,4},{7,5},{8,10},{9,11},{10,... | collective-permute-start | bytes 147464 | tf_op jit(solution)/shard_map/ppermute | solution.py:259
  19.0 2.7 %collective-permute-done.11.refs_10_ = bf16[192,128]{1,0:T(8,128)(2,1)S(1)} collective-permute-done((bf16[192,128]{1,0:T(8,128)(2,1)S(1)}, bf16[192,128]{1,0:T(8,128)(2,1)S(1)}, u32[]{:S(2)}, u32[]{:S(2)}) %collective-permute-start.11) | collective-permute-done | bytes 49184 | tf_op jit(solution)/shard_map/ppermute | solution.py:259
  21.6 3.4 %collective-permute-start.3 = (bf16[384,128]{1,0:T(8,128)(2,1)S(1)}, bf16[384,128]{1,0:T(8,128)(2,1)S(1)}, u32[]{:S(2)}, u32[]{:S(2)}) collective-permute-start(bf16[384,128]{1,0:T(8,128)(2,1)S(1)} %get-tuple-element.54.refs_0_), channel_id=1, source_target_pairs={{0,16},{1,17},{2,18},{3,19},{4,20},{5,21},{6,22},{7,23},{8,24},{9,... | collective-permute-start | bytes 294920 | tf_op jit(solution)/shard_map/ppermute | solution.py:274
  25.2 1.3 collective-permute-start.4
  26.5 1.3 collective-permute-start.5
  27.9 1.3 collective-permute-done.12.refs_11_
  30.0 2.2 %collective-permute-start.8 = (bf16[576,128]{1,0:T(8,128)(2,1)S(1)}, bf16[576,128]{1,0:T(8,128)(2,1)S(1)}, u32[]{:S(2)}, u32[]{:S(2)}) collective-permute-start(bf16[576,128]{1,0:T(8,128)(2,1)S(1)} %get-tuple-element.63), channel_id=1, source_target_pairs={{0,2},{1,3},{2,0},{3,1},{4,6},{5,7},{6,4},{7,5},{8,10},{9,11},{10,... | collective-permute-start | bytes 442376 | tf_op jit(solution)/shard_map/ppermute | solution.py:259
  32.1 2.2 %collective-permute-start.9 = (bf16[576,128]{1,0:T(8,128)(2,1)S(1)}, bf16[576,128]{1,0:T(8,128)(2,1)S(1)}, u32[]{:S(2)}, u32[]{:S(2)}) collective-permute-start(bf16[576,128]{1,0:T(8,128)(2,1)S(1)} %get-tuple-element.65), channel_id=1, source_target_pairs={{0,3},{1,0},{2,1},{3,2},{4,7},{5,4},{6,5},{7,6},{8,11},{9,8},{10,9... | collective-permute-start | bytes 442376 | tf_op jit(solution)/shard_map/ppermute | solution.py:259
  34.3 2.2 %collective-permute-start.6 = (bf16[384,128]{1,0:T(8,128)(2,1)S(1)}, bf16[384,128]{1,0:T(8,128)(2,1)S(1)}, u32[]{:S(2)}, u32[]{:S(2)}) collective-permute-start(bf16[384,128]{1,0:T(8,128)(2,1)S(1)} %collective-permute-done.2.refs_3_), channel_id=1, source_target_pairs={{0,16},{1,17},{2,18},{3,19},{4,20},{5,21},{6,22},{7,23},{8,24},{9,... | collective-permute-start | bytes 294920 | tf_op jit(solution)/shard_map/ppermute | solution.py:274
  36.7 2.0 %collective-permute-done.6.refs_7_ = bf16[384,128]{1,0:T(8,128)(2,1)S(1)} collective-permute-done((bf16[384,128]{1,0:T(8,128)(2,1)S(1)}, bf16[384,128]{1,0:T(8,128)(2,1)S(1)}, u32[]{:S(2)}, u32[]{:S(2)}) %collective-permute-start.6) | collective-permute-done | bytes 98336 | tf_op jit(solution)/shard_map/ppermute | solution.py:274
  38.7 3.4 %attend.2 = (bf16[2,48,512]{2,1,0:T(8,128)(2,1)S(1)}, bf16[2,48,512]{2,1,0:T(8,128)(2,1)S(1)}, bf16[512,8192]{1,0:T(8,128)(2,1)S(1)}) custom-call(f32[8,1,768]{2,1,0:T(1,128)S(1)} %reshape.55.key_doc, bf16[384,128]{1,0:T(8,128)(2,1)S(1)} %get-tuple-element.54.refs_0_, bf16[384,128]{1,0:T(8,128)(2,1)S(1)} %collective-permute-done.refs_1_, ...), custom_call_target="tpu_custom_call" | custom-call | flops 301989888 | tf_op jit(solution)/shard_map/attend/pallas_call | solution.py:180
  42.2 3.4 %first_half.1 = (f32[96,8192]{1,0:T(8,128)S(1)}, bf16[512,8192]{1,0:T(8,128)(2,1)S(1)}) custom-call(bf16[96,512]{1,0:T(8,128)(2,1)S(1)} %bitcast.19, bf16[512,8192]{1,0:T(8,128)(2,1)S(1)} %get-tuple-element.72.weight, bf16[512,8192]{1,0:T(8,128)(2,1)} %collective-permute-done.14.fetch.refs_13_), custom_call_target="tpu_custom_call" | custom-call | tf_op jit(solution)/shard_map/first_half/pallas_call | solution.py:204
  45.6 1.5 %project.2 = (bf16[48,4096]{1,0:T(8,128)(2,1)S(1)}, bf16[48,4096]{1,0:T(8,128)(2,1)S(1)}, bf16[48,4096]{1,0:T(8,128)(2,1)S(1)}, bf16[48,4096]{1,0:T(8,128)(2,1)S(1)}) custom-call(bf16[96,512]{1,0:T(8,128)(2,1)S(1)} %bitcast.18, bf16[512,8192]{1,0:T(8,128)(2,1)S(1)} %get-tuple-element.73.refs_1_, f32[96,8192]{1,0:T(8,128)S(1)} %get-tuple-element.74.refs_2_), custom_call_target="tpu_custom_call" | custom-call | tf_op jit(solution)/shard_map/project/pallas_call | solution.py:233
  47.1 1.6 %collective-permute-start.25 = (bf16[48,4096]{1,0:T(8,128)(2,1)S(1)}, bf16[48,4096]{1,0:T(8,128)(2,1)}, u32[]{:S(2)}, u32[]{:S(2)}) collective-permute-start(bf16[48,4096]{1,0:T(8,128)(2,1)S(1)} %get-tuple-element.78), channel_id=1, source_target_pairs={{0,8},{4,12},{8,0},{12,4},{1,9},{5,13},{9,1},{13,5},{2,10},{6,14},... | collective-permute-start | bytes 1179656 | tf_op jit(solution)/shard_map/ppermute | solution.py:373
  48.7 6.6 %attend.3 = (bf16[2,144,512]{2,1,0:T(8,128)(2,1)S(1)}, bf16[2,144,512]{2,1,0:T(8,128)(2,1)}, bf16[512,8192]{1,0:T(8,128)(2,1)S(1)}, bf16[512,8192]{1,0:T(8,128)(2,1)S(1)}) custom-call(f32[8,1,768]{2,1,0:T(1,128)S(1)} %reshape.55.key_doc, bf16[384,128]{1,0:T(8,128)(2,1)S(1)} %get-tuple-element.54.refs_0_, bf16[384,128]{1,0:T(8,128)(2,1)S(1)} %collective-permute-done.refs_1_, ...), custom_call_target="tpu_custom_call" | custom-call | flops 905969664 | tf_op jit(solution)/shard_map/attend/pallas_call | solution.py:180
  55.3 3.3 %copy-done = bf16[512,8192]{1,0:T(8,128)(2,1)} copy-done((bf16[512,8192]{1,0:T(8,128)(2,1)}, bf16[512,8192]{1,0:T(8,128)(2,1)S(1)}, u32[]{:S(2)}) %copy-start) | copy-done | bytes 8388632
  58.6 3.2 %copy-done.2 = bf16[512,8192]{1,0:T(8,128)(2,1)} copy-done((bf16[512,8192]{1,0:T(8,128)(2,1)}, bf16[512,8192]{1,0:T(8,128)(2,1)S(1)}, u32[]{:S(2)}) %copy-start.2) | copy-done | bytes 8388632
  62.6 1.1 collective-permute-done.15
  63.6 3.4 %copy-done.1 = bf16[512,8192]{1,0:T(8,128)(2,1)S(1)} copy-done((bf16[512,8192]{1,0:T(8,128)(2,1)S(1)}, bf16[512,8192]{1,0:T(8,128)(2,1)}, u32[]{:S(2)}) %copy-start.1) | copy-done | bytes 8388632
  67.0 3.4 %copy-done.3 = bf16[512,8192]{1,0:T(8,128)(2,1)S(1)} copy-done((bf16[512,8192]{1,0:T(8,128)(2,1)S(1)}, bf16[512,8192]{1,0:T(8,128)(2,1)}, u32[]{:S(2)}) %copy-start.3) | copy-done | bytes 8388632
  70.4 5.0 %project.3 = (bf16[48,4096]{1,0:T(8,128)(2,1)S(1)}, bf16[48,4096]{1,0:T(8,128)(2,1)S(1)}, bf16[48,4096]{1,0:T(8,128)(2,1)S(1)}, bf16[48,4096]{1,0:T(8,128)(2,1)S...) custom-call(bf16[288,512]{1,0:T(8,128)(2,1)S(1)} %bitcast.16, ...), custom_call_target="tpu_custom_call" | custom-call | tf_op jit(solution)/shard_map/project/pallas_call | solution.py:233
  76.0 1.5 %collective-permute-start.17 = (bf16[48,4096]{1,0:T(8,128)(2,1)S(1)}, bf16[48,4096]{1,0:T(8,128)(2,1)S(1)}, u32[]{:S(2)}, u32[]{:S(2)}) collective-permute-start(bf16[48,4096]{1,0:T(8,128)(2,1)S(1)} %get-tuple-element.90), channel_id=1, source_target_pairs={{0,8},{4,12},{8,0},{12,4},{1,9},{5,13},{9,1},{13,5},{2,10},{6,14},... | collective-permute-start | bytes 1179656 | tf_op jit(solution)/shard_map/ppermute | solution.py:373
  77.5 1.1 add_convert_fusion.6
  78.6 2.0 %collective-permute-start.27 = (bf16[48,4096]{1,0:T(8,128)(2,1)S(1)}, bf16[48,4096]{1,0:T(8,128)(2,1)S(1)}, u32[]{:S(2)}, u32[]{:S(2)}) collective-permute-start(bf16[48,4096]{1,0:T(8,128)(2,1)S(1)} %add_convert_fusion.6), channel_id=1, source_target_pairs={{0,1},{3,2},{4,5},{7,6},{8,9},{11,10},{12,13},{15,14},{16,17},{19,... | collective-permute-start | bytes 1179656 | tf_op jit(solution)/shard_map/ppermute | solution.py:380
  81.3 1.3 collective-permute-start.18
  82.6 4.8 %collective-permute-done.26 = bf16[48,4096]{1,0:T(8,128)(2,1)S(1)} collective-permute-done((bf16[48,4096]{1,0:T(8,128)(2,1)S(1)}, bf16[48,4096]{1,0:T(8,128)(2,1)S(1)}, u32[]{:S(2)}, u32[]{:S(2)}) %collective-permute-start.26) | collective-permute-done | bytes 393248 | tf_op jit(solution)/shard_map/ppermute | solution.py:373
  88.0 2.1 %collective-permute-done.27 = bf16[48,4096]{1,0:T(8,128)(2,1)S(1)} collective-permute-done((bf16[48,4096]{1,0:T(8,128)(2,1)S(1)}, bf16[48,4096]{1,0:T(8,128)(2,1)S(1)}, u32[]{:S(2)}, u32[]{:S(2)}) %collective-permute-start.27) | collective-permute-done | bytes 393248 | tf_op jit(solution)/shard_map/ppermute | solution.py:380
  90.3 4.4 %collective-permute-start.30 = (bf16[48,4096]{1,0:T(8,128)(2,1)S(1)}, bf16[48,4096]{1,0:T(8,128)(2,1)S(1)}, u32[]{:S(2)}, u32[]{:S(2)}) collective-permute-start(bf16[48,4096]{1,0:T(8,128)(2,1)S(1)} %get-tuple-element.105), channel_id=1, source_target_pairs={{0,1},{1,2},{4,5},{5,6},{8,9},{9,10},{12,13},{13,14},{16,17},{17,1... | collective-permute-start | bytes 1179656 | tf_op jit(solution)/shard_map/ppermute | solution.py:389
  94.9 1.0 collective-permute-done.17
  96.6 2.0 %collective-permute-done.18 = bf16[48,4096]{1,0:T(8,128)(2,1)S(1)} collective-permute-done((bf16[48,4096]{1,0:T(8,128)(2,1)S(1)}, bf16[48,4096]{1,0:T(8,128)(2,1)S(1)}, u32[]{:S(2)}, u32[]{:S(2)}) %collective-permute-start.18) | collective-permute-done | bytes 393248 | tf_op jit(solution)/shard_map/ppermute | solution.py:380
  98.8 4.4 %collective-permute-start.21 = (bf16[48,4096]{1,0:T(8,128)(2,1)S(1)}, bf16[48,4096]{1,0:T(8,128)(2,1)S(1)}, u32[]{:S(2)}, u32[]{:S(2)}) collective-permute-start(bf16[48,4096]{1,0:T(8,128)(2,1)S(1)} %get-tuple-element.103), channel_id=1, source_target_pairs={{0,1},{1,2},{4,5},{5,6},{8,9},{9,10},{12,13},{13,14},{16,17},{17,1... | collective-permute-start | bytes 1179656 | tf_op jit(solution)/shard_map/ppermute | solution.py:389
  103.3 1.0 collective-permute-done.29
  105.0 2.0 %collective-permute-done.30 = bf16[48,4096]{1,0:T(8,128)(2,1)S(1)} collective-permute-done((bf16[48,4096]{1,0:T(8,128)(2,1)S(1)}, bf16[48,4096]{1,0:T(8,128)(2,1)S(1)}, u32[]{:S(2)}, u32[]{:S(2)}) %collective-permute-start.30) | collective-permute-done | bytes 393248 | tf_op jit(solution)/shard_map/ppermute | solution.py:389
  107.5 1.5 %collective-permute-start.19 = (bf16[48,4096]{1,0:T(8,128)(2,1)S(1)}, bf16[48,4096]{1,0:T(8,128)(2,1)S(1)}, u32[]{:S(2)}, u32[]{:S(2)}) collective-permute-start(bf16[48,4096]{1,0:T(8,128)(2,1)S(1)} %get-tuple-element.91), channel_id=1, source_target_pairs={{0,8},{4,12},{8,0},{12,4},{1,9},{5,13},{9,1},{13,5},{2,10},{6,14},... | collective-permute-start | bytes 1179656 | tf_op jit(solution)/shard_map/ppermute | solution.py:373
  109.3 3.4 %collective-permute-done.20 = bf16[48,4096]{1,0:T(8,128)(2,1)S(1)} collective-permute-done((bf16[48,4096]{1,0:T(8,128)(2,1)S(1)}, bf16[48,4096]{1,0:T(8,128)(2,1)S(1)}, u32[]{:S(2)}, u32[]{:S(2)}) %collective-permute-start.20) | collective-permute-done | bytes 393248 | tf_op jit(solution)/shard_map/ppermute | solution.py:373
  112.7 1.3 collective-permute-start.33
  114.0 4.6 %collective-permute-start.31 = (bf16[48,4096]{1,0:T(8,128)(2,1)S(1)}, bf16[48,4096]{1,0:T(8,128)(2,1)S(1)}, u32[]{:S(2)}, u32[]{:S(2)}) collective-permute-start(bf16[48,4096]{1,0:T(8,128)(2,1)S(1)} %get-tuple-element.109), channel_id=1, source_target_pairs={{0,1},{1,2},{2,3},{4,5},{5,6},{6,7},{8,9},{9,10},{10,11},{12,13},{... | collective-permute-start | bytes 1179656 | tf_op jit(solution)/shard_map/ppermute | solution.py:389
  119.0 1.3 collective-permute-start.24
  121.2 3.7 %collective-permute-start.22 = (bf16[48,4096]{1,0:T(8,128)(2,1)S(1)}, bf16[48,4096]{1,0:T(8,128)(2,1)S(1)}, u32[]{:S(2)}, u32[]{:S(2)}) collective-permute-start(bf16[48,4096]{1,0:T(8,128)(2,1)S(1)} %get-tuple-element.107), channel_id=1, source_target_pairs={{0,1},{1,2},{2,3},{4,5},{5,6},{6,7},{8,9},{9,10},{10,11},{12,13},{... | collective-permute-start | bytes 1179656 | tf_op jit(solution)/shard_map/ppermute | solution.py:389
  124.9 1.8 %collective-permute-done.33 = bf16[48,4096]{1,0:T(8,128)(2,1)S(1)} collective-permute-done((bf16[48,4096]{1,0:T(8,128)(2,1)S(1)}, bf16[48,4096]{1,0:T(8,128)(2,1)S(1)}, u32[]{:S(2)}, u32[]{:S(2)}) %collective-permute-start.33) | collective-permute-done | bytes 393248 | tf_op jit(solution)/shard_map/ppermute | solution.py:389
  126.7 1.5 %collective-permute-done.31 = bf16[48,4096]{1,0:T(8,128)(2,1)S(1)} collective-permute-done((bf16[48,4096]{1,0:T(8,128)(2,1)S(1)}, bf16[48,4096]{1,0:T(8,128)(2,1)S(1)}, u32[]{:S(2)}, u32[]{:S(2)}) %collective-permute-start.31) | collective-permute-done | bytes 393248 | tf_op jit(solution)/shard_map/ppermute | solution.py:389
  128.9 3.9 %collective-permute-done.24 = bf16[48,4096]{1,0:T(8,128)(2,1)S(1)} collective-permute-done((bf16[48,4096]{1,0:T(8,128)(2,1)S(1)}, bf16[48,4096]{1,0:T(8,128)(2,1)S(1)}, u32[]{:S(2)}, u32[]{:S(2)}) %collective-permute-start.24) | collective-permute-done | bytes 393248 | tf_op jit(solution)/shard_map/ppermute | solution.py:389
  132.7 1.4 %collective-permute-done.22 = bf16[48,4096]{1,0:T(8,128)(2,1)S(1)} collective-permute-done((bf16[48,4096]{1,0:T(8,128)(2,1)S(1)}, bf16[48,4096]{1,0:T(8,128)(2,1)S(1)}, u32[]{:S(2)}, u32[]{:S(2)}) %collective-permute-start.22) | collective-permute-done | bytes 393248 | tf_op jit(solution)/shard_map/ppermute | solution.py:389
  (56 shorter events, 12.6 us)
Async XLA Ops:
  0.0 42.2 %collective-permute-start.14 = (bf16[512,8192]{1,0:T(8,128)(2,1)}, bf16[512,8192]{1,0:T(8,128)(2,1)}, u32[]{:S(2)}, u32[]{:S(2)}) collective-permute-start(bf16[512,8192]{1,0:T(8,128)(2,1)} %refs_12_.3), channel_id=1, source_target_pairs={{0,4},{4,0},{8,12},{12,8},{1,5},{5,1},{9,13},{13,9},{2,6},{6,2},{1... | collective-permute-start | bytes 25165832 | tf_op jit(solution)/shard_map/ppermute | solution.py:276
  2.6 22.5 %collective-permute-start = (bf16[384,128]{1,0:T(8,128)(2,1)S(1)}, bf16[384,128]{1,0:T(8,128)(2,1)S(1)}, u32[]{:S(2)}, u32[]{:S(2)}) collective-permute-start(bf16[384,128]{1,0:T(8,128)(2,1)S(1)} %get-tuple-element.55), channel_id=1, source_target_pairs={{0,1},{1,2},{2,3},{3,0},{4,5},{5,6},{6,7},{7,4},{8,9},{9,10},{10,1... | collective-permute-start | bytes 294920 | tf_op jit(solution)/shard_map/ppermute | solution.py:259
  5.2 19.9 %collective-permute-start.1 = (bf16[384,128]{1,0:T(8,128)(2,1)S(1)}, bf16[384,128]{1,0:T(8,128)(2,1)S(1)}, u32[]{:S(2)}, u32[]{:S(2)}) collective-permute-start(bf16[384,128]{1,0:T(8,128)(2,1)S(1)} %get-tuple-element.56), channel_id=1, source_target_pairs={{0,2},{1,3},{2,0},{3,1},{4,6},{5,7},{6,4},{7,5},{8,10},{9,11},{10,... | collective-permute-start | bytes 294920 | tf_op jit(solution)/shard_map/ppermute | solution.py:259
  7.8 18.7 %collective-permute-start.2 = (bf16[384,128]{1,0:T(8,128)(2,1)S(1)}, bf16[384,128]{1,0:T(8,128)(2,1)S(1)}, u32[]{:S(2)}, u32[]{:S(2)}) collective-permute-start(bf16[384,128]{1,0:T(8,128)(2,1)S(1)} %get-tuple-element.57), channel_id=1, source_target_pairs={{0,3},{1,0},{2,1},{3,2},{4,7},{5,4},{6,5},{7,6},{8,11},{9,8},{10,9... | collective-permute-start | bytes 294920 | tf_op jit(solution)/shard_map/ppermute | solution.py:259
  9.2 7.0 %collective-permute-start.10 = (bf16[192,128]{1,0:T(8,128)(2,1)S(1)}, bf16[192,128]{1,0:T(8,128)(2,1)S(1)}, u32[]{:S(2)}, u32[]{:S(2)}) collective-permute-start(bf16[192,128]{1,0:T(8,128)(2,1)S(1)} %get-tuple-element.67), channel_id=1, source_target_pairs={{0,1},{1,2},{2,3},{3,0},{4,5},{5,6},{6,7},{7,4},{8,9},{9,10},{10,1... | collective-permute-start | bytes 147464 | tf_op jit(solution)/shard_map/ppermute | solution.py:259
  16.1 5.5 %collective-permute-start.11 = (bf16[192,128]{1,0:T(8,128)(2,1)S(1)}, bf16[192,128]{1,0:T(8,128)(2,1)S(1)}, u32[]{:S(2)}, u32[]{:S(2)}) collective-permute-start(bf16[192,128]{1,0:T(8,128)(2,1)S(1)} %get-tuple-element.68), channel_id=1, source_target_pairs={{0,2},{1,3},{2,0},{3,1},{4,6},{5,7},{6,4},{7,5},{8,10},{9,11},{10,... | collective-permute-start | bytes 147464 | tf_op jit(solution)/shard_map/ppermute | solution.py:259
  21.6 8.3 %collective-permute-start.3 = (bf16[384,128]{1,0:T(8,128)(2,1)S(1)}, bf16[384,128]{1,0:T(8,128)(2,1)S(1)}, u32[]{:S(2)}, u32[]{:S(2)}) collective-permute-start(bf16[384,128]{1,0:T(8,128)(2,1)S(1)} %get-tuple-element.54.refs_0_), channel_id=1, source_target_pairs={{0,16},{1,17},{2,18},{3,19},{4,20},{5,21},{6,22},{7,23},{8,24},{9,... | collective-permute-start | bytes 294920 | tf_op jit(solution)/shard_map/ppermute | solution.py:274
  25.1 4.1 %collective-permute-start.12 = (bf16[192,128]{1,0:T(8,128)(2,1)S(1)}, bf16[192,128]{1,0:T(8,128)(2,1)S(1)}, u32[]{:S(2)}, u32[]{:S(2)}) collective-permute-start(bf16[192,128]{1,0:T(8,128)(2,1)S(1)} %get-tuple-element.69), channel_id=1, source_target_pairs={{0,3},{1,0},{2,1},{3,2},{4,7},{5,4},{6,5},{7,6},{8,11},{9,8},{10,9... | collective-permute-start | bytes 147464 | tf_op jit(solution)/shard_map/ppermute | solution.py:259
  25.2 7.0 %collective-permute-start.4 = (bf16[384,128]{1,0:T(8,128)(2,1)S(1)}, bf16[384,128]{1,0:T(8,128)(2,1)S(1)}, u32[]{:S(2)}, u32[]{:S(2)}) collective-permute-start(bf16[384,128]{1,0:T(8,128)(2,1)S(1)} %collective-permute-done.refs_1_), channel_id=1, source_target_pairs={{0,16},{1,17},{2,18},{3,19},{4,20},{5,21},{6,22},{7,23},{8,24},{9,... | collective-permute-start | bytes 294920 | tf_op jit(solution)/shard_map/ppermute | solution.py:274
  26.5 7.8 %collective-permute-start.5 = (bf16[384,128]{1,0:T(8,128)(2,1)S(1)}, bf16[384,128]{1,0:T(8,128)(2,1)S(1)}, u32[]{:S(2)}, u32[]{:S(2)}) collective-permute-start(bf16[384,128]{1,0:T(8,128)(2,1)S(1)} %collective-permute-done.1.refs_2_), channel_id=1, source_target_pairs={{0,16},{1,17},{2,18},{3,19},{4,20},{5,21},{6,22},{7,23},{8,24},{9,... | collective-permute-start | bytes 294920 | tf_op jit(solution)/shard_map/ppermute | solution.py:274
  29.2 19.4 %collective-permute-start.7 = (bf16[576,128]{1,0:T(8,128)(2,1)}, bf16[576,128]{1,0:T(8,128)(2,1)S(1)}, u32[]{:S(2)}, u32[]{:S(2)}) collective-permute-start(bf16[576,128]{1,0:T(8,128)(2,1)} %get-tuple-element.61), channel_id=1, source_target_pairs={{0,1},{1,2},{2,3},{3,0},{4,5},{5,6},{6,7},{7,4},{8,9},{9,10},{10,1... | collective-permute-start | bytes 442376 | tf_op jit(solution)/shard_map/ppermute | solution.py:259
  30.0 18.7 %collective-permute-start.8 = (bf16[576,128]{1,0:T(8,128)(2,1)S(1)}, bf16[576,128]{1,0:T(8,128)(2,1)S(1)}, u32[]{:S(2)}, u32[]{:S(2)}) collective-permute-start(bf16[576,128]{1,0:T(8,128)(2,1)S(1)} %get-tuple-element.63), channel_id=1, source_target_pairs={{0,2},{1,3},{2,0},{3,1},{4,6},{5,7},{6,4},{7,5},{8,10},{9,11},{10,... | collective-permute-start | bytes 442376 | tf_op jit(solution)/shard_map/ppermute | solution.py:259
  32.1 16.6 %collective-permute-start.9 = (bf16[576,128]{1,0:T(8,128)(2,1)S(1)}, bf16[576,128]{1,0:T(8,128)(2,1)S(1)}, u32[]{:S(2)}, u32[]{:S(2)}) collective-permute-start(bf16[576,128]{1,0:T(8,128)(2,1)S(1)} %get-tuple-element.65), channel_id=1, source_target_pairs={{0,3},{1,0},{2,1},{3,2},{4,7},{5,4},{6,5},{7,6},{8,11},{9,8},{10,9... | collective-permute-start | bytes 442376 | tf_op jit(solution)/shard_map/ppermute | solution.py:259
  34.3 4.4 %collective-permute-start.6 = (bf16[384,128]{1,0:T(8,128)(2,1)S(1)}, bf16[384,128]{1,0:T(8,128)(2,1)S(1)}, u32[]{:S(2)}, u32[]{:S(2)}) collective-permute-start(bf16[384,128]{1,0:T(8,128)(2,1)S(1)} %collective-permute-done.2.refs_3_), channel_id=1, source_target_pairs={{0,16},{1,17},{2,18},{3,19},{4,20},{5,21},{6,22},{7,23},{8,24},{9,... | collective-permute-start | bytes 294920 | tf_op jit(solution)/shard_map/ppermute | solution.py:274
  42.1 3.5 %collective-permute-start.13 = (bf16[2,48,512]{2,1,0:T(8,128)(2,1)S(1)}, bf16[2,48,512]{2,1,0:T(8,128)(2,1)S(1)}, u32[]{:S(2)}, u32[]{:S(2)}) collective-permute-start(bf16[2,48,512]{2,1,0:T(8,128)(2,1)S(1)} %get-tuple-element.70), channel_id=1, source_target_pairs={{0,4},{4,0},{8,12},{12,8},{1,5},{5,1},{9,13},{13,9},{2,6},{6,2},{1... | collective-permute-start | bytes 294920 | tf_op jit(solution)/shard_map/ppermute | solution.py:327
  47.1 30.4 %collective-permute-start.25 = (bf16[48,4096]{1,0:T(8,128)(2,1)S(1)}, bf16[48,4096]{1,0:T(8,128)(2,1)}, u32[]{:S(2)}, u32[]{:S(2)}) collective-permute-start(bf16[48,4096]{1,0:T(8,128)(2,1)S(1)} %get-tuple-element.78), channel_id=1, source_target_pairs={{0,8},{4,12},{8,0},{12,4},{1,9},{5,13},{9,1},{13,5},{2,10},{6,14},... | collective-permute-start | bytes 1179656 | tf_op jit(solution)/shard_map/ppermute | solution.py:373
  55.3 3.3 %copy-start = (bf16[512,8192]{1,0:T(8,128)(2,1)}, bf16[512,8192]{1,0:T(8,128)(2,1)S(1)}, u32[]{:S(2)}) copy-start(bf16[512,8192]{1,0:T(8,128)(2,1)S(1)} %get-tuple-element.85.refs_2_) | copy-start | bytes 25165828
  58.6 3.2 %copy-start.2 = (bf16[512,8192]{1,0:T(8,128)(2,1)}, bf16[512,8192]{1,0:T(8,128)(2,1)S(1)}, u32[]{:S(2)}) copy-start(bf16[512,8192]{1,0:T(8,128)(2,1)S(1)} %get-tuple-element.86.refs_3_) | copy-start | bytes 25165828
  61.8 1.8 %collective-permute-start.15 = (bf16[2,144,512]{2,1,0:T(8,128)(2,1)}, bf16[2,144,512]{2,1,0:T(8,128)(2,1)S(1)}, u32[]{:S(2)}, u32[]{:S(2)}) collective-permute-start(bf16[2,144,512]{2,1,0:T(8,128)(2,1)} %get-tuple-element.84), channel_id=1, source_target_pairs={{0,4},{4,0},{8,12},{12,8},{1,5},{5,1},{9,13},{13,9},{2,6},{6,2},{1... | collective-permute-start | bytes 884744 | tf_op jit(solution)/shard_map/ppermute | solution.py:327
  62.0 19.2 %collective-permute-start.16 = (bf16[48,4096]{1,0:T(8,128)(2,1)S(1)}, bf16[48,4096]{1,0:T(8,128)(2,1)S(1)}, u32[]{:S(2)}, u32[]{:S(2)}) collective-permute-start(bf16[48,4096]{1,0:T(8,128)(2,1)S(1)} %get-tuple-element.77), channel_id=1, source_target_pairs={{0,8},{4,12},{8,0},{12,4},{1,9},{5,13},{9,1},{13,5},{2,10},{6,14},... | collective-permute-start | bytes 1179656 | tf_op jit(solution)/shard_map/ppermute | solution.py:373
  63.6 3.4 %copy-start.1 = (bf16[512,8192]{1,0:T(8,128)(2,1)S(1)}, bf16[512,8192]{1,0:T(8,128)(2,1)}, u32[]{:S(2)}) copy-start(bf16[512,8192]{1,0:T(8,128)(2,1)} %copy-done) | copy-start | bytes 25165828
  67.0 3.4 %copy-start.3 = (bf16[512,8192]{1,0:T(8,128)(2,1)S(1)}, bf16[512,8192]{1,0:T(8,128)(2,1)}, u32[]{:S(2)}) copy-start(bf16[512,8192]{1,0:T(8,128)(2,1)} %copy-done.2) | copy-start | bytes 25165828
  75.4 12.0 %collective-permute-start.26 = (bf16[48,4096]{1,0:T(8,128)(2,1)S(1)}, bf16[48,4096]{1,0:T(8,128)(2,1)S(1)}, u32[]{:S(2)}, u32[]{:S(2)}) collective-permute-start(bf16[48,4096]{1,0:T(8,128)(2,1)S(1)} %get-tuple-element.98), channel_id=1, source_target_pairs={{0,8},{4,12},{8,0},{12,4},{1,9},{5,13},{9,1},{13,5},{2,10},{6,14},... | collective-permute-start | bytes 1179656 | tf_op jit(solution)/shard_map/ppermute | solution.py:373
  76.0 19.8 %collective-permute-start.17 = (bf16[48,4096]{1,0:T(8,128)(2,1)S(1)}, bf16[48,4096]{1,0:T(8,128)(2,1)S(1)}, u32[]{:S(2)}, u32[]{:S(2)}) collective-permute-start(bf16[48,4096]{1,0:T(8,128)(2,1)S(1)} %get-tuple-element.90), channel_id=1, source_target_pairs={{0,8},{4,12},{8,0},{12,4},{1,9},{5,13},{9,1},{13,5},{2,10},{6,14},... | collective-permute-start | bytes 1179656 | tf_op jit(solution)/shard_map/ppermute | solution.py:373
  78.6 11.5 %collective-permute-start.27 = (bf16[48,4096]{1,0:T(8,128)(2,1)S(1)}, bf16[48,4096]{1,0:T(8,128)(2,1)S(1)}, u32[]{:S(2)}, u32[]{:S(2)}) collective-permute-start(bf16[48,4096]{1,0:T(8,128)(2,1)S(1)} %add_convert_fusion.6), channel_id=1, source_target_pairs={{0,1},{3,2},{4,5},{7,6},{8,9},{11,10},{12,13},{15,14},{16,17},{19,... | collective-permute-start | bytes 1179656 | tf_op jit(solution)/shard_map/ppermute | solution.py:380
  80.6 23.7 %collective-permute-start.29 = (bf16[48,4096]{1,0:T(8,128)(2,1)S(1)}, bf16[48,4096]{1,0:T(8,128)(2,1)S(1)}, u32[]{:S(2)}, u32[]{:S(2)}) collective-permute-start(bf16[48,4096]{1,0:T(8,128)(2,1)S(1)} %get-tuple-element.102), channel_id=1, source_target_pairs={{0,8},{4,12},{8,0},{12,4},{1,9},{5,13},{9,1},{13,5},{2,10},{6,14},... | collective-permute-start | bytes 1179656 | tf_op jit(solution)/shard_map/ppermute | solution.py:373
  81.3 17.2 %collective-permute-start.18 = (bf16[48,4096]{1,0:T(8,128)(2,1)S(1)}, bf16[48,4096]{1,0:T(8,128)(2,1)S(1)}, u32[]{:S(2)}, u32[]{:S(2)}) collective-permute-start(bf16[48,4096]{1,0:T(8,128)(2,1)S(1)} %add_convert_fusion.13), channel_id=1, source_target_pairs={{0,1},{3,2},{4,5},{7,6},{8,9},{11,10},{12,13},{15,14},{16,17},{19,... | collective-permute-start | bytes 1179656 | tf_op jit(solution)/shard_map/ppermute | solution.py:380
  87.5 25.3 %collective-permute-start.20 = (bf16[48,4096]{1,0:T(8,128)(2,1)S(1)}, bf16[48,4096]{1,0:T(8,128)(2,1)S(1)}, u32[]{:S(2)}, u32[]{:S(2)}) collective-permute-start(bf16[48,4096]{1,0:T(8,128)(2,1)S(1)} %get-tuple-element.94), channel_id=1, source_target_pairs={{0,8},{4,12},{8,0},{12,4},{1,9},{5,13},{9,1},{13,5},{2,10},{6,14},... | collective-permute-start | bytes 1179656 | tf_op jit(solution)/shard_map/ppermute | solution.py:373
  90.3 16.6 %collective-permute-start.30 = (bf16[48,4096]{1,0:T(8,128)(2,1)S(1)}, bf16[48,4096]{1,0:T(8,128)(2,1)S(1)}, u32[]{:S(2)}, u32[]{:S(2)}) collective-permute-start(bf16[48,4096]{1,0:T(8,128)(2,1)S(1)} %get-tuple-element.105), channel_id=1, source_target_pairs={{0,1},{1,2},{4,5},{5,6},{8,9},{9,10},{12,13},{13,14},{16,17},{17,1... | collective-permute-start | bytes 1179656 | tf_op jit(solution)/shard_map/ppermute | solution.py:389
  95.9 11.6 %collective-permute-start.32 = (bf16[48,4096]{1,0:T(8,128)(2,1)S(1)}, bf16[48,4096]{1,0:T(8,128)(2,1)S(1)}, u32[]{:S(2)}, u32[]{:S(2)}) collective-permute-start(bf16[48,4096]{1,0:T(8,128)(2,1)S(1)} %fusion.3), channel_id=1, source_target_pairs={{2,1},{3,2},{6,5},{7,6},{10,9},{11,10},{14,13},{15,14},{18,17},{19... | collective-permute-start | bytes 1179656 | tf_op jit(solution)/shard_map/ppermute | solution.py:389
  98.8 15.3 %collective-permute-start.21 = (bf16[48,4096]{1,0:T(8,128)(2,1)S(1)}, bf16[48,4096]{1,0:T(8,128)(2,1)S(1)}, u32[]{:S(2)}, u32[]{:S(2)}) collective-permute-start(bf16[48,4096]{1,0:T(8,128)(2,1)S(1)} %get-tuple-element.103), channel_id=1, source_target_pairs={{0,1},{1,2},{4,5},{5,6},{8,9},{9,10},{12,13},{13,14},{16,17},{17,1... | collective-permute-start | bytes 1179656 | tf_op jit(solution)/shard_map/ppermute | solution.py:389
  104.3 14.3 %collective-permute-start.23 = (bf16[48,4096]{1,0:T(8,128)(2,1)S(1)}, bf16[48,4096]{1,0:T(8,128)(2,1)S(1)}, u32[]{:S(2)}, u32[]{:S(2)}) collective-permute-start(bf16[48,4096]{1,0:T(8,128)(2,1)S(1)} %fusion.1), channel_id=1, source_target_pairs={{2,1},{3,2},{6,5},{7,6},{10,9},{11,10},{14,13},{15,14},{18,17},{19... | collective-permute-start | bytes 1179656 | tf_op jit(solution)/shard_map/ppermute | solution.py:389
  107.0 14.2 %collective-permute-start.28 = (bf16[48,4096]{1,0:T(8,128)(2,1)S(1)}, bf16[48,4096]{1,0:T(8,128)(2,1)S(1)}, u32[]{:S(2)}, u32[]{:S(2)}) collective-permute-start(bf16[48,4096]{1,0:T(8,128)(2,1)S(1)} %get-tuple-element.99), channel_id=1, source_target_pairs={{0,8},{4,12},{8,0},{12,4},{1,9},{5,13},{9,1},{13,5},{2,10},{6,14},... | collective-permute-start | bytes 1179656 | tf_op jit(solution)/shard_map/ppermute | solution.py:373
  107.5 21.4 %collective-permute-start.19 = (bf16[48,4096]{1,0:T(8,128)(2,1)S(1)}, bf16[48,4096]{1,0:T(8,128)(2,1)S(1)}, u32[]{:S(2)}, u32[]{:S(2)}) collective-permute-start(bf16[48,4096]{1,0:T(8,128)(2,1)S(1)} %get-tuple-element.91), channel_id=1, source_target_pairs={{0,8},{4,12},{8,0},{12,4},{1,9},{5,13},{9,1},{13,5},{2,10},{6,14},... | collective-permute-start | bytes 1179656 | tf_op jit(solution)/shard_map/ppermute | solution.py:373
  112.7 13.9 %collective-permute-start.33 = (bf16[48,4096]{1,0:T(8,128)(2,1)S(1)}, bf16[48,4096]{1,0:T(8,128)(2,1)S(1)}, u32[]{:S(2)}, u32[]{:S(2)}) collective-permute-start(bf16[48,4096]{1,0:T(8,128)(2,1)S(1)} %get-tuple-element.110), channel_id=1, source_target_pairs={{1,0},{2,1},{3,2},{5,4},{6,5},{7,6},{9,8},{10,9},{11,10},{13,12},{... | collective-permute-start | bytes 1179656 | tf_op jit(solution)/shard_map/ppermute | solution.py:389
  114.0 14.1 %collective-permute-start.31 = (bf16[48,4096]{1,0:T(8,128)(2,1)S(1)}, bf16[48,4096]{1,0:T(8,128)(2,1)S(1)}, u32[]{:S(2)}, u32[]{:S(2)}) collective-permute-start(bf16[48,4096]{1,0:T(8,128)(2,1)S(1)} %get-tuple-element.109), channel_id=1, source_target_pairs={{0,1},{1,2},{2,3},{4,5},{5,6},{6,7},{8,9},{9,10},{10,11},{12,13},{... | collective-permute-start | bytes 1179656 | tf_op jit(solution)/shard_map/ppermute | solution.py:389
  119.0 13.8 %collective-permute-start.24 = (bf16[48,4096]{1,0:T(8,128)(2,1)S(1)}, bf16[48,4096]{1,0:T(8,128)(2,1)S(1)}, u32[]{:S(2)}, u32[]{:S(2)}) collective-permute-start(bf16[48,4096]{1,0:T(8,128)(2,1)S(1)} %get-tuple-element.108), channel_id=1, source_target_pairs={{1,0},{2,1},{3,2},{5,4},{6,5},{7,6},{9,8},{10,9},{11,10},{13,12},{... | collective-permute-start | bytes 1179656 | tf_op jit(solution)/shard_map/ppermute | solution.py:389
  121.2 12.9 %collective-permute-start.22 = (bf16[48,4096]{1,0:T(8,128)(2,1)S(1)}, bf16[48,4096]{1,0:T(8,128)(2,1)S(1)}, u32[]{:S(2)}, u32[]{:S(2)}) collective-permute-start(bf16[48,4096]{1,0:T(8,128)(2,1)S(1)} %get-tuple-element.107), channel_id=1, source_target_pairs={{0,1},{1,2},{2,3},{4,5},{5,6},{6,7},{8,9},{9,10},{10,11},{12,13},{... | collective-permute-start | bytes 1179656 | tf_op jit(solution)/shard_map/ppermute | solution.py:389

commit v6 on v5

--- a/solution.py
+++ b/solution.py
@@ -20,7 +20,7 @@
 VMEM = pl.BlockSpec(memory_space=pltpu.VMEM)
 SMEM = pl.BlockSpec(memory_space=pltpu.SMEM)
 HBM = pl.BlockSpec(memory_space=pltpu.HBM)
-LIMIT = pltpu.CompilerParams(vmem_limit_bytes=20 << 20)
+LIMIT = pltpu.CompilerParams(vmem_limit_bytes=14 << 20)
 TILE = 1024
 FREE = pl.CostEstimate(flops=0, bytes_accessed=0, transcendentals=0)
 
@@ -72,9 +72,9 @@
             first = pl.multiple_of(lax.div(target * kv_local, slabs) * HEAD_SIZE, HEAD_SIZE)
             outs[k][n * block : (n + 1) * block, :] = pairs[n][1][:, pl.ds(first, HEAD_SIZE)]
     copies[2].wait()
-    for n, stage in enumerate(stages, 1):
+    for n, stage in enumerate(stages):
         for k, target in enumerate(targets):
-            place = 0
+            place = 2 * block if n == 0 else 0
             for h in range(heads):
                 column = pl.multiple_of((target * heads + h) * HEAD_SIZE, HEAD_SIZE)
                 for i in stage:
@@ -88,7 +88,7 @@
 
 def pack(queries, keys, values, *, slabs, heads, kv_local, order, share, stages):
     block = queries.shape[0]
-    counts = [2 * block] + [heads * share * len(stage) for stage in stages]
+    counts = [heads * share * len(stage) + (2 * block if n == 0 else 0) for n, stage in enumerate(stages)]
     return pl.pallas_call(
         partial(
             pack_kernel, slabs=slabs, heads=heads, kv_local=kv_local, order=order, share=share, stages=stages
@@ -104,7 +104,7 @@
     )(in_hbm(queries), in_hbm(keys), in_hbm(values))
 
 
-def attend_kernel(key_doc, *refs, slabs, heads, share, stage, order, columns_x, per_shard, fetched):
+def attend_kernel(key_doc, *refs, slabs, heads, share, stage, order, offset, columns_x, per_shard, fetched):
     refs = list(refs)
     take = lambda n: [refs.pop(0) for _ in range(n)]
     now, before, queries, weights = take(slabs), take(slabs), take(slabs), take(fetched)
@@ -142,7 +142,7 @@
         query_doc = joined([jnp.max(jnp.where(b == 0, docs, -2.0), axis=1, keepdims=True) for b in behind])
         visible = causal & (query_doc == docs)
         scores = lax.dot_general(
-            queries[k][...],
+            queries[k][offset : offset + heads * rows, :],
             key_rows[...],
             (((1,), (1,)), ((), ())),
             preferred_element_type=F32,
@@ -270,15 +270,18 @@
         stages=stages,
     )
     loads = [packed[0]] + [around(packed[k], k) for k in range(1, slabs)]
+    behind = [loads[0]] + loads[:0:-1]
+    cuts = [behind[: slabs // 2], behind[slabs // 2 :]] if slabs > 1 else [behind]
+    cuts = [joined([a[: 2 * block] for a in cut]) for cut in cuts]
+    cuts = [lax.ppermute(cut, "srv", [(g, g + 1) for g in range(groups - 1)]) for cut in cuts]
     before = [
-        lax.ppermute(a, "srv", [(g, g + 1) for g in range(groups - 1)]) for a in loads
+        cut[n * 2 * block : (n + 1) * 2 * block] for cut in cuts for n in range(cut.shape[0] // (2 * block))
     ]
+    before = [before[0]] + before[:0:-1]
     weight_sibling = lax.ppermute(out_weight, "head", siblings)
-    stage_queries = []
-    for n in range(len(stages)):
-        sent = packed[(n + 1) * slabs : (n + 2) * slabs]
-        if n:
-            sent = [after(a, *loads) for a in sent]
+    stage_queries = [loads]
+    for n in range(1, len(stages)):
+        sent = [after(a, *loads) for a in packed[n * slabs : (n + 1) * slabs]]
         stage_queries.append([sent[0]] + [around(sent[k], k) for k in range(1, slabs)])
 
     reach = SLAB_REACH - 1
@@ -294,18 +297,18 @@
     for n, (stage, arrived) in enumerate(zip(stages, stage_queries)):
         if n:
             arrived = after(arrived, *results)
-        fetch = [out_weight] if n == 0 else [out_weight, weight_sibling]
         keep, send, *fetched = attend(
             key_doc,
             loads,
             before,
             arrived,
-            fetch,
+            [out_weight],
             slabs=slabs,
             heads=heads,
             share=rows_at_once,
             stage=stage,
             order=order,
+            offset=2 * block if n == 0 else 0,
             columns_x=columns_x,
             per_shard=per_shard,
         )
@@ -326,12 +329,11 @@
             )
         theirs = lax.ppermute(send, "head", siblings)
         keep, theirs = (a.reshape(-1, a.shape[-1]) for a in (keep, theirs))
-        if n == 0 and staged:
+        if staged:
             begun, far = first_half(keep, fetched[0], weight_sibling)
             results = project([theirs], [far], [begun], share, halves)
         else:
-            weights = fetched if n else [fetched[0], weight_sibling]
-            results = project([keep, theirs], weights, [], share, halves)
+            results = project([keep, theirs], [fetched[0], weight_sibling], [], share, halves)
         for m in range(len(pieces)):
             partials.append(
                 [
@@ -360,7 +362,7 @@
         return (picked.astype(F32) + arrived.astype(F32)).astype(BF16)
 
     sums = [[] for _ in range(halves)]
-    messages = [[] for _ in range(halves)]
+    crossed = [None] * halves
     arrived = [{1: None, -1: None} for _ in range(halves)]
     for t in range(slabs):
         for half in range(halves):
@@ -368,9 +370,10 @@
             for k in range(1, columns_x):
                 route = [(h, (h + 2 * k) % head_shards) for h in range(head_shards)]
                 piece = partials[t][k][half]
-                if t >= 2:
-                    piece = after(piece, *messages[half][t - 2])
-                total = total + lax.ppermute(piece, "head", route).astype(F32)
+                if t:
+                    piece = after(piece, crossed[half])
+                crossed[half] = lax.ppermute(piece, "head", route)
+                total = total + crossed[half].astype(F32)
             sums[half].append(total.astype(BF16))
             if t == slabs - 1:
                 continue
@@ -379,7 +382,6 @@
                 sent = message({**up, **down}, sums[half], arrived[half][1])
                 both = lax.ppermute(sent, "wsh", [(i, i + 1) for i in up] + [(i, i - 1) for i in down])
                 arrived[half] = {1: both, -1: both}
-                messages[half].append([sent])
             else:
                 sent = {
                     direction: message(found, sums[half], arrived[half][direction])
@@ -389,7 +391,6 @@
                     arrived[half][direction] = lax.ppermute(
                         sent[direction], "wsh", [(i, i + direction) for i in found]
                     )
-                messages[half].append(list(sent.values()))
     outs = []
     for half in range(halves):
         total = sums[half][-1].astype(F32)

time: 136 us -> 119 us (0.88)
  waiting for transfers between devices: 38 us -> 27.6 us
  local copies, waits for them, and re-layouts: 13.6 us -> 6.98 us
  starting transfers between devices: 55.7 us -> 57.4 us
    unnamed x8 -> x4, local copies, waits for them, and re-layouts: 13.3 us -> 6.63 us
    pallas_call x1 -> x2, Pallas kernels: 3.39 us -> 6.78 us  [first_half(): pl.pallas_call(first_half_kernel, out_shape=[pltpu.VMEM((rows_here.shape[...]
    ppermute x9 -> x6, waiting for transfers between devices: 8.69 us -> 5.37 us  [around(): lax.ppermute(array, 'wsh', [(i, (i + k) % slabs) for i in range(slabs)])]
    ppermute x12 -> x10, waiting for transfers between devices: 13.6 us -> 10.9 us  [the longest x8 10.9 us: on_device(): crossed[half] = lax.ppermute(piece, 'head', route)]
    ppermute x8, waiting for transfers between devices: 10.5 us -> 8 us  [on_device(): lax.ppermute(sent[direction], 'wsh', [(i, i + direction) for i in found])]
    pallas_call x2, Pallas kernels: 6.5 us -> 4.08 us  [project(): pl.pallas_call(partial(project_kernel, terms=len(lhs), begun=len(start),...]
    ppermute x2, starting transfers between devices: 3.29 us -> 5.35 us  [on_device(): lax.ppermute(sent, 'wsh', [(i, i + 1) for i in up] + [(i, i - 1) for i in...]
    ppermute x12 -> x10, starting transfers between devices: 15.6 us -> 13.6 us  [the longest x8 8.57 us: on_device(): crossed[half] = lax.ppermute(piece, 'head', route)]
  transfers between devices with their start and end apart: 34 -> 29, of which waited for: 18 -> 10; matrix products, arithmetic and copies ran while one was open for 4% -> 3% of each run, Pallas kernels for 16% -> 18%
where the time goes in v6:
time: 119 us
  starting transfers between devices  57.4 us (48%)
  waiting for transfers between devices  27.6 us (23%)
  Pallas kernels  21.6 us (18%)
  local copies, waits for them, and re-layouts  6.98 us (6%)
  other arithmetic  4.65 us (4%)
    ppermute x8, starting transfers between devices, on_device(): lax.ppermute(sent[direction], 'wsh', [(i, i + direction) for i in found])  22 us
    ppermute x6, starting transfers between devices, around(): lax.ppermute(array, 'wsh', [(i, (i + k) % slabs) for i in range(slabs)])  15.7 us
    ppermute x8, waiting for transfers between devices, on_device(): crossed[half] = lax.ppermute(piece, 'head', route)  10.9 us
    pallas_call x2, Pallas kernels, attend(): pl.pallas_call(partial(attend_kernel, slabs=slabs, heads=heads, share=sha...  9.26 us
    ppermute x8, starting transfers between devices, on_device(): crossed[half] = lax.ppermute(piece, 'head', route)  8.57 us
    ppermute x8, waiting for transfers between devices, on_device(): lax.ppermute(sent[direction], 'wsh', [(i, i + direction) for i in found])  8 us
    pallas_call x2, Pallas kernels, first_half(): pl.pallas_call(first_half_kernel, out_shape=[pltpu.VMEM((rows_here.shape[...  6.78 us
    unnamed x4, local copies, waits for them, and re-layouts  6.63 us
  transfers between devices with their start and end apart: 29, of which 10 were waited for; matrix products, arithmetic and copies ran while one was open for 3% of the time, Pallas kernels for 18%

profile of v6, /device:TPU:0, one launch (start us, length us, event | category | flops | bytes accessed | tf_op | source)
XLA Modules:
  0.0 118.6 jit_solution(4772040617098300177)
XLA Ops:
  0.5 1.5 %pack.1 = (bf16[576,128]{1,0:T(8,128)(2,1)S(1)}, bf16[576,128]{1,0:T(8,128)(2,1)S(1)}, bf16[576,128]{1,0:T(8,128)(2,1)S(1)}, bf16[576,128]{1,0:T(8,128)(2,1)S(1)...) custom-call(bf16[192,2048]{1,0:T(8,128)(2,1)} %queries.1, ...), custom_call_target="tpu_custom_call" | custom-call | tf_op jit(solution)/shard_map/pack/pallas_call | solution.py:92
  1.9 3.7 %collective-permute-start.1 = (bf16[576,128]{1,0:T(8,128)(2,1)S(1)}, bf16[576,128]{1,0:T(8,128)(2,1)S(1)}, u32[]{:S(2)}, u32[]{:S(2)}) collective-permute-start(bf16[576,128]{1,0:T(8,128)(2,1)S(1)} %get-tuple-element.55), channel_id=1, source_target_pairs={{0,2},{1,3},{2,0},{3,1},{4,6},{5,7},{6,4},{7,5},{8,10},{9,11},{10,... | collective-permute-start | bytes 442376 | tf_op jit(solution)/shard_map/ppermute | solution.py:259
  5.6 1.6 %collective-permute-start = (bf16[576,128]{1,0:T(8,128)(2,1)S(1)}, bf16[576,128]{1,0:T(8,128)(2,1)S(1)}, u32[]{:S(2)}, u32[]{:S(2)}) collective-permute-start(bf16[576,128]{1,0:T(8,128)(2,1)S(1)} %get-tuple-element.54), channel_id=1, source_target_pairs={{0,1},{1,2},{2,3},{3,0},{4,5},{5,6},{6,7},{7,4},{8,9},{9,10},{10,1... | collective-permute-start | bytes 442376 | tf_op jit(solution)/shard_map/ppermute | solution.py:259
  7.2 2.2 %collective-permute-start.2 = (bf16[576,128]{1,0:T(8,128)(2,1)S(1)}, bf16[576,128]{1,0:T(8,128)(2,1)S(1)}, u32[]{:S(2)}, u32[]{:S(2)}) collective-permute-start(bf16[576,128]{1,0:T(8,128)(2,1)S(1)} %get-tuple-element.56), channel_id=1, source_target_pairs={{0,3},{1,0},{2,1},{3,2},{4,7},{5,4},{6,5},{7,6},{8,11},{9,8},{10,9... | collective-permute-start | bytes 442376 | tf_op jit(solution)/shard_map/ppermute | solution.py:259
  9.4 0.7 convert_element_type.180
  10.3 0.8 compare_bitcast_fusion.3
  11.3 5.4 %collective-permute-done.1.refs_2_.refs_10_ = bf16[576,128]{1,0:T(8,128)(2,1)S(1)} collective-permute-done((bf16[576,128]{1,0:T(8,128)(2,1)S(1)}, bf16[576,128]{1,0:T(8,128)(2,1)S(1)}, u32[]{:S(2)}, u32[]{:S(2)}) %collective-permute-start.1) | collective-permute-done | bytes 147488 | tf_op jit(solution)/shard_map/ppermute | solution.py:259
  16.7 3.7 %collective-permute-start.4 = (bf16[768,128]{1,0:T(8,128)(2,1)S(1)}, bf16[768,128]{1,0:T(8,128)(2,1)S(1)}, u32[]{:S(2)}, u32[]{:S(2)}) collective-permute-start(bf16[768,128]{1,0:T(8,128)(2,1)S(1)} %pad_maximum_fusion.2), channel_id=1, source_target_pairs={{0,16},{1,17},{2,18},{3,19},{4,20},{5,21},{6,22},{7,23},{8,24},{9,... | collective-permute-start | bytes 589832 | tf_op jit(solution)/shard_map/ppermute | solution.py:276
  20.6 1.3 %collective-permute-start.3 = (bf16[768,128]{1,0:T(8,128)(2,1)S(1)}, bf16[768,128]{1,0:T(8,128)(2,1)S(1)}, u32[]{:S(2)}, u32[]{:S(2)}) collective-permute-start(bf16[768,128]{1,0:T(8,128)(2,1)S(1)} %pad_maximum_fusion.1), channel_id=1, source_target_pairs={{0,16},{1,17},{2,18},{3,19},{4,20},{5,21},{6,22},{7,23},{8,24},{9,... | collective-permute-start | bytes 589832 | tf_op jit(solution)/shard_map/ppermute | solution.py:276
  21.9 3.4 %collective-permute-start.5 = (bf16[576,128]{1,0:T(8,128)(2,1)S(1)}, bf16[576,128]{1,0:T(8,128)(2,1)S(1)}, u32[]{:S(2)}, u32[]{:S(2)}) collective-permute-start(bf16[576,128]{1,0:T(8,128)(2,1)S(1)} %get-tuple-element.60), channel_id=1, source_target_pairs={{0,1},{1,2},{2,3},{3,0},{4,5},{5,6},{6,7},{7,4},{8,9},{9,10},{10,1... | collective-permute-start | bytes 442376 | tf_op jit(solution)/shard_map/ppermute | solution.py:259
  25.4 2.0 %collective-permute-start.6 = (bf16[576,128]{1,0:T(8,128)(2,1)S(1)}, bf16[576,128]{1,0:T(8,128)(2,1)S(1)}, u32[]{:S(2)}, u32[]{:S(2)}) collective-permute-start(bf16[576,128]{1,0:T(8,128)(2,1)S(1)} %get-tuple-element.62), channel_id=1, source_target_pairs={{0,2},{1,3},{2,0},{3,1},{4,6},{5,7},{6,4},{7,5},{8,10},{9,11},{10,... | collective-permute-start | bytes 442376 | tf_op jit(solution)/shard_map/ppermute | solution.py:259
  27.4 2.8 %collective-permute-start.7 = (bf16[576,128]{1,0:T(8,128)(2,1)S(1)}, bf16[576,128]{1,0:T(8,128)(2,1)S(1)}, u32[]{:S(2)}, u32[]{:S(2)}) collective-permute-start(bf16[576,128]{1,0:T(8,128)(2,1)S(1)} %get-tuple-element.64), channel_id=1, source_target_pairs={{0,3},{1,0},{2,1},{3,2},{4,7},{5,4},{6,5},{7,6},{8,11},{9,8},{10,9... | collective-permute-start | bytes 442376 | tf_op jit(solution)/shard_map/ppermute | solution.py:259
  30.3 3.4 %attend.2 = (bf16[2,48,512]{2,1,0:T(8,128)(2,1)S(1)}, bf16[2,48,512]{2,1,0:T(8,128)(2,1)S(1)}, bf16[512,8192]{1,0:T(8,128)(2,1)S(1)}) custom-call(f32[8,1,768]{2,1,0:T(1,128)S(1)} %reshape.55.key_doc, bf16[576,128]{1,0:T(8,128)(2,1)S(1)} %get-tuple-element.53.refs_0_.refs_8_, bf16[576,128]{1,0:T(8,128)(2,1)S(1)} %collective-permute-done.refs_1_.refs_9_, ...), custom_call_target="tpu_custom_call" | custom-call | flops 301989888 | tf_op jit(solution)/shard_map/attend/pallas_call | solution.py:180
  33.8 3.4 %first_half.2 = (f32[96,8192]{1,0:T(8,128)S(1)}, bf16[512,8192]{1,0:T(8,128)(2,1)S(1)}) custom-call(bf16[96,512]{1,0:T(8,128)(2,1)S(1)} %bitcast.19, bf16[512,8192]{1,0:T(8,128)(2,1)S(1)} %get-tuple-element.67.weight, bf16[512,8192]{1,0:T(8,128)(2,1)} %collective-permute-done.9.fetch), custom_call_target="tpu_custom_call" | custom-call | tf_op jit(solution)/shard_map/first_half/pallas_call | solution.py:204
  37.2 1.5 %project.2 = (bf16[48,4096]{1,0:T(8,128)(2,1)S(1)}, bf16[48,4096]{1,0:T(8,128)(2,1)S(1)}, bf16[48,4096]{1,0:T(8,128)(2,1)S(1)}, bf16[48,4096]{1,0:T(8,128)(2,1)S(1)}) custom-call(bf16[96,512]{1,0:T(8,128)(2,1)S(1)} %bitcast.18, bf16[512,8192]{1,0:T(8,128)(2,1)S(1)} %get-tuple-element.68.refs_1_, f32[96,8192]{1,0:T(8,128)S(1)} %get-tuple-element.69.refs_2_), custom_call_target="tpu_custom_call" | custom-call | tf_op jit(solution)/shard_map/project/pallas_call | solution.py:233
  38.6 1.6 %collective-permute-start.11 = (bf16[48,4096]{1,0:T(8,128)(2,1)S(1)}, bf16[48,4096]{1,0:T(8,128)(2,1)S(1)}, u32[]{:S(2)}, u32[]{:S(2)}) collective-permute-start(bf16[48,4096]{1,0:T(8,128)(2,1)S(1)} %get-tuple-element.72), channel_id=1, source_target_pairs={{0,8},{4,12},{8,0},{12,4},{1,9},{5,13},{9,1},{13,5},{2,10},{6,14},... | collective-permute-start | bytes 1179656 | tf_op jit(solution)/shard_map/ppermute | solution.py:375
  40.2 5.9 %attend.3 = (bf16[2,144,512]{2,1,0:T(8,128)(2,1)S(1)}, bf16[2,144,512]{2,1,0:T(8,128)(2,1)S(1)}, bf16[512,8192]{1,0:T(8,128)(2,1)S(1)}) custom-call(f32[8,1,768]{2,1,0:T(1,128)S(1)} %reshape.55.key_doc, bf16[576,128]{1,0:T(8,128)(2,1)S(1)} %get-tuple-element.53.refs_0_.refs_8_, bf16[576,128]{1,0:T(8,128)(2,1)S(1)} %collective-permute-done.refs_1_.refs_9_, ...), custom_call_target="tpu_custom_call" | custom-call | flops 905969664 | tf_op jit(solution)/shard_map/attend/pallas_call | solution.py:180
  46.1 3.2 %copy-done = bf16[512,8192]{1,0:T(8,128)(2,1)} copy-done((bf16[512,8192]{1,0:T(8,128)(2,1)}, bf16[512,8192]{1,0:T(8,128)(2,1)S(1)}, u32[]{:S(2)}) %copy-start) | copy-done | bytes 8388632
  49.5 0.5 collective-permute-start.20
  50.1 3.4 %copy-done.1 = bf16[512,8192]{1,0:T(8,128)(2,1)S(1)} copy-done((bf16[512,8192]{1,0:T(8,128)(2,1)S(1)}, bf16[512,8192]{1,0:T(8,128)(2,1)}, u32[]{:S(2)}) %copy-start.1) | copy-done | bytes 8388632
  53.5 3.4 %first_half.3 = (f32[288,8192]{1,0:T(8,128)S(1)}, bf16[512,8192]{1,0:T(8,128)(2,1)S(1)}) custom-call(bf16[288,512]{1,0:T(8,128)(2,1)S(1)} %bitcast.17, bf16[512,8192]{1,0:T(8,128)(2,1)S(1)} %copy-done.1, bf16[512,8192]{1,0:T(8,128)(2,1)} %collective-permute-done.9.fetch), custom_call_target="tpu_custom_call" | custom-call | tf_op jit(solution)/shard_map/first_half/pallas_call | solution.py:204
  56.9 2.6 %project.3 = (bf16[48,4096]{1,0:T(8,128)(2,1)S(1)}, bf16[48,4096]{1,0:T(8,128)(2,1)S(1)}, bf16[48,4096]{1,0:T(8,128)(2,1)S(1)}, bf16[48,4096]{1,0:T(8,128)(2,1)S...) custom-call(bf16[288,512]{1,0:T(8,128)(2,1)S(1)} %bitcast.16, ...), custom_call_target="tpu_custom_call" | custom-call | tf_op jit(solution)/shard_map/project/pallas_call | solution.py:233
  59.5 1.6 %collective-permute-start.12 = (bf16[48,4096]{1,0:T(8,128)(2,1)S(1)}, bf16[48,4096]{1,0:T(8,128)(2,1)S(1)}, u32[]{:S(2)}, u32[]{:S(2)}) collective-permute-start(bf16[48,4096]{1,0:T(8,128)(2,1)S(1)} %get-tuple-element.87), channel_id=1, source_target_pairs={{0,8},{4,12},{8,0},{12,4},{1,9},{5,13},{9,1},{13,5},{2,10},{6,14},... | collective-permute-start | bytes 1179656 | tf_op jit(solution)/shard_map/ppermute | solution.py:375
  61.2 4.0 %collective-permute-start.15 = (bf16[48,4096]{1,0:T(8,128)(2,1)S(1)}, bf16[48,4096]{1,0:T(8,128)(2,1)S(1)}, u32[]{:S(2)}, u32[]{:S(2)}) collective-permute-start(bf16[48,4096]{1,0:T(8,128)(2,1)S(1)} %add_convert_fusion.10), channel_id=1, source_target_pairs={{0,1},{3,2},{4,5},{7,6},{8,9},{11,10},{12,13},{15,14},{16,17},{19,... | collective-permute-start | bytes 1179656 | tf_op jit(solution)/shard_map/ppermute | solution.py:383
  65.2 0.6 collective-permute-start.21
  65.9 1.3 %collective-permute-start.24 = (bf16[48,4096]{1,0:T(8,128)(2,1)S(1)}, bf16[48,4096]{1,0:T(8,128)(2,1)S(1)}, u32[]{:S(2)}, u32[]{:S(2)}) collective-permute-start(bf16[48,4096]{1,0:T(8,128)(2,1)S(1)} %add_convert_fusion.3), channel_id=1, source_target_pairs={{0,1},{3,2},{4,5},{7,6},{8,9},{11,10},{12,13},{15,14},{16,17},{19,... | collective-permute-start | bytes 1179656 | tf_op jit(solution)/shard_map/ppermute | solution.py:383
  67.2 4.3 %collective-permute-done.12 = bf16[48,4096]{1,0:T(8,128)(2,1)S(1)} collective-permute-done((bf16[48,4096]{1,0:T(8,128)(2,1)S(1)}, bf16[48,4096]{1,0:T(8,128)(2,1)S(1)}, u32[]{:S(2)}, u32[]{:S(2)}) %collective-permute-start.12) | collective-permute-done | bytes 393248 | tf_op jit(solution)/shard_map/ppermute | solution.py:375
  71.5 1.5 %collective-permute-start.13 = (bf16[48,4096]{1,0:T(8,128)(2,1)S(1)}, bf16[48,4096]{1,0:T(8,128)(2,1)S(1)}, u32[]{:S(2)}, u32[]{:S(2)}) collective-permute-start(bf16[48,4096]{1,0:T(8,128)(2,1)S(1)} %get-tuple-element.88), channel_id=1, source_target_pairs={{0,8},{4,12},{8,0},{12,4},{1,9},{5,13},{9,1},{13,5},{2,10},{6,14},... | collective-permute-start | bytes 1179656 | tf_op jit(solution)/shard_map/ppermute | solution.py:375
  73.0 1.7 %collective-permute-done.15 = bf16[48,4096]{1,0:T(8,128)(2,1)S(1)} collective-permute-done((bf16[48,4096]{1,0:T(8,128)(2,1)S(1)}, bf16[48,4096]{1,0:T(8,128)(2,1)S(1)}, u32[]{:S(2)}, u32[]{:S(2)}) %collective-permute-start.15) | collective-permute-done | bytes 393248 | tf_op jit(solution)/shard_map/ppermute | solution.py:383
  75.1 0.7 collective-permute-start.18
  75.8 5.0 %collective-permute-start.16 = (bf16[48,4096]{1,0:T(8,128)(2,1)S(1)}, bf16[48,4096]{1,0:T(8,128)(2,1)S(1)}, u32[]{:S(2)}, u32[]{:S(2)}) collective-permute-start(bf16[48,4096]{1,0:T(8,128)(2,1)S(1)} %get-tuple-element.101), channel_id=1, source_target_pairs={{0,1},{1,2},{4,5},{5,6},{8,9},{9,10},{12,13},{13,14},{16,17},{17,1... | collective-permute-start | bytes 1179656 | tf_op jit(solution)/shard_map/ppermute | solution.py:391
  80.8 0.7 collective-permute-start.22
  81.5 1.7 %collective-permute-done.24 = bf16[48,4096]{1,0:T(8,128)(2,1)S(1)} collective-permute-done((bf16[48,4096]{1,0:T(8,128)(2,1)S(1)}, bf16[48,4096]{1,0:T(8,128)(2,1)S(1)}, u32[]{:S(2)}, u32[]{:S(2)}) %collective-permute-start.24) | collective-permute-done | bytes 393248 | tf_op jit(solution)/shard_map/ppermute | solution.py:383
  83.5 0.7 collective-permute-start.27
  84.2 4.2 %collective-permute-done.13 = bf16[48,4096]{1,0:T(8,128)(2,1)S(1)} collective-permute-done((bf16[48,4096]{1,0:T(8,128)(2,1)S(1)}, bf16[48,4096]{1,0:T(8,128)(2,1)S(1)}, u32[]{:S(2)}, u32[]{:S(2)}) %collective-permute-start.13) | collective-permute-done | bytes 393248 | tf_op jit(solution)/shard_map/ppermute | solution.py:375
  88.4 4.0 %collective-permute-start.25 = (bf16[48,4096]{1,0:T(8,128)(2,1)S(1)}, bf16[48,4096]{1,0:T(8,128)(2,1)S(1)}, u32[]{:S(2)}, u32[]{:S(2)}) collective-permute-start(bf16[48,4096]{1,0:T(8,128)(2,1)S(1)} %get-tuple-element.103), channel_id=1, source_target_pairs={{0,1},{1,2},{4,5},{5,6},{8,9},{9,10},{12,13},{13,14},{16,17},{17,1... | collective-permute-start | bytes 1179656 | tf_op jit(solution)/shard_map/ppermute | solution.py:391
  92.4 1.6 %collective-permute-start.14 = (bf16[48,4096]{1,0:T(8,128)(2,1)S(1)}, bf16[48,4096]{1,0:T(8,128)(2,1)S(1)}, u32[]{:S(2)}, u32[]{:S(2)}) collective-permute-start(bf16[48,4096]{1,0:T(8,128)(2,1)S(1)} %get-tuple-element.89), channel_id=1, source_target_pairs={{0,8},{4,12},{8,0},{12,4},{1,9},{5,13},{9,1},{13,5},{2,10},{6,14},... | collective-permute-start | bytes 1179656 | tf_op jit(solution)/shard_map/ppermute | solution.py:375
  94.3 4.4 %collective-permute-start.17 = (bf16[48,4096]{1,0:T(8,128)(2,1)S(1)}, bf16[48,4096]{1,0:T(8,128)(2,1)S(1)}, u32[]{:S(2)}, u32[]{:S(2)}) collective-permute-start(bf16[48,4096]{1,0:T(8,128)(2,1)S(1)} %get-tuple-element.105), channel_id=1, source_target_pairs={{0,1},{1,2},{2,3},{4,5},{5,6},{6,7},{8,9},{9,10},{10,11},{12,13},{... | collective-permute-start | bytes 1179656 | tf_op jit(solution)/shard_map/ppermute | solution.py:391
  98.8 1.3 %collective-permute-start.19 = (bf16[48,4096]{1,0:T(8,128)(2,1)S(1)}, bf16[48,4096]{1,0:T(8,128)(2,1)S(1)}, u32[]{:S(2)}, u32[]{:S(2)}) collective-permute-start(bf16[48,4096]{1,0:T(8,128)(2,1)S(1)} %get-tuple-element.106), channel_id=1, source_target_pairs={{1,0},{2,1},{3,2},{5,4},{6,5},{7,6},{9,8},{10,9},{11,10},{13,12},{... | collective-permute-start | bytes 1179656 | tf_op jit(solution)/shard_map/ppermute | solution.py:391
  100.1 0.6 collective-permute-start.23
  100.7 1.1 collective-permute-done.25
  102.1 4.6 %collective-permute-start.26 = (bf16[48,4096]{1,0:T(8,128)(2,1)S(1)}, bf16[48,4096]{1,0:T(8,128)(2,1)S(1)}, u32[]{:S(2)}, u32[]{:S(2)}) collective-permute-start(bf16[48,4096]{1,0:T(8,128)(2,1)S(1)} %get-tuple-element.107), channel_id=1, source_target_pairs={{0,1},{1,2},{2,3},{4,5},{5,6},{6,7},{8,9},{9,10},{10,11},{12,13},{... | collective-permute-start | bytes 1179656 | tf_op jit(solution)/shard_map/ppermute | solution.py:391
  106.7 1.3 %collective-permute-start.28 = (bf16[48,4096]{1,0:T(8,128)(2,1)S(1)}, bf16[48,4096]{1,0:T(8,128)(2,1)S(1)}, u32[]{:S(2)}, u32[]{:S(2)}) collective-permute-start(bf16[48,4096]{1,0:T(8,128)(2,1)S(1)} %get-tuple-element.108), channel_id=1, source_target_pairs={{1,0},{2,1},{3,2},{5,4},{6,5},{7,6},{9,8},{10,9},{11,10},{13,12},{... | collective-permute-start | bytes 1179656 | tf_op jit(solution)/shard_map/ppermute | solution.py:391
  108.0 2.1 %collective-permute-done.17 = bf16[48,4096]{1,0:T(8,128)(2,1)S(1)} collective-permute-done((bf16[48,4096]{1,0:T(8,128)(2,1)S(1)}, bf16[48,4096]{1,0:T(8,128)(2,1)S(1)}, u32[]{:S(2)}, u32[]{:S(2)}) %collective-permute-start.17) | collective-permute-done | bytes 393248 | tf_op jit(solution)/shard_map/ppermute | solution.py:391
  110.4 2.4 %collective-permute-done.23 = bf16[48,4096]{1,0:T(8,128)(2,1)S(1)} collective-permute-done((bf16[48,4096]{1,0:T(8,128)(2,1)S(1)}, bf16[48,4096]{1,0:T(8,128)(2,1)S(1)}, u32[]{:S(2)}, u32[]{:S(2)}) %collective-permute-start.23) | collective-permute-done | bytes 393248 | tf_op jit(solution)/shard_map/ppermute | solution.py:375
  112.7 3.3 %collective-permute-done.26 = bf16[48,4096]{1,0:T(8,128)(2,1)S(1)} collective-permute-done((bf16[48,4096]{1,0:T(8,128)(2,1)S(1)}, bf16[48,4096]{1,0:T(8,128)(2,1)S(1)}, u32[]{:S(2)}, u32[]{:S(2)}) %collective-permute-start.26) | collective-permute-done | bytes 393248 | tf_op jit(solution)/shard_map/ppermute | solution.py:391
  116.0 1.5 %collective-permute-done.28 = bf16[48,4096]{1,0:T(8,128)(2,1)S(1)} collective-permute-done((bf16[48,4096]{1,0:T(8,128)(2,1)S(1)}, bf16[48,4096]{1,0:T(8,128)(2,1)S(1)}, u32[]{:S(2)}, u32[]{:S(2)}) %collective-permute-start.28) | collective-permute-done | bytes 393248 | tf_op jit(solution)/shard_map/ppermute | solution.py:391
  117.7 0.9 pad_maximum_fusion
  (51 shorter events, 3.3 us)
Async XLA Ops:
  0.0 33.7 %collective-permute-start.9 = (bf16[512,8192]{1,0:T(8,128)(2,1)}, bf16[512,8192]{1,0:T(8,128)(2,1)}, u32[]{:S(2)}, u32[]{:S(2)}) collective-permute-start(bf16[512,8192]{1,0:T(8,128)(2,1)} %refs_12_.3), channel_id=1, source_target_pairs={{0,4},{4,0},{8,12},{12,8},{1,5},{5,1},{9,13},{13,9},{2,6},{6,2},{1... | collective-permute-start | bytes 25165832 | tf_op jit(solution)/shard_map/ppermute | solution.py:281
  1.9 14.7 %collective-permute-start.1 = (bf16[576,128]{1,0:T(8,128)(2,1)S(1)}, bf16[576,128]{1,0:T(8,128)(2,1)S(1)}, u32[]{:S(2)}, u32[]{:S(2)}) collective-permute-start(bf16[576,128]{1,0:T(8,128)(2,1)S(1)} %get-tuple-element.55), channel_id=1, source_target_pairs={{0,2},{1,3},{2,0},{3,1},{4,6},{5,7},{6,4},{7,5},{8,10},{9,11},{10,... | collective-permute-start | bytes 442376 | tf_op jit(solution)/shard_map/ppermute | solution.py:259
  5.6 11.1 %collective-permute-start = (bf16[576,128]{1,0:T(8,128)(2,1)S(1)}, bf16[576,128]{1,0:T(8,128)(2,1)S(1)}, u32[]{:S(2)}, u32[]{:S(2)}) collective-permute-start(bf16[576,128]{1,0:T(8,128)(2,1)S(1)} %get-tuple-element.54), channel_id=1, source_target_pairs={{0,1},{1,2},{2,3},{3,0},{4,5},{5,6},{6,7},{7,4},{8,9},{9,10},{10,1... | collective-permute-start | bytes 442376 | tf_op jit(solution)/shard_map/ppermute | solution.py:259
  7.2 13.4 %collective-permute-start.2 = (bf16[576,128]{1,0:T(8,128)(2,1)S(1)}, bf16[576,128]{1,0:T(8,128)(2,1)S(1)}, u32[]{:S(2)}, u32[]{:S(2)}) collective-permute-start(bf16[576,128]{1,0:T(8,128)(2,1)S(1)} %get-tuple-element.56), channel_id=1, source_target_pairs={{0,3},{1,0},{2,1},{3,2},{4,7},{5,4},{6,5},{7,6},{8,11},{9,8},{10,9... | collective-permute-start | bytes 442376 | tf_op jit(solution)/shard_map/ppermute | solution.py:259
  16.7 10.7 %collective-permute-start.4 = (bf16[768,128]{1,0:T(8,128)(2,1)S(1)}, bf16[768,128]{1,0:T(8,128)(2,1)S(1)}, u32[]{:S(2)}, u32[]{:S(2)}) collective-permute-start(bf16[768,128]{1,0:T(8,128)(2,1)S(1)} %pad_maximum_fusion.2), channel_id=1, source_target_pairs={{0,16},{1,17},{2,18},{3,19},{4,20},{5,21},{6,22},{7,23},{8,24},{9,... | collective-permute-start | bytes 589832 | tf_op jit(solution)/shard_map/ppermute | solution.py:276
  20.6 9.6 %collective-permute-start.3 = (bf16[768,128]{1,0:T(8,128)(2,1)S(1)}, bf16[768,128]{1,0:T(8,128)(2,1)S(1)}, u32[]{:S(2)}, u32[]{:S(2)}) collective-permute-start(bf16[768,128]{1,0:T(8,128)(2,1)S(1)} %pad_maximum_fusion.1), channel_id=1, source_target_pairs={{0,16},{1,17},{2,18},{3,19},{4,20},{5,21},{6,22},{7,23},{8,24},{9,... | collective-permute-start | bytes 589832 | tf_op jit(solution)/shard_map/ppermute | solution.py:276
  21.9 18.3 %collective-permute-start.5 = (bf16[576,128]{1,0:T(8,128)(2,1)S(1)}, bf16[576,128]{1,0:T(8,128)(2,1)S(1)}, u32[]{:S(2)}, u32[]{:S(2)}) collective-permute-start(bf16[576,128]{1,0:T(8,128)(2,1)S(1)} %get-tuple-element.60), channel_id=1, source_target_pairs={{0,1},{1,2},{2,3},{3,0},{4,5},{5,6},{6,7},{7,4},{8,9},{9,10},{10,1... | collective-permute-start | bytes 442376 | tf_op jit(solution)/shard_map/ppermute | solution.py:259
  25.4 14.8 %collective-permute-start.6 = (bf16[576,128]{1,0:T(8,128)(2,1)S(1)}, bf16[576,128]{1,0:T(8,128)(2,1)S(1)}, u32[]{:S(2)}, u32[]{:S(2)}) collective-permute-start(bf16[576,128]{1,0:T(8,128)(2,1)S(1)} %get-tuple-element.62), channel_id=1, source_target_pairs={{0,2},{1,3},{2,0},{3,1},{4,6},{5,7},{6,4},{7,5},{8,10},{9,11},{10,... | collective-permute-start | bytes 442376 | tf_op jit(solution)/shard_map/ppermute | solution.py:259
  27.4 12.8 %collective-permute-start.7 = (bf16[576,128]{1,0:T(8,128)(2,1)S(1)}, bf16[576,128]{1,0:T(8,128)(2,1)S(1)}, u32[]{:S(2)}, u32[]{:S(2)}) collective-permute-start(bf16[576,128]{1,0:T(8,128)(2,1)S(1)} %get-tuple-element.64), channel_id=1, source_target_pairs={{0,3},{1,0},{2,1},{3,2},{4,7},{5,4},{6,5},{7,6},{8,11},{9,8},{10,9... | collective-permute-start | bytes 442376 | tf_op jit(solution)/shard_map/ppermute | solution.py:259
  33.7 3.5 %collective-permute-start.8 = (bf16[2,48,512]{2,1,0:T(8,128)(2,1)S(1)}, bf16[2,48,512]{2,1,0:T(8,128)(2,1)S(1)}, u32[]{:S(2)}, u32[]{:S(2)}) collective-permute-start(bf16[2,48,512]{2,1,0:T(8,128)(2,1)S(1)} %get-tuple-element.65), channel_id=1, source_target_pairs={{0,4},{4,0},{8,12},{12,8},{1,5},{5,1},{9,13},{13,9},{2,6},{6,2},{1... | collective-permute-start | bytes 294920 | tf_op jit(solution)/shard_map/ppermute | solution.py:330
  38.6 20.9 %collective-permute-start.11 = (bf16[48,4096]{1,0:T(8,128)(2,1)S(1)}, bf16[48,4096]{1,0:T(8,128)(2,1)S(1)}, u32[]{:S(2)}, u32[]{:S(2)}) collective-permute-start(bf16[48,4096]{1,0:T(8,128)(2,1)S(1)} %get-tuple-element.72), channel_id=1, source_target_pairs={{0,8},{4,12},{8,0},{12,4},{1,9},{5,13},{9,1},{13,5},{2,10},{6,14},... | collective-permute-start | bytes 1179656 | tf_op jit(solution)/shard_map/ppermute | solution.py:375
  46.1 3.3 %copy-start = (bf16[512,8192]{1,0:T(8,128)(2,1)}, bf16[512,8192]{1,0:T(8,128)(2,1)S(1)}, u32[]{:S(2)}) copy-start(bf16[512,8192]{1,0:T(8,128)(2,1)S(1)} %get-tuple-element.80.weight) | copy-start | bytes 25165828
  49.3 7.5 %collective-permute-start.10 = (bf16[2,144,512]{2,1,0:T(8,128)(2,1)S(1)}, bf16[2,144,512]{2,1,0:T(8,128)(2,1)S(1)}, u32[]{:S(2)}, u32[]{:S(2)}) collective-permute-start(bf16[2,144,512]{2,1,0:T(8,128)(2,1)S(1)} %get-tuple-element.78), channel_id=1, source_target_pairs={{0,4},{4,0},{8,12},{12,8},{1,5},{5,1},{9,13},{13,9},{2,6},{6,2},{1... | collective-permute-start | bytes 884744 | tf_op jit(solution)/shard_map/ppermute | solution.py:330
  49.5 15.7 %collective-permute-start.20 = (bf16[48,4096]{1,0:T(8,128)(2,1)S(1)}, bf16[48,4096]{1,0:T(8,128)(2,1)S(1)}, u32[]{:S(2)}, u32[]{:S(2)}) collective-permute-start(bf16[48,4096]{1,0:T(8,128)(2,1)S(1)} %get-tuple-element.73), channel_id=1, source_target_pairs={{0,8},{4,12},{8,0},{12,4},{1,9},{5,13},{9,1},{13,5},{2,10},{6,14},... | collective-permute-start | bytes 1179656 | tf_op jit(solution)/shard_map/ppermute | solution.py:375
  50.1 3.4 %copy-start.1 = (bf16[512,8192]{1,0:T(8,128)(2,1)S(1)}, bf16[512,8192]{1,0:T(8,128)(2,1)}, u32[]{:S(2)}) copy-start(bf16[512,8192]{1,0:T(8,128)(2,1)} %copy-done) | copy-start | bytes 25165828
  59.5 12.0 %collective-permute-start.12 = (bf16[48,4096]{1,0:T(8,128)(2,1)S(1)}, bf16[48,4096]{1,0:T(8,128)(2,1)S(1)}, u32[]{:S(2)}, u32[]{:S(2)}) collective-permute-start(bf16[48,4096]{1,0:T(8,128)(2,1)S(1)} %get-tuple-element.87), channel_id=1, source_target_pairs={{0,8},{4,12},{8,0},{12,4},{1,9},{5,13},{9,1},{13,5},{2,10},{6,14},... | collective-permute-start | bytes 1179656 | tf_op jit(solution)/shard_map/ppermute | solution.py:375
  61.2 13.5 %collective-permute-start.15 = (bf16[48,4096]{1,0:T(8,128)(2,1)S(1)}, bf16[48,4096]{1,0:T(8,128)(2,1)S(1)}, u32[]{:S(2)}, u32[]{:S(2)}) collective-permute-start(bf16[48,4096]{1,0:T(8,128)(2,1)S(1)} %add_convert_fusion.10), channel_id=1, source_target_pairs={{0,1},{3,2},{4,5},{7,6},{8,9},{11,10},{12,13},{15,14},{16,17},{19,... | collective-permute-start | bytes 1179656 | tf_op jit(solution)/shard_map/ppermute | solution.py:383
  65.2 15.6 %collective-permute-start.21 = (bf16[48,4096]{1,0:T(8,128)(2,1)S(1)}, bf16[48,4096]{1,0:T(8,128)(2,1)S(1)}, u32[]{:S(2)}, u32[]{:S(2)}) collective-permute-start(bf16[48,4096]{1,0:T(8,128)(2,1)S(1)} %get-tuple-element.96), channel_id=1, source_target_pairs={{0,8},{4,12},{8,0},{12,4},{1,9},{5,13},{9,1},{13,5},{2,10},{6,14},... | collective-permute-start | bytes 1179656 | tf_op jit(solution)/shard_map/ppermute | solution.py:375
  65.9 17.2 %collective-permute-start.24 = (bf16[48,4096]{1,0:T(8,128)(2,1)S(1)}, bf16[48,4096]{1,0:T(8,128)(2,1)S(1)}, u32[]{:S(2)}, u32[]{:S(2)}) collective-permute-start(bf16[48,4096]{1,0:T(8,128)(2,1)S(1)} %add_convert_fusion.3), channel_id=1, source_target_pairs={{0,1},{3,2},{4,5},{7,6},{8,9},{11,10},{12,13},{15,14},{16,17},{19,... | collective-permute-start | bytes 1179656 | tf_op jit(solution)/shard_map/ppermute | solution.py:383
  71.5 16.9 %collective-permute-start.13 = (bf16[48,4096]{1,0:T(8,128)(2,1)S(1)}, bf16[48,4096]{1,0:T(8,128)(2,1)S(1)}, u32[]{:S(2)}, u32[]{:S(2)}) collective-permute-start(bf16[48,4096]{1,0:T(8,128)(2,1)S(1)} %get-tuple-element.88), channel_id=1, source_target_pairs={{0,8},{4,12},{8,0},{12,4},{1,9},{5,13},{9,1},{13,5},{2,10},{6,14},... | collective-permute-start | bytes 1179656 | tf_op jit(solution)/shard_map/ppermute | solution.py:375
  75.1 17.4 %collective-permute-start.18 = (bf16[48,4096]{1,0:T(8,128)(2,1)S(1)}, bf16[48,4096]{1,0:T(8,128)(2,1)S(1)}, u32[]{:S(2)}, u32[]{:S(2)}) collective-permute-start(bf16[48,4096]{1,0:T(8,128)(2,1)S(1)} %fusion.1), channel_id=1, source_target_pairs={{2,1},{3,2},{6,5},{7,6},{10,9},{11,10},{14,13},{15,14},{18,17},{19... | collective-permute-start | bytes 1179656 | tf_op jit(solution)/shard_map/ppermute | solution.py:391
  75.8 18.2 %collective-permute-start.16 = (bf16[48,4096]{1,0:T(8,128)(2,1)S(1)}, bf16[48,4096]{1,0:T(8,128)(2,1)S(1)}, u32[]{:S(2)}, u32[]{:S(2)}) collective-permute-start(bf16[48,4096]{1,0:T(8,128)(2,1)S(1)} %get-tuple-element.101), channel_id=1, source_target_pairs={{0,1},{1,2},{4,5},{5,6},{8,9},{9,10},{12,13},{13,14},{16,17},{17,1... | collective-permute-start | bytes 1179656 | tf_op jit(solution)/shard_map/ppermute | solution.py:391
  80.8 18.0 %collective-permute-start.22 = (bf16[48,4096]{1,0:T(8,128)(2,1)S(1)}, bf16[48,4096]{1,0:T(8,128)(2,1)S(1)}, u32[]{:S(2)}, u32[]{:S(2)}) collective-permute-start(bf16[48,4096]{1,0:T(8,128)(2,1)S(1)} %get-tuple-element.97), channel_id=1, source_target_pairs={{0,8},{4,12},{8,0},{12,4},{1,9},{5,13},{9,1},{13,5},{2,10},{6,14},... | collective-permute-start | bytes 1179656 | tf_op jit(solution)/shard_map/ppermute | solution.py:375
  83.5 16.6 %collective-permute-start.27 = (bf16[48,4096]{1,0:T(8,128)(2,1)S(1)}, bf16[48,4096]{1,0:T(8,128)(2,1)S(1)}, u32[]{:S(2)}, u32[]{:S(2)}) collective-permute-start(bf16[48,4096]{1,0:T(8,128)(2,1)S(1)} %fusion.3), channel_id=1, source_target_pairs={{2,1},{3,2},{6,5},{7,6},{10,9},{11,10},{14,13},{15,14},{18,17},{19... | collective-permute-start | bytes 1179656 | tf_op jit(solution)/shard_map/ppermute | solution.py:391
  88.4 13.4 %collective-permute-start.25 = (bf16[48,4096]{1,0:T(8,128)(2,1)S(1)}, bf16[48,4096]{1,0:T(8,128)(2,1)S(1)}, u32[]{:S(2)}, u32[]{:S(2)}) collective-permute-start(bf16[48,4096]{1,0:T(8,128)(2,1)S(1)} %get-tuple-element.103), channel_id=1, source_target_pairs={{0,1},{1,2},{4,5},{5,6},{8,9},{9,10},{12,13},{13,14},{16,17},{17,1... | collective-permute-start | bytes 1179656 | tf_op jit(solution)/shard_map/ppermute | solution.py:391
  92.4 14.3 %collective-permute-start.14 = (bf16[48,4096]{1,0:T(8,128)(2,1)S(1)}, bf16[48,4096]{1,0:T(8,128)(2,1)S(1)}, u32[]{:S(2)}, u32[]{:S(2)}) collective-permute-start(bf16[48,4096]{1,0:T(8,128)(2,1)S(1)} %get-tuple-element.89), channel_id=1, source_target_pairs={{0,8},{4,12},{8,0},{12,4},{1,9},{5,13},{9,1},{13,5},{2,10},{6,14},... | collective-permute-start | bytes 1179656 | tf_op jit(solution)/shard_map/ppermute | solution.py:375
  94.3 15.8 %collective-permute-start.17 = (bf16[48,4096]{1,0:T(8,128)(2,1)S(1)}, bf16[48,4096]{1,0:T(8,128)(2,1)S(1)}, u32[]{:S(2)}, u32[]{:S(2)}) collective-permute-start(bf16[48,4096]{1,0:T(8,128)(2,1)S(1)} %get-tuple-element.105), channel_id=1, source_target_pairs={{0,1},{1,2},{2,3},{4,5},{5,6},{6,7},{8,9},{9,10},{10,11},{12,13},{... | collective-permute-start | bytes 1179656 | tf_op jit(solution)/shard_map/ppermute | solution.py:391
  98.8 11.4 %collective-permute-start.19 = (bf16[48,4096]{1,0:T(8,128)(2,1)S(1)}, bf16[48,4096]{1,0:T(8,128)(2,1)S(1)}, u32[]{:S(2)}, u32[]{:S(2)}) collective-permute-start(bf16[48,4096]{1,0:T(8,128)(2,1)S(1)} %get-tuple-element.106), channel_id=1, source_target_pairs={{1,0},{2,1},{3,2},{5,4},{6,5},{7,6},{9,8},{10,9},{11,10},{13,12},{... | collective-permute-start | bytes 1179656 | tf_op jit(solution)/shard_map/ppermute | solution.py:391
  100.1 12.7 %collective-permute-start.23 = (bf16[48,4096]{1,0:T(8,128)(2,1)S(1)}, bf16[48,4096]{1,0:T(8,128)(2,1)S(1)}, u32[]{:S(2)}, u32[]{:S(2)}) collective-permute-start(bf16[48,4096]{1,0:T(8,128)(2,1)S(1)} %get-tuple-element.98), channel_id=1, source_target_pairs={{0,8},{4,12},{8,0},{12,4},{1,9},{5,13},{9,1},{13,5},{2,10},{6,14},... | collective-permute-start | bytes 1179656 | tf_op jit(solution)/shard_map/ppermute | solution.py:375
  102.1 13.9 %collective-permute-start.26 = (bf16[48,4096]{1,0:T(8,128)(2,1)S(1)}, bf16[48,4096]{1,0:T(8,128)(2,1)S(1)}, u32[]{:S(2)}, u32[]{:S(2)}) collective-permute-start(bf16[48,4096]{1,0:T(8,128)(2,1)S(1)} %get-tuple-element.107), channel_id=1, source_target_pairs={{0,1},{1,2},{2,3},{4,5},{5,6},{6,7},{8,9},{9,10},{10,11},{12,13},{... | collective-permute-start | bytes 1179656 | tf_op jit(solution)/shard_map/ppermute | solution.py:391
  106.7 10.8 %collective-permute-start.28 = (bf16[48,4096]{1,0:T(8,128)(2,1)S(1)}, bf16[48,4096]{1,0:T(8,128)(2,1)S(1)}, u32[]{:S(2)}, u32[]{:S(2)}) collective-permute-start(bf16[48,4096]{1,0:T(8,128)(2,1)S(1)} %get-tuple-element.108), channel_id=1, source_target_pairs={{1,0},{2,1},{3,2},{5,4},{6,5},{7,6},{9,8},{10,9},{11,10},{13,12},{... | collective-permute-start | bytes 1179656 | tf_op jit(solution)/shard_map/ppermute | solution.py:391

commit v7 on v6

--- a/solution.py
+++ b/solution.py
@@ -20,7 +20,7 @@
 VMEM = pl.BlockSpec(memory_space=pltpu.VMEM)
 SMEM = pl.BlockSpec(memory_space=pltpu.SMEM)
 HBM = pl.BlockSpec(memory_space=pltpu.HBM)
-LIMIT = pltpu.CompilerParams(vmem_limit_bytes=14 << 20)
+LIMIT = pltpu.CompilerParams(vmem_limit_bytes=18 << 20)
 TILE = 1024
 FREE = pl.CostEstimate(flops=0, bytes_accessed=0, transcendentals=0)
 
@@ -192,25 +192,31 @@
     )(key_doc, *now, *before, *queries, *[in_hbm(w) for w in weights])
 
 
-def first_half_kernel(rows_here, weight, fetch, total, fetched, semaphore):
-    copy = pltpu.make_async_copy(fetch, fetched, semaphore)
-    copy.start()
+def first_half_kernel(rows_here, near, far, total, far_held, semaphores, *held):
+    copies = [pltpu.make_async_copy(far, far_held, semaphores.at[0])]
+    for near_held in held:
+        copies.insert(0, pltpu.make_async_copy(near, near_held, semaphores.at[1]))
+    for copy in copies:
+        copy.start()
+    for copy in copies[:-1]:
+        copy.wait()
+    weight = held[0] if held else near
     for n in range(0, total.shape[1], TILE):
         total[:, n : n + TILE] = jnp.dot(rows_here[...], weight[:, n : n + TILE], preferred_element_type=F32)
-    copy.wait()
-
-
-def first_half(rows_here, weight, fetch):
+    copies[-1].wait()
+
+
+def first_half(rows_here, near, far, near_held):
     return pl.pallas_call(
         first_half_kernel,
-        out_shape=[pltpu.VMEM((rows_here.shape[0], weight.shape[1]), F32), pltpu.VMEM(fetch.shape, fetch.dtype)],
-        in_specs=[VMEM, VMEM, HBM],
+        out_shape=[pltpu.VMEM((rows_here.shape[0], near.shape[1]), F32), pltpu.VMEM(far.shape, far.dtype)],
+        in_specs=[VMEM, VMEM if near_held else HBM, HBM],
         out_specs=[VMEM, VMEM],
-        scratch_shapes=[pltpu.SemaphoreType.DMA],
+        scratch_shapes=[pltpu.SemaphoreType.DMA((2,))] + [pltpu.VMEM(near.shape, near.dtype)] * (not near_held),
         compiler_params=LIMIT,
         cost_estimate=FREE,
         name="first_half",
-    )(rows_here, in_vmem(weight), in_hbm(fetch))
+    )(rows_here, in_vmem(near) if near_held else in_hbm(near), in_hbm(far))
 
 
 def project_kernel(*refs, terms, begun, share, halves):
@@ -270,14 +276,9 @@
         stages=stages,
     )
     loads = [packed[0]] + [around(packed[k], k) for k in range(1, slabs)]
-    behind = [loads[0]] + loads[:0:-1]
-    cuts = [behind[: slabs // 2], behind[slabs // 2 :]] if slabs > 1 else [behind]
-    cuts = [joined([a[: 2 * block] for a in cut]) for cut in cuts]
-    cuts = [lax.ppermute(cut, "srv", [(g, g + 1) for g in range(groups - 1)]) for cut in cuts]
     before = [
-        cut[n * 2 * block : (n + 1) * 2 * block] for cut in cuts for n in range(cut.shape[0] // (2 * block))
+        lax.ppermute(a[: 2 * block], "srv", [(g, g + 1) for g in range(groups - 1)]) for a in loads
     ]
-    before = [before[0]] + before[:0:-1]
     weight_sibling = lax.ppermute(out_weight, "head", siblings)
     stage_queries = [loads]
     for n in range(1, len(stages)):
@@ -302,7 +303,7 @@
             loads,
             before,
             arrived,
-            [out_weight],
+            [out_weight] if n == 0 else [],
             slabs=slabs,
             heads=heads,
             share=rows_at_once,
@@ -330,14 +331,16 @@
         theirs = lax.ppermute(send, "head", siblings)
         keep, theirs = (a.reshape(-1, a.shape[-1]) for a in (keep, theirs))
         if staged:
-            begun, far = first_half(keep, fetched[0], weight_sibling)
-            results = project([theirs], [far], [begun], share, halves)
+            near = fetched[0] if fetched else out_weight
+            begun, far = first_half(keep, near, weight_sibling, bool(fetched))
+            results = project([theirs], [far], [begun], share, 1 if n == 0 else halves)
         else:
             results = project([keep, theirs], [fetched[0], weight_sibling], [], share, halves)
+        cuts = len(results) // (len(pieces) * columns_x)
         for m in range(len(pieces)):
             partials.append(
                 [
-                    [results[(k * len(pieces) + m) * halves + half] for half in range(halves)]
+                    [results[(k * len(pieces) + m) * cuts + cut] for cut in range(cuts)]
                     for k in range(columns_x)
                 ]
             )
@@ -363,17 +366,23 @@
 
     sums = [[] for _ in range(halves)]
     crossed = [None] * halves
+    routes = [[(h, (h + 2 * k) % head_shards) for h in range(head_shards)] for k in range(columns_x)]
     arrived = [{1: None, -1: None} for _ in range(halves)]
     for t in range(slabs):
         for half in range(halves):
-            total = partials[t][0][half].astype(F32)
-            for k in range(1, columns_x):
-                route = [(h, (h + 2 * k) % head_shards) for h in range(head_shards)]
-                piece = partials[t][k][half]
+            whole = len(partials[t][0]) < halves
+            if whole and half == 0:
+                crossed = [[lax.ppermute(partials[t][k][0], "head", routes[k]) for k in range(1, columns_x)]] * halves
+            elif not whole:
+                pieces = [partials[t][k][half] for k in range(1, columns_x)]
                 if t:
-                    piece = after(piece, crossed[half])
-                crossed[half] = lax.ppermute(piece, "head", route)
-                total = total + crossed[half].astype(F32)
+                    pieces = [after(piece, *crossed[half]) for piece in pieces]
+                crossed[half] = [lax.ppermute(a, "head", r) for a, r in zip(pieces, routes[1:])]
+            total = 0.0
+            for piece in [partials[t][0][0 if whole else half]] + crossed[half]:
+                if whole:
+                    piece = piece[:, half * (piece.shape[1] // halves) : (half + 1) * (piece.shape[1] // halves)]
+                total = total + piece.astype(F32)
             sums[half].append(total.astype(BF16))
             if t == slabs - 1:
                 continue

time: 119 us -> 131 us (1.10)
  the two profiles are of different devices: /device:TPU:0 before, /device:TPU:12 now
where the time goes in v7:
time: 131 us
  waiting for transfers between devices  51.6 us (39%)
  starting transfers between devices  43.6 us (33%)
  Pallas kernels  24.9 us (19%)
  other arithmetic  9.92 us (8%)
    ppermute x8, starting transfers between devices, on_device(): lax.ppermute(sent[direction], 'wsh', [(i, i + direction) for i in found])  18.7 us
    ppermute x6, waiting for transfers between devices, around(): lax.ppermute(array, 'wsh', [(i, (i + k) % slabs) for i in range(slabs)])  17.9 us
    ppermute x8, waiting for transfers between devices, on_device(): lax.ppermute(sent[direction], 'wsh', [(i, i + direction) for i in found])  16 us
    ppermute x2, waiting for transfers between devices, on_device(): lax.ppermute(sent, 'wsh', [(i, i + 1) for i in up] + [(i, i - 1) for i in...  11.2 us
    ppermute x6, starting transfers between devices, around(): lax.ppermute(array, 'wsh', [(i, (i + k) % slabs) for i in range(slabs)])  10.1 us
    pallas_call x2, Pallas kernels, first_half(): pl.pallas_call(first_half_kernel, out_shape=[pltpu.VMEM((rows_here.shape[...  9.42 us
    pallas_call x2, Pallas kernels, attend(): pl.pallas_call(partial(attend_kernel, slabs=slabs, heads=heads, share=sha...  9.23 us
    convert_element_type x6, other arithmetic, message(): return (picked.astype(F32) + arrived.astype(F32)).astype(BF16)  5.72 us
  transfers between devices with their start and end apart: 30, of which 16 were waited for; matrix products, arithmetic and copies ran while one was open for 6% of the time, Pallas kernels for 18%

profile of v7, /device:TPU:12, one launch (start us, length us, event | category | flops | bytes accessed | tf_op | source)
XLA Modules:
  0.0 130.6 jit_solution(15493514155728979128)
XLA Ops:
  0.0 1.5 %pack.1 = (bf16[576,128]{1,0:T(8,128)(2,1)S(1)}, bf16[576,128]{1,0:T(8,128)(2,1)S(1)}, bf16[576,128]{1,0:T(8,128)(2,1)S(1)}, bf16[576,128]{1,0:T(8,128)(2,1)S(1)...) custom-call(bf16[192,2048]{1,0:T(8,128)(2,1)} %queries.1, ...), custom_call_target="tpu_custom_call" | custom-call | tf_op jit(solution)/shard_map/pack/pallas_call | solution.py:92
  1.5 1.6 %collective-permute-start = (bf16[576,128]{1,0:T(8,128)(2,1)S(1)}, bf16[576,128]{1,0:T(8,128)(2,1)S(1)}, u32[]{:S(2)}, u32[]{:S(2)}) collective-permute-start(bf16[576,128]{1,0:T(8,128)(2,1)S(1)} %get-tuple-element.51), channel_id=1, source_target_pairs={{0,1},{1,2},{2,3},{3,0},{4,5},{5,6},{6,7},{7,4},{8,9},{9,10},{10,1... | collective-permute-start | bytes 442376 | tf_op jit(solution)/shard_map/ppermute | solution.py:265
  3.1 1.2 collective-permute-start.1
  4.4 1.8 %collective-permute-start.2 = (bf16[576,128]{1,0:T(8,128)(2,1)S(1)}, bf16[576,128]{1,0:T(8,128)(2,1)S(1)}, u32[]{:S(2)}, u32[]{:S(2)}) collective-permute-start(bf16[576,128]{1,0:T(8,128)(2,1)S(1)} %get-tuple-element.53), channel_id=1, source_target_pairs={{0,3},{1,0},{2,1},{3,2},{4,7},{5,4},{6,5},{7,6},{8,11},{9,8},{10,9... | collective-permute-start | bytes 442376 | tf_op jit(solution)/shard_map/ppermute | solution.py:265
  6.2 1.3 collective-permute-start.3
  9.3 4.1 %collective-permute-done.refs_1_.refs_9_ = bf16[576,128]{1,0:T(8,128)(2,1)S(1)} collective-permute-done((bf16[576,128]{1,0:T(8,128)(2,1)S(1)}, bf16[576,128]{1,0:T(8,128)(2,1)S(1)}, u32[]{:S(2)}, u32[]{:S(2)}) %collective-permute-start) | collective-permute-done | bytes 147488 | tf_op jit(solution)/shard_map/ppermute | solution.py:265
  13.5 1.3 collective-permute-start.4
  14.7 1.6 %collective-permute-done.1.refs_2_.refs_10_ = bf16[576,128]{1,0:T(8,128)(2,1)S(1)} collective-permute-done((bf16[576,128]{1,0:T(8,128)(2,1)S(1)}, bf16[576,128]{1,0:T(8,128)(2,1)S(1)}, u32[]{:S(2)}, u32[]{:S(2)}) %collective-permute-start.1) | collective-permute-done | bytes 147488 | tf_op jit(solution)/shard_map/ppermute | solution.py:265
  16.4 1.3 collective-permute-start.5
  18.1 1.3 collective-permute-start.6
  20.0 3.1 %collective-permute-done.5.refs_6_ = bf16[384,128]{1,0:T(8,128)(2,1)S(1)} collective-permute-done((bf16[384,128]{1,0:T(8,128)(2,1)S(1)}, bf16[384,128]{1,0:T(8,128)(2,1)S(1)}, u32[]{:S(2)}, u32[]{:S(2)}) %collective-permute-start.5) | collective-permute-done | bytes 98336 | tf_op jit(solution)/shard_map/ppermute | solution.py:280
  23.1 1.9 %collective-permute-done.6.refs_7_ = bf16[384,128]{1,0:T(8,128)(2,1)S(1)} collective-permute-done((bf16[384,128]{1,0:T(8,128)(2,1)S(1)}, bf16[384,128]{1,0:T(8,128)(2,1)S(1)}, u32[]{:S(2)}, u32[]{:S(2)}) %collective-permute-start.6) | collective-permute-done | bytes 98336 | tf_op jit(solution)/shard_map/ppermute | solution.py:280
  25.0 3.4 %attend.2 = (bf16[2,48,512]{2,1,0:T(8,128)(2,1)S(1)}, bf16[2,48,512]{2,1,0:T(8,128)(2,1)S(1)}, bf16[512,8192]{1,0:T(8,128)(2,1)S(1)}) custom-call(f32[8,1,768]{2,1,0:T(1,128)S(1)} %reshape.55.key_doc, bf16[576,128]{1,0:T(8,128)(2,1)S(1)} %get-tuple-element.50.refs_0_.refs_8_, bf16[576,128]{1,0:T(8,128)(2,1)S(1)} %collective-permute-done.refs_1_.refs_9_, ...), custom_call_target="tpu_custom_call" | custom-call | flops 301989888 | tf_op jit(solution)/shard_map/attend/pallas_call | solution.py:180
  28.5 3.4 %first_half.2 = (f32[96,8192]{1,0:T(8,128)S(1)}, bf16[512,8192]{1,0:T(8,128)(2,1)S(1)}) custom-call(bf16[96,512]{1,0:T(8,128)(2,1)S(1)} %bitcast.19, bf16[512,8192]{1,0:T(8,128)(2,1)S(1)} %get-tuple-element.64.near, bf16[512,8192]{1,0:T(8,128)(2,1)} %collective-permute-done.11.far), custom_call_target="tpu_custom_call" | custom-call | tf_op jit(solution)/shard_map/first_half/pallas_call | solution.py:210
  31.9 1.5 %project.2 = (bf16[48,8192]{1,0:T(8,128)(2,1)S(1)}, bf16[48,8192]{1,0:T(8,128)(2,1)S(1)}) custom-call(bf16[96,512]{1,0:T(8,128)(2,1)S(1)} %bitcast.18, bf16[512,8192]{1,0:T(8,128)(2,1)S(1)} %get-tuple-element.65.refs_1_, f32[96,8192]{1,0:T(8,128)S(1)} %get-tuple-element.66.refs_2_), custom_call_target="tpu_custom_call" | custom-call | tf_op jit(solution)/shard_map/project/pallas_call | solution.py:239
  33.4 1.6 %collective-permute-start.13 = (bf16[48,8192]{1,0:T(8,128)(2,1)S(1)}, bf16[48,8192]{1,0:T(8,128)(2,1)S(1)}, u32[]{:S(2)}, u32[]{:S(2)}) collective-permute-start(bf16[48,8192]{1,0:T(8,128)(2,1)S(1)} %get-tuple-element.68), channel_id=1, source_target_pairs={{0,8},{4,12},{8,0},{12,4},{1,9},{5,13},{9,1},{13,5},{2,10},{6,14},... | collective-permute-start | bytes 2359304 | tf_op jit(solution)/shard_map/ppermute | solution.py:375
  35.7 2.6 %collective-permute-start.8 = (bf16[576,128]{1,0:T(8,128)(2,1)S(1)}, bf16[576,128]{1,0:T(8,128)(2,1)S(1)}, u32[]{:S(2)}, u32[]{:S(2)}) collective-permute-start(bf16[576,128]{1,0:T(8,128)(2,1)S(1)} %get-tuple-element.59), channel_id=1, source_target_pairs={{0,2},{1,3},{2,0},{3,1},{4,6},{5,7},{6,4},{7,5},{8,10},{9,11},{10,... | collective-permute-start | bytes 442376 | tf_op jit(solution)/shard_map/ppermute | solution.py:265
  38.3 2.0 %collective-permute-start.9 = (bf16[576,128]{1,0:T(8,128)(2,1)S(1)}, bf16[576,128]{1,0:T(8,128)(2,1)S(1)}, u32[]{:S(2)}, u32[]{:S(2)}) collective-permute-start(bf16[576,128]{1,0:T(8,128)(2,1)S(1)} %get-tuple-element.61), channel_id=1, source_target_pairs={{0,3},{1,0},{2,1},{3,2},{4,7},{5,4},{6,5},{7,6},{8,11},{9,8},{10,9... | collective-permute-start | bytes 442376 | tf_op jit(solution)/shard_map/ppermute | solution.py:265
  40.9 7.8 %collective-permute-done.8.refs_10_ = bf16[576,128]{1,0:T(8,128)(2,1)S(1)} collective-permute-done((bf16[576,128]{1,0:T(8,128)(2,1)S(1)}, bf16[576,128]{1,0:T(8,128)(2,1)S(1)}, u32[]{:S(2)}, u32[]{:S(2)}) %collective-permute-start.8) | collective-permute-done | bytes 147488 | tf_op jit(solution)/shard_map/ppermute | solution.py:265
  48.6 3.4 %collective-permute-done.9.refs_11_ = bf16[576,128]{1,0:T(8,128)(2,1)S(1)} collective-permute-done((bf16[576,128]{1,0:T(8,128)(2,1)S(1)}, bf16[576,128]{1,0:T(8,128)(2,1)S(1)}, u32[]{:S(2)}, u32[]{:S(2)}) %collective-permute-start.9) | collective-permute-done | bytes 147488 | tf_op jit(solution)/shard_map/ppermute | solution.py:265
  52.0 5.8 %attend.3 = (bf16[2,144,512]{2,1,0:T(8,128)(2,1)S(1)}, bf16[2,144,512]{2,1,0:T(8,128)(2,1)S(1)}) custom-call(f32[8,1,768]{2,1,0:T(1,128)S(1)} %reshape.55.key_doc, bf16[576,128]{1,0:T(8,128)(2,1)S(1)} %get-tuple-element.50.refs_0_.refs_8_, bf16[576,128]{1,0:T(8,128)(2,1)S(1)} %collective-permute-done.refs_1_.refs_9_, ...), custom_call_target="tpu_custom_call" | custom-call | flops 905969664 | tf_op jit(solution)/shard_map/attend/pallas_call | solution.py:180
  58.0 6.0 %first_half.3 = (f32[288,8192]{1,0:T(8,128)S(1)}, bf16[512,8192]{1,0:T(8,128)(2,1)S(1)}) custom-call(bf16[288,512]{1,0:T(8,128)(2,1)S(1)} %bitcast.17, bf16[512,8192]{1,0:T(8,128)(2,1)} %near.1, bf16[512,8192]{1,0:T(8,128)(2,1)} %collective-permute-done.11.far), custom_call_target="tpu_custom_call" | custom-call | tf_op jit(solution)/shard_map/first_half/pallas_call | solution.py:210
  64.0 3.3 %project.3 = (bf16[48,4096]{1,0:T(8,128)(2,1)S(1)}, bf16[48,4096]{1,0:T(8,128)(2,1)S(1)}, bf16[48,4096]{1,0:T(8,128)(2,1)S(1)}, bf16[48,4096]{1,0:T(8,128)(2,1)S...) custom-call(bf16[288,512]{1,0:T(8,128)(2,1)S(1)} %bitcast.16, ...), custom_call_target="tpu_custom_call" | custom-call | tf_op jit(solution)/shard_map/project/pallas_call | solution.py:239
  67.3 1.1 add_convert_fusion.10
  68.5 1.3 collective-permute-start.25
  70.4 1.3 collective-permute-start.17
  71.7 1.6 %collective-permute-start.14 = (bf16[48,4096]{1,0:T(8,128)(2,1)}, bf16[48,4096]{1,0:T(8,128)(2,1)S(1)}, u32[]{:S(2)}, u32[]{:S(2)}) collective-permute-start(bf16[48,4096]{1,0:T(8,128)(2,1)} %copy-done.1), channel_id=1, source_target_pairs={{0,8},{4,12},{8,0},{12,4},{1,9},{5,13},{9,1},{13,5},{2,10},{6,14},... | collective-permute-start | bytes 1179656 | tf_op jit(solution)/shard_map/ppermute | solution.py:380
  73.2 9.4 %collective-permute-done.25 = bf16[48,4096]{1,0:T(8,128)(2,1)} collective-permute-done((bf16[48,4096]{1,0:T(8,128)(2,1)}, bf16[48,4096]{1,0:T(8,128)(2,1)}, u32[]{:S(2)}, u32[]{:S(2)}) %collective-permute-start.25) | collective-permute-done | bytes 393248 | tf_op jit(solution)/shard_map/ppermute | solution.py:392
  82.6 1.4 %fusion.2 = (bf16[48,4096]{1,0:T(8,128)(2,1)S(1)}, bf16[48,4096]{1,0:T(8,128)(2,1)S(1)}) fusion(bf16[48,4096]{1,0:T(8,128)(2,1)} %collective-permute-done.25, bf16[48,4096]{1,0:T(8,128)(2,1)} %get-tuple-element.100, pred[]{:T(512)S(6)} %eq.7, bf16[48,4096]{1,0:T(8,128)(2,1)} %collective-permute-done.22, bf16[48,4096]{1,0:T(8,128)(2,1)S(1)} %get-tuple-element.94), kind=kLoop, calls=%fused_computation.6 | loop fusion | flops 1769472 | bytes 2359297 | tf_op jit(solution)/shard_map/convert_element_type | solution.py:365
  84.0 1.9 %collective-permute-start.26 = (bf16[48,4096]{1,0:T(8,128)(2,1)S(1)}, bf16[48,4096]{1,0:T(8,128)(2,1)S(1)}, u32[]{:S(2)}, u32[]{:S(2)}) collective-permute-start(bf16[48,4096]{1,0:T(8,128)(2,1)S(1)} %get-tuple-element.97), channel_id=1, source_target_pairs={{0,1},{1,2},{4,5},{5,6},{8,9},{9,10},{12,13},{13,14},{16,17},{17,1... | collective-permute-start | bytes 1179656 | tf_op jit(solution)/shard_map/ppermute | solution.py:400
  86.6 1.3 fusion.3
  87.8 1.3 collective-permute-start.28
  89.1 1.8 %collective-permute-done.17 = bf16[48,4096]{1,0:T(8,128)(2,1)S(1)} collective-permute-done((bf16[48,4096]{1,0:T(8,128)(2,1)}, bf16[48,4096]{1,0:T(8,128)(2,1)S(1)}, u32[]{:S(2)}, u32[]{:S(2)}) %collective-permute-start.17) | collective-permute-done | bytes 393248 | tf_op jit(solution)/shard_map/ppermute | solution.py:392
  90.9 1.2 fusion
  92.1 1.9 %collective-permute-start.18 = (bf16[48,4096]{1,0:T(8,128)(2,1)S(1)}, bf16[48,4096]{1,0:T(8,128)(2,1)S(1)}, u32[]{:S(2)}, u32[]{:S(2)}) collective-permute-start(bf16[48,4096]{1,0:T(8,128)(2,1)S(1)} %get-tuple-element.95), channel_id=1, source_target_pairs={{0,1},{1,2},{4,5},{5,6},{8,9},{9,10},{12,13},{13,14},{16,17},{17,1... | collective-permute-start | bytes 1179656 | tf_op jit(solution)/shard_map/ppermute | solution.py:400
  94.1 1.4 %collective-permute-start.15 = (bf16[48,4096]{1,0:T(8,128)(2,1)S(1)}, bf16[48,4096]{1,0:T(8,128)(2,1)S(1)}, u32[]{:S(2)}, u32[]{:S(2)}) collective-permute-start(bf16[48,4096]{1,0:T(8,128)(2,1)S(1)} %get-tuple-element.82), channel_id=1, source_target_pairs={{0,8},{4,12},{8,0},{12,4},{1,9},{5,13},{9,1},{13,5},{2,10},{6,14},... | collective-permute-start | bytes 1179656 | tf_op jit(solution)/shard_map/ppermute | solution.py:380
  95.5 1.1 fusion.1
  96.6 2.7 %collective-permute-done.26 = bf16[48,4096]{1,0:T(8,128)(2,1)S(1)} collective-permute-done((bf16[48,4096]{1,0:T(8,128)(2,1)S(1)}, bf16[48,4096]{1,0:T(8,128)(2,1)S(1)}, u32[]{:S(2)}, u32[]{:S(2)}) %collective-permute-start.26) | collective-permute-done | bytes 393248 | tf_op jit(solution)/shard_map/ppermute | solution.py:400
  99.4 1.3 collective-permute-start.20
  101.0 3.4 %collective-permute-start.29 = (bf16[48,4096]{1,0:T(8,128)(2,1)S(1)}, bf16[48,4096]{1,0:T(8,128)(2,1)S(1)}, u32[]{:S(2)}, u32[]{:S(2)}) collective-permute-start(bf16[48,4096]{1,0:T(8,128)(2,1)S(1)} %get-tuple-element.104), channel_id=1, source_target_pairs={{1,0},{2,1},{3,2},{5,4},{6,5},{7,6},{9,8},{10,9},{11,10},{13,12},{... | collective-permute-start | bytes 1179656 | tf_op jit(solution)/shard_map/ppermute | solution.py:400
  104.4 3.0 %collective-permute-start.27 = (bf16[48,4096]{1,0:T(8,128)(2,1)S(1)}, bf16[48,4096]{1,0:T(8,128)(2,1)S(1)}, u32[]{:S(2)}, u32[]{:S(2)}) collective-permute-start(bf16[48,4096]{1,0:T(8,128)(2,1)S(1)} %get-tuple-element.103), channel_id=1, source_target_pairs={{0,1},{1,2},{2,3},{4,5},{5,6},{6,7},{8,9},{9,10},{10,11},{12,13},{... | collective-permute-start | bytes 1179656 | tf_op jit(solution)/shard_map/ppermute | solution.py:400
  108.1 5.2 %collective-permute-done.20 = bf16[48,4096]{1,0:T(8,128)(2,1)S(1)} collective-permute-done((bf16[48,4096]{1,0:T(8,128)(2,1)S(1)}, bf16[48,4096]{1,0:T(8,128)(2,1)S(1)}, u32[]{:S(2)}, u32[]{:S(2)}) %collective-permute-start.20) | collective-permute-done | bytes 393248 | tf_op jit(solution)/shard_map/ppermute | solution.py:400
  113.6 1.9 %collective-permute-start.21 = (bf16[48,4096]{1,0:T(8,128)(2,1)S(1)}, bf16[48,4096]{1,0:T(8,128)(2,1)S(1)}, u32[]{:S(2)}, u32[]{:S(2)}) collective-permute-start(bf16[48,4096]{1,0:T(8,128)(2,1)S(1)} %get-tuple-element.102), channel_id=1, source_target_pairs={{1,0},{2,1},{3,2},{5,4},{6,5},{7,6},{9,8},{10,9},{11,10},{13,12},{... | collective-permute-start | bytes 1179656 | tf_op jit(solution)/shard_map/ppermute | solution.py:400
  115.6 3.9 %collective-permute-start.19 = (bf16[48,4096]{1,0:T(8,128)(2,1)S(1)}, bf16[48,4096]{1,0:T(8,128)(2,1)S(1)}, u32[]{:S(2)}, u32[]{:S(2)}) collective-permute-start(bf16[48,4096]{1,0:T(8,128)(2,1)S(1)} %get-tuple-element.101), channel_id=1, source_target_pairs={{0,1},{1,2},{2,3},{4,5},{5,6},{6,7},{8,9},{9,10},{10,11},{12,13},{... | collective-permute-start | bytes 1179656 | tf_op jit(solution)/shard_map/ppermute | solution.py:400
  119.5 2.2 %collective-permute-done.29 = bf16[48,4096]{1,0:T(8,128)(2,1)S(1)} collective-permute-done((bf16[48,4096]{1,0:T(8,128)(2,1)S(1)}, bf16[48,4096]{1,0:T(8,128)(2,1)S(1)}, u32[]{:S(2)}, u32[]{:S(2)}) %collective-permute-start.29) | collective-permute-done | bytes 393248 | tf_op jit(solution)/shard_map/ppermute | solution.py:400
  122.5 5.9 %collective-permute-done.21 = bf16[48,4096]{1,0:T(8,128)(2,1)S(1)} collective-permute-done((bf16[48,4096]{1,0:T(8,128)(2,1)S(1)}, bf16[48,4096]{1,0:T(8,128)(2,1)S(1)}, u32[]{:S(2)}, u32[]{:S(2)}) %collective-permute-start.21) | collective-permute-done | bytes 393248 | tf_op jit(solution)/shard_map/ppermute | solution.py:400
  128.4 1.1 collective-permute-done.16
  129.7 0.9 pad_maximum_fusion
  (48 shorter events, 7.8 us)
Async XLA Ops:
  0.0 28.5 %collective-permute-start.11 = (bf16[512,8192]{1,0:T(8,128)(2,1)}, bf16[512,8192]{1,0:T(8,128)(2,1)}, u32[]{:S(2)}, u32[]{:S(2)}) collective-permute-start(bf16[512,8192]{1,0:T(8,128)(2,1)} %near.1), channel_id=1, source_target_pairs={{0,4},{4,0},{8,12},{12,8},{1,5},{5,1},{9,13},{13,9},{2,6},{6,2},{1... | collective-permute-start | bytes 25165832 | tf_op jit(solution)/shard_map/ppermute | solution.py:282
  1.5 12.0 %collective-permute-start = (bf16[576,128]{1,0:T(8,128)(2,1)S(1)}, bf16[576,128]{1,0:T(8,128)(2,1)S(1)}, u32[]{:S(2)}, u32[]{:S(2)}) collective-permute-start(bf16[576,128]{1,0:T(8,128)(2,1)S(1)} %get-tuple-element.51), channel_id=1, source_target_pairs={{0,1},{1,2},{2,3},{3,0},{4,5},{5,6},{6,7},{7,4},{8,9},{9,10},{10,1... | collective-permute-start | bytes 442376 | tf_op jit(solution)/shard_map/ppermute | solution.py:265
  3.1 13.3 %collective-permute-start.1 = (bf16[576,128]{1,0:T(8,128)(2,1)S(1)}, bf16[576,128]{1,0:T(8,128)(2,1)S(1)}, u32[]{:S(2)}, u32[]{:S(2)}) collective-permute-start(bf16[576,128]{1,0:T(8,128)(2,1)S(1)} %get-tuple-element.52), channel_id=1, source_target_pairs={{0,2},{1,3},{2,0},{3,1},{4,6},{5,7},{6,4},{7,5},{8,10},{9,11},{10,... | collective-permute-start | bytes 442376 | tf_op jit(solution)/shard_map/ppermute | solution.py:265
  4.4 13.8 %collective-permute-start.2 = (bf16[576,128]{1,0:T(8,128)(2,1)S(1)}, bf16[576,128]{1,0:T(8,128)(2,1)S(1)}, u32[]{:S(2)}, u32[]{:S(2)}) collective-permute-start(bf16[576,128]{1,0:T(8,128)(2,1)S(1)} %get-tuple-element.53), channel_id=1, source_target_pairs={{0,3},{1,0},{2,1},{3,2},{4,7},{5,4},{6,5},{7,6},{8,11},{9,8},{10,9... | collective-permute-start | bytes 442376 | tf_op jit(solution)/shard_map/ppermute | solution.py:265
  6.2 13.4 %collective-permute-start.3 = (bf16[384,128]{1,0:T(8,128)(2,1)S(1)}, bf16[384,128]{1,0:T(8,128)(2,1)S(1)}, u32[]{:S(2)}, u32[]{:S(2)}) collective-permute-start(bf16[384,128]{1,0:T(8,128)(2,1)S(1)} %slice.52), channel_id=1, source_target_pairs={{0,16},{1,17},{2,18},{3,19},{4,20},{5,21},{6,22},{7,23},{8,24},{9,... | collective-permute-start | bytes 294920 | tf_op jit(solution)/shard_map/ppermute | solution.py:280
  13.5 6.5 %collective-permute-start.4 = (bf16[384,128]{1,0:T(8,128)(2,1)S(1)}, bf16[384,128]{1,0:T(8,128)(2,1)S(1)}, u32[]{:S(2)}, u32[]{:S(2)}) collective-permute-start(bf16[384,128]{1,0:T(8,128)(2,1)S(1)} %slice.60), channel_id=1, source_target_pairs={{0,16},{1,17},{2,18},{3,19},{4,20},{5,21},{6,22},{7,23},{8,24},{9,... | collective-permute-start | bytes 294920 | tf_op jit(solution)/shard_map/ppermute | solution.py:280
  16.4 6.7 %collective-permute-start.5 = (bf16[384,128]{1,0:T(8,128)(2,1)S(1)}, bf16[384,128]{1,0:T(8,128)(2,1)S(1)}, u32[]{:S(2)}, u32[]{:S(2)}) collective-permute-start(bf16[384,128]{1,0:T(8,128)(2,1)S(1)} %slice.61), channel_id=1, source_target_pairs={{0,16},{1,17},{2,18},{3,19},{4,20},{5,21},{6,22},{7,23},{8,24},{9,... | collective-permute-start | bytes 294920 | tf_op jit(solution)/shard_map/ppermute | solution.py:280
  18.1 6.8 %collective-permute-start.6 = (bf16[384,128]{1,0:T(8,128)(2,1)S(1)}, bf16[384,128]{1,0:T(8,128)(2,1)S(1)}, u32[]{:S(2)}, u32[]{:S(2)}) collective-permute-start(bf16[384,128]{1,0:T(8,128)(2,1)S(1)} %slice.62), channel_id=1, source_target_pairs={{0,16},{1,17},{2,18},{3,19},{4,20},{5,21},{6,22},{7,23},{8,24},{9,... | collective-permute-start | bytes 294920 | tf_op jit(solution)/shard_map/ppermute | solution.py:280
  28.4 3.5 %collective-permute-start.10 = (bf16[2,48,512]{2,1,0:T(8,128)(2,1)S(1)}, bf16[2,48,512]{2,1,0:T(8,128)(2,1)S(1)}, u32[]{:S(2)}, u32[]{:S(2)}) collective-permute-start(bf16[2,48,512]{2,1,0:T(8,128)(2,1)S(1)} %get-tuple-element.62), channel_id=1, source_target_pairs={{0,4},{4,0},{8,12},{12,8},{1,5},{5,1},{9,13},{13,9},{2,6},{6,2},{1... | collective-permute-start | bytes 294920 | tf_op jit(solution)/shard_map/ppermute | solution.py:331
  33.4 34.0 %collective-permute-start.13 = (bf16[48,8192]{1,0:T(8,128)(2,1)S(1)}, bf16[48,8192]{1,0:T(8,128)(2,1)S(1)}, u32[]{:S(2)}, u32[]{:S(2)}) collective-permute-start(bf16[48,8192]{1,0:T(8,128)(2,1)S(1)} %get-tuple-element.68), channel_id=1, source_target_pairs={{0,8},{4,12},{8,0},{12,4},{1,9},{5,13},{9,1},{13,5},{2,10},{6,14},... | collective-permute-start | bytes 2359304 | tf_op jit(solution)/shard_map/ppermute | solution.py:375
  34.9 6.0 %collective-permute-start.7 = (bf16[576,128]{1,0:T(8,128)(2,1)S(1)}, bf16[576,128]{1,0:T(8,128)(2,1)S(1)}, u32[]{:S(2)}, u32[]{:S(2)}) collective-permute-start(bf16[576,128]{1,0:T(8,128)(2,1)S(1)} %get-tuple-element.57), channel_id=1, source_target_pairs={{0,1},{1,2},{2,3},{3,0},{4,5},{5,6},{6,7},{7,4},{8,9},{9,10},{10,1... | collective-permute-start | bytes 442376 | tf_op jit(solution)/shard_map/ppermute | solution.py:265
  35.7 13.0 %collective-permute-start.8 = (bf16[576,128]{1,0:T(8,128)(2,1)S(1)}, bf16[576,128]{1,0:T(8,128)(2,1)S(1)}, u32[]{:S(2)}, u32[]{:S(2)}) collective-permute-start(bf16[576,128]{1,0:T(8,128)(2,1)S(1)} %get-tuple-element.59), channel_id=1, source_target_pairs={{0,2},{1,3},{2,0},{3,1},{4,6},{5,7},{6,4},{7,5},{8,10},{9,11},{10,... | collective-permute-start | bytes 442376 | tf_op jit(solution)/shard_map/ppermute | solution.py:265
  38.3 13.7 %collective-permute-start.9 = (bf16[576,128]{1,0:T(8,128)(2,1)S(1)}, bf16[576,128]{1,0:T(8,128)(2,1)S(1)}, u32[]{:S(2)}, u32[]{:S(2)}) collective-permute-start(bf16[576,128]{1,0:T(8,128)(2,1)S(1)} %get-tuple-element.61), channel_id=1, source_target_pairs={{0,3},{1,0},{2,1},{3,2},{4,7},{5,4},{6,5},{7,6},{8,11},{9,8},{10,9... | collective-permute-start | bytes 442376 | tf_op jit(solution)/shard_map/ppermute | solution.py:265
  57.9 6.1 %collective-permute-start.12 = (bf16[2,144,512]{2,1,0:T(8,128)(2,1)S(1)}, bf16[2,144,512]{2,1,0:T(8,128)(2,1)S(1)}, u32[]{:S(2)}, u32[]{:S(2)}) collective-permute-start(bf16[2,144,512]{2,1,0:T(8,128)(2,1)S(1)} %get-tuple-element.73), channel_id=1, source_target_pairs={{0,4},{4,0},{8,12},{12,8},{1,5},{5,1},{9,13},{13,9},{2,6},{6,2},{1... | collective-permute-start | bytes 884744 | tf_op jit(solution)/shard_map/ppermute | solution.py:331
  67.3 1.2 copy-start
  67.3 1.2 copy-start.1
  68.5 14.1 %collective-permute-start.25 = (bf16[48,4096]{1,0:T(8,128)(2,1)}, bf16[48,4096]{1,0:T(8,128)(2,1)}, u32[]{:S(2)}, u32[]{:S(2)}) collective-permute-start(bf16[48,4096]{1,0:T(8,128)(2,1)} %get-tuple-element.100), channel_id=1, source_target_pairs={{0,1},{3,2},{4,5},{7,6},{8,9},{11,10},{12,13},{15,14},{16,17},{19,... | collective-permute-start | bytes 1179656 | tf_op jit(solution)/shard_map/ppermute | solution.py:392
  69.8 12.8 %collective-permute-start.22 = (bf16[48,4096]{1,0:T(8,128)(2,1)}, bf16[48,4096]{1,0:T(8,128)(2,1)}, u32[]{:S(2)}, u32[]{:S(2)}) collective-permute-start(bf16[48,4096]{1,0:T(8,128)(2,1)} %get-tuple-element.90), channel_id=1, source_target_pairs={{0,8},{4,12},{8,0},{12,4},{1,9},{5,13},{9,1},{13,5},{2,10},{6,14},... | collective-permute-start | bytes 1179656 | tf_op jit(solution)/shard_map/ppermute | solution.py:380
  70.4 20.5 %collective-permute-start.17 = (bf16[48,4096]{1,0:T(8,128)(2,1)}, bf16[48,4096]{1,0:T(8,128)(2,1)S(1)}, u32[]{:S(2)}, u32[]{:S(2)}) collective-permute-start(bf16[48,4096]{1,0:T(8,128)(2,1)} %get-tuple-element.99), channel_id=1, source_target_pairs={{0,1},{3,2},{4,5},{7,6},{8,9},{11,10},{12,13},{15,14},{16,17},{19,... | collective-permute-start | bytes 1179656 | tf_op jit(solution)/shard_map/ppermute | solution.py:392
  71.7 19.3 %collective-permute-start.14 = (bf16[48,4096]{1,0:T(8,128)(2,1)}, bf16[48,4096]{1,0:T(8,128)(2,1)S(1)}, u32[]{:S(2)}, u32[]{:S(2)}) collective-permute-start(bf16[48,4096]{1,0:T(8,128)(2,1)} %copy-done.1), channel_id=1, source_target_pairs={{0,8},{4,12},{8,0},{12,4},{1,9},{5,13},{9,1},{13,5},{2,10},{6,14},... | collective-permute-start | bytes 1179656 | tf_op jit(solution)/shard_map/ppermute | solution.py:380
  84.0 15.3 %collective-permute-start.26 = (bf16[48,4096]{1,0:T(8,128)(2,1)S(1)}, bf16[48,4096]{1,0:T(8,128)(2,1)S(1)}, u32[]{:S(2)}, u32[]{:S(2)}) collective-permute-start(bf16[48,4096]{1,0:T(8,128)(2,1)S(1)} %get-tuple-element.97), channel_id=1, source_target_pairs={{0,1},{1,2},{4,5},{5,6},{8,9},{9,10},{12,13},{13,14},{16,17},{17,1... | collective-permute-start | bytes 1179656 | tf_op jit(solution)/shard_map/ppermute | solution.py:400
  86.0 14.7 %collective-permute-start.23 = (bf16[48,4096]{1,0:T(8,128)(2,1)}, bf16[48,4096]{1,0:T(8,128)(2,1)S(1)}, u32[]{:S(2)}, u32[]{:S(2)}) collective-permute-start(bf16[48,4096]{1,0:T(8,128)(2,1)} %copy-done), channel_id=1, source_target_pairs={{0,8},{4,12},{8,0},{12,4},{1,9},{5,13},{9,1},{13,5},{2,10},{6,14},... | collective-permute-start | bytes 1179656 | tf_op jit(solution)/shard_map/ppermute | solution.py:380
  87.8 12.8 %collective-permute-start.28 = (bf16[48,4096]{1,0:T(8,128)(2,1)S(1)}, bf16[48,4096]{1,0:T(8,128)(2,1)S(1)}, u32[]{:S(2)}, u32[]{:S(2)}) collective-permute-start(bf16[48,4096]{1,0:T(8,128)(2,1)S(1)} %fusion.3), channel_id=1, source_target_pairs={{2,1},{3,2},{6,5},{7,6},{10,9},{11,10},{14,13},{15,14},{18,17},{19... | collective-permute-start | bytes 1179656 | tf_op jit(solution)/shard_map/ppermute | solution.py:400
  92.1 15.4 %collective-permute-start.18 = (bf16[48,4096]{1,0:T(8,128)(2,1)S(1)}, bf16[48,4096]{1,0:T(8,128)(2,1)S(1)}, u32[]{:S(2)}, u32[]{:S(2)}) collective-permute-start(bf16[48,4096]{1,0:T(8,128)(2,1)S(1)} %get-tuple-element.95), channel_id=1, source_target_pairs={{0,1},{1,2},{4,5},{5,6},{8,9},{9,10},{12,13},{13,14},{16,17},{17,1... | collective-permute-start | bytes 1179656 | tf_op jit(solution)/shard_map/ppermute | solution.py:400
  94.1 14.0 %collective-permute-start.15 = (bf16[48,4096]{1,0:T(8,128)(2,1)S(1)}, bf16[48,4096]{1,0:T(8,128)(2,1)S(1)}, u32[]{:S(2)}, u32[]{:S(2)}) collective-permute-start(bf16[48,4096]{1,0:T(8,128)(2,1)S(1)} %get-tuple-element.82), channel_id=1, source_target_pairs={{0,8},{4,12},{8,0},{12,4},{1,9},{5,13},{9,1},{13,5},{2,10},{6,14},... | collective-permute-start | bytes 1179656 | tf_op jit(solution)/shard_map/ppermute | solution.py:380
  99.4 13.9 %collective-permute-start.20 = (bf16[48,4096]{1,0:T(8,128)(2,1)S(1)}, bf16[48,4096]{1,0:T(8,128)(2,1)S(1)}, u32[]{:S(2)}, u32[]{:S(2)}) collective-permute-start(bf16[48,4096]{1,0:T(8,128)(2,1)S(1)} %fusion.1), channel_id=1, source_target_pairs={{2,1},{3,2},{6,5},{7,6},{10,9},{11,10},{14,13},{15,14},{18,17},{19... | collective-permute-start | bytes 1179656 | tf_op jit(solution)/shard_map/ppermute | solution.py:400
  101.0 20.7 %collective-permute-start.29 = (bf16[48,4096]{1,0:T(8,128)(2,1)S(1)}, bf16[48,4096]{1,0:T(8,128)(2,1)S(1)}, u32[]{:S(2)}, u32[]{:S(2)}) collective-permute-start(bf16[48,4096]{1,0:T(8,128)(2,1)S(1)} %get-tuple-element.104), channel_id=1, source_target_pairs={{1,0},{2,1},{3,2},{5,4},{6,5},{7,6},{9,8},{10,9},{11,10},{13,12},{... | collective-permute-start | bytes 1179656 | tf_op jit(solution)/shard_map/ppermute | solution.py:400
  104.4 17.8 %collective-permute-start.27 = (bf16[48,4096]{1,0:T(8,128)(2,1)S(1)}, bf16[48,4096]{1,0:T(8,128)(2,1)S(1)}, u32[]{:S(2)}, u32[]{:S(2)}) collective-permute-start(bf16[48,4096]{1,0:T(8,128)(2,1)S(1)} %get-tuple-element.103), channel_id=1, source_target_pairs={{0,1},{1,2},{2,3},{4,5},{5,6},{6,7},{8,9},{9,10},{10,11},{12,13},{... | collective-permute-start | bytes 1179656 | tf_op jit(solution)/shard_map/ppermute | solution.py:400
  107.5 14.8 %collective-permute-start.24 = (bf16[48,4096]{1,0:T(8,128)(2,1)S(1)}, bf16[48,4096]{1,0:T(8,128)(2,1)S(1)}, u32[]{:S(2)}, u32[]{:S(2)}) collective-permute-start(bf16[48,4096]{1,0:T(8,128)(2,1)S(1)} %get-tuple-element.92), channel_id=1, source_target_pairs={{0,8},{4,12},{8,0},{12,4},{1,9},{5,13},{9,1},{13,5},{2,10},{6,14},... | collective-permute-start | bytes 1179656 | tf_op jit(solution)/shard_map/ppermute | solution.py:380
  113.6 14.7 %collective-permute-start.21 = (bf16[48,4096]{1,0:T(8,128)(2,1)S(1)}, bf16[48,4096]{1,0:T(8,128)(2,1)S(1)}, u32[]{:S(2)}, u32[]{:S(2)}) collective-permute-start(bf16[48,4096]{1,0:T(8,128)(2,1)S(1)} %get-tuple-element.102), channel_id=1, source_target_pairs={{1,0},{2,1},{3,2},{5,4},{6,5},{7,6},{9,8},{10,9},{11,10},{13,12},{... | collective-permute-start | bytes 1179656 | tf_op jit(solution)/shard_map/ppermute | solution.py:400
  115.6 12.8 %collective-permute-start.19 = (bf16[48,4096]{1,0:T(8,128)(2,1)S(1)}, bf16[48,4096]{1,0:T(8,128)(2,1)S(1)}, u32[]{:S(2)}, u32[]{:S(2)}) collective-permute-start(bf16[48,4096]{1,0:T(8,128)(2,1)S(1)} %get-tuple-element.101), channel_id=1, source_target_pairs={{0,1},{1,2},{2,3},{4,5},{5,6},{6,7},{8,9},{9,10},{10,11},{12,13},{... | collective-permute-start | bytes 1179656 | tf_op jit(solution)/shard_map/ppermute | solution.py:400
  121.7 7.8 %collective-permute-start.16 = (bf16[48,4096]{1,0:T(8,128)(2,1)S(1)}, bf16[48,4096]{1,0:T(8,128)(2,1)S(1)}, u32[]{:S(2)}, u32[]{:S(2)}) collective-permute-start(bf16[48,4096]{1,0:T(8,128)(2,1)S(1)} %get-tuple-element.83), channel_id=1, source_target_pairs={{0,8},{4,12},{8,0},{12,4},{1,9},{5,13},{9,1},{13,5},{2,10},{6,14},... | collective-permute-start | bytes 1179656 | tf_op jit(solution)/shard_map/ppermute | solution.py:380

commit v8 on v7

--- a/solution.py
+++ b/solution.py
@@ -276,9 +276,13 @@
         stages=stages,
     )
     loads = [packed[0]] + [around(packed[k], k) for k in range(1, slabs)]
-    before = [
-        lax.ppermute(a[: 2 * block], "srv", [(g, g + 1) for g in range(groups - 1)]) for a in loads
-    ]
+    cuts = [loads[:1], loads[1:2], loads[2:]]
+    before = []
+    for cut in cuts:
+        if cut:
+            kv = joined([a[: 2 * block] for a in cut])
+            kv = lax.ppermute(kv, "srv", [(g, g + 1) for g in range(groups - 1)])
+            before += [kv[n * 2 * block : (n + 1) * 2 * block] for n in range(len(cut))]
     weight_sibling = lax.ppermute(out_weight, "head", siblings)
     stage_queries = [loads]
     for n in range(1, len(stages)):
@@ -333,14 +337,13 @@
         if staged:
             near = fetched[0] if fetched else out_weight
             begun, far = first_half(keep, near, weight_sibling, bool(fetched))
-            results = project([theirs], [far], [begun], share, 1 if n == 0 else halves)
+            results = project([theirs], [far], [begun], share, halves)
         else:
             results = project([keep, theirs], [fetched[0], weight_sibling], [], share, halves)
-        cuts = len(results) // (len(pieces) * columns_x)
         for m in range(len(pieces)):
             partials.append(
                 [
-                    [results[(k * len(pieces) + m) * cuts + cut] for cut in range(cuts)]
+                    [results[(k * len(pieces) + m) * halves + half] for half in range(halves)]
                     for k in range(columns_x)
                 ]
             )
@@ -370,19 +373,11 @@
     arrived = [{1: None, -1: None} for _ in range(halves)]
     for t in range(slabs):
         for half in range(halves):
-            whole = len(partials[t][0]) < halves
-            if whole and half == 0:
-                crossed = [[lax.ppermute(partials[t][k][0], "head", routes[k]) for k in range(1, columns_x)]] * halves
-            elif not whole:
-                pieces = [partials[t][k][half] for k in range(1, columns_x)]
-                if t:
-                    pieces = [after(piece, *crossed[half]) for piece in pieces]
-                crossed[half] = [lax.ppermute(a, "head", r) for a, r in zip(pieces, routes[1:])]
-            total = 0.0
-            for piece in [partials[t][0][0 if whole else half]] + crossed[half]:
-                if whole:
-                    piece = piece[:, half * (piece.shape[1] // halves) : (half + 1) * (piece.shape[1] // halves)]
-                total = total + piece.astype(F32)
+            pieces = [partials[t][k][half] for k in range(1, columns_x)]
+            if t:
+                pieces = [after(piece, *crossed[half]) for piece in pieces]
+            crossed[half] = [lax.ppermute(a, "head", r) for a, r in zip(pieces, routes[1:])]
+            total = sum(a.astype(F32) for a in [partials[t][0][half]] + crossed[half])
             sums[half].append(total.astype(BF16))
             if t == slabs - 1:
                 continue

time: 131 us -> 117 us (0.89)
  the two profiles are of different devices: /device:TPU:12 before, /device:TPU:0 now
where the time goes in v8:
time: 117 us; the launch traced here: 115 us
  starting transfers between devices  57 us (49%)
  waiting for transfers between devices  28.4 us (24%)
  Pallas kernels  24.2 us (21%)
  other arithmetic  4.63 us (4%)
    ppermute x8, starting transfers between devices, on_device(): lax.ppermute(sent[direction], 'wsh', [(i, i + direction) for i in found])  20.8 us
    ppermute x6, starting transfers between devices, around(): lax.ppermute(array, 'wsh', [(i, (i + k) % slabs) for i in range(slabs)])  14.7 us
    ppermute x8, waiting for transfers between devices, on_device(): lax.ppermute(a, 'head', r)  10.3 us
    pallas_call x2, Pallas kernels, first_half(): pl.pallas_call(first_half_kernel, out_shape=[pltpu.VMEM((rows_here.shape[...  9.42 us
    pallas_call x2, Pallas kernels, attend(): pl.pallas_call(partial(attend_kernel, slabs=slabs, heads=heads, share=sha...  9.25 us
    ppermute x8, starting transfers between devices, on_device(): lax.ppermute(a, 'head', r)  8.28 us
    ppermute x3, starting transfers between devices, on_device(): kv = lax.ppermute(kv, 'srv', [(g, g + 1) for g in range(groups - 1)])  8.15 us
    ppermute x2, waiting for transfers between devices, on_device(): lax.ppermute(sent, 'wsh', [(i, i + 1) for i in up] + [(i, i - 1) for i in...  7.45 us
  transfers between devices with their start and end apart: 30, of which 12 were waited for; matrix products, arithmetic and copies ran while one was open for 3% of the time, Pallas kernels for 21%

profile of v8, /device:TPU:0, one launch (start us, length us, event | category | flops | bytes accessed | tf_op | source)
XLA Modules:
  0.0 115.0 jit_solution(18378598689275001563)
XLA Ops:
  0.5 1.5 %pack.1 = (bf16[576,128]{1,0:T(8,128)(2,1)S(1)}, bf16[576,128]{1,0:T(8,128)(2,1)S(1)}, bf16[576,128]{1,0:T(8,128)(2,1)S(1)}, bf16[576,128]{1,0:T(8,128)(2,1)S(1)...) custom-call(bf16[192,2048]{1,0:T(8,128)(2,1)} %queries.1, ...), custom_call_target="tpu_custom_call" | custom-call | tf_op jit(solution)/shard_map/pack/pallas_call | solution.py:92
  1.9 2.6 %collective-permute-start = (bf16[576,128]{1,0:T(8,128)(2,1)S(1)}, bf16[576,128]{1,0:T(8,128)(2,1)S(1)}, u32[]{:S(2)}, u32[]{:S(2)}) collective-permute-start(bf16[576,128]{1,0:T(8,128)(2,1)S(1)} %get-tuple-element.53), channel_id=1, source_target_pairs={{0,1},{1,2},{2,3},{3,0},{4,5},{5,6},{6,7},{7,4},{8,9},{9,10},{10,1... | collective-permute-start | bytes 442376 | tf_op jit(solution)/shard_map/ppermute | solution.py:265
  4.6 2.6 %collective-permute-start.1 = (bf16[576,128]{1,0:T(8,128)(2,1)S(1)}, bf16[576,128]{1,0:T(8,128)(2,1)S(1)}, u32[]{:S(2)}, u32[]{:S(2)}) collective-permute-start(bf16[576,128]{1,0:T(8,128)(2,1)S(1)} %get-tuple-element.54), channel_id=1, source_target_pairs={{0,2},{1,3},{2,0},{3,1},{4,6},{5,7},{6,4},{7,5},{8,10},{9,11},{10,... | collective-permute-start | bytes 442376 | tf_op jit(solution)/shard_map/ppermute | solution.py:265
  7.1 1.3 %collective-permute-start.2 = (bf16[576,128]{1,0:T(8,128)(2,1)S(1)}, bf16[576,128]{1,0:T(8,128)(2,1)S(1)}, u32[]{:S(2)}, u32[]{:S(2)}) collective-permute-start(bf16[576,128]{1,0:T(8,128)(2,1)S(1)} %get-tuple-element.55), channel_id=1, source_target_pairs={{0,3},{1,0},{2,1},{3,2},{4,7},{5,4},{6,5},{7,6},{8,11},{9,8},{10,9... | collective-permute-start | bytes 442376 | tf_op jit(solution)/shard_map/ppermute | solution.py:265
  8.5 3.4 %collective-permute-start.3 = (bf16[384,128]{1,0:T(8,128)(2,1)S(1)}, bf16[384,128]{1,0:T(8,128)(2,1)S(1)}, u32[]{:S(2)}, u32[]{:S(2)}) collective-permute-start(bf16[384,128]{1,0:T(8,128)(2,1)S(1)} %slice.46), channel_id=1, source_target_pairs={{0,16},{1,17},{2,18},{3,19},{4,20},{5,21},{6,22},{7,23},{8,24},{9,... | collective-permute-start | bytes 294920 | tf_op jit(solution)/shard_map/ppermute | solution.py:284
  11.9 0.7 convert_element_type.180
  12.8 0.8 compare_bitcast_fusion.3
  13.7 1.0 collective-permute-done.2.refs_3_.refs_11_
  14.7 2.8 %collective-permute-done.1.refs_2_.refs_10_ = bf16[576,128]{1,0:T(8,128)(2,1)S(1)} collective-permute-done((bf16[576,128]{1,0:T(8,128)(2,1)S(1)}, bf16[576,128]{1,0:T(8,128)(2,1)S(1)}, u32[]{:S(2)}, u32[]{:S(2)}) %collective-permute-start.1) | collective-permute-done | bytes 147488 | tf_op jit(solution)/shard_map/ppermute | solution.py:265
  17.5 3.4 %collective-permute-start.5 = (bf16[768,128]{1,0:T(8,128)(2,1)S(1)}, bf16[768,128]{1,0:T(8,128)(2,1)S(1)}, u32[]{:S(2)}, u32[]{:S(2)}) collective-permute-start(bf16[768,128]{1,0:T(8,128)(2,1)S(1)} %pad_maximum_fusion.1), channel_id=1, source_target_pairs={{0,16},{1,17},{2,18},{3,19},{4,20},{5,21},{6,22},{7,23},{8,24},{9,... | collective-permute-start | bytes 589832 | tf_op jit(solution)/shard_map/ppermute | solution.py:284
  21.3 1.3 %collective-permute-start.4 = (bf16[384,128]{1,0:T(8,128)(2,1)S(1)}, bf16[384,128]{1,0:T(8,128)(2,1)S(1)}, u32[]{:S(2)}, u32[]{:S(2)}) collective-permute-start(bf16[384,128]{1,0:T(8,128)(2,1)S(1)} %slice.52), channel_id=1, source_target_pairs={{0,16},{1,17},{2,18},{3,19},{4,20},{5,21},{6,22},{7,23},{8,24},{9,... | collective-permute-start | bytes 294920 | tf_op jit(solution)/shard_map/ppermute | solution.py:284
  22.6 3.7 %collective-permute-start.6 = (bf16[576,128]{1,0:T(8,128)(2,1)S(1)}, bf16[576,128]{1,0:T(8,128)(2,1)S(1)}, u32[]{:S(2)}, u32[]{:S(2)}) collective-permute-start(bf16[576,128]{1,0:T(8,128)(2,1)S(1)} %get-tuple-element.59), channel_id=1, source_target_pairs={{0,1},{1,2},{2,3},{3,0},{4,5},{5,6},{6,7},{7,4},{8,9},{9,10},{10,1... | collective-permute-start | bytes 442376 | tf_op jit(solution)/shard_map/ppermute | solution.py:265
  26.3 1.6 %collective-permute-start.7 = (bf16[576,128]{1,0:T(8,128)(2,1)S(1)}, bf16[576,128]{1,0:T(8,128)(2,1)S(1)}, u32[]{:S(2)}, u32[]{:S(2)}) collective-permute-start(bf16[576,128]{1,0:T(8,128)(2,1)S(1)} %get-tuple-element.61), channel_id=1, source_target_pairs={{0,2},{1,3},{2,0},{3,1},{4,6},{5,7},{6,4},{7,5},{8,10},{9,11},{10,... | collective-permute-start | bytes 442376 | tf_op jit(solution)/shard_map/ppermute | solution.py:265
  27.9 2.8 %collective-permute-start.8 = (bf16[576,128]{1,0:T(8,128)(2,1)S(1)}, bf16[576,128]{1,0:T(8,128)(2,1)S(1)}, u32[]{:S(2)}, u32[]{:S(2)}) collective-permute-start(bf16[576,128]{1,0:T(8,128)(2,1)S(1)} %get-tuple-element.63), channel_id=1, source_target_pairs={{0,3},{1,0},{2,1},{3,2},{4,7},{5,4},{6,5},{7,6},{8,11},{9,8},{10,9... | collective-permute-start | bytes 442376 | tf_op jit(solution)/shard_map/ppermute | solution.py:265
  30.8 3.4 %attend.2 = (bf16[2,48,512]{2,1,0:T(8,128)(2,1)S(1)}, bf16[2,48,512]{2,1,0:T(8,128)(2,1)S(1)}, bf16[512,8192]{1,0:T(8,128)(2,1)S(1)}) custom-call(f32[8,1,768]{2,1,0:T(1,128)S(1)} %reshape.55.key_doc, bf16[576,128]{1,0:T(8,128)(2,1)S(1)} %get-tuple-element.52.refs_0_.refs_8_, bf16[576,128]{1,0:T(8,128)(2,1)S(1)} %collective-permute-done.refs_1_.refs_9_, ...), custom_call_target="tpu_custom_call" | custom-call | flops 301989888 | tf_op jit(solution)/shard_map/attend/pallas_call | solution.py:180
  34.3 3.4 %first_half.2 = (f32[96,8192]{1,0:T(8,128)S(1)}, bf16[512,8192]{1,0:T(8,128)(2,1)S(1)}) custom-call(bf16[96,512]{1,0:T(8,128)(2,1)S(1)} %bitcast.19, bf16[512,8192]{1,0:T(8,128)(2,1)S(1)} %get-tuple-element.66.near, bf16[512,8192]{1,0:T(8,128)(2,1)} %collective-permute-done.10.far), custom_call_target="tpu_custom_call" | custom-call | tf_op jit(solution)/shard_map/first_half/pallas_call | solution.py:210
  37.7 1.5 %project.2 = (bf16[48,4096]{1,0:T(8,128)(2,1)S(1)}, bf16[48,4096]{1,0:T(8,128)(2,1)S(1)}, bf16[48,4096]{1,0:T(8,128)(2,1)S(1)}, bf16[48,4096]{1,0:T(8,128)(2,1)S(1)}) custom-call(bf16[96,512]{1,0:T(8,128)(2,1)S(1)} %bitcast.18, bf16[512,8192]{1,0:T(8,128)(2,1)S(1)} %get-tuple-element.67.refs_1_, f32[96,8192]{1,0:T(8,128)S(1)} %get-tuple-element.68.refs_2_), custom_call_target="tpu_custom_call" | custom-call | tf_op jit(solution)/shard_map/project/pallas_call | solution.py:239
  39.2 1.6 %collective-permute-start.21 = (bf16[48,4096]{1,0:T(8,128)(2,1)S(1)}, bf16[48,4096]{1,0:T(8,128)(2,1)S(1)}, u32[]{:S(2)}, u32[]{:S(2)}) collective-permute-start(bf16[48,4096]{1,0:T(8,128)(2,1)S(1)} %get-tuple-element.72), channel_id=1, source_target_pairs={{0,8},{4,12},{8,0},{12,4},{1,9},{5,13},{9,1},{13,5},{2,10},{6,14},... | collective-permute-start | bytes 1179656 | tf_op jit(solution)/shard_map/ppermute | solution.py:379
  40.7 5.9 %attend.3 = (bf16[2,144,512]{2,1,0:T(8,128)(2,1)S(1)}, bf16[2,144,512]{2,1,0:T(8,128)(2,1)S(1)}) custom-call(f32[8,1,768]{2,1,0:T(1,128)S(1)} %reshape.55.key_doc, bf16[576,128]{1,0:T(8,128)(2,1)S(1)} %get-tuple-element.52.refs_0_.refs_8_, bf16[576,128]{1,0:T(8,128)(2,1)S(1)} %collective-permute-done.refs_1_.refs_9_, ...), custom_call_target="tpu_custom_call" | custom-call | flops 905969664 | tf_op jit(solution)/shard_map/attend/pallas_call | solution.py:180
  46.9 0.5 collective-permute-start.12
  47.4 6.0 %first_half.3 = (f32[288,8192]{1,0:T(8,128)S(1)}, bf16[512,8192]{1,0:T(8,128)(2,1)S(1)}) custom-call(bf16[288,512]{1,0:T(8,128)(2,1)S(1)} %bitcast.17, bf16[512,8192]{1,0:T(8,128)(2,1)} %near.1, bf16[512,8192]{1,0:T(8,128)(2,1)} %collective-permute-done.10.far), custom_call_target="tpu_custom_call" | custom-call | tf_op jit(solution)/shard_map/first_half/pallas_call | solution.py:210
  53.4 2.6 %project.3 = (bf16[48,4096]{1,0:T(8,128)(2,1)S(1)}, bf16[48,4096]{1,0:T(8,128)(2,1)S(1)}, bf16[48,4096]{1,0:T(8,128)(2,1)S(1)}, bf16[48,4096]{1,0:T(8,128)(2,1)S...) custom-call(bf16[288,512]{1,0:T(8,128)(2,1)S(1)} %bitcast.16, ...), custom_call_target="tpu_custom_call" | custom-call | tf_op jit(solution)/shard_map/project/pallas_call | solution.py:239
  56.2 2.9 %collective-permute-start.25 = (bf16[48,4096]{1,0:T(8,128)(2,1)S(1)}, bf16[48,4096]{1,0:T(8,128)(2,1)S(1)}, u32[]{:S(2)}, u32[]{:S(2)}) collective-permute-start(bf16[48,4096]{1,0:T(8,128)(2,1)S(1)} %add_convert_fusion.3), channel_id=1, source_target_pairs={{0,1},{3,2},{4,5},{7,6},{8,9},{11,10},{12,13},{15,14},{16,17},{19,... | collective-permute-start | bytes 1179656 | tf_op jit(solution)/shard_map/ppermute | solution.py:387
  59.1 0.9 collective-permute-start.22
  60.1 1.4 %collective-permute-start.16 = (bf16[48,4096]{1,0:T(8,128)(2,1)S(1)}, bf16[48,4096]{1,0:T(8,128)(2,1)S(1)}, u32[]{:S(2)}, u32[]{:S(2)}) collective-permute-start(bf16[48,4096]{1,0:T(8,128)(2,1)S(1)} %add_convert_fusion.10), channel_id=1, source_target_pairs={{0,1},{3,2},{4,5},{7,6},{8,9},{11,10},{12,13},{15,14},{16,17},{19,... | collective-permute-start | bytes 1179656 | tf_op jit(solution)/shard_map/ppermute | solution.py:387
  61.5 1.6 %collective-permute-start.13 = (bf16[48,4096]{1,0:T(8,128)(2,1)S(1)}, bf16[48,4096]{1,0:T(8,128)(2,1)S(1)}, u32[]{:S(2)}, u32[]{:S(2)}) collective-permute-start(bf16[48,4096]{1,0:T(8,128)(2,1)S(1)} %get-tuple-element.85), channel_id=1, source_target_pairs={{0,8},{4,12},{8,0},{12,4},{1,9},{5,13},{9,1},{13,5},{2,10},{6,14},... | collective-permute-start | bytes 1179656 | tf_op jit(solution)/shard_map/ppermute | solution.py:379
  63.1 5.4 %collective-permute-done.25 = bf16[48,4096]{1,0:T(8,128)(2,1)S(1)} collective-permute-done((bf16[48,4096]{1,0:T(8,128)(2,1)S(1)}, bf16[48,4096]{1,0:T(8,128)(2,1)S(1)}, u32[]{:S(2)}, u32[]{:S(2)}) %collective-permute-start.25) | collective-permute-done | bytes 393248 | tf_op jit(solution)/shard_map/ppermute | solution.py:387
  68.5 2.6 %collective-permute-done.22 = bf16[48,4096]{1,0:T(8,128)(2,1)S(1)} collective-permute-done((bf16[48,4096]{1,0:T(8,128)(2,1)S(1)}, bf16[48,4096]{1,0:T(8,128)(2,1)S(1)}, u32[]{:S(2)}, u32[]{:S(2)}) %collective-permute-start.22) | collective-permute-done | bytes 393248 | tf_op jit(solution)/shard_map/ppermute | solution.py:379
  71.3 1.8 %collective-permute-start.26 = (bf16[48,4096]{1,0:T(8,128)(2,1)S(1)}, bf16[48,4096]{1,0:T(8,128)(2,1)S(1)}, u32[]{:S(2)}, u32[]{:S(2)}) collective-permute-start(bf16[48,4096]{1,0:T(8,128)(2,1)S(1)} %get-tuple-element.101), channel_id=1, source_target_pairs={{0,1},{1,2},{4,5},{5,6},{8,9},{9,10},{12,13},{13,14},{16,17},{17,1... | collective-permute-start | bytes 1179656 | tf_op jit(solution)/shard_map/ppermute | solution.py:395
  73.1 0.9 collective-permute-start.23
  74.2 0.7 collective-permute-start.28
  74.9 2.0 %collective-permute-done.16 = bf16[48,4096]{1,0:T(8,128)(2,1)S(1)} collective-permute-done((bf16[48,4096]{1,0:T(8,128)(2,1)S(1)}, bf16[48,4096]{1,0:T(8,128)(2,1)S(1)}, u32[]{:S(2)}, u32[]{:S(2)}) %collective-permute-start.16) | collective-permute-done | bytes 393248 | tf_op jit(solution)/shard_map/ppermute | solution.py:387
  76.9 2.6 %collective-permute-done.13 = bf16[48,4096]{1,0:T(8,128)(2,1)S(1)} collective-permute-done((bf16[48,4096]{1,0:T(8,128)(2,1)S(1)}, bf16[48,4096]{1,0:T(8,128)(2,1)S(1)}, u32[]{:S(2)}, u32[]{:S(2)}) %collective-permute-start.13) | collective-permute-done | bytes 393248 | tf_op jit(solution)/shard_map/ppermute | solution.py:379
  79.8 1.8 %collective-permute-start.17 = (bf16[48,4096]{1,0:T(8,128)(2,1)S(1)}, bf16[48,4096]{1,0:T(8,128)(2,1)S(1)}, u32[]{:S(2)}, u32[]{:S(2)}) collective-permute-start(bf16[48,4096]{1,0:T(8,128)(2,1)S(1)} %get-tuple-element.99), channel_id=1, source_target_pairs={{0,1},{1,2},{4,5},{5,6},{8,9},{9,10},{12,13},{13,14},{16,17},{17,1... | collective-permute-start | bytes 1179656 | tf_op jit(solution)/shard_map/ppermute | solution.py:395
  81.6 0.9 collective-permute-start.14
  82.6 2.7 %collective-permute-done.26 = bf16[48,4096]{1,0:T(8,128)(2,1)S(1)} collective-permute-done((bf16[48,4096]{1,0:T(8,128)(2,1)S(1)}, bf16[48,4096]{1,0:T(8,128)(2,1)S(1)}, u32[]{:S(2)}, u32[]{:S(2)}) %collective-permute-start.26) | collective-permute-done | bytes 393248 | tf_op jit(solution)/shard_map/ppermute | solution.py:395
  85.3 0.7 collective-permute-start.19
  86.0 1.9 %collective-permute-done.23 = bf16[48,4096]{1,0:T(8,128)(2,1)S(1)} collective-permute-done((bf16[48,4096]{1,0:T(8,128)(2,1)S(1)}, bf16[48,4096]{1,0:T(8,128)(2,1)S(1)}, u32[]{:S(2)}, u32[]{:S(2)}) %collective-permute-start.23) | collective-permute-done | bytes 393248 | tf_op jit(solution)/shard_map/ppermute | solution.py:379
  88.3 1.3 %collective-permute-start.29 = (bf16[48,4096]{1,0:T(8,128)(2,1)S(1)}, bf16[48,4096]{1,0:T(8,128)(2,1)S(1)}, u32[]{:S(2)}, u32[]{:S(2)}) collective-permute-start(bf16[48,4096]{1,0:T(8,128)(2,1)S(1)} %get-tuple-element.106), channel_id=1, source_target_pairs={{1,0},{2,1},{3,2},{5,4},{6,5},{7,6},{9,8},{10,9},{11,10},{13,12},{... | collective-permute-start | bytes 1179656 | tf_op jit(solution)/shard_map/ppermute | solution.py:395
  89.6 4.6 %collective-permute-start.27 = (bf16[48,4096]{1,0:T(8,128)(2,1)S(1)}, bf16[48,4096]{1,0:T(8,128)(2,1)S(1)}, u32[]{:S(2)}, u32[]{:S(2)}) collective-permute-start(bf16[48,4096]{1,0:T(8,128)(2,1)S(1)} %get-tuple-element.105), channel_id=1, source_target_pairs={{0,1},{1,2},{2,3},{4,5},{5,6},{6,7},{8,9},{9,10},{10,11},{12,13},{... | collective-permute-start | bytes 1179656 | tf_op jit(solution)/shard_map/ppermute | solution.py:395
  94.2 0.9 collective-permute-start.24
  96.0 1.3 %collective-permute-start.20 = (bf16[48,4096]{1,0:T(8,128)(2,1)S(1)}, bf16[48,4096]{1,0:T(8,128)(2,1)S(1)}, u32[]{:S(2)}, u32[]{:S(2)}) collective-permute-start(bf16[48,4096]{1,0:T(8,128)(2,1)S(1)} %get-tuple-element.104), channel_id=1, source_target_pairs={{1,0},{2,1},{3,2},{5,4},{6,5},{7,6},{9,8},{10,9},{11,10},{13,12},{... | collective-permute-start | bytes 1179656 | tf_op jit(solution)/shard_map/ppermute | solution.py:395
  97.3 8.7 %collective-permute-start.18 = (bf16[48,4096]{1,0:T(8,128)(2,1)S(1)}, bf16[48,4096]{1,0:T(8,128)(2,1)S(1)}, u32[]{:S(2)}, u32[]{:S(2)}) collective-permute-start(bf16[48,4096]{1,0:T(8,128)(2,1)S(1)} %get-tuple-element.103), channel_id=1, source_target_pairs={{0,1},{1,2},{2,3},{4,5},{5,6},{6,7},{8,9},{9,10},{10,11},{12,13},{... | collective-permute-start | bytes 1179656 | tf_op jit(solution)/shard_map/ppermute | solution.py:395
  106.0 0.9 collective-permute-start.15
  107.1 2.6 %collective-permute-done.20 = bf16[48,4096]{1,0:T(8,128)(2,1)S(1)} collective-permute-done((bf16[48,4096]{1,0:T(8,128)(2,1)S(1)}, bf16[48,4096]{1,0:T(8,128)(2,1)S(1)}, u32[]{:S(2)}, u32[]{:S(2)}) %collective-permute-start.20) | collective-permute-done | bytes 393248 | tf_op jit(solution)/shard_map/ppermute | solution.py:395
  109.8 1.5 %collective-permute-done.18 = bf16[48,4096]{1,0:T(8,128)(2,1)S(1)} collective-permute-done((bf16[48,4096]{1,0:T(8,128)(2,1)S(1)}, bf16[48,4096]{1,0:T(8,128)(2,1)S(1)}, u32[]{:S(2)}, u32[]{:S(2)}) %collective-permute-start.18) | collective-permute-done | bytes 393248 | tf_op jit(solution)/shard_map/ppermute | solution.py:395
  111.2 2.6 %collective-permute-done.15 = bf16[48,4096]{1,0:T(8,128)(2,1)S(1)} collective-permute-done((bf16[48,4096]{1,0:T(8,128)(2,1)S(1)}, bf16[48,4096]{1,0:T(8,128)(2,1)S(1)}, u32[]{:S(2)}, u32[]{:S(2)}) %collective-permute-start.15) | collective-permute-done | bytes 393248 | tf_op jit(solution)/shard_map/ppermute | solution.py:379
  114.0 0.9 pad_maximum_fusion
  (47 shorter events, 3.8 us)
Async XLA Ops:
  0.0 34.3 %collective-permute-start.10 = (bf16[512,8192]{1,0:T(8,128)(2,1)}, bf16[512,8192]{1,0:T(8,128)(2,1)}, u32[]{:S(2)}, u32[]{:S(2)}) collective-permute-start(bf16[512,8192]{1,0:T(8,128)(2,1)} %near.1), channel_id=1, source_target_pairs={{0,4},{4,0},{8,12},{12,8},{1,5},{5,1},{9,13},{13,9},{2,6},{6,2},{1... | collective-permute-start | bytes 25165832 | tf_op jit(solution)/shard_map/ppermute | solution.py:286
  1.9 19.3 %collective-permute-start = (bf16[576,128]{1,0:T(8,128)(2,1)S(1)}, bf16[576,128]{1,0:T(8,128)(2,1)S(1)}, u32[]{:S(2)}, u32[]{:S(2)}) collective-permute-start(bf16[576,128]{1,0:T(8,128)(2,1)S(1)} %get-tuple-element.53), channel_id=1, source_target_pairs={{0,1},{1,2},{2,3},{3,0},{4,5},{5,6},{6,7},{7,4},{8,9},{9,10},{10,1... | collective-permute-start | bytes 442376 | tf_op jit(solution)/shard_map/ppermute | solution.py:265
  4.6 12.9 %collective-permute-start.1 = (bf16[576,128]{1,0:T(8,128)(2,1)S(1)}, bf16[576,128]{1,0:T(8,128)(2,1)S(1)}, u32[]{:S(2)}, u32[]{:S(2)}) collective-permute-start(bf16[576,128]{1,0:T(8,128)(2,1)S(1)} %get-tuple-element.54), channel_id=1, source_target_pairs={{0,2},{1,3},{2,0},{3,1},{4,6},{5,7},{6,4},{7,5},{8,10},{9,11},{10,... | collective-permute-start | bytes 442376 | tf_op jit(solution)/shard_map/ppermute | solution.py:265
  7.1 7.6 %collective-permute-start.2 = (bf16[576,128]{1,0:T(8,128)(2,1)S(1)}, bf16[576,128]{1,0:T(8,128)(2,1)S(1)}, u32[]{:S(2)}, u32[]{:S(2)}) collective-permute-start(bf16[576,128]{1,0:T(8,128)(2,1)S(1)} %get-tuple-element.55), channel_id=1, source_target_pairs={{0,3},{1,0},{2,1},{3,2},{4,7},{5,4},{6,5},{7,6},{8,11},{9,8},{10,9... | collective-permute-start | bytes 442376 | tf_op jit(solution)/shard_map/ppermute | solution.py:265
  8.5 17.8 %collective-permute-start.3 = (bf16[384,128]{1,0:T(8,128)(2,1)S(1)}, bf16[384,128]{1,0:T(8,128)(2,1)S(1)}, u32[]{:S(2)}, u32[]{:S(2)}) collective-permute-start(bf16[384,128]{1,0:T(8,128)(2,1)S(1)} %slice.46), channel_id=1, source_target_pairs={{0,16},{1,17},{2,18},{3,19},{4,20},{5,21},{6,22},{7,23},{8,24},{9,... | collective-permute-start | bytes 294920 | tf_op jit(solution)/shard_map/ppermute | solution.py:284
  17.5 10.4 %collective-permute-start.5 = (bf16[768,128]{1,0:T(8,128)(2,1)S(1)}, bf16[768,128]{1,0:T(8,128)(2,1)S(1)}, u32[]{:S(2)}, u32[]{:S(2)}) collective-permute-start(bf16[768,128]{1,0:T(8,128)(2,1)S(1)} %pad_maximum_fusion.1), channel_id=1, source_target_pairs={{0,16},{1,17},{2,18},{3,19},{4,20},{5,21},{6,22},{7,23},{8,24},{9,... | collective-permute-start | bytes 589832 | tf_op jit(solution)/shard_map/ppermute | solution.py:284
  21.3 9.5 %collective-permute-start.4 = (bf16[384,128]{1,0:T(8,128)(2,1)S(1)}, bf16[384,128]{1,0:T(8,128)(2,1)S(1)}, u32[]{:S(2)}, u32[]{:S(2)}) collective-permute-start(bf16[384,128]{1,0:T(8,128)(2,1)S(1)} %slice.52), channel_id=1, source_target_pairs={{0,16},{1,17},{2,18},{3,19},{4,20},{5,21},{6,22},{7,23},{8,24},{9,... | collective-permute-start | bytes 294920 | tf_op jit(solution)/shard_map/ppermute | solution.py:284
  22.6 18.2 %collective-permute-start.6 = (bf16[576,128]{1,0:T(8,128)(2,1)S(1)}, bf16[576,128]{1,0:T(8,128)(2,1)S(1)}, u32[]{:S(2)}, u32[]{:S(2)}) collective-permute-start(bf16[576,128]{1,0:T(8,128)(2,1)S(1)} %get-tuple-element.59), channel_id=1, source_target_pairs={{0,1},{1,2},{2,3},{3,0},{4,5},{5,6},{6,7},{7,4},{8,9},{9,10},{10,1... | collective-permute-start | bytes 442376 | tf_op jit(solution)/shard_map/ppermute | solution.py:265
  26.3 14.4 %collective-permute-start.7 = (bf16[576,128]{1,0:T(8,128)(2,1)S(1)}, bf16[576,128]{1,0:T(8,128)(2,1)S(1)}, u32[]{:S(2)}, u32[]{:S(2)}) collective-permute-start(bf16[576,128]{1,0:T(8,128)(2,1)S(1)} %get-tuple-element.61), channel_id=1, source_target_pairs={{0,2},{1,3},{2,0},{3,1},{4,6},{5,7},{6,4},{7,5},{8,10},{9,11},{10,... | collective-permute-start | bytes 442376 | tf_op jit(solution)/shard_map/ppermute | solution.py:265
  27.9 12.8 %collective-permute-start.8 = (bf16[576,128]{1,0:T(8,128)(2,1)S(1)}, bf16[576,128]{1,0:T(8,128)(2,1)S(1)}, u32[]{:S(2)}, u32[]{:S(2)}) collective-permute-start(bf16[576,128]{1,0:T(8,128)(2,1)S(1)} %get-tuple-element.63), channel_id=1, source_target_pairs={{0,3},{1,0},{2,1},{3,2},{4,7},{5,4},{6,5},{7,6},{8,11},{9,8},{10,9... | collective-permute-start | bytes 442376 | tf_op jit(solution)/shard_map/ppermute | solution.py:265
  34.2 3.5 %collective-permute-start.9 = (bf16[2,48,512]{2,1,0:T(8,128)(2,1)S(1)}, bf16[2,48,512]{2,1,0:T(8,128)(2,1)S(1)}, u32[]{:S(2)}, u32[]{:S(2)}) collective-permute-start(bf16[2,48,512]{2,1,0:T(8,128)(2,1)S(1)} %get-tuple-element.64), channel_id=1, source_target_pairs={{0,4},{4,0},{8,12},{12,8},{1,5},{5,1},{9,13},{13,9},{2,6},{6,2},{1... | collective-permute-start | bytes 294920 | tf_op jit(solution)/shard_map/ppermute | solution.py:335
  39.2 16.9 %collective-permute-start.21 = (bf16[48,4096]{1,0:T(8,128)(2,1)S(1)}, bf16[48,4096]{1,0:T(8,128)(2,1)S(1)}, u32[]{:S(2)}, u32[]{:S(2)}) collective-permute-start(bf16[48,4096]{1,0:T(8,128)(2,1)S(1)} %get-tuple-element.72), channel_id=1, source_target_pairs={{0,8},{4,12},{8,0},{12,4},{1,9},{5,13},{9,1},{13,5},{2,10},{6,14},... | collective-permute-start | bytes 1179656 | tf_op jit(solution)/shard_map/ppermute | solution.py:379
  46.6 6.8 %collective-permute-start.11 = (bf16[2,144,512]{2,1,0:T(8,128)(2,1)S(1)}, bf16[2,144,512]{2,1,0:T(8,128)(2,1)S(1)}, u32[]{:S(2)}, u32[]{:S(2)}) collective-permute-start(bf16[2,144,512]{2,1,0:T(8,128)(2,1)S(1)} %get-tuple-element.77), channel_id=1, source_target_pairs={{0,4},{4,0},{8,12},{12,8},{1,5},{5,1},{9,13},{13,9},{2,6},{6,2},{1... | collective-permute-start | bytes 884744 | tf_op jit(solution)/shard_map/ppermute | solution.py:335
  46.9 13.1 %collective-permute-start.12 = (bf16[48,4096]{1,0:T(8,128)(2,1)S(1)}, bf16[48,4096]{1,0:T(8,128)(2,1)S(1)}, u32[]{:S(2)}, u32[]{:S(2)}) collective-permute-start(bf16[48,4096]{1,0:T(8,128)(2,1)S(1)} %get-tuple-element.71), channel_id=1, source_target_pairs={{0,8},{4,12},{8,0},{12,4},{1,9},{5,13},{9,1},{13,5},{2,10},{6,14},... | collective-permute-start | bytes 1179656 | tf_op jit(solution)/shard_map/ppermute | solution.py:379
  56.2 12.3 %collective-permute-start.25 = (bf16[48,4096]{1,0:T(8,128)(2,1)S(1)}, bf16[48,4096]{1,0:T(8,128)(2,1)S(1)}, u32[]{:S(2)}, u32[]{:S(2)}) collective-permute-start(bf16[48,4096]{1,0:T(8,128)(2,1)S(1)} %add_convert_fusion.3), channel_id=1, source_target_pairs={{0,1},{3,2},{4,5},{7,6},{8,9},{11,10},{12,13},{15,14},{16,17},{19,... | collective-permute-start | bytes 1179656 | tf_op jit(solution)/shard_map/ppermute | solution.py:387
  59.1 12.1 %collective-permute-start.22 = (bf16[48,4096]{1,0:T(8,128)(2,1)S(1)}, bf16[48,4096]{1,0:T(8,128)(2,1)S(1)}, u32[]{:S(2)}, u32[]{:S(2)}) collective-permute-start(bf16[48,4096]{1,0:T(8,128)(2,1)S(1)} %get-tuple-element.94), channel_id=1, source_target_pairs={{0,8},{4,12},{8,0},{12,4},{1,9},{5,13},{9,1},{13,5},{2,10},{6,14},... | collective-permute-start | bytes 1179656 | tf_op jit(solution)/shard_map/ppermute | solution.py:379
  60.1 16.8 %collective-permute-start.16 = (bf16[48,4096]{1,0:T(8,128)(2,1)S(1)}, bf16[48,4096]{1,0:T(8,128)(2,1)S(1)}, u32[]{:S(2)}, u32[]{:S(2)}) collective-permute-start(bf16[48,4096]{1,0:T(8,128)(2,1)S(1)} %add_convert_fusion.10), channel_id=1, source_target_pairs={{0,1},{3,2},{4,5},{7,6},{8,9},{11,10},{12,13},{15,14},{16,17},{19,... | collective-permute-start | bytes 1179656 | tf_op jit(solution)/shard_map/ppermute | solution.py:387
  61.5 18.0 %collective-permute-start.13 = (bf16[48,4096]{1,0:T(8,128)(2,1)S(1)}, bf16[48,4096]{1,0:T(8,128)(2,1)S(1)}, u32[]{:S(2)}, u32[]{:S(2)}) collective-permute-start(bf16[48,4096]{1,0:T(8,128)(2,1)S(1)} %get-tuple-element.85), channel_id=1, source_target_pairs={{0,8},{4,12},{8,0},{12,4},{1,9},{5,13},{9,1},{13,5},{2,10},{6,14},... | collective-permute-start | bytes 1179656 | tf_op jit(solution)/shard_map/ppermute | solution.py:379
  71.3 14.0 %collective-permute-start.26 = (bf16[48,4096]{1,0:T(8,128)(2,1)S(1)}, bf16[48,4096]{1,0:T(8,128)(2,1)S(1)}, u32[]{:S(2)}, u32[]{:S(2)}) collective-permute-start(bf16[48,4096]{1,0:T(8,128)(2,1)S(1)} %get-tuple-element.101), channel_id=1, source_target_pairs={{0,1},{1,2},{4,5},{5,6},{8,9},{9,10},{12,13},{13,14},{16,17},{17,1... | collective-permute-start | bytes 1179656 | tf_op jit(solution)/shard_map/ppermute | solution.py:395
  73.1 14.8 %collective-permute-start.23 = (bf16[48,4096]{1,0:T(8,128)(2,1)S(1)}, bf16[48,4096]{1,0:T(8,128)(2,1)S(1)}, u32[]{:S(2)}, u32[]{:S(2)}) collective-permute-start(bf16[48,4096]{1,0:T(8,128)(2,1)S(1)} %get-tuple-element.95), channel_id=1, source_target_pairs={{0,8},{4,12},{8,0},{12,4},{1,9},{5,13},{9,1},{13,5},{2,10},{6,14},... | collective-permute-start | bytes 1179656 | tf_op jit(solution)/shard_map/ppermute | solution.py:379
  74.2 13.8 %collective-permute-start.28 = (bf16[48,4096]{1,0:T(8,128)(2,1)S(1)}, bf16[48,4096]{1,0:T(8,128)(2,1)S(1)}, u32[]{:S(2)}, u32[]{:S(2)}) collective-permute-start(bf16[48,4096]{1,0:T(8,128)(2,1)S(1)} %fusion.3), channel_id=1, source_target_pairs={{2,1},{3,2},{6,5},{7,6},{10,9},{11,10},{14,13},{15,14},{18,17},{19... | collective-permute-start | bytes 1179656 | tf_op jit(solution)/shard_map/ppermute | solution.py:395
  79.8 14.4 %collective-permute-start.17 = (bf16[48,4096]{1,0:T(8,128)(2,1)S(1)}, bf16[48,4096]{1,0:T(8,128)(2,1)S(1)}, u32[]{:S(2)}, u32[]{:S(2)}) collective-permute-start(bf16[48,4096]{1,0:T(8,128)(2,1)S(1)} %get-tuple-element.99), channel_id=1, source_target_pairs={{0,1},{1,2},{4,5},{5,6},{8,9},{9,10},{12,13},{13,14},{16,17},{17,1... | collective-permute-start | bytes 1179656 | tf_op jit(solution)/shard_map/ppermute | solution.py:395
  81.6 14.1 %collective-permute-start.14 = (bf16[48,4096]{1,0:T(8,128)(2,1)S(1)}, bf16[48,4096]{1,0:T(8,128)(2,1)S(1)}, u32[]{:S(2)}, u32[]{:S(2)}) collective-permute-start(bf16[48,4096]{1,0:T(8,128)(2,1)S(1)} %get-tuple-element.86), channel_id=1, source_target_pairs={{0,8},{4,12},{8,0},{12,4},{1,9},{5,13},{9,1},{13,5},{2,10},{6,14},... | collective-permute-start | bytes 1179656 | tf_op jit(solution)/shard_map/ppermute | solution.py:379
  85.3 10.3 %collective-permute-start.19 = (bf16[48,4096]{1,0:T(8,128)(2,1)S(1)}, bf16[48,4096]{1,0:T(8,128)(2,1)S(1)}, u32[]{:S(2)}, u32[]{:S(2)}) collective-permute-start(bf16[48,4096]{1,0:T(8,128)(2,1)S(1)} %fusion.1), channel_id=1, source_target_pairs={{2,1},{3,2},{6,5},{7,6},{10,9},{11,10},{14,13},{15,14},{18,17},{19... | collective-permute-start | bytes 1179656 | tf_op jit(solution)/shard_map/ppermute | solution.py:395
  88.3 17.7 %collective-permute-start.29 = (bf16[48,4096]{1,0:T(8,128)(2,1)S(1)}, bf16[48,4096]{1,0:T(8,128)(2,1)S(1)}, u32[]{:S(2)}, u32[]{:S(2)}) collective-permute-start(bf16[48,4096]{1,0:T(8,128)(2,1)S(1)} %get-tuple-element.106), channel_id=1, source_target_pairs={{1,0},{2,1},{3,2},{5,4},{6,5},{7,6},{9,8},{10,9},{11,10},{13,12},{... | collective-permute-start | bytes 1179656 | tf_op jit(solution)/shard_map/ppermute | solution.py:395
  89.6 17.3 %collective-permute-start.27 = (bf16[48,4096]{1,0:T(8,128)(2,1)S(1)}, bf16[48,4096]{1,0:T(8,128)(2,1)S(1)}, u32[]{:S(2)}, u32[]{:S(2)}) collective-permute-start(bf16[48,4096]{1,0:T(8,128)(2,1)S(1)} %get-tuple-element.105), channel_id=1, source_target_pairs={{0,1},{1,2},{2,3},{4,5},{5,6},{6,7},{8,9},{9,10},{10,11},{12,13},{... | collective-permute-start | bytes 1179656 | tf_op jit(solution)/shard_map/ppermute | solution.py:395
  94.2 12.7 %collective-permute-start.24 = (bf16[48,4096]{1,0:T(8,128)(2,1)S(1)}, bf16[48,4096]{1,0:T(8,128)(2,1)S(1)}, u32[]{:S(2)}, u32[]{:S(2)}) collective-permute-start(bf16[48,4096]{1,0:T(8,128)(2,1)S(1)} %get-tuple-element.96), channel_id=1, source_target_pairs={{0,8},{4,12},{8,0},{12,4},{1,9},{5,13},{9,1},{13,5},{2,10},{6,14},... | collective-permute-start | bytes 1179656 | tf_op jit(solution)/shard_map/ppermute | solution.py:379
  96.0 13.8 %collective-permute-start.20 = (bf16[48,4096]{1,0:T(8,128)(2,1)S(1)}, bf16[48,4096]{1,0:T(8,128)(2,1)S(1)}, u32[]{:S(2)}, u32[]{:S(2)}) collective-permute-start(bf16[48,4096]{1,0:T(8,128)(2,1)S(1)} %get-tuple-element.104), channel_id=1, source_target_pairs={{1,0},{2,1},{3,2},{5,4},{6,5},{7,6},{9,8},{10,9},{11,10},{13,12},{... | collective-permute-start | bytes 1179656 | tf_op jit(solution)/shard_map/ppermute | solution.py:395
  97.3 14.0 %collective-permute-start.18 = (bf16[48,4096]{1,0:T(8,128)(2,1)S(1)}, bf16[48,4096]{1,0:T(8,128)(2,1)S(1)}, u32[]{:S(2)}, u32[]{:S(2)}) collective-permute-start(bf16[48,4096]{1,0:T(8,128)(2,1)S(1)} %get-tuple-element.103), channel_id=1, source_target_pairs={{0,1},{1,2},{2,3},{4,5},{5,6},{6,7},{8,9},{9,10},{10,11},{12,13},{... | collective-permute-start | bytes 1179656 | tf_op jit(solution)/shard_map/ppermute | solution.py:395
  106.0 7.8 %collective-permute-start.15 = (bf16[48,4096]{1,0:T(8,128)(2,1)S(1)}, bf16[48,4096]{1,0:T(8,128)(2,1)S(1)}, u32[]{:S(2)}, u32[]{:S(2)}) collective-permute-start(bf16[48,4096]{1,0:T(8,128)(2,1)S(1)} %get-tuple-element.87), channel_id=1, source_target_pairs={{0,8},{4,12},{8,0},{12,4},{1,9},{5,13},{9,1},{13,5},{2,10},{6,14},... | collective-permute-start | bytes 1179656 | tf_op jit(solution)/shard_map/ppermute | solution.py:379

commit v9 on v8

--- a/solution.py
+++ b/solution.py
@@ -276,18 +276,16 @@
         stages=stages,
     )
     loads = [packed[0]] + [around(packed[k], k) for k in range(1, slabs)]
-    cuts = [loads[:1], loads[1:2], loads[2:]]
-    before = []
-    for cut in cuts:
-        if cut:
-            kv = joined([a[: 2 * block] for a in cut])
-            kv = lax.ppermute(kv, "srv", [(g, g + 1) for g in range(groups - 1)])
-            before += [kv[n * 2 * block : (n + 1) * 2 * block] for n in range(len(cut))]
+    before = [
+        lax.ppermute(a[: 2 * block], "srv", [(g, g + 1) for g in range(groups - 1)]) for a in loads
+    ]
     weight_sibling = lax.ppermute(out_weight, "head", siblings)
     stage_queries = [loads]
     for n in range(1, len(stages)):
-        sent = [after(a, *loads) for a in packed[n * slabs : (n + 1) * slabs]]
-        stage_queries.append([sent[0]] + [around(sent[k], k) for k in range(1, slabs)])
+        sent = packed[n * slabs : (n + 1) * slabs]
+        stage_queries.append(
+            [sent[0]] + [around(after(sent[k], *loads, before[k - 1]), k) for k in range(1, slabs)]
+        )
 
     reach = SLAB_REACH - 1
     padded = jnp.concatenate([jnp.full((reach, block), -1.0, F32), doc_ids.reshape(-1, block).astype(F32)])
@@ -349,28 +347,18 @@
             )
 
     position = np.argsort(order, axis=1)
-
-    def senders(direction, t):
-        found = {}
-        for i in range(slabs):
-            step = i if direction > 0 else slabs - 1 - i
-            if step <= t:
-                d = slabs - 1 - t + step
-                found[i] = int(position[i, d if direction > 0 else slabs - 1 - d])
-        return found
-
-    def message(which, own, arrived):
-        picked = None
-        for i, piece in which.items():
-            picked = own[piece] if picked is None else jnp.where(z == i, own[piece], picked)
-        if arrived is None:
-            return picked
-        return (picked.astype(F32) + arrived.astype(F32)).astype(BF16)
+    middle = slabs // 2 - 1
+
+    def inward(c):
+        return [(c, c + 1), (slabs - 1 - c, slabs - 2 - c)]
+
+    def outward(c):
+        return [(b, a) for a, b in inward(c)]
 
     sums = [[] for _ in range(halves)]
     crossed = [None] * halves
     routes = [[(h, (h + 2 * k) % head_shards) for h in range(head_shards)] for k in range(columns_x)]
-    arrived = [{1: None, -1: None} for _ in range(halves)]
+    passed = [{} for _ in range(halves)]
     for t in range(slabs):
         for half in range(halves):
             pieces = [partials[t][k][half] for k in range(1, columns_x)]
@@ -381,25 +369,25 @@
             sums[half].append(total.astype(BF16))
             if t == slabs - 1:
                 continue
-            up, down = senders(1, t), senders(-1, t)
-            if t + 1 < slabs - 2 - t:
-                sent = message({**up, **down}, sums[half], arrived[half][1])
-                both = lax.ppermute(sent, "wsh", [(i, i + 1) for i in up] + [(i, i - 1) for i in down])
-                arrived[half] = {1: both, -1: both}
-            else:
-                sent = {
-                    direction: message(found, sums[half], arrived[half][direction])
-                    for direction, found in ((1, up), (-1, down))
-                }
-                for direction, found in ((1, up), (-1, down)):
-                    arrived[half][direction] = lax.ppermute(
-                        sent[direction], "wsh", [(i, i + direction) for i in found]
-                    )
+            now = {}
+            for c in range(min(t, middle) + 1):
+                message = sums[half][position[c, slabs - 1 - t + c]]
+                if c:
+                    message = (message.astype(F32) + passed[half][c - 1].astype(F32)).astype(BF16)
+                route = inward(c)
+                if c < middle and t >= slabs - 2 - c:
+                    z_out = slabs - 2 - c
+                    back = sums[half][position[z_out, slabs - 1 - t + z_out]]
+                    back = (back.astype(F32) + passed[half][c + 1].astype(F32)).astype(BF16)
+                    message = jnp.where((z == c) | (z == slabs - 1 - c), message, back)
+                    route = route + outward(c)
+                now[c] = lax.ppermute(message, "wsh", route)
+            passed[half] = now
     outs = []
     for half in range(halves):
         total = sums[half][-1].astype(F32)
-        if slabs > 1:
-            total = total + arrived[half][1].astype(F32) + arrived[half][-1].astype(F32)
+        for a in passed[half].values():
+            total = total + a.astype(F32)
         outs.append(total.astype(BF16))
     return jnp.concatenate(outs, axis=1)
 

time: 117 us -> 115 us (0.983); the launches traced: 115 us -> 115 us
  waiting for transfers between devices: 28.4 us -> 26.2 us
    ppermute x6, starting transfers between devices: 14.7 us -> 12.8 us  [around(): lax.ppermute(array, 'wsh', [(i, (i + k) % slabs) for i in range(slabs)])]
    ppermute x13 -> x14, starting transfers between devices: 33.2 us -> 34.7 us  [the longest x10 25.3 us: on_device(): now[c] = lax.ppermute(message, 'wsh', route)]
    ppermute x6, waiting for transfers between devices: 3.78 us -> 2.48 us  [around(): lax.ppermute(array, 'wsh', [(i, (i + k) % slabs) for i in range(slabs)])]
    convert_element_type x2 -> x4, other arithmetic: 0.19 us -> 1.37 us  [on_device(): sums[half].append(total.astype(BF16))]
    ppermute x13 -> x14, waiting for transfers between devices: 14.3 us -> 14.4 us  [the longest x10 14.4 us: on_device(): now[c] = lax.ppermute(message, 'wsh', route)]
  transfers between devices with their start and end apart: 30 -> 31, of which waited for: 12 -> 9; matrix products, arithmetic and copies ran while one was open for 3% -> 4% of each run, Pallas kernels for 21% -> 22%
where the time goes in v9:
time: 115 us
  starting transfers between devices  57.6 us (50%)
  waiting for transfers between devices  26.2 us (23%)
  Pallas kernels  25.2 us (22%)
  other arithmetic  5.14 us (4%)
    ppermute x10, starting transfers between devices, on_device(): now[c] = lax.ppermute(message, 'wsh', route)  25.3 us
    ppermute x10, waiting for transfers between devices, on_device(): now[c] = lax.ppermute(message, 'wsh', route)  14.4 us
    ppermute x6, starting transfers between devices, around(): lax.ppermute(array, 'wsh', [(i, (i + k) % slabs) for i in range(slabs)])  12.8 us
    pallas_call x2, Pallas kernels, attend(): pl.pallas_call(partial(attend_kernel, slabs=slabs, heads=heads, share=sha...  10.2 us
    ppermute x4, starting transfers between devices, on_device(): lax.ppermute(a[:2 * block], 'srv', [(g, g + 1) for g in range(groups - 1)])  9.44 us
    pallas_call x2, Pallas kernels, first_half(): pl.pallas_call(first_half_kernel, out_shape=[pltpu.VMEM((rows_here.shape[...  9.42 us
    ppermute x8, starting transfers between devices, on_device(): lax.ppermute(a, 'head', r)  9.32 us
    ppermute x8, waiting for transfers between devices, on_device(): lax.ppermute(a, 'head', r)  9.25 us
  transfers between devices with their start and end apart: 31, of which 9 were waited for; matrix products, arithmetic and copies ran while one was open for 4% of the time, Pallas kernels for 22%

profile of v9, /device:TPU:0, one launch (start us, length us, event | category | flops | bytes accessed | tf_op | source)
XLA Modules:
  0.0 114.8 jit_solution(750981010123551082)
XLA Ops:
  0.5 1.5 %pack.1 = (bf16[576,128]{1,0:T(8,128)(2,1)S(1)}, bf16[576,128]{1,0:T(8,128)(2,1)S(1)}, bf16[576,128]{1,0:T(8,128)(2,1)S(1)}, bf16[576,128]{1,0:T(8,128)(2,1)S(1)...) custom-call(bf16[192,2048]{1,0:T(8,128)(2,1)} %queries.1, ...), custom_call_target="tpu_custom_call" | custom-call | tf_op jit(solution)/shard_map/pack/pallas_call | solution.py:92
  1.9 2.6 %collective-permute-start = (bf16[576,128]{1,0:T(8,128)(2,1)S(1)}, bf16[576,128]{1,0:T(8,128)(2,1)S(1)}, u32[]{:S(2)}, u32[]{:S(2)}) collective-permute-start(bf16[576,128]{1,0:T(8,128)(2,1)S(1)} %get-tuple-element.52), channel_id=1, source_target_pairs={{0,1},{1,2},{2,3},{3,0},{4,5},{5,6},{6,7},{7,4},{8,9},{9,10},{10,1... | collective-permute-start | bytes 442376 | tf_op jit(solution)/shard_map/ppermute | solution.py:265
  4.6 2.6 %collective-permute-start.1 = (bf16[576,128]{1,0:T(8,128)(2,1)S(1)}, bf16[576,128]{1,0:T(8,128)(2,1)S(1)}, u32[]{:S(2)}, u32[]{:S(2)}) collective-permute-start(bf16[576,128]{1,0:T(8,128)(2,1)S(1)} %get-tuple-element.53), channel_id=1, source_target_pairs={{0,2},{1,3},{2,0},{3,1},{4,6},{5,7},{6,4},{7,5},{8,10},{9,11},{10,... | collective-permute-start | bytes 442376 | tf_op jit(solution)/shard_map/ppermute | solution.py:265
  7.1 1.3 %collective-permute-start.2 = (bf16[576,128]{1,0:T(8,128)(2,1)S(1)}, bf16[576,128]{1,0:T(8,128)(2,1)S(1)}, u32[]{:S(2)}, u32[]{:S(2)}) collective-permute-start(bf16[576,128]{1,0:T(8,128)(2,1)S(1)} %get-tuple-element.54), channel_id=1, source_target_pairs={{0,3},{1,0},{2,1},{3,2},{4,7},{5,4},{6,5},{7,6},{8,11},{9,8},{10,9... | collective-permute-start | bytes 442376 | tf_op jit(solution)/shard_map/ppermute | solution.py:265
  8.5 3.4 %collective-permute-start.3 = (bf16[384,128]{1,0:T(8,128)(2,1)S(1)}, bf16[384,128]{1,0:T(8,128)(2,1)S(1)}, u32[]{:S(2)}, u32[]{:S(2)}) collective-permute-start(bf16[384,128]{1,0:T(8,128)(2,1)S(1)} %slice.40), channel_id=1, source_target_pairs={{0,16},{1,17},{2,18},{3,19},{4,20},{5,21},{6,22},{7,23},{8,24},{9,... | collective-permute-start | bytes 294920 | tf_op jit(solution)/shard_map/ppermute | solution.py:280
  11.9 0.7 convert_element_type.166
  12.8 0.8 compare_bitcast_fusion.3
  13.7 1.3 %collective-permute-start.4 = (bf16[384,128]{1,0:T(8,128)(2,1)S(1)}, bf16[384,128]{1,0:T(8,128)(2,1)S(1)}, u32[]{:S(2)}, u32[]{:S(2)}) collective-permute-start(bf16[384,128]{1,0:T(8,128)(2,1)S(1)} %slice.44), channel_id=1, source_target_pairs={{0,16},{1,17},{2,18},{3,19},{4,20},{5,21},{6,22},{7,23},{8,24},{9,... | collective-permute-start | bytes 294920 | tf_op jit(solution)/shard_map/ppermute | solution.py:280
  15.0 2.5 %collective-permute-done.1.refs_2_.refs_10_ = bf16[576,128]{1,0:T(8,128)(2,1)S(1)} collective-permute-done((bf16[576,128]{1,0:T(8,128)(2,1)S(1)}, bf16[576,128]{1,0:T(8,128)(2,1)S(1)}, u32[]{:S(2)}, u32[]{:S(2)}) %collective-permute-start.1) | collective-permute-done | bytes 147488 | tf_op jit(solution)/shard_map/ppermute | solution.py:265
  17.5 3.4 %collective-permute-start.5 = (bf16[384,128]{1,0:T(8,128)(2,1)S(1)}, bf16[384,128]{1,0:T(8,128)(2,1)S(1)}, u32[]{:S(2)}, u32[]{:S(2)}) collective-permute-start(bf16[384,128]{1,0:T(8,128)(2,1)S(1)} %slice.45), channel_id=1, source_target_pairs={{0,16},{1,17},{2,18},{3,19},{4,20},{5,21},{6,22},{7,23},{8,24},{9,... | collective-permute-start | bytes 294920 | tf_op jit(solution)/shard_map/ppermute | solution.py:280
  21.1 1.3 %collective-permute-start.6 = (bf16[384,128]{1,0:T(8,128)(2,1)S(1)}, bf16[384,128]{1,0:T(8,128)(2,1)S(1)}, u32[]{:S(2)}, u32[]{:S(2)}) collective-permute-start(bf16[384,128]{1,0:T(8,128)(2,1)S(1)} %slice.46), channel_id=1, source_target_pairs={{0,16},{1,17},{2,18},{3,19},{4,20},{5,21},{6,22},{7,23},{8,24},{9,... | collective-permute-start | bytes 294920 | tf_op jit(solution)/shard_map/ppermute | solution.py:280
  22.4 2.3 %collective-permute-start.7 = (bf16[576,128]{1,0:T(8,128)(2,1)S(1)}, bf16[576,128]{1,0:T(8,128)(2,1)S(1)}, u32[]{:S(2)}, u32[]{:S(2)}) collective-permute-start(bf16[576,128]{1,0:T(8,128)(2,1)S(1)} %get-tuple-element.57), channel_id=1, source_target_pairs={{0,1},{1,2},{2,3},{3,0},{4,5},{5,6},{6,7},{7,4},{8,9},{9,10},{10,1... | collective-permute-start | bytes 442376 | tf_op jit(solution)/shard_map/ppermute | solution.py:265
  24.7 3.1 %collective-permute-start.8 = (bf16[576,128]{1,0:T(8,128)(2,1)S(1)}, bf16[576,128]{1,0:T(8,128)(2,1)}, u32[]{:S(2)}, u32[]{:S(2)}) collective-permute-start(bf16[576,128]{1,0:T(8,128)(2,1)S(1)} %get-tuple-element.59), channel_id=1, source_target_pairs={{0,2},{1,3},{2,0},{3,1},{4,6},{5,7},{6,4},{7,5},{8,10},{9,11},{10,... | collective-permute-start | bytes 442376 | tf_op jit(solution)/shard_map/ppermute | solution.py:265
  27.7 0.9 collective-permute-start.9
  28.8 3.4 %attend.2 = (bf16[2,48,512]{2,1,0:T(8,128)(2,1)S(1)}, bf16[2,48,512]{2,1,0:T(8,128)(2,1)S(1)}, bf16[512,8192]{1,0:T(8,128)(2,1)S(1)}) custom-call(f32[8,1,768]{2,1,0:T(1,128)S(1)} %reshape.55.key_doc, bf16[576,128]{1,0:T(8,128)(2,1)S(1)} %get-tuple-element.51.refs_0_.refs_8_, bf16[576,128]{1,0:T(8,128)(2,1)S(1)} %collective-permute-done.refs_1_.refs_9_, ...), custom_call_target="tpu_custom_call" | custom-call | flops 301989888 | tf_op jit(solution)/shard_map/attend/pallas_call | solution.py:180
  32.3 3.4 %first_half.2 = (f32[96,8192]{1,0:T(8,128)S(1)}, bf16[512,8192]{1,0:T(8,128)(2,1)S(1)}) custom-call(bf16[96,512]{1,0:T(8,128)(2,1)S(1)} %bitcast.19, bf16[512,8192]{1,0:T(8,128)(2,1)S(1)} %get-tuple-element.64.near, bf16[512,8192]{1,0:T(8,128)(2,1)} %collective-permute-done.11.far), custom_call_target="tpu_custom_call" | custom-call | tf_op jit(solution)/shard_map/first_half/pallas_call | solution.py:210
  35.7 1.5 %project.2 = (bf16[48,4096]{1,0:T(8,128)(2,1)S(1)}, bf16[48,4096]{1,0:T(8,128)(2,1)S(1)}, bf16[48,4096]{1,0:T(8,128)(2,1)S(1)}, bf16[48,4096]{1,0:T(8,128)(2,1)S(1)}) custom-call(bf16[96,512]{1,0:T(8,128)(2,1)S(1)} %bitcast.18, bf16[512,8192]{1,0:T(8,128)(2,1)S(1)} %get-tuple-element.65.refs_1_, f32[96,8192]{1,0:T(8,128)S(1)} %get-tuple-element.66.refs_2_), custom_call_target="tpu_custom_call" | custom-call | tf_op jit(solution)/shard_map/project/pallas_call | solution.py:239
  37.1 1.6 %collective-permute-start.22 = (bf16[48,4096]{1,0:T(8,128)(2,1)S(1)}, bf16[48,4096]{1,0:T(8,128)(2,1)}, u32[]{:S(2)}, u32[]{:S(2)}) collective-permute-start(bf16[48,4096]{1,0:T(8,128)(2,1)S(1)} %get-tuple-element.70), channel_id=1, source_target_pairs={{0,8},{4,12},{8,0},{12,4},{1,9},{5,13},{9,1},{13,5},{2,10},{6,14},... | collective-permute-start | bytes 1179656 | tf_op jit(solution)/shard_map/ppermute | solution.py:367
  38.7 6.8 %attend.3 = (bf16[2,144,512]{2,1,0:T(8,128)(2,1)S(1)}, bf16[2,144,512]{2,1,0:T(8,128)(2,1)S(1)}) custom-call(f32[8,1,768]{2,1,0:T(1,128)S(1)} %reshape.55.key_doc, bf16[576,128]{1,0:T(8,128)(2,1)S(1)} %get-tuple-element.51.refs_0_.refs_8_, bf16[576,128]{1,0:T(8,128)(2,1)S(1)} %collective-permute-done.refs_1_.refs_9_, ...), custom_call_target="tpu_custom_call" | custom-call | flops 905969664 | tf_op jit(solution)/shard_map/attend/pallas_call | solution.py:180
  45.8 0.5 collective-permute-start.13
  46.4 6.0 %first_half.3 = (f32[288,8192]{1,0:T(8,128)S(1)}, bf16[512,8192]{1,0:T(8,128)(2,1)S(1)}) custom-call(bf16[288,512]{1,0:T(8,128)(2,1)S(1)} %bitcast.17, bf16[512,8192]{1,0:T(8,128)(2,1)} %near.1, bf16[512,8192]{1,0:T(8,128)(2,1)} %collective-permute-done.11.far), custom_call_target="tpu_custom_call" | custom-call | tf_op jit(solution)/shard_map/first_half/pallas_call | solution.py:210
  52.4 2.6 %project.3 = (bf16[48,4096]{1,0:T(8,128)(2,1)S(1)}, bf16[48,4096]{1,0:T(8,128)(2,1)S(1)}, bf16[48,4096]{1,0:T(8,128)(2,1)S(1)}, bf16[48,4096]{1,0:T(8,128)(2,1)S...) custom-call(bf16[288,512]{1,0:T(8,128)(2,1)S(1)} %bitcast.16, ...), custom_call_target="tpu_custom_call" | custom-call | tf_op jit(solution)/shard_map/project/pallas_call | solution.py:239
  55.0 1.6 %collective-permute-start.23 = (bf16[48,4096]{1,0:T(8,128)(2,1)S(1)}, bf16[48,4096]{1,0:T(8,128)(2,1)S(1)}, u32[]{:S(2)}, u32[]{:S(2)}) collective-permute-start(bf16[48,4096]{1,0:T(8,128)(2,1)S(1)} %get-tuple-element.92), channel_id=1, source_target_pairs={{0,8},{4,12},{8,0},{12,4},{1,9},{5,13},{9,1},{13,5},{2,10},{6,14},... | collective-permute-start | bytes 1179656 | tf_op jit(solution)/shard_map/ppermute | solution.py:367
  56.6 1.1 add_convert_fusion.5
  57.7 3.9 %collective-permute-start.26 = (bf16[48,4096]{1,0:T(8,128)(2,1)S(1)}, bf16[48,4096]{1,0:T(8,128)(2,1)S(1)}, u32[]{:S(2)}, u32[]{:S(2)}) collective-permute-start(bf16[48,4096]{1,0:T(8,128)(2,1)S(1)} %add_convert_fusion.5), channel_id=1, source_target_pairs={{0,1},{3,2},{4,5},{7,6},{8,9},{11,10},{12,13},{15,14},{16,17},{19,... | collective-permute-start | bytes 1179656 | tf_op jit(solution)/shard_map/ppermute | solution.py:384
  61.6 1.6 %collective-permute-start.14 = (bf16[48,4096]{1,0:T(8,128)(2,1)S(1)}, bf16[48,4096]{1,0:T(8,128)(2,1)S(1)}, u32[]{:S(2)}, u32[]{:S(2)}) collective-permute-start(bf16[48,4096]{1,0:T(8,128)(2,1)S(1)} %get-tuple-element.83), channel_id=1, source_target_pairs={{0,8},{4,12},{8,0},{12,4},{1,9},{5,13},{9,1},{13,5},{2,10},{6,14},... | collective-permute-start | bytes 1179656 | tf_op jit(solution)/shard_map/ppermute | solution.py:367
  63.2 1.3 %collective-permute-start.17 = (bf16[48,4096]{1,0:T(8,128)(2,1)S(1)}, bf16[48,4096]{1,0:T(8,128)(2,1)S(1)}, u32[]{:S(2)}, u32[]{:S(2)}) collective-permute-start(bf16[48,4096]{1,0:T(8,128)(2,1)S(1)} %add_convert_fusion.13), channel_id=1, source_target_pairs={{0,1},{3,2},{4,5},{7,6},{8,9},{11,10},{12,13},{15,14},{16,17},{19,... | collective-permute-start | bytes 1179656 | tf_op jit(solution)/shard_map/ppermute | solution.py:384
  64.5 2.5 %collective-permute-done.23 = bf16[48,4096]{1,0:T(8,128)(2,1)S(1)} collective-permute-done((bf16[48,4096]{1,0:T(8,128)(2,1)S(1)}, bf16[48,4096]{1,0:T(8,128)(2,1)S(1)}, u32[]{:S(2)}, u32[]{:S(2)}) %collective-permute-start.23) | collective-permute-done | bytes 393248 | tf_op jit(solution)/shard_map/ppermute | solution.py:367
  67.2 4.8 %collective-permute-start.29 = (bf16[48,4096]{1,0:T(8,128)(2,1)S(1)}, bf16[48,4096]{1,0:T(8,128)(2,1)S(1)}, u32[]{:S(2)}, u32[]{:S(2)}) collective-permute-start(bf16[48,4096]{1,0:T(8,128)(2,1)S(1)} %add_convert_fusion.2), channel_id=1, source_target_pairs={{0,1},{3,2},{4,5},{7,6},{8,9},{11,10},{12,13},{15,14},{16,17},{19,... | collective-permute-start | bytes 1179656 | tf_op jit(solution)/shard_map/ppermute | solution.py:384
  72.1 0.7 collective-permute-start.27
  72.8 0.6 collective-permute-start.24
  73.4 2.0 %collective-permute-done.14 = bf16[48,4096]{1,0:T(8,128)(2,1)S(1)} collective-permute-done((bf16[48,4096]{1,0:T(8,128)(2,1)S(1)}, bf16[48,4096]{1,0:T(8,128)(2,1)S(1)}, u32[]{:S(2)}, u32[]{:S(2)}) %collective-permute-start.14) | collective-permute-done | bytes 393248 | tf_op jit(solution)/shard_map/ppermute | solution.py:367
  75.5 5.0 %collective-permute-start.20 = (bf16[48,4096]{1,0:T(8,128)(2,1)S(1)}, bf16[48,4096]{1,0:T(8,128)(2,1)S(1)}, u32[]{:S(2)}, u32[]{:S(2)}) collective-permute-start(bf16[48,4096]{1,0:T(8,128)(2,1)S(1)} %add_convert_fusion.10), channel_id=1, source_target_pairs={{0,1},{3,2},{4,5},{7,6},{8,9},{11,10},{12,13},{15,14},{16,17},{19,... | collective-permute-start | bytes 1179656 | tf_op jit(solution)/shard_map/ppermute | solution.py:384
  80.5 0.7 collective-permute-start.18
  81.2 6.7 %collective-permute-done.29 = bf16[48,4096]{1,0:T(8,128)(2,1)S(1)} collective-permute-done((bf16[48,4096]{1,0:T(8,128)(2,1)S(1)}, bf16[48,4096]{1,0:T(8,128)(2,1)S(1)}, u32[]{:S(2)}, u32[]{:S(2)}) %collective-permute-start.29) | collective-permute-done | bytes 393248 | tf_op jit(solution)/shard_map/ppermute | solution.py:384
  87.9 1.5 %collective-permute-start.15 = (bf16[48,4096]{1,0:T(8,128)(2,1)S(1)}, bf16[48,4096]{1,0:T(8,128)(2,1)S(1)}, u32[]{:S(2)}, u32[]{:S(2)}) collective-permute-start(bf16[48,4096]{1,0:T(8,128)(2,1)S(1)} %get-tuple-element.84), channel_id=1, source_target_pairs={{0,8},{4,12},{8,0},{12,4},{1,9},{5,13},{9,1},{13,5},{2,10},{6,14},... | collective-permute-start | bytes 1179656 | tf_op jit(solution)/shard_map/ppermute | solution.py:367
  89.5 0.7 collective-permute-start.30
  90.4 3.8 %collective-permute-start.28 = (bf16[48,4096]{1,0:T(8,128)(2,1)S(1)}, bf16[48,4096]{1,0:T(8,128)(2,1)S(1)}, u32[]{:S(2)}, u32[]{:S(2)}) collective-permute-start(bf16[48,4096]{1,0:T(8,128)(2,1)S(1)} %fusion.1), channel_id=1, source_target_pairs={{0,1},{3,2},{1,0},{2,3},{4,5},{7,6},{5,4},{6,7},{8,9},{11,10},{9,8... | collective-permute-start | bytes 1179656 | tf_op jit(solution)/shard_map/ppermute | solution.py:384
  94.2 2.2 %collective-permute-done.20 = bf16[48,4096]{1,0:T(8,128)(2,1)S(1)} collective-permute-done((bf16[48,4096]{1,0:T(8,128)(2,1)S(1)}, bf16[48,4096]{1,0:T(8,128)(2,1)S(1)}, u32[]{:S(2)}, u32[]{:S(2)}) %collective-permute-start.20) | collective-permute-done | bytes 393248 | tf_op jit(solution)/shard_map/ppermute | solution.py:384
  96.3 1.5 %collective-permute-start.25 = (bf16[48,4096]{1,0:T(8,128)(2,1)S(1)}, bf16[48,4096]{1,0:T(8,128)(2,1)S(1)}, u32[]{:S(2)}, u32[]{:S(2)}) collective-permute-start(bf16[48,4096]{1,0:T(8,128)(2,1)S(1)} %get-tuple-element.94), channel_id=1, source_target_pairs={{0,8},{4,12},{8,0},{12,4},{1,9},{5,13},{9,1},{13,5},{2,10},{6,14},... | collective-permute-start | bytes 1179656 | tf_op jit(solution)/shard_map/ppermute | solution.py:367
  97.9 0.7 collective-permute-start.21
  98.8 3.8 %collective-permute-start.19 = (bf16[48,4096]{1,0:T(8,128)(2,1)S(1)}, bf16[48,4096]{1,0:T(8,128)(2,1)S(1)}, u32[]{:S(2)}, u32[]{:S(2)}) collective-permute-start(bf16[48,4096]{1,0:T(8,128)(2,1)S(1)} %fusion), channel_id=1, source_target_pairs={{0,1},{3,2},{1,0},{2,3},{4,5},{7,6},{5,4},{6,7},{8,9},{11,10},{9,8... | collective-permute-start | bytes 1179656 | tf_op jit(solution)/shard_map/ppermute | solution.py:384
  102.6 0.5 collective-permute-start.16
  103.1 1.6 %collective-permute-done.28 = bf16[48,4096]{1,0:T(8,128)(2,1)S(1)} collective-permute-done((bf16[48,4096]{1,0:T(8,128)(2,1)S(1)}, bf16[48,4096]{1,0:T(8,128)(2,1)S(1)}, u32[]{:S(2)}, u32[]{:S(2)}) %collective-permute-start.28) | collective-permute-done | bytes 393248 | tf_op jit(solution)/shard_map/ppermute | solution.py:384
  104.7 3.1 %collective-permute-done.25 = bf16[48,4096]{1,0:T(8,128)(2,1)S(1)} collective-permute-done((bf16[48,4096]{1,0:T(8,128)(2,1)S(1)}, bf16[48,4096]{1,0:T(8,128)(2,1)S(1)}, u32[]{:S(2)}, u32[]{:S(2)}) %collective-permute-start.25) | collective-permute-done | bytes 393248 | tf_op jit(solution)/shard_map/ppermute | solution.py:367
  108.1 4.0 %collective-permute-done.19 = bf16[48,4096]{1,0:T(8,128)(2,1)S(1)} collective-permute-done((bf16[48,4096]{1,0:T(8,128)(2,1)S(1)}, bf16[48,4096]{1,0:T(8,128)(2,1)S(1)}, u32[]{:S(2)}, u32[]{:S(2)}) %collective-permute-start.19) | collective-permute-done | bytes 393248 | tf_op jit(solution)/shard_map/ppermute | solution.py:384
  112.1 1.6 %collective-permute-done.16 = bf16[48,4096]{1,0:T(8,128)(2,1)S(1)} collective-permute-done((bf16[48,4096]{1,0:T(8,128)(2,1)S(1)}, bf16[48,4096]{1,0:T(8,128)(2,1)S(1)}, u32[]{:S(2)}, u32[]{:S(2)}) %collective-permute-start.16) | collective-permute-done | bytes 393248 | tf_op jit(solution)/shard_map/ppermute | solution.py:367
  113.9 0.9 pad_maximum_fusion
  (49 shorter events, 2.8 us)
Async XLA Ops:
  0.0 32.3 %collective-permute-start.11 = (bf16[512,8192]{1,0:T(8,128)(2,1)}, bf16[512,8192]{1,0:T(8,128)(2,1)}, u32[]{:S(2)}, u32[]{:S(2)}) collective-permute-start(bf16[512,8192]{1,0:T(8,128)(2,1)} %near.1), channel_id=1, source_target_pairs={{0,4},{4,0},{8,12},{12,8},{1,5},{5,1},{9,13},{13,9},{2,6},{6,2},{1... | collective-permute-start | bytes 25165832 | tf_op jit(solution)/shard_map/ppermute | solution.py:282
  1.9 11.8 %collective-permute-start = (bf16[576,128]{1,0:T(8,128)(2,1)S(1)}, bf16[576,128]{1,0:T(8,128)(2,1)S(1)}, u32[]{:S(2)}, u32[]{:S(2)}) collective-permute-start(bf16[576,128]{1,0:T(8,128)(2,1)S(1)} %get-tuple-element.52), channel_id=1, source_target_pairs={{0,1},{1,2},{2,3},{3,0},{4,5},{5,6},{6,7},{7,4},{8,9},{9,10},{10,1... | collective-permute-start | bytes 442376 | tf_op jit(solution)/shard_map/ppermute | solution.py:265
  4.6 12.9 %collective-permute-start.1 = (bf16[576,128]{1,0:T(8,128)(2,1)S(1)}, bf16[576,128]{1,0:T(8,128)(2,1)S(1)}, u32[]{:S(2)}, u32[]{:S(2)}) collective-permute-start(bf16[576,128]{1,0:T(8,128)(2,1)S(1)} %get-tuple-element.53), channel_id=1, source_target_pairs={{0,2},{1,3},{2,0},{3,1},{4,6},{5,7},{6,4},{7,5},{8,10},{9,11},{10,... | collective-permute-start | bytes 442376 | tf_op jit(solution)/shard_map/ppermute | solution.py:265
  7.1 13.9 %collective-permute-start.2 = (bf16[576,128]{1,0:T(8,128)(2,1)S(1)}, bf16[576,128]{1,0:T(8,128)(2,1)S(1)}, u32[]{:S(2)}, u32[]{:S(2)}) collective-permute-start(bf16[576,128]{1,0:T(8,128)(2,1)S(1)} %get-tuple-element.54), channel_id=1, source_target_pairs={{0,3},{1,0},{2,1},{3,2},{4,7},{5,4},{6,5},{7,6},{8,11},{9,8},{10,9... | collective-permute-start | bytes 442376 | tf_op jit(solution)/shard_map/ppermute | solution.py:265
  8.5 13.9 %collective-permute-start.3 = (bf16[384,128]{1,0:T(8,128)(2,1)S(1)}, bf16[384,128]{1,0:T(8,128)(2,1)S(1)}, u32[]{:S(2)}, u32[]{:S(2)}) collective-permute-start(bf16[384,128]{1,0:T(8,128)(2,1)S(1)} %slice.40), channel_id=1, source_target_pairs={{0,16},{1,17},{2,18},{3,19},{4,20},{5,21},{6,22},{7,23},{8,24},{9,... | collective-permute-start | bytes 294920 | tf_op jit(solution)/shard_map/ppermute | solution.py:280
  13.7 10.9 %collective-permute-start.4 = (bf16[384,128]{1,0:T(8,128)(2,1)S(1)}, bf16[384,128]{1,0:T(8,128)(2,1)S(1)}, u32[]{:S(2)}, u32[]{:S(2)}) collective-permute-start(bf16[384,128]{1,0:T(8,128)(2,1)S(1)} %slice.44), channel_id=1, source_target_pairs={{0,16},{1,17},{2,18},{3,19},{4,20},{5,21},{6,22},{7,23},{8,24},{9,... | collective-permute-start | bytes 294920 | tf_op jit(solution)/shard_map/ppermute | solution.py:280
  17.5 10.2 %collective-permute-start.5 = (bf16[384,128]{1,0:T(8,128)(2,1)S(1)}, bf16[384,128]{1,0:T(8,128)(2,1)S(1)}, u32[]{:S(2)}, u32[]{:S(2)}) collective-permute-start(bf16[384,128]{1,0:T(8,128)(2,1)S(1)} %slice.45), channel_id=1, source_target_pairs={{0,16},{1,17},{2,18},{3,19},{4,20},{5,21},{6,22},{7,23},{8,24},{9,... | collective-permute-start | bytes 294920 | tf_op jit(solution)/shard_map/ppermute | solution.py:280
  21.1 7.7 %collective-permute-start.6 = (bf16[384,128]{1,0:T(8,128)(2,1)S(1)}, bf16[384,128]{1,0:T(8,128)(2,1)S(1)}, u32[]{:S(2)}, u32[]{:S(2)}) collective-permute-start(bf16[384,128]{1,0:T(8,128)(2,1)S(1)} %slice.46), channel_id=1, source_target_pairs={{0,16},{1,17},{2,18},{3,19},{4,20},{5,21},{6,22},{7,23},{8,24},{9,... | collective-permute-start | bytes 294920 | tf_op jit(solution)/shard_map/ppermute | solution.py:280
  22.4 16.3 %collective-permute-start.7 = (bf16[576,128]{1,0:T(8,128)(2,1)S(1)}, bf16[576,128]{1,0:T(8,128)(2,1)S(1)}, u32[]{:S(2)}, u32[]{:S(2)}) collective-permute-start(bf16[576,128]{1,0:T(8,128)(2,1)S(1)} %get-tuple-element.57), channel_id=1, source_target_pairs={{0,1},{1,2},{2,3},{3,0},{4,5},{5,6},{6,7},{7,4},{8,9},{9,10},{10,1... | collective-permute-start | bytes 442376 | tf_op jit(solution)/shard_map/ppermute | solution.py:265
  24.7 14.1 %collective-permute-start.8 = (bf16[576,128]{1,0:T(8,128)(2,1)S(1)}, bf16[576,128]{1,0:T(8,128)(2,1)}, u32[]{:S(2)}, u32[]{:S(2)}) collective-permute-start(bf16[576,128]{1,0:T(8,128)(2,1)S(1)} %get-tuple-element.59), channel_id=1, source_target_pairs={{0,2},{1,3},{2,0},{3,1},{4,6},{5,7},{6,4},{7,5},{8,10},{9,11},{10,... | collective-permute-start | bytes 442376 | tf_op jit(solution)/shard_map/ppermute | solution.py:265
  27.7 11.0 %collective-permute-start.9 = (bf16[576,128]{1,0:T(8,128)(2,1)S(1)}, bf16[576,128]{1,0:T(8,128)(2,1)}, u32[]{:S(2)}, u32[]{:S(2)}) collective-permute-start(bf16[576,128]{1,0:T(8,128)(2,1)S(1)} %get-tuple-element.61), channel_id=1, source_target_pairs={{0,3},{1,0},{2,1},{3,2},{4,7},{5,4},{6,5},{7,6},{8,11},{9,8},{10,9... | collective-permute-start | bytes 442376 | tf_op jit(solution)/shard_map/ppermute | solution.py:265
  32.2 3.5 %collective-permute-start.10 = (bf16[2,48,512]{2,1,0:T(8,128)(2,1)S(1)}, bf16[2,48,512]{2,1,0:T(8,128)(2,1)S(1)}, u32[]{:S(2)}, u32[]{:S(2)}) collective-permute-start(bf16[2,48,512]{2,1,0:T(8,128)(2,1)S(1)} %get-tuple-element.62), channel_id=1, source_target_pairs={{0,4},{4,0},{8,12},{12,8},{1,5},{5,1},{9,13},{13,9},{2,6},{6,2},{1... | collective-permute-start | bytes 294920 | tf_op jit(solution)/shard_map/ppermute | solution.py:333
  37.1 17.9 %collective-permute-start.22 = (bf16[48,4096]{1,0:T(8,128)(2,1)S(1)}, bf16[48,4096]{1,0:T(8,128)(2,1)}, u32[]{:S(2)}, u32[]{:S(2)}) collective-permute-start(bf16[48,4096]{1,0:T(8,128)(2,1)S(1)} %get-tuple-element.70), channel_id=1, source_target_pairs={{0,8},{4,12},{8,0},{12,4},{1,9},{5,13},{9,1},{13,5},{2,10},{6,14},... | collective-permute-start | bytes 1179656 | tf_op jit(solution)/shard_map/ppermute | solution.py:367
  45.6 6.8 %collective-permute-start.12 = (bf16[2,144,512]{2,1,0:T(8,128)(2,1)S(1)}, bf16[2,144,512]{2,1,0:T(8,128)(2,1)S(1)}, u32[]{:S(2)}, u32[]{:S(2)}) collective-permute-start(bf16[2,144,512]{2,1,0:T(8,128)(2,1)S(1)} %get-tuple-element.75), channel_id=1, source_target_pairs={{0,4},{4,0},{8,12},{12,8},{1,5},{5,1},{9,13},{13,9},{2,6},{6,2},{1... | collective-permute-start | bytes 884744 | tf_op jit(solution)/shard_map/ppermute | solution.py:333
  45.8 15.7 %collective-permute-start.13 = (bf16[48,4096]{1,0:T(8,128)(2,1)S(1)}, bf16[48,4096]{1,0:T(8,128)(2,1)S(1)}, u32[]{:S(2)}, u32[]{:S(2)}) collective-permute-start(bf16[48,4096]{1,0:T(8,128)(2,1)S(1)} %get-tuple-element.69), channel_id=1, source_target_pairs={{0,8},{4,12},{8,0},{12,4},{1,9},{5,13},{9,1},{13,5},{2,10},{6,14},... | collective-permute-start | bytes 1179656 | tf_op jit(solution)/shard_map/ppermute | solution.py:367
  55.0 12.0 %collective-permute-start.23 = (bf16[48,4096]{1,0:T(8,128)(2,1)S(1)}, bf16[48,4096]{1,0:T(8,128)(2,1)S(1)}, u32[]{:S(2)}, u32[]{:S(2)}) collective-permute-start(bf16[48,4096]{1,0:T(8,128)(2,1)S(1)} %get-tuple-element.92), channel_id=1, source_target_pairs={{0,8},{4,12},{8,0},{12,4},{1,9},{5,13},{9,1},{13,5},{2,10},{6,14},... | collective-permute-start | bytes 1179656 | tf_op jit(solution)/shard_map/ppermute | solution.py:367
  57.7 14.3 %collective-permute-start.26 = (bf16[48,4096]{1,0:T(8,128)(2,1)S(1)}, bf16[48,4096]{1,0:T(8,128)(2,1)S(1)}, u32[]{:S(2)}, u32[]{:S(2)}) collective-permute-start(bf16[48,4096]{1,0:T(8,128)(2,1)S(1)} %add_convert_fusion.5), channel_id=1, source_target_pairs={{0,1},{3,2},{4,5},{7,6},{8,9},{11,10},{12,13},{15,14},{16,17},{19,... | collective-permute-start | bytes 1179656 | tf_op jit(solution)/shard_map/ppermute | solution.py:384
  61.6 13.8 %collective-permute-start.14 = (bf16[48,4096]{1,0:T(8,128)(2,1)S(1)}, bf16[48,4096]{1,0:T(8,128)(2,1)S(1)}, u32[]{:S(2)}, u32[]{:S(2)}) collective-permute-start(bf16[48,4096]{1,0:T(8,128)(2,1)S(1)} %get-tuple-element.83), channel_id=1, source_target_pairs={{0,8},{4,12},{8,0},{12,4},{1,9},{5,13},{9,1},{13,5},{2,10},{6,14},... | collective-permute-start | bytes 1179656 | tf_op jit(solution)/shard_map/ppermute | solution.py:367
  63.2 17.2 %collective-permute-start.17 = (bf16[48,4096]{1,0:T(8,128)(2,1)S(1)}, bf16[48,4096]{1,0:T(8,128)(2,1)S(1)}, u32[]{:S(2)}, u32[]{:S(2)}) collective-permute-start(bf16[48,4096]{1,0:T(8,128)(2,1)S(1)} %add_convert_fusion.13), channel_id=1, source_target_pairs={{0,1},{3,2},{4,5},{7,6},{8,9},{11,10},{12,13},{15,14},{16,17},{19,... | collective-permute-start | bytes 1179656 | tf_op jit(solution)/shard_map/ppermute | solution.py:384
  67.2 20.7 %collective-permute-start.29 = (bf16[48,4096]{1,0:T(8,128)(2,1)S(1)}, bf16[48,4096]{1,0:T(8,128)(2,1)S(1)}, u32[]{:S(2)}, u32[]{:S(2)}) collective-permute-start(bf16[48,4096]{1,0:T(8,128)(2,1)S(1)} %add_convert_fusion.2), channel_id=1, source_target_pairs={{0,1},{3,2},{4,5},{7,6},{8,9},{11,10},{12,13},{15,14},{16,17},{19,... | collective-permute-start | bytes 1179656 | tf_op jit(solution)/shard_map/ppermute | solution.py:384
  72.1 17.4 %collective-permute-start.27 = (bf16[48,4096]{1,0:T(8,128)(2,1)S(1)}, bf16[48,4096]{1,0:T(8,128)(2,1)S(1)}, u32[]{:S(2)}, u32[]{:S(2)}) collective-permute-start(bf16[48,4096]{1,0:T(8,128)(2,1)S(1)} %add_convert_fusion.4), channel_id=1, source_target_pairs={{1,2},{2,1},{5,6},{6,5},{9,10},{10,9},{13,14},{14,13},{17,18},{18,... | collective-permute-start | bytes 1179656 | tf_op jit(solution)/shard_map/ppermute | solution.py:384
  72.8 17.4 %collective-permute-start.24 = (bf16[48,4096]{1,0:T(8,128)(2,1)S(1)}, bf16[48,4096]{1,0:T(8,128)(2,1)S(1)}, u32[]{:S(2)}, u32[]{:S(2)}) collective-permute-start(bf16[48,4096]{1,0:T(8,128)(2,1)S(1)} %get-tuple-element.93), channel_id=1, source_target_pairs={{0,8},{4,12},{8,0},{12,4},{1,9},{5,13},{9,1},{13,5},{2,10},{6,14},... | collective-permute-start | bytes 1179656 | tf_op jit(solution)/shard_map/ppermute | solution.py:367
  75.5 20.9 %collective-permute-start.20 = (bf16[48,4096]{1,0:T(8,128)(2,1)S(1)}, bf16[48,4096]{1,0:T(8,128)(2,1)S(1)}, u32[]{:S(2)}, u32[]{:S(2)}) collective-permute-start(bf16[48,4096]{1,0:T(8,128)(2,1)S(1)} %add_convert_fusion.10), channel_id=1, source_target_pairs={{0,1},{3,2},{4,5},{7,6},{8,9},{11,10},{12,13},{15,14},{16,17},{19,... | collective-permute-start | bytes 1179656 | tf_op jit(solution)/shard_map/ppermute | solution.py:384
  80.5 17.4 %collective-permute-start.18 = (bf16[48,4096]{1,0:T(8,128)(2,1)S(1)}, bf16[48,4096]{1,0:T(8,128)(2,1)S(1)}, u32[]{:S(2)}, u32[]{:S(2)}) collective-permute-start(bf16[48,4096]{1,0:T(8,128)(2,1)S(1)} %add_convert_fusion.12), channel_id=1, source_target_pairs={{1,2},{2,1},{5,6},{6,5},{9,10},{10,9},{13,14},{14,13},{17,18},{18,... | collective-permute-start | bytes 1179656 | tf_op jit(solution)/shard_map/ppermute | solution.py:384
  87.9 10.7 %collective-permute-start.15 = (bf16[48,4096]{1,0:T(8,128)(2,1)S(1)}, bf16[48,4096]{1,0:T(8,128)(2,1)S(1)}, u32[]{:S(2)}, u32[]{:S(2)}) collective-permute-start(bf16[48,4096]{1,0:T(8,128)(2,1)S(1)} %get-tuple-element.84), channel_id=1, source_target_pairs={{0,8},{4,12},{8,0},{12,4},{1,9},{5,13},{9,1},{13,5},{2,10},{6,14},... | collective-permute-start | bytes 1179656 | tf_op jit(solution)/shard_map/ppermute | solution.py:367
  89.5 13.1 %collective-permute-start.30 = (bf16[48,4096]{1,0:T(8,128)(2,1)S(1)}, bf16[48,4096]{1,0:T(8,128)(2,1)S(1)}, u32[]{:S(2)}, u32[]{:S(2)}) collective-permute-start(bf16[48,4096]{1,0:T(8,128)(2,1)S(1)} %add_convert_fusion.1), channel_id=1, source_target_pairs={{1,2},{2,1},{5,6},{6,5},{9,10},{10,9},{13,14},{14,13},{17,18},{18,... | collective-permute-start | bytes 1179656 | tf_op jit(solution)/shard_map/ppermute | solution.py:384
  90.4 14.4 %collective-permute-start.28 = (bf16[48,4096]{1,0:T(8,128)(2,1)S(1)}, bf16[48,4096]{1,0:T(8,128)(2,1)S(1)}, u32[]{:S(2)}, u32[]{:S(2)}) collective-permute-start(bf16[48,4096]{1,0:T(8,128)(2,1)S(1)} %fusion.1), channel_id=1, source_target_pairs={{0,1},{3,2},{1,0},{2,3},{4,5},{7,6},{5,4},{6,7},{8,9},{11,10},{9,8... | collective-permute-start | bytes 1179656 | tf_op jit(solution)/shard_map/ppermute | solution.py:384
  96.3 11.6 %collective-permute-start.25 = (bf16[48,4096]{1,0:T(8,128)(2,1)S(1)}, bf16[48,4096]{1,0:T(8,128)(2,1)S(1)}, u32[]{:S(2)}, u32[]{:S(2)}) collective-permute-start(bf16[48,4096]{1,0:T(8,128)(2,1)S(1)} %get-tuple-element.94), channel_id=1, source_target_pairs={{0,8},{4,12},{8,0},{12,4},{1,9},{5,13},{9,1},{13,5},{2,10},{6,14},... | collective-permute-start | bytes 1179656 | tf_op jit(solution)/shard_map/ppermute | solution.py:367
  97.9 10.2 %collective-permute-start.21 = (bf16[48,4096]{1,0:T(8,128)(2,1)S(1)}, bf16[48,4096]{1,0:T(8,128)(2,1)S(1)}, u32[]{:S(2)}, u32[]{:S(2)}) collective-permute-start(bf16[48,4096]{1,0:T(8,128)(2,1)S(1)} %add_convert_fusion.9), channel_id=1, source_target_pairs={{1,2},{2,1},{5,6},{6,5},{9,10},{10,9},{13,14},{14,13},{17,18},{18,... | collective-permute-start | bytes 1179656 | tf_op jit(solution)/shard_map/ppermute | solution.py:384
  98.8 13.3 %collective-permute-start.19 = (bf16[48,4096]{1,0:T(8,128)(2,1)S(1)}, bf16[48,4096]{1,0:T(8,128)(2,1)S(1)}, u32[]{:S(2)}, u32[]{:S(2)}) collective-permute-start(bf16[48,4096]{1,0:T(8,128)(2,1)S(1)} %fusion), channel_id=1, source_target_pairs={{0,1},{3,2},{1,0},{2,3},{4,5},{7,6},{5,4},{6,7},{8,9},{11,10},{9,8... | collective-permute-start | bytes 1179656 | tf_op jit(solution)/shard_map/ppermute | solution.py:384
  102.6 11.1 %collective-permute-start.16 = (bf16[48,4096]{1,0:T(8,128)(2,1)S(1)}, bf16[48,4096]{1,0:T(8,128)(2,1)S(1)}, u32[]{:S(2)}, u32[]{:S(2)}) collective-permute-start(bf16[48,4096]{1,0:T(8,128)(2,1)S(1)} %get-tuple-element.85), channel_id=1, source_target_pairs={{0,8},{4,12},{8,0},{12,4},{1,9},{5,13},{9,1},{13,5},{2,10},{6,14},... | collective-permute-start | bytes 1179656 | tf_op jit(solution)/shard_map/ppermute | solution.py:367

commit v10 on v9

--- a/solution.py
+++ b/solution.py
@@ -22,7 +22,16 @@
 HBM = pl.BlockSpec(memory_space=pltpu.HBM)
 LIMIT = pltpu.CompilerParams(vmem_limit_bytes=18 << 20)
 TILE = 1024
+HALVES = 2
+UNDER_WAY = 2
+ATTEND_US = {0: 1.0, 1: 0.84, 2: 1.05}
+FIRST_HALF_US = {True: 1.02, False: 1.74}
+PROJECT_US = {1: 0.45, 2: 0.45}
 FREE = pl.CostEstimate(flops=0, bytes_accessed=0, transcendentals=0)
+
+
+def worth(us):
+    return pl.CostEstimate(flops=int(us * 1.15e9), bytes_accessed=0, transcendentals=0)
 
 
 def destination_order(count):
@@ -104,7 +113,7 @@
     )(in_hbm(queries), in_hbm(keys), in_hbm(values))
 
 
-def attend_kernel(key_doc, *refs, slabs, heads, share, stage, order, offset, columns_x, per_shard, fetched):
+def attend_kernel(key_doc, *refs, slabs, heads, share, stage, stages, order, offset, columns_x, per_shard, fetched):
     refs = list(refs)
     take = lambda n: [refs.pop(0) for _ in range(n)]
     now, before, queries, weights = take(slabs), take(slabs), take(slabs), take(fetched)
@@ -123,6 +132,7 @@
     row = lax.broadcasted_iota(jnp.int32, (share, span), 0)
     behind = [column - row - (0 if share == block else chosen(order, z, i) * share) for i in stage]
     causal = joined([b <= 0 for b in behind])
+    places = [offset + (h * len(stages) + stages.index(stage[0])) * share for h in range(heads)]
     for k in range(slabs):
         slab = lax.rem(z - k + slabs, slabs)
         for o in range(SLAB_REACH):
@@ -142,7 +152,7 @@
         query_doc = joined([jnp.max(jnp.where(b == 0, docs, -2.0), axis=1, keepdims=True) for b in behind])
         visible = causal & (query_doc == docs)
         scores = lax.dot_general(
-            queries[k][offset : offset + heads * rows, :],
+            joined([queries[k][start : start + rows, :] for start in places]),
             key_rows[...],
             (((1,), (1,)), ((), ())),
             preferred_element_type=F32,
@@ -187,7 +197,7 @@
         scratch_shapes=[pltpu.VMEM((span, HEAD_SIZE), BF16)] * 2
         + [pltpu.SemaphoreType.DMA((fetched,))] * (fetched > 0),
         compiler_params=LIMIT,
-        cost_estimate=pl.CostEstimate(flops=4 * terms * HEAD_SIZE, bytes_accessed=0, transcendentals=terms),
+        cost_estimate=worth(ATTEND_US[0 if stage[0] == 0 else min(len(stage), 2)]),
         name="attend",
     )(key_doc, *now, *before, *queries, *[in_hbm(w) for w in weights])
 
@@ -214,37 +224,53 @@
         out_specs=[VMEM, VMEM],
         scratch_shapes=[pltpu.SemaphoreType.DMA((2,))] + [pltpu.VMEM(near.shape, near.dtype)] * (not near_held),
         compiler_params=LIMIT,
-        cost_estimate=FREE,
+        cost_estimate=worth(FIRST_HALF_US[near_held]),
         name="first_half",
     )(rows_here, in_vmem(near) if near_held else in_hbm(near), in_hbm(far))
 
 
-def project_kernel(*refs, terms, begun, share, halves):
+def project_kernel(*refs, terms, begun, share, splits, columns_x):
     lhs, rhs, start = refs[:terms], refs[terms : 2 * terms], refs[2 * terms : 2 * terms + begun]
     outs = refs[2 * terms + begun :]
-    half = outs[0].shape[1]
-    for n in range(0, half * halves, TILE):
+    width = rhs[0].shape[1]
+    for n in range(0, width, TILE):
         total = sum(
             jnp.dot(a[...], w[:, n : n + TILE], preferred_element_type=F32) for a, w in zip(lhs, rhs)
         )
         for s in start:
             total = total + s[:, n : n + TILE]
-        for m in range(total.shape[0] // share):
-            outs[m * halves + n // half][:, n % half : n % half + TILE] = total[m * share : (m + 1) * share].astype(BF16)
-
-
-def project(lhs, rhs, start, share, halves):
-    count, depth = lhs[0].shape
+        place = 0
+        for i, split in enumerate(splits):
+            part = width // split
+            for k in range(columns_x):
+                row = (k * len(splits) + i) * share
+                out = outs[place + k * split + n // part]
+                out[:, n % part : n % part + TILE] = total[row : row + share].astype(BF16)
+            place += columns_x * split
+
+
+def project(lhs, rhs, start, share, splits):
     width = rhs[0].shape[1]
-    return pl.pallas_call(
-        partial(project_kernel, terms=len(lhs), begun=len(start), share=share, halves=halves),
-        out_shape=[jax.ShapeDtypeStruct((share, width // halves), BF16)] * (count // share * halves),
+    columns_x = lhs[0].shape[0] // (share * len(splits))
+    shapes = [
+        jax.ShapeDtypeStruct((share, width // split), BF16) for split in splits for _ in range(columns_x * split)
+    ]
+    results = pl.pallas_call(
+        partial(
+            project_kernel, terms=len(lhs), begun=len(start), share=share, splits=splits, columns_x=columns_x
+        ),
+        out_shape=shapes,
         in_specs=[VMEM] * (2 * len(lhs) + len(start)),
-        out_specs=[VMEM] * (count // share * halves),
+        out_specs=[VMEM] * len(shapes),
         compiler_params=LIMIT,
-        cost_estimate=FREE,
+        cost_estimate=worth(PROJECT_US[min(len(splits), 2)]),
         name="project",
     )(*lhs, *[in_vmem(w) for w in rhs], *[in_vmem(s) for s in start])
+    pieces = []
+    for split in splits:
+        pieces.append([results[k * split : (k + 1) * split] for k in range(columns_x)])
+        results = results[columns_x * split :]
+    return pieces
 
 
 def on_device(queries, keys, values, doc_ids, block_mask, out_weight, *, order):
@@ -257,8 +283,8 @@
     per_shard = slabs // head_shards
     staged = per_shard == 1
     stages = [[0], list(range(1, slabs))] if staged else [[0]]
+    rounds = [[0], list(range(1, slabs - 1)), [slabs - 1]] if staged and slabs > 2 else stages
     rows_at_once = share if staged else block
-    halves = 2
     siblings = [(h, h ^ 1) for h in range(head_shards)]
 
     def around(array, k):
@@ -295,11 +321,58 @@
         axis=1,
     ).reshape(count, 1, SLAB_REACH * block)
 
+    position = np.argsort(order, axis=1)
+    middle = slabs // 2 - 1
+
+    def inward(c):
+        return [(c, c + 1), (slabs - 1 - c, slabs - 2 - c)]
+
+    def outward(c):
+        return [(b, a) for a, b in inward(c)]
+
+    def add(*terms):
+        return sum(a.astype(F32) for a in terms).astype(BF16)
+
+    routes = [[(h, (h + 2 * k) % head_shards) for h in range(head_shards)] for k in range(columns_x)]
+    sums, crossed, sent = [], [], []
+
+    def cross(t):
+        own, *others = partials[t]
+        total = [None] * HALVES
+        for n in range(HALVES):
+            pieces = [other[n] for other in others]
+            if len(crossed) >= UNDER_WAY:
+                pieces = [after(piece, *crossed[-UNDER_WAY]) for piece in pieces]
+            crossed.append([lax.ppermute(a, "head", r) for a, r in zip(pieces, routes[1:])])
+            total[n] = add(own[n], *crossed[-1])
+        sums.append(total)
+
+    def step(t):
+        passed = sent[-1] if sent else {}
+        now = {}
+        for n in range(HALVES):
+            for c in range(min(t, middle) + 1):
+                message = sums[position[c, slabs - 1 - t + c]][n]
+                if c:
+                    message = add(message, passed[c - 1][n])
+                route = inward(c)
+                if c < middle and t >= slabs - 2 - c:
+                    z_out = slabs - 2 - c
+                    back = add(sums[position[z_out, slabs - 1 - t + z_out]][n], passed[c + 1][n])
+                    message = jnp.where((z == c) | (z == slabs - 1 - c), message, back)
+                    route = route + outward(c)
+                now.setdefault(c, {})[n] = lax.ppermute(message, "wsh", route)
+        sent.append(now)
+
     partials = []
     results = None
-    for n, (stage, arrived) in enumerate(zip(stages, stage_queries)):
+    for n, stage in enumerate(rounds):
+        payload = 0 if n == 0 else 1
+        arrived = stage_queries[payload]
         if n:
-            arrived = after(arrived, *results)
+            arrived = after(arrived, *results[0][0])
+        if n > 1:
+            arrived = after(arrived, *crossed[HALVES - 1])
         keep, send, *fetched = attend(
             key_doc,
             loads,
@@ -312,6 +385,7 @@
             stage=stage,
             order=order,
             offset=2 * block if n == 0 else 0,
+            stages=stages[payload],
             columns_x=columns_x,
             per_shard=per_shard,
         )
@@ -332,63 +406,22 @@
             )
         theirs = lax.ppermute(send, "head", siblings)
         keep, theirs = (a.reshape(-1, a.shape[-1]) for a in (keep, theirs))
+        splits = [HALVES] * len(pieces)
         if staged:
             near = fetched[0] if fetched else out_weight
             begun, far = first_half(keep, near, weight_sibling, bool(fetched))
-            results = project([theirs], [far], [begun], share, halves)
+            results = project([theirs], [far], [begun], share, splits)
         else:
-            results = project([keep, theirs], [fetched[0], weight_sibling], [], share, halves)
-        for m in range(len(pieces)):
-            partials.append(
-                [
-                    [results[(k * len(pieces) + m) * halves + half] for half in range(halves)]
-                    for k in range(columns_x)
-                ]
-            )
-
-    position = np.argsort(order, axis=1)
-    middle = slabs // 2 - 1
-
-    def inward(c):
-        return [(c, c + 1), (slabs - 1 - c, slabs - 2 - c)]
-
-    def outward(c):
-        return [(b, a) for a, b in inward(c)]
-
-    sums = [[] for _ in range(halves)]
-    crossed = [None] * halves
-    routes = [[(h, (h + 2 * k) % head_shards) for h in range(head_shards)] for k in range(columns_x)]
-    passed = [{} for _ in range(halves)]
-    for t in range(slabs):
-        for half in range(halves):
-            pieces = [partials[t][k][half] for k in range(1, columns_x)]
-            if t:
-                pieces = [after(piece, *crossed[half]) for piece in pieces]
-            crossed[half] = [lax.ppermute(a, "head", r) for a, r in zip(pieces, routes[1:])]
-            total = sum(a.astype(F32) for a in [partials[t][0][half]] + crossed[half])
-            sums[half].append(total.astype(BF16))
-            if t == slabs - 1:
-                continue
-            now = {}
-            for c in range(min(t, middle) + 1):
-                message = sums[half][position[c, slabs - 1 - t + c]]
-                if c:
-                    message = (message.astype(F32) + passed[half][c - 1].astype(F32)).astype(BF16)
-                route = inward(c)
-                if c < middle and t >= slabs - 2 - c:
-                    z_out = slabs - 2 - c
-                    back = sums[half][position[z_out, slabs - 1 - t + z_out]]
-                    back = (back.astype(F32) + passed[half][c + 1].astype(F32)).astype(BF16)
-                    message = jnp.where((z == c) | (z == slabs - 1 - c), message, back)
-                    route = route + outward(c)
-                now[c] = lax.ppermute(message, "wsh", route)
-            passed[half] = now
+            results = project([keep, theirs], [fetched[0], weight_sibling], [], share, splits)
+        partials += results
+        for t in range(len(sums), len(partials)):
+            cross(t)
+            if t < slabs - 1:
+                step(t)
+
     outs = []
-    for half in range(halves):
-        total = sums[half][-1].astype(F32)
-        for a in passed[half].values():
-            total = total + a.astype(F32)
-        outs.append(total.astype(BF16))
+    for n in range(HALVES):
+        outs.append(add(sums[-1][n], *[a[n] for a in (sent[-1] if sent else {}).values()]))
     return jnp.concatenate(outs, axis=1)
 
 

time: 115 us -> 112 us (0.974)
  Pallas kernels: 25.2 us -> 31.4 us
  starting transfers between devices: 57.6 us -> 52.2 us
  waiting for transfers between devices: 26.2 us -> 21.6 us
    pallas_call x2 -> x3, Pallas kernels: 9.42 us -> 15 us  [first_half(): pl.pallas_call(first_half_kernel, out_shape=[pltpu.VMEM((rows_here.shape[...]
    ppermute x18, starting transfers between devices: 34.6 us -> 29.1 us  [the longest x10 19.7 us: step(): now.setdefault(c, {})[n] = lax.ppermute(message, 'wsh', route)]
    ppermute x18, waiting for transfers between devices: 23.7 us -> 19.3 us  [the longest x10 14.3 us: step(): now.setdefault(c, {})[n] = lax.ppermute(message, 'wsh', route)]
    pallas_call x2 -> x3, Pallas kernels: 4.09 us -> 4.76 us  [project(): pl.pallas_call(partial(project_kernel, terms=len(lhs), begun=len(start),...]
    pallas_call x2 -> x3, Pallas kernels: 10.2 us -> 10.2 us  [attend(): pl.pallas_call(partial(attend_kernel, slabs=slabs, heads=heads, share=sha...]
  transfers between devices with their start and end apart: 31 -> 32, of which waited for: 9 -> 8; matrix products, arithmetic and copies ran while one was open for 4% -> 4% of each run, Pallas kernels for 22% -> 28%
where the time goes in v10:
time: 112 us; the launch traced here: 111 us
  starting transfers between devices  52.2 us (47%)
  Pallas kernels  31.4 us (28%)
  waiting for transfers between devices  21.6 us (19%)
  other arithmetic  5.14 us (5%)
    ppermute x10, starting transfers between devices, step(): now.setdefault(c, {})[n] = lax.ppermute(message, 'wsh', route)  19.7 us
    pallas_call x3, Pallas kernels, first_half(): pl.pallas_call(first_half_kernel, out_shape=[pltpu.VMEM((rows_here.shape[...  15 us
    ppermute x10, waiting for transfers between devices, step(): now.setdefault(c, {})[n] = lax.ppermute(message, 'wsh', route)  14.3 us
    ppermute x6, starting transfers between devices, around(): lax.ppermute(array, 'wsh', [(i, (i + k) % slabs) for i in range(slabs)])  12.9 us
    pallas_call x3, Pallas kernels, attend(): pl.pallas_call(partial(attend_kernel, slabs=slabs, heads=heads, share=sha...  10.2 us
    ppermute x4, starting transfers between devices, on_device(): lax.ppermute(a[:2 * block], 'srv', [(g, g + 1) for g in range(groups - 1)])  9.44 us
    ppermute x8, starting transfers between devices, cross(): lax.ppermute(a, 'head', r)  9.32 us
    ppermute x8, waiting for transfers between devices, cross(): lax.ppermute(a, 'head', r)  5.01 us
  transfers between devices with their start and end apart: 32, of which 8 were waited for; matrix products, arithmetic and copies ran while one was open for 4% of the time, Pallas kernels for 28%

profile of v10, /device:TPU:0, one launch (start us, length us, event | category | flops | bytes accessed | tf_op | source)
XLA Modules:
  0.0 111.2 jit_solution(17545272807101608129)
XLA Ops:
  0.5 1.5 %pack.1 = (bf16[576,128]{1,0:T(8,128)(2,1)S(1)}, bf16[576,128]{1,0:T(8,128)(2,1)S(1)}, bf16[576,128]{1,0:T(8,128)(2,1)S(1)}, bf16[576,128]{1,0:T(8,128)(2,1)S(1)...) custom-call(bf16[192,2048]{1,0:T(8,128)(2,1)} %queries.1, ...), custom_call_target="tpu_custom_call" | custom-call | tf_op jit(solution)/shard_map/pack/pallas_call | solution.py:101
  1.9 2.6 %collective-permute-start = (bf16[576,128]{1,0:T(8,128)(2,1)S(1)}, bf16[576,128]{1,0:T(8,128)(2,1)S(1)}, u32[]{:S(2)}, u32[]{:S(2)}) collective-permute-start(bf16[576,128]{1,0:T(8,128)(2,1)S(1)} %get-tuple-element.64), channel_id=1, source_target_pairs={{0,1},{1,2},{2,3},{3,0},{4,5},{5,6},{6,7},{7,4},{8,9},{9,10},{10,1... | collective-permute-start | bytes 442376 | tf_op jit(solution)/shard_map/ppermute | solution.py:291
  4.6 2.6 %collective-permute-start.1 = (bf16[576,128]{1,0:T(8,128)(2,1)S(1)}, bf16[576,128]{1,0:T(8,128)(2,1)S(1)}, u32[]{:S(2)}, u32[]{:S(2)}) collective-permute-start(bf16[576,128]{1,0:T(8,128)(2,1)S(1)} %get-tuple-element.65), channel_id=1, source_target_pairs={{0,2},{1,3},{2,0},{3,1},{4,6},{5,7},{6,4},{7,5},{8,10},{9,11},{10,... | collective-permute-start | bytes 442376 | tf_op jit(solution)/shard_map/ppermute | solution.py:291
  7.1 1.3 %collective-permute-start.2 = (bf16[576,128]{1,0:T(8,128)(2,1)S(1)}, bf16[576,128]{1,0:T(8,128)(2,1)S(1)}, u32[]{:S(2)}, u32[]{:S(2)}) collective-permute-start(bf16[576,128]{1,0:T(8,128)(2,1)S(1)} %get-tuple-element.66), channel_id=1, source_target_pairs={{0,3},{1,0},{2,1},{3,2},{4,7},{5,4},{6,5},{7,6},{8,11},{9,8},{10,9... | collective-permute-start | bytes 442376 | tf_op jit(solution)/shard_map/ppermute | solution.py:291
  8.5 3.4 %collective-permute-start.3 = (bf16[384,128]{1,0:T(8,128)(2,1)S(1)}, bf16[384,128]{1,0:T(8,128)(2,1)S(1)}, u32[]{:S(2)}, u32[]{:S(2)}) collective-permute-start(bf16[384,128]{1,0:T(8,128)(2,1)S(1)} %slice.40), channel_id=1, source_target_pairs={{0,16},{1,17},{2,18},{3,19},{4,20},{5,21},{6,22},{7,23},{8,24},{9,... | collective-permute-start | bytes 294920 | tf_op jit(solution)/shard_map/ppermute | solution.py:306
  11.9 0.7 convert_element_type.166
  12.8 0.8 compare_bitcast_fusion.3
  13.9 1.3 %collective-permute-start.4 = (bf16[384,128]{1,0:T(8,128)(2,1)S(1)}, bf16[384,128]{1,0:T(8,128)(2,1)S(1)}, u32[]{:S(2)}, u32[]{:S(2)}) collective-permute-start(bf16[384,128]{1,0:T(8,128)(2,1)S(1)} %slice.44), channel_id=1, source_target_pairs={{0,16},{1,17},{2,18},{3,19},{4,20},{5,21},{6,22},{7,23},{8,24},{9,... | collective-permute-start | bytes 294920 | tf_op jit(solution)/shard_map/ppermute | solution.py:306
  15.2 2.3 %collective-permute-done.1.refs_2_.refs_10_ = bf16[576,128]{1,0:T(8,128)(2,1)S(1)} collective-permute-done((bf16[576,128]{1,0:T(8,128)(2,1)S(1)}, bf16[576,128]{1,0:T(8,128)(2,1)S(1)}, u32[]{:S(2)}, u32[]{:S(2)}) %collective-permute-start.1) | collective-permute-done | bytes 147488 | tf_op jit(solution)/shard_map/ppermute | solution.py:291
  17.5 3.4 %collective-permute-start.5 = (bf16[384,128]{1,0:T(8,128)(2,1)S(1)}, bf16[384,128]{1,0:T(8,128)(2,1)S(1)}, u32[]{:S(2)}, u32[]{:S(2)}) collective-permute-start(bf16[384,128]{1,0:T(8,128)(2,1)S(1)} %slice.45), channel_id=1, source_target_pairs={{0,16},{1,17},{2,18},{3,19},{4,20},{5,21},{6,22},{7,23},{8,24},{9,... | collective-permute-start | bytes 294920 | tf_op jit(solution)/shard_map/ppermute | solution.py:306
  21.0 1.3 %collective-permute-start.6 = (bf16[384,128]{1,0:T(8,128)(2,1)S(1)}, bf16[384,128]{1,0:T(8,128)(2,1)S(1)}, u32[]{:S(2)}, u32[]{:S(2)}) collective-permute-start(bf16[384,128]{1,0:T(8,128)(2,1)S(1)} %slice.46), channel_id=1, source_target_pairs={{0,16},{1,17},{2,18},{3,19},{4,20},{5,21},{6,22},{7,23},{8,24},{9,... | collective-permute-start | bytes 294920 | tf_op jit(solution)/shard_map/ppermute | solution.py:306
  22.4 2.4 %collective-permute-start.7 = (bf16[576,128]{1,0:T(8,128)(2,1)S(1)}, bf16[576,128]{1,0:T(8,128)(2,1)S(1)}, u32[]{:S(2)}, u32[]{:S(2)}) collective-permute-start(bf16[576,128]{1,0:T(8,128)(2,1)S(1)} %get-tuple-element.69), channel_id=1, source_target_pairs={{0,1},{1,2},{2,3},{3,0},{4,5},{5,6},{6,7},{7,4},{8,9},{9,10},{10,1... | collective-permute-start | bytes 442376 | tf_op jit(solution)/shard_map/ppermute | solution.py:291
  24.8 3.0 %collective-permute-start.8 = (bf16[576,128]{1,0:T(8,128)(2,1)S(1)}, bf16[576,128]{1,0:T(8,128)(2,1)S(1)}, u32[]{:S(2)}, u32[]{:S(2)}) collective-permute-start(bf16[576,128]{1,0:T(8,128)(2,1)S(1)} %get-tuple-element.71), channel_id=1, source_target_pairs={{0,2},{1,3},{2,0},{3,1},{4,6},{5,7},{6,4},{7,5},{8,10},{9,11},{10,... | collective-permute-start | bytes 442376 | tf_op jit(solution)/shard_map/ppermute | solution.py:291
  27.8 1.0 collective-permute-start.9
  28.7 3.4 %attend.3 = (bf16[2,48,512]{2,1,0:T(8,128)(2,1)S(1)}, bf16[2,48,512]{2,1,0:T(8,128)(2,1)S(1)}, bf16[512,8192]{1,0:T(8,128)(2,1)S(1)}) custom-call(f32[8,1,768]{2,1,0:T(1,128)S(1)} %reshape.61.key_doc, bf16[576,128]{1,0:T(8,128)(2,1)S(1)} %get-tuple-element.63.refs_0_.refs_8_, bf16[576,128]{1,0:T(8,128)(2,1)S(1)} %collective-permute-done.refs_1_.refs_9_, ...), custom_call_target="tpu_custom_call" | custom-call | flops 1150000000 | tf_op jit(solution)/shard_map/attend/pallas_call | solution.py:190
  32.2 3.4 %first_half.3 = (f32[96,8192]{1,0:T(8,128)S(1)}, bf16[512,8192]{1,0:T(8,128)(2,1)S(1)}) custom-call(bf16[96,512]{1,0:T(8,128)(2,1)S(1)} %bitcast.23, bf16[512,8192]{1,0:T(8,128)(2,1)S(1)} %get-tuple-element.76.near, bf16[512,8192]{1,0:T(8,128)(2,1)} %collective-permute-done.11.far), custom_call_target="tpu_custom_call" | custom-call | flops 1172999936 | tf_op jit(solution)/shard_map/first_half/pallas_call | solution.py:220
  35.6 1.5 %project.3 = (bf16[48,4096]{1,0:T(8,128)(2,1)S(1)}, bf16[48,4096]{1,0:T(8,128)(2,1)S(1)}, bf16[48,4096]{1,0:T(8,128)(2,1)S(1)}, bf16[48,4096]{1,0:T(8,128)(2,1)S(1)}) custom-call(bf16[96,512]{1,0:T(8,128)(2,1)S(1)} %bitcast.22, bf16[512,8192]{1,0:T(8,128)(2,1)S(1)} %get-tuple-element.77.refs_1_, f32[96,8192]{1,0:T(8,128)S(1)} %get-tuple-element.78.refs_2_), custom_call_target="tpu_custom_call" | custom-call | flops 517500000 | tf_op jit(solution)/shard_map/project/pallas_call | solution.py:258
  37.1 1.6 %collective-permute-start.13 = (bf16[48,4096]{1,0:T(8,128)(2,1)S(1)}, bf16[48,4096]{1,0:T(8,128)(2,1)}, u32[]{:S(2)}, u32[]{:S(2)}) collective-permute-start(bf16[48,4096]{1,0:T(8,128)(2,1)S(1)} %get-tuple-element.95), channel_id=1, source_target_pairs={{0,8},{4,12},{8,0},{12,4},{1,9},{5,13},{9,1},{13,5},{2,10},{6,14},... | collective-permute-start | bytes 1179656 | tf_op jit(solution)/shard_map/ppermute | solution.py:346
  38.7 4.3 %attend.4 = (bf16[2,96,512]{2,1,0:T(8,128)(2,1)S(1)}, bf16[2,96,512]{2,1,0:T(8,128)(2,1)S(1)}) custom-call(f32[8,1,768]{2,1,0:T(1,128)S(1)} %reshape.61.key_doc, bf16[576,128]{1,0:T(8,128)(2,1)S(1)} %get-tuple-element.63.refs_0_.refs_8_, bf16[576,128]{1,0:T(8,128)(2,1)S(1)} %collective-permute-done.refs_1_.refs_9_, ...), custom_call_target="tpu_custom_call" | custom-call | flops 1207500032 | tf_op jit(solution)/shard_map/attend/pallas_call | solution.py:190
  43.3 0.5 collective-permute-start.15
  43.9 5.8 %first_half.4 = (f32[192,8192]{1,0:T(8,128)S(1)}, bf16[512,8192]{1,0:T(8,128)(2,1)S(1)}) custom-call(bf16[192,512]{1,0:T(8,128)(2,1)S(1)} %bitcast.19, bf16[512,8192]{1,0:T(8,128)(2,1)} %near.3, bf16[512,8192]{1,0:T(8,128)(2,1)} %collective-permute-done.11.far), custom_call_target="tpu_custom_call" | custom-call | flops 2000999936 | tf_op jit(solution)/shard_map/first_half/pallas_call | solution.py:220
  49.7 1.8 %project.4 = (bf16[48,4096]{1,0:T(8,128)(2,1)S(1)}, bf16[48,4096]{1,0:T(8,128)(2,1)S(1)}, bf16[48,4096]{1,0:T(8,128)(2,1)S(1)}, bf16[48,4096]{1,0:T(8,128)(2,1)S...) custom-call(bf16[192,512]{1,0:T(8,128)(2,1)S(1)} %bitcast.18, ...), custom_call_target="tpu_custom_call" | custom-call | flops 517500000 | tf_op jit(solution)/shard_map/project/pallas_call | solution.py:258
  51.5 1.6 %collective-permute-start.24 = (bf16[48,4096]{1,0:T(8,128)(2,1)S(1)}, bf16[48,4096]{1,0:T(8,128)(2,1)S(1)}, u32[]{:S(2)}, u32[]{:S(2)}) collective-permute-start(bf16[48,4096]{1,0:T(8,128)(2,1)S(1)} %get-tuple-element.117), channel_id=1, source_target_pairs={{0,8},{4,12},{8,0},{12,4},{1,9},{5,13},{9,1},{13,5},{2,10},{6,14},... | collective-permute-start | bytes 1179656 | tf_op jit(solution)/shard_map/ppermute | solution.py:346
  53.1 1.1 add_convert_fusion.5
  54.2 3.8 %collective-permute-start.27 = (bf16[48,4096]{1,0:T(8,128)(2,1)S(1)}, bf16[48,4096]{1,0:T(8,128)(2,1)S(1)}, u32[]{:S(2)}, u32[]{:S(2)}) collective-permute-start(bf16[48,4096]{1,0:T(8,128)(2,1)S(1)} %add_convert_fusion.5), channel_id=1, source_target_pairs={{0,1},{3,2},{4,5},{7,6},{8,9},{11,10},{12,13},{15,14},{16,17},{19,... | collective-permute-start | bytes 1179656 | tf_op jit(solution)/shard_map/ppermute | solution.py:364
  58.0 2.5 %attend.5 = (bf16[2,48,512]{2,1,0:T(8,128)(2,1)S(1)}, bf16[2,48,512]{2,1,0:T(8,128)(2,1)S(1)}) custom-call(f32[8,1,768]{2,1,0:T(1,128)S(1)} %reshape.61.key_doc, bf16[576,128]{1,0:T(8,128)(2,1)S(1)} %get-tuple-element.63.refs_0_.refs_8_, bf16[576,128]{1,0:T(8,128)(2,1)S(1)} %collective-permute-done.refs_1_.refs_9_, ...), custom_call_target="tpu_custom_call" | custom-call | flops 966000000 | tf_op jit(solution)/shard_map/attend/pallas_call | solution.py:190
  60.6 1.5 %collective-permute-start.16 = (bf16[48,4096]{1,0:T(8,128)(2,1)S(1)}, bf16[48,4096]{1,0:T(8,128)(2,1)S(1)}, u32[]{:S(2)}, u32[]{:S(2)}) collective-permute-start(bf16[48,4096]{1,0:T(8,128)(2,1)S(1)} %get-tuple-element.109), channel_id=1, source_target_pairs={{0,8},{4,12},{8,0},{12,4},{1,9},{5,13},{9,1},{13,5},{2,10},{6,14},... | collective-permute-start | bytes 1179656 | tf_op jit(solution)/shard_map/ppermute | solution.py:346
  62.2 1.3 %collective-permute-start.19 = (bf16[48,4096]{1,0:T(8,128)(2,1)S(1)}, bf16[48,4096]{1,0:T(8,128)(2,1)S(1)}, u32[]{:S(2)}, u32[]{:S(2)}) collective-permute-start(bf16[48,4096]{1,0:T(8,128)(2,1)S(1)} %add_convert_fusion.13), channel_id=1, source_target_pairs={{0,1},{3,2},{4,5},{7,6},{8,9},{11,10},{12,13},{15,14},{16,17},{19,... | collective-permute-start | bytes 1179656 | tf_op jit(solution)/shard_map/ppermute | solution.py:364
  63.5 5.8 %first_half.5 = (f32[96,8192]{1,0:T(8,128)S(1)}, bf16[512,8192]{1,0:T(8,128)(2,1)S(1)}) custom-call(bf16[96,512]{1,0:T(8,128)(2,1)S(1)} %bitcast.20, bf16[512,8192]{1,0:T(8,128)(2,1)} %near.3, bf16[512,8192]{1,0:T(8,128)(2,1)} %collective-permute-done.11.far), custom_call_target="tpu_custom_call" | custom-call | flops 2000999936 | tf_op jit(solution)/shard_map/first_half/pallas_call | solution.py:220
  69.4 1.5 %project.5 = (bf16[48,4096]{1,0:T(8,128)(2,1)S(1)}, bf16[48,4096]{1,0:T(8,128)(2,1)S(1)}, bf16[48,4096]{1,0:T(8,128)(2,1)S(1)}, bf16[48,4096]{1,0:T(8,128)(2,1)S(1)}) custom-call(bf16[96,512]{1,0:T(8,128)(2,1)S(1)} %bitcast.21, bf16[512,8192]{1,0:T(8,128)(2,1)S(1)} %get-tuple-element.102.refs_1_, f32[96,8192]{1,0:T(8,128)S(1)} %get-tuple-element.103.refs_2_), custom_call_target="tpu_custom_call" | custom-call | flops 517500000 | tf_op jit(solution)/shard_map/project/pallas_call | solution.py:258
  70.9 1.3 %collective-permute-start.30 = (bf16[48,4096]{1,0:T(8,128)(2,1)S(1)}, bf16[48,4096]{1,0:T(8,128)(2,1)S(1)}, u32[]{:S(2)}, u32[]{:S(2)}) collective-permute-start(bf16[48,4096]{1,0:T(8,128)(2,1)S(1)} %add_convert_fusion.2), channel_id=1, source_target_pairs={{0,1},{3,2},{4,5},{7,6},{8,9},{11,10},{12,13},{15,14},{16,17},{19,... | collective-permute-start | bytes 1179656 | tf_op jit(solution)/shard_map/ppermute | solution.py:364
  72.4 0.7 collective-permute-start.28
  73.1 0.6 collective-permute-start.25
  74.1 3.0 %collective-permute-start.22 = (bf16[48,4096]{1,0:T(8,128)(2,1)S(1)}, bf16[48,4096]{1,0:T(8,128)(2,1)S(1)}, u32[]{:S(2)}, u32[]{:S(2)}) collective-permute-start(bf16[48,4096]{1,0:T(8,128)(2,1)S(1)} %add_convert_fusion.10), channel_id=1, source_target_pairs={{0,1},{3,2},{4,5},{7,6},{8,9},{11,10},{12,13},{15,14},{16,17},{19,... | collective-permute-start | bytes 1179656 | tf_op jit(solution)/shard_map/ppermute | solution.py:364
  77.2 0.7 collective-permute-start.20
  77.9 6.5 %collective-permute-done.30 = bf16[48,4096]{1,0:T(8,128)(2,1)S(1)} collective-permute-done((bf16[48,4096]{1,0:T(8,128)(2,1)S(1)}, bf16[48,4096]{1,0:T(8,128)(2,1)S(1)}, u32[]{:S(2)}, u32[]{:S(2)}) %collective-permute-start.30) | collective-permute-done | bytes 393248 | tf_op jit(solution)/shard_map/ppermute | solution.py:364
  84.3 1.5 %collective-permute-start.17 = (bf16[48,4096]{1,0:T(8,128)(2,1)S(1)}, bf16[48,4096]{1,0:T(8,128)(2,1)S(1)}, u32[]{:S(2)}, u32[]{:S(2)}) collective-permute-start(bf16[48,4096]{1,0:T(8,128)(2,1)S(1)} %get-tuple-element.110), channel_id=1, source_target_pairs={{0,8},{4,12},{8,0},{12,4},{1,9},{5,13},{9,1},{13,5},{2,10},{6,14},... | collective-permute-start | bytes 1179656 | tf_op jit(solution)/shard_map/ppermute | solution.py:346
  85.9 0.7 collective-permute-start.31
  86.8 3.8 %collective-permute-start.29 = (bf16[48,4096]{1,0:T(8,128)(2,1)S(1)}, bf16[48,4096]{1,0:T(8,128)(2,1)S(1)}, u32[]{:S(2)}, u32[]{:S(2)}) collective-permute-start(bf16[48,4096]{1,0:T(8,128)(2,1)S(1)} %fusion.1), channel_id=1, source_target_pairs={{0,1},{3,2},{1,0},{2,3},{4,5},{7,6},{5,4},{6,7},{8,9},{11,10},{9,8... | collective-permute-start | bytes 1179656 | tf_op jit(solution)/shard_map/ppermute | solution.py:364
  90.6 2.2 %collective-permute-done.22 = bf16[48,4096]{1,0:T(8,128)(2,1)S(1)} collective-permute-done((bf16[48,4096]{1,0:T(8,128)(2,1)S(1)}, bf16[48,4096]{1,0:T(8,128)(2,1)S(1)}, u32[]{:S(2)}, u32[]{:S(2)}) %collective-permute-start.22) | collective-permute-done | bytes 393248 | tf_op jit(solution)/shard_map/ppermute | solution.py:364
  92.8 1.5 %collective-permute-start.26 = (bf16[48,4096]{1,0:T(8,128)(2,1)S(1)}, bf16[48,4096]{1,0:T(8,128)(2,1)S(1)}, u32[]{:S(2)}, u32[]{:S(2)}) collective-permute-start(bf16[48,4096]{1,0:T(8,128)(2,1)S(1)} %get-tuple-element.119), channel_id=1, source_target_pairs={{0,8},{4,12},{8,0},{12,4},{1,9},{5,13},{9,1},{13,5},{2,10},{6,14},... | collective-permute-start | bytes 1179656 | tf_op jit(solution)/shard_map/ppermute | solution.py:346
  94.4 0.7 collective-permute-start.23
  95.2 3.8 %collective-permute-start.21 = (bf16[48,4096]{1,0:T(8,128)(2,1)S(1)}, bf16[48,4096]{1,0:T(8,128)(2,1)S(1)}, u32[]{:S(2)}, u32[]{:S(2)}) collective-permute-start(bf16[48,4096]{1,0:T(8,128)(2,1)S(1)} %fusion), channel_id=1, source_target_pairs={{0,1},{3,2},{1,0},{2,3},{4,5},{7,6},{5,4},{6,7},{8,9},{11,10},{9,8... | collective-permute-start | bytes 1179656 | tf_op jit(solution)/shard_map/ppermute | solution.py:364
  99.6 1.6 %collective-permute-done.29 = bf16[48,4096]{1,0:T(8,128)(2,1)S(1)} collective-permute-done((bf16[48,4096]{1,0:T(8,128)(2,1)S(1)}, bf16[48,4096]{1,0:T(8,128)(2,1)S(1)}, u32[]{:S(2)}, u32[]{:S(2)}) %collective-permute-start.29) | collective-permute-done | bytes 393248 | tf_op jit(solution)/shard_map/ppermute | solution.py:364
  101.2 3.1 %collective-permute-done.26 = bf16[48,4096]{1,0:T(8,128)(2,1)S(1)} collective-permute-done((bf16[48,4096]{1,0:T(8,128)(2,1)S(1)}, bf16[48,4096]{1,0:T(8,128)(2,1)S(1)}, u32[]{:S(2)}, u32[]{:S(2)}) %collective-permute-start.26) | collective-permute-done | bytes 393248 | tf_op jit(solution)/shard_map/ppermute | solution.py:346
  104.5 4.0 %collective-permute-done.21 = bf16[48,4096]{1,0:T(8,128)(2,1)S(1)} collective-permute-done((bf16[48,4096]{1,0:T(8,128)(2,1)S(1)}, bf16[48,4096]{1,0:T(8,128)(2,1)S(1)}, u32[]{:S(2)}, u32[]{:S(2)}) %collective-permute-start.21) | collective-permute-done | bytes 393248 | tf_op jit(solution)/shard_map/ppermute | solution.py:364
  108.5 1.6 %collective-permute-done.18 = bf16[48,4096]{1,0:T(8,128)(2,1)S(1)} collective-permute-done((bf16[48,4096]{1,0:T(8,128)(2,1)S(1)}, bf16[48,4096]{1,0:T(8,128)(2,1)S(1)}, u32[]{:S(2)}, u32[]{:S(2)}) %collective-permute-start.18) | collective-permute-done | bytes 393248 | tf_op jit(solution)/shard_map/ppermute | solution.py:346
  110.3 0.9 pad_maximum_fusion
  (62 shorter events, 3.7 us)
Async XLA Ops:
  0.0 32.2 %collective-permute-start.11 = (bf16[512,8192]{1,0:T(8,128)(2,1)}, bf16[512,8192]{1,0:T(8,128)(2,1)}, u32[]{:S(2)}, u32[]{:S(2)}) collective-permute-start(bf16[512,8192]{1,0:T(8,128)(2,1)} %near.3), channel_id=1, source_target_pairs={{0,4},{4,0},{8,12},{12,8},{1,5},{5,1},{9,13},{13,9},{2,6},{6,2},{1... | collective-permute-start | bytes 25165832 | tf_op jit(solution)/shard_map/ppermute | solution.py:308
  1.9 11.9 %collective-permute-start = (bf16[576,128]{1,0:T(8,128)(2,1)S(1)}, bf16[576,128]{1,0:T(8,128)(2,1)S(1)}, u32[]{:S(2)}, u32[]{:S(2)}) collective-permute-start(bf16[576,128]{1,0:T(8,128)(2,1)S(1)} %get-tuple-element.64), channel_id=1, source_target_pairs={{0,1},{1,2},{2,3},{3,0},{4,5},{5,6},{6,7},{7,4},{8,9},{9,10},{10,1... | collective-permute-start | bytes 442376 | tf_op jit(solution)/shard_map/ppermute | solution.py:291
  4.6 12.9 %collective-permute-start.1 = (bf16[576,128]{1,0:T(8,128)(2,1)S(1)}, bf16[576,128]{1,0:T(8,128)(2,1)S(1)}, u32[]{:S(2)}, u32[]{:S(2)}) collective-permute-start(bf16[576,128]{1,0:T(8,128)(2,1)S(1)} %get-tuple-element.65), channel_id=1, source_target_pairs={{0,2},{1,3},{2,0},{3,1},{4,6},{5,7},{6,4},{7,5},{8,10},{9,11},{10,... | collective-permute-start | bytes 442376 | tf_op jit(solution)/shard_map/ppermute | solution.py:291
  7.1 13.8 %collective-permute-start.2 = (bf16[576,128]{1,0:T(8,128)(2,1)S(1)}, bf16[576,128]{1,0:T(8,128)(2,1)S(1)}, u32[]{:S(2)}, u32[]{:S(2)}) collective-permute-start(bf16[576,128]{1,0:T(8,128)(2,1)S(1)} %get-tuple-element.66), channel_id=1, source_target_pairs={{0,3},{1,0},{2,1},{3,2},{4,7},{5,4},{6,5},{7,6},{8,11},{9,8},{10,9... | collective-permute-start | bytes 442376 | tf_op jit(solution)/shard_map/ppermute | solution.py:291
  8.5 13.9 %collective-permute-start.3 = (bf16[384,128]{1,0:T(8,128)(2,1)S(1)}, bf16[384,128]{1,0:T(8,128)(2,1)S(1)}, u32[]{:S(2)}, u32[]{:S(2)}) collective-permute-start(bf16[384,128]{1,0:T(8,128)(2,1)S(1)} %slice.40), channel_id=1, source_target_pairs={{0,16},{1,17},{2,18},{3,19},{4,20},{5,21},{6,22},{7,23},{8,24},{9,... | collective-permute-start | bytes 294920 | tf_op jit(solution)/shard_map/ppermute | solution.py:306
  13.9 11.0 %collective-permute-start.4 = (bf16[384,128]{1,0:T(8,128)(2,1)S(1)}, bf16[384,128]{1,0:T(8,128)(2,1)S(1)}, u32[]{:S(2)}, u32[]{:S(2)}) collective-permute-start(bf16[384,128]{1,0:T(8,128)(2,1)S(1)} %slice.44), channel_id=1, source_target_pairs={{0,16},{1,17},{2,18},{3,19},{4,20},{5,21},{6,22},{7,23},{8,24},{9,... | collective-permute-start | bytes 294920 | tf_op jit(solution)/shard_map/ppermute | solution.py:306
  17.5 10.3 %collective-permute-start.5 = (bf16[384,128]{1,0:T(8,128)(2,1)S(1)}, bf16[384,128]{1,0:T(8,128)(2,1)S(1)}, u32[]{:S(2)}, u32[]{:S(2)}) collective-permute-start(bf16[384,128]{1,0:T(8,128)(2,1)S(1)} %slice.45), channel_id=1, source_target_pairs={{0,16},{1,17},{2,18},{3,19},{4,20},{5,21},{6,22},{7,23},{8,24},{9,... | collective-permute-start | bytes 294920 | tf_op jit(solution)/shard_map/ppermute | solution.py:306
  21.0 7.8 %collective-permute-start.6 = (bf16[384,128]{1,0:T(8,128)(2,1)S(1)}, bf16[384,128]{1,0:T(8,128)(2,1)S(1)}, u32[]{:S(2)}, u32[]{:S(2)}) collective-permute-start(bf16[384,128]{1,0:T(8,128)(2,1)S(1)} %slice.46), channel_id=1, source_target_pairs={{0,16},{1,17},{2,18},{3,19},{4,20},{5,21},{6,22},{7,23},{8,24},{9,... | collective-permute-start | bytes 294920 | tf_op jit(solution)/shard_map/ppermute | solution.py:306
  22.4 16.2 %collective-permute-start.7 = (bf16[576,128]{1,0:T(8,128)(2,1)S(1)}, bf16[576,128]{1,0:T(8,128)(2,1)S(1)}, u32[]{:S(2)}, u32[]{:S(2)}) collective-permute-start(bf16[576,128]{1,0:T(8,128)(2,1)S(1)} %get-tuple-element.69), channel_id=1, source_target_pairs={{0,1},{1,2},{2,3},{3,0},{4,5},{5,6},{6,7},{7,4},{8,9},{9,10},{10,1... | collective-permute-start | bytes 442376 | tf_op jit(solution)/shard_map/ppermute | solution.py:291
  24.8 13.9 %collective-permute-start.8 = (bf16[576,128]{1,0:T(8,128)(2,1)S(1)}, bf16[576,128]{1,0:T(8,128)(2,1)S(1)}, u32[]{:S(2)}, u32[]{:S(2)}) collective-permute-start(bf16[576,128]{1,0:T(8,128)(2,1)S(1)} %get-tuple-element.71), channel_id=1, source_target_pairs={{0,2},{1,3},{2,0},{3,1},{4,6},{5,7},{6,4},{7,5},{8,10},{9,11},{10,... | collective-permute-start | bytes 442376 | tf_op jit(solution)/shard_map/ppermute | solution.py:291
  27.8 10.9 %collective-permute-start.9 = (bf16[576,128]{1,0:T(8,128)(2,1)S(1)}, bf16[576,128]{1,0:T(8,128)(2,1)S(1)}, u32[]{:S(2)}, u32[]{:S(2)}) collective-permute-start(bf16[576,128]{1,0:T(8,128)(2,1)S(1)} %get-tuple-element.73), channel_id=1, source_target_pairs={{0,3},{1,0},{2,1},{3,2},{4,7},{5,4},{6,5},{7,6},{8,11},{9,8},{10,9... | collective-permute-start | bytes 442376 | tf_op jit(solution)/shard_map/ppermute | solution.py:291
  32.1 3.5 %collective-permute-start.10 = (bf16[2,48,512]{2,1,0:T(8,128)(2,1)S(1)}, bf16[2,48,512]{2,1,0:T(8,128)(2,1)S(1)}, u32[]{:S(2)}, u32[]{:S(2)}) collective-permute-start(bf16[2,48,512]{2,1,0:T(8,128)(2,1)S(1)} %get-tuple-element.74), channel_id=1, source_target_pairs={{0,4},{4,0},{8,12},{12,8},{1,5},{5,1},{9,13},{13,9},{2,6},{6,2},{1... | collective-permute-start | bytes 294920 | tf_op jit(solution)/shard_map/ppermute | solution.py:407
  37.1 14.4 %collective-permute-start.13 = (bf16[48,4096]{1,0:T(8,128)(2,1)S(1)}, bf16[48,4096]{1,0:T(8,128)(2,1)}, u32[]{:S(2)}, u32[]{:S(2)}) collective-permute-start(bf16[48,4096]{1,0:T(8,128)(2,1)S(1)} %get-tuple-element.95), channel_id=1, source_target_pairs={{0,8},{4,12},{8,0},{12,4},{1,9},{5,13},{9,1},{13,5},{2,10},{6,14},... | collective-permute-start | bytes 1179656 | tf_op jit(solution)/shard_map/ppermute | solution.py:346
  38.7 4.7 %copy-start = (bf16[576,128]{1,0:T(8,128)(2,1)}, bf16[576,128]{1,0:T(8,128)(2,1)S(1)}, u32[]{:S(2)}) copy-start(bf16[576,128]{1,0:T(8,128)(2,1)S(1)} %collective-permute-done.8.refs_10_) | copy-start | bytes 442372
  38.7 4.6 %copy-start.2 = (bf16[576,128]{1,0:T(8,128)(2,1)}, bf16[576,128]{1,0:T(8,128)(2,1)S(1)}, u32[]{:S(2)}) copy-start(bf16[576,128]{1,0:T(8,128)(2,1)S(1)} %collective-permute-done.9.refs_11_) | copy-start | bytes 442372
  43.1 6.6 %collective-permute-start.12 = (bf16[2,96,512]{2,1,0:T(8,128)(2,1)S(1)}, bf16[2,96,512]{2,1,0:T(8,128)(2,1)S(1)}, u32[]{:S(2)}, u32[]{:S(2)}) collective-permute-start(bf16[2,96,512]{2,1,0:T(8,128)(2,1)S(1)} %get-tuple-element.85), channel_id=1, source_target_pairs={{0,4},{4,0},{8,12},{12,8},{1,5},{5,1},{9,13},{13,9},{2,6},{6,2},{1... | collective-permute-start | bytes 589832 | tf_op jit(solution)/shard_map/ppermute | solution.py:407
  43.3 17.2 %collective-permute-start.15 = (bf16[48,4096]{1,0:T(8,128)(2,1)S(1)}, bf16[48,4096]{1,0:T(8,128)(2,1)S(1)}, u32[]{:S(2)}, u32[]{:S(2)}) collective-permute-start(bf16[48,4096]{1,0:T(8,128)(2,1)S(1)} %get-tuple-element.108), channel_id=1, source_target_pairs={{0,8},{4,12},{8,0},{12,4},{1,9},{5,13},{9,1},{13,5},{2,10},{6,14},... | collective-permute-start | bytes 1179656 | tf_op jit(solution)/shard_map/ppermute | solution.py:346
  49.7 8.4 %copy-start.1 = (bf16[576,128]{1,0:T(8,128)(2,1)S(1)}, bf16[576,128]{1,0:T(8,128)(2,1)}, u32[]{:S(2)}) copy-start(bf16[576,128]{1,0:T(8,128)(2,1)} %copy-done) | copy-start | bytes 442372
  49.7 8.3 %copy-start.3 = (bf16[576,128]{1,0:T(8,128)(2,1)S(1)}, bf16[576,128]{1,0:T(8,128)(2,1)}, u32[]{:S(2)}) copy-start(bf16[576,128]{1,0:T(8,128)(2,1)} %copy-done.2) | copy-start | bytes 442372
  51.5 19.3 %collective-permute-start.24 = (bf16[48,4096]{1,0:T(8,128)(2,1)S(1)}, bf16[48,4096]{1,0:T(8,128)(2,1)S(1)}, u32[]{:S(2)}, u32[]{:S(2)}) collective-permute-start(bf16[48,4096]{1,0:T(8,128)(2,1)S(1)} %get-tuple-element.117), channel_id=1, source_target_pairs={{0,8},{4,12},{8,0},{12,4},{1,9},{5,13},{9,1},{13,5},{2,10},{6,14},... | collective-permute-start | bytes 1179656 | tf_op jit(solution)/shard_map/ppermute | solution.py:346
  54.2 18.1 %collective-permute-start.27 = (bf16[48,4096]{1,0:T(8,128)(2,1)S(1)}, bf16[48,4096]{1,0:T(8,128)(2,1)S(1)}, u32[]{:S(2)}, u32[]{:S(2)}) collective-permute-start(bf16[48,4096]{1,0:T(8,128)(2,1)S(1)} %add_convert_fusion.5), channel_id=1, source_target_pairs={{0,1},{3,2},{4,5},{7,6},{8,9},{11,10},{12,13},{15,14},{16,17},{19,... | collective-permute-start | bytes 1179656 | tf_op jit(solution)/shard_map/ppermute | solution.py:364
  60.5 8.9 %collective-permute-start.14 = (bf16[2,48,512]{2,1,0:T(8,128)(2,1)S(1)}, bf16[2,48,512]{2,1,0:T(8,128)(2,1)S(1)}, u32[]{:S(2)}, u32[]{:S(2)}) collective-permute-start(bf16[2,48,512]{2,1,0:T(8,128)(2,1)S(1)} %get-tuple-element.100), channel_id=1, source_target_pairs={{0,4},{4,0},{8,12},{12,8},{1,5},{5,1},{9,13},{13,9},{2,6},{6,2},{1... | collective-permute-start | bytes 294920 | tf_op jit(solution)/shard_map/ppermute | solution.py:407
  60.6 13.4 %collective-permute-start.16 = (bf16[48,4096]{1,0:T(8,128)(2,1)S(1)}, bf16[48,4096]{1,0:T(8,128)(2,1)S(1)}, u32[]{:S(2)}, u32[]{:S(2)}) collective-permute-start(bf16[48,4096]{1,0:T(8,128)(2,1)S(1)} %get-tuple-element.109), channel_id=1, source_target_pairs={{0,8},{4,12},{8,0},{12,4},{1,9},{5,13},{9,1},{13,5},{2,10},{6,14},... | collective-permute-start | bytes 1179656 | tf_op jit(solution)/shard_map/ppermute | solution.py:346
  62.2 14.8 %collective-permute-start.19 = (bf16[48,4096]{1,0:T(8,128)(2,1)S(1)}, bf16[48,4096]{1,0:T(8,128)(2,1)S(1)}, u32[]{:S(2)}, u32[]{:S(2)}) collective-permute-start(bf16[48,4096]{1,0:T(8,128)(2,1)S(1)} %add_convert_fusion.13), channel_id=1, source_target_pairs={{0,1},{3,2},{4,5},{7,6},{8,9},{11,10},{12,13},{15,14},{16,17},{19,... | collective-permute-start | bytes 1179656 | tf_op jit(solution)/shard_map/ppermute | solution.py:364
  70.9 13.4 %collective-permute-start.30 = (bf16[48,4096]{1,0:T(8,128)(2,1)S(1)}, bf16[48,4096]{1,0:T(8,128)(2,1)S(1)}, u32[]{:S(2)}, u32[]{:S(2)}) collective-permute-start(bf16[48,4096]{1,0:T(8,128)(2,1)S(1)} %add_convert_fusion.2), channel_id=1, source_target_pairs={{0,1},{3,2},{4,5},{7,6},{8,9},{11,10},{12,13},{15,14},{16,17},{19,... | collective-permute-start | bytes 1179656 | tf_op jit(solution)/shard_map/ppermute | solution.py:364
  72.4 13.6 %collective-permute-start.28 = (bf16[48,4096]{1,0:T(8,128)(2,1)S(1)}, bf16[48,4096]{1,0:T(8,128)(2,1)S(1)}, u32[]{:S(2)}, u32[]{:S(2)}) collective-permute-start(bf16[48,4096]{1,0:T(8,128)(2,1)S(1)} %add_convert_fusion.4), channel_id=1, source_target_pairs={{1,2},{2,1},{5,6},{6,5},{9,10},{10,9},{13,14},{14,13},{17,18},{18,... | collective-permute-start | bytes 1179656 | tf_op jit(solution)/shard_map/ppermute | solution.py:364
  73.1 13.6 %collective-permute-start.25 = (bf16[48,4096]{1,0:T(8,128)(2,1)S(1)}, bf16[48,4096]{1,0:T(8,128)(2,1)S(1)}, u32[]{:S(2)}, u32[]{:S(2)}) collective-permute-start(bf16[48,4096]{1,0:T(8,128)(2,1)S(1)} %get-tuple-element.118), channel_id=1, source_target_pairs={{0,8},{4,12},{8,0},{12,4},{1,9},{5,13},{9,1},{13,5},{2,10},{6,14},... | collective-permute-start | bytes 1179656 | tf_op jit(solution)/shard_map/ppermute | solution.py:346
  74.1 18.7 %collective-permute-start.22 = (bf16[48,4096]{1,0:T(8,128)(2,1)S(1)}, bf16[48,4096]{1,0:T(8,128)(2,1)S(1)}, u32[]{:S(2)}, u32[]{:S(2)}) collective-permute-start(bf16[48,4096]{1,0:T(8,128)(2,1)S(1)} %add_convert_fusion.10), channel_id=1, source_target_pairs={{0,1},{3,2},{4,5},{7,6},{8,9},{11,10},{12,13},{15,14},{16,17},{19,... | collective-permute-start | bytes 1179656 | tf_op jit(solution)/shard_map/ppermute | solution.py:364
  77.2 17.2 %collective-permute-start.20 = (bf16[48,4096]{1,0:T(8,128)(2,1)S(1)}, bf16[48,4096]{1,0:T(8,128)(2,1)S(1)}, u32[]{:S(2)}, u32[]{:S(2)}) collective-permute-start(bf16[48,4096]{1,0:T(8,128)(2,1)S(1)} %add_convert_fusion.12), channel_id=1, source_target_pairs={{1,2},{2,1},{5,6},{6,5},{9,10},{10,9},{13,14},{14,13},{17,18},{18,... | collective-permute-start | bytes 1179656 | tf_op jit(solution)/shard_map/ppermute | solution.py:364
  84.3 10.7 %collective-permute-start.17 = (bf16[48,4096]{1,0:T(8,128)(2,1)S(1)}, bf16[48,4096]{1,0:T(8,128)(2,1)S(1)}, u32[]{:S(2)}, u32[]{:S(2)}) collective-permute-start(bf16[48,4096]{1,0:T(8,128)(2,1)S(1)} %get-tuple-element.110), channel_id=1, source_target_pairs={{0,8},{4,12},{8,0},{12,4},{1,9},{5,13},{9,1},{13,5},{2,10},{6,14},... | collective-permute-start | bytes 1179656 | tf_op jit(solution)/shard_map/ppermute | solution.py:346
  85.9 13.1 %collective-permute-start.31 = (bf16[48,4096]{1,0:T(8,128)(2,1)S(1)}, bf16[48,4096]{1,0:T(8,128)(2,1)S(1)}, u32[]{:S(2)}, u32[]{:S(2)}) collective-permute-start(bf16[48,4096]{1,0:T(8,128)(2,1)S(1)} %add_convert_fusion.1), channel_id=1, source_target_pairs={{1,2},{2,1},{5,6},{6,5},{9,10},{10,9},{13,14},{14,13},{17,18},{18,... | collective-permute-start | bytes 1179656 | tf_op jit(solution)/shard_map/ppermute | solution.py:364
  86.8 14.4 %collective-permute-start.29 = (bf16[48,4096]{1,0:T(8,128)(2,1)S(1)}, bf16[48,4096]{1,0:T(8,128)(2,1)S(1)}, u32[]{:S(2)}, u32[]{:S(2)}) collective-permute-start(bf16[48,4096]{1,0:T(8,128)(2,1)S(1)} %fusion.1), channel_id=1, source_target_pairs={{0,1},{3,2},{1,0},{2,3},{4,5},{7,6},{5,4},{6,7},{8,9},{11,10},{9,8... | collective-permute-start | bytes 1179656 | tf_op jit(solution)/shard_map/ppermute | solution.py:364
  92.8 11.5 %collective-permute-start.26 = (bf16[48,4096]{1,0:T(8,128)(2,1)S(1)}, bf16[48,4096]{1,0:T(8,128)(2,1)S(1)}, u32[]{:S(2)}, u32[]{:S(2)}) collective-permute-start(bf16[48,4096]{1,0:T(8,128)(2,1)S(1)} %get-tuple-element.119), channel_id=1, source_target_pairs={{0,8},{4,12},{8,0},{12,4},{1,9},{5,13},{9,1},{13,5},{2,10},{6,14},... | collective-permute-start | bytes 1179656 | tf_op jit(solution)/shard_map/ppermute | solution.py:346
  94.4 10.1 %collective-permute-start.23 = (bf16[48,4096]{1,0:T(8,128)(2,1)S(1)}, bf16[48,4096]{1,0:T(8,128)(2,1)S(1)}, u32[]{:S(2)}, u32[]{:S(2)}) collective-permute-start(bf16[48,4096]{1,0:T(8,128)(2,1)S(1)} %add_convert_fusion.9), channel_id=1, source_target_pairs={{1,2},{2,1},{5,6},{6,5},{9,10},{10,9},{13,14},{14,13},{17,18},{18,... | collective-permute-start | bytes 1179656 | tf_op jit(solution)/shard_map/ppermute | solution.py:364
  95.2 13.3 %collective-permute-start.21 = (bf16[48,4096]{1,0:T(8,128)(2,1)S(1)}, bf16[48,4096]{1,0:T(8,128)(2,1)S(1)}, u32[]{:S(2)}, u32[]{:S(2)}) collective-permute-start(bf16[48,4096]{1,0:T(8,128)(2,1)S(1)} %fusion), channel_id=1, source_target_pairs={{0,1},{3,2},{1,0},{2,3},{4,5},{7,6},{5,4},{6,7},{8,9},{11,10},{9,8... | collective-permute-start | bytes 1179656 | tf_op jit(solution)/shard_map/ppermute | solution.py:364
  99.0 11.1 %collective-permute-start.18 = (bf16[48,4096]{1,0:T(8,128)(2,1)S(1)}, bf16[48,4096]{1,0:T(8,128)(2,1)S(1)}, u32[]{:S(2)}, u32[]{:S(2)}) collective-permute-start(bf16[48,4096]{1,0:T(8,128)(2,1)S(1)} %get-tuple-element.111), channel_id=1, source_target_pairs={{0,8},{4,12},{8,0},{12,4},{1,9},{5,13},{9,1},{13,5},{2,10},{6,14},... | collective-permute-start | bytes 1179656 | tf_op jit(solution)/shard_map/ppermute | solution.py:346

commit v11 on v10

--- a/solution.py
+++ b/solution.py
@@ -287,6 +287,14 @@
     rows_at_once = share if staged else block
     siblings = [(h, h ^ 1) for h in range(head_shards)]
 
+    def within_reach(k):
+        return [
+            (g * slabs + i, (g + 1) * slabs + i)
+            for g in range(groups - 1)
+            for i in range(slabs)
+            if (i - k) % slabs > slabs - SLAB_REACH
+        ]
+
     def around(array, k):
         return lax.ppermute(array, "wsh", [(i, (i + k) % slabs) for i in range(slabs)])
 
@@ -303,7 +311,7 @@
     )
     loads = [packed[0]] + [around(packed[k], k) for k in range(1, slabs)]
     before = [
-        lax.ppermute(a[: 2 * block], "srv", [(g, g + 1) for g in range(groups - 1)]) for a in loads
+        lax.ppermute(a[: 2 * block], ("srv", "wsh"), within_reach(k)) for k, a in enumerate(loads)
     ]
     weight_sibling = lax.ppermute(out_weight, "head", siblings)
     stage_queries = [loads]

time: 112 us -> 111 us (level)
  no operation moved by 1% of the time
where the time goes in v11:
time: 111 us
  starting transfers between devices  51.4 us (46%)
  Pallas kernels  31.4 us (28%)
  waiting for transfers between devices  21.9 us (20%)
  other arithmetic  5.14 us (5%)
    ppermute x10, starting transfers between devices, step(): now.setdefault(c, {})[n] = lax.ppermute(message, 'wsh', route)  20.3 us
    pallas_call x3, Pallas kernels, first_half(): pl.pallas_call(first_half_kernel, out_shape=[pltpu.VMEM((rows_here.shape[...  15 us
    ppermute x10, waiting for transfers between devices, step(): now.setdefault(c, {})[n] = lax.ppermute(message, 'wsh', route)  14.3 us
    ppermute x6, starting transfers between devices, around(): lax.ppermute(array, 'wsh', [(i, (i + k) % slabs) for i in range(slabs)])  12 us
    pallas_call x3, Pallas kernels, attend(): pl.pallas_call(partial(attend_kernel, slabs=slabs, heads=heads, share=sha...  10.2 us
    ppermute x8, starting transfers between devices, cross(): lax.ppermute(a, 'head', r)  9.31 us
    ppermute x4, starting transfers between devices, on_device(): lax.ppermute(a[:2 * block], ('srv', 'wsh'), within_reach(k))  8.94 us
    ppermute x8, waiting for transfers between devices, cross(): lax.ppermute(a, 'head', r)  4.76 us
  transfers between devices with their start and end apart: 32, of which 8 were waited for; matrix products, arithmetic and copies ran while one was open for 4% of the time, Pallas kernels for 28%

profile of v11, /device:TPU:0, one launch (start us, length us, event | category | flops | bytes accessed | tf_op | source)
XLA Modules:
  0.0 110.6 jit_solution(1599185487972562721)
XLA Ops:
  0.5 1.5 %pack.1 = (bf16[576,128]{1,0:T(8,128)(2,1)S(1)}, bf16[576,128]{1,0:T(8,128)(2,1)S(1)}, bf16[576,128]{1,0:T(8,128)(2,1)S(1)}, bf16[576,128]{1,0:T(8,128)(2,1)S(1)...) custom-call(bf16[192,2048]{1,0:T(8,128)(2,1)} %queries.1, ...), custom_call_target="tpu_custom_call" | custom-call | tf_op jit(solution)/shard_map/pack/pallas_call | solution.py:101
  1.9 2.6 %collective-permute-start = (bf16[576,128]{1,0:T(8,128)(2,1)S(1)}, bf16[576,128]{1,0:T(8,128)(2,1)S(1)}, u32[]{:S(2)}, u32[]{:S(2)}) collective-permute-start(bf16[576,128]{1,0:T(8,128)(2,1)S(1)} %get-tuple-element.64), channel_id=1, source_target_pairs={{0,1},{1,2},{2,3},{3,0},{4,5},{5,6},{6,7},{7,4},{8,9},{9,10},{10,1... | collective-permute-start | bytes 442376 | tf_op jit(solution)/shard_map/ppermute | solution.py:299
  4.6 2.6 %collective-permute-start.1 = (bf16[576,128]{1,0:T(8,128)(2,1)S(1)}, bf16[576,128]{1,0:T(8,128)(2,1)S(1)}, u32[]{:S(2)}, u32[]{:S(2)}) collective-permute-start(bf16[576,128]{1,0:T(8,128)(2,1)S(1)} %get-tuple-element.65), channel_id=1, source_target_pairs={{0,2},{1,3},{2,0},{3,1},{4,6},{5,7},{6,4},{7,5},{8,10},{9,11},{10,... | collective-permute-start | bytes 442376 | tf_op jit(solution)/shard_map/ppermute | solution.py:299
  7.1 1.3 %collective-permute-start.2 = (bf16[576,128]{1,0:T(8,128)(2,1)S(1)}, bf16[576,128]{1,0:T(8,128)(2,1)S(1)}, u32[]{:S(2)}, u32[]{:S(2)}) collective-permute-start(bf16[576,128]{1,0:T(8,128)(2,1)S(1)} %get-tuple-element.66), channel_id=1, source_target_pairs={{0,3},{1,0},{2,1},{3,2},{4,7},{5,4},{6,5},{7,6},{8,11},{9,8},{10,9... | collective-permute-start | bytes 442376 | tf_op jit(solution)/shard_map/ppermute | solution.py:299
  8.5 0.7 collective-permute-start.3
  9.2 0.7 convert_element_type.166
  10.0 0.8 compare_bitcast_fusion.3
  11.4 3.6 %collective-permute-start.4 = (bf16[384,128]{1,0:T(8,128)(2,1)S(1)}, bf16[384,128]{1,0:T(8,128)(2,1)S(1)}, u32[]{:S(2)}, u32[]{:S(2)}) collective-permute-start(bf16[384,128]{1,0:T(8,128)(2,1)S(1)} %slice.44), channel_id=1, source_target_pairs={{0,16},{2,18},{3,19},{4,20},{6,22},{7,23},{8,24},{10,26},{11,27},{... | collective-permute-start | bytes 294920 | tf_op jit(solution)/shard_map/ppermute | solution.py:314
  15.0 2.5 %collective-permute-done.1.refs_2_.refs_10_ = bf16[576,128]{1,0:T(8,128)(2,1)S(1)} collective-permute-done((bf16[576,128]{1,0:T(8,128)(2,1)S(1)}, bf16[576,128]{1,0:T(8,128)(2,1)S(1)}, u32[]{:S(2)}, u32[]{:S(2)}) %collective-permute-start.1) | collective-permute-done | bytes 147488 | tf_op jit(solution)/shard_map/ppermute | solution.py:299
  17.5 3.4 %collective-permute-start.5 = (bf16[384,128]{1,0:T(8,128)(2,1)S(1)}, bf16[384,128]{1,0:T(8,128)(2,1)S(1)}, u32[]{:S(2)}, u32[]{:S(2)}) collective-permute-start(bf16[384,128]{1,0:T(8,128)(2,1)S(1)} %slice.45), channel_id=1, source_target_pairs={{0,16},{1,17},{3,19},{4,20},{5,21},{7,23},{8,24},{9,25},{11,27},{1... | collective-permute-start | bytes 294920 | tf_op jit(solution)/shard_map/ppermute | solution.py:314
  21.0 1.3 %collective-permute-start.6 = (bf16[384,128]{1,0:T(8,128)(2,1)S(1)}, bf16[384,128]{1,0:T(8,128)(2,1)S(1)}, u32[]{:S(2)}, u32[]{:S(2)}) collective-permute-start(bf16[384,128]{1,0:T(8,128)(2,1)S(1)} %slice.46), channel_id=1, source_target_pairs={{0,16},{1,17},{2,18},{4,20},{5,21},{6,22},{8,24},{9,25},{10,26},{1... | collective-permute-start | bytes 294920 | tf_op jit(solution)/shard_map/ppermute | solution.py:314
  22.4 2.4 %collective-permute-start.7 = (bf16[576,128]{1,0:T(8,128)(2,1)S(1)}, bf16[576,128]{1,0:T(8,128)(2,1)S(1)}, u32[]{:S(2)}, u32[]{:S(2)}) collective-permute-start(bf16[576,128]{1,0:T(8,128)(2,1)S(1)} %get-tuple-element.69), channel_id=1, source_target_pairs={{0,1},{1,2},{2,3},{3,0},{4,5},{5,6},{6,7},{7,4},{8,9},{9,10},{10,1... | collective-permute-start | bytes 442376 | tf_op jit(solution)/shard_map/ppermute | solution.py:299
  24.8 2.3 %collective-permute-start.8 = (bf16[576,128]{1,0:T(8,128)(2,1)S(1)}, bf16[576,128]{1,0:T(8,128)(2,1)S(1)}, u32[]{:S(2)}, u32[]{:S(2)}) collective-permute-start(bf16[576,128]{1,0:T(8,128)(2,1)S(1)} %get-tuple-element.71), channel_id=1, source_target_pairs={{0,2},{1,3},{2,0},{3,1},{4,6},{5,7},{6,4},{7,5},{8,10},{9,11},{10,... | collective-permute-start | bytes 442376 | tf_op jit(solution)/shard_map/ppermute | solution.py:299
  27.1 0.7 collective-permute-start.9
  27.9 3.4 %attend.3 = (bf16[2,48,512]{2,1,0:T(8,128)(2,1)S(1)}, bf16[2,48,512]{2,1,0:T(8,128)(2,1)S(1)}, bf16[512,8192]{1,0:T(8,128)(2,1)S(1)}) custom-call(f32[8,1,768]{2,1,0:T(1,128)S(1)} %reshape.61.key_doc, bf16[576,128]{1,0:T(8,128)(2,1)S(1)} %get-tuple-element.63.refs_0_.refs_8_, bf16[576,128]{1,0:T(8,128)(2,1)S(1)} %collective-permute-done.refs_1_.refs_9_, ...), custom_call_target="tpu_custom_call" | custom-call | flops 1150000000 | tf_op jit(solution)/shard_map/attend/pallas_call | solution.py:190
  31.3 3.4 %first_half.3 = (f32[96,8192]{1,0:T(8,128)S(1)}, bf16[512,8192]{1,0:T(8,128)(2,1)S(1)}) custom-call(bf16[96,512]{1,0:T(8,128)(2,1)S(1)} %bitcast.23, bf16[512,8192]{1,0:T(8,128)(2,1)S(1)} %get-tuple-element.76.near, bf16[512,8192]{1,0:T(8,128)(2,1)} %collective-permute-done.11.far), custom_call_target="tpu_custom_call" | custom-call | flops 1172999936 | tf_op jit(solution)/shard_map/first_half/pallas_call | solution.py:220
  34.8 1.5 %project.3 = (bf16[48,4096]{1,0:T(8,128)(2,1)S(1)}, bf16[48,4096]{1,0:T(8,128)(2,1)S(1)}, bf16[48,4096]{1,0:T(8,128)(2,1)S(1)}, bf16[48,4096]{1,0:T(8,128)(2,1)S(1)}) custom-call(bf16[96,512]{1,0:T(8,128)(2,1)S(1)} %bitcast.22, bf16[512,8192]{1,0:T(8,128)(2,1)S(1)} %get-tuple-element.77.refs_1_, f32[96,8192]{1,0:T(8,128)S(1)} %get-tuple-element.78.refs_2_), custom_call_target="tpu_custom_call" | custom-call | flops 517500000 | tf_op jit(solution)/shard_map/project/pallas_call | solution.py:258
  36.2 1.6 %collective-permute-start.13 = (bf16[48,4096]{1,0:T(8,128)(2,1)S(1)}, bf16[48,4096]{1,0:T(8,128)(2,1)}, u32[]{:S(2)}, u32[]{:S(2)}) collective-permute-start(bf16[48,4096]{1,0:T(8,128)(2,1)S(1)} %get-tuple-element.95), channel_id=1, source_target_pairs={{0,8},{4,12},{8,0},{12,4},{1,9},{5,13},{9,1},{13,5},{2,10},{6,14},... | collective-permute-start | bytes 1179656 | tf_op jit(solution)/shard_map/ppermute | solution.py:354
  37.8 4.3 %attend.4 = (bf16[2,96,512]{2,1,0:T(8,128)(2,1)S(1)}, bf16[2,96,512]{2,1,0:T(8,128)(2,1)S(1)}) custom-call(f32[8,1,768]{2,1,0:T(1,128)S(1)} %reshape.61.key_doc, bf16[576,128]{1,0:T(8,128)(2,1)S(1)} %get-tuple-element.63.refs_0_.refs_8_, bf16[576,128]{1,0:T(8,128)(2,1)S(1)} %collective-permute-done.refs_1_.refs_9_, ...), custom_call_target="tpu_custom_call" | custom-call | flops 1207500032 | tf_op jit(solution)/shard_map/attend/pallas_call | solution.py:190
  43.0 5.8 %first_half.4 = (f32[192,8192]{1,0:T(8,128)S(1)}, bf16[512,8192]{1,0:T(8,128)(2,1)S(1)}) custom-call(bf16[192,512]{1,0:T(8,128)(2,1)S(1)} %bitcast.19, bf16[512,8192]{1,0:T(8,128)(2,1)} %near.3, bf16[512,8192]{1,0:T(8,128)(2,1)} %collective-permute-done.11.far), custom_call_target="tpu_custom_call" | custom-call | flops 2000999936 | tf_op jit(solution)/shard_map/first_half/pallas_call | solution.py:220
  48.8 1.8 %project.4 = (bf16[48,4096]{1,0:T(8,128)(2,1)S(1)}, bf16[48,4096]{1,0:T(8,128)(2,1)S(1)}, bf16[48,4096]{1,0:T(8,128)(2,1)S(1)}, bf16[48,4096]{1,0:T(8,128)(2,1)S...) custom-call(bf16[192,512]{1,0:T(8,128)(2,1)S(1)} %bitcast.18, ...), custom_call_target="tpu_custom_call" | custom-call | flops 517500000 | tf_op jit(solution)/shard_map/project/pallas_call | solution.py:258
  50.6 1.6 %collective-permute-start.24 = (bf16[48,4096]{1,0:T(8,128)(2,1)S(1)}, bf16[48,4096]{1,0:T(8,128)(2,1)S(1)}, u32[]{:S(2)}, u32[]{:S(2)}) collective-permute-start(bf16[48,4096]{1,0:T(8,128)(2,1)S(1)} %get-tuple-element.117), channel_id=1, source_target_pairs={{0,8},{4,12},{8,0},{12,4},{1,9},{5,13},{9,1},{13,5},{2,10},{6,14},... | collective-permute-start | bytes 1179656 | tf_op jit(solution)/shard_map/ppermute | solution.py:354
  52.2 1.1 add_convert_fusion.5
  53.3 4.1 %collective-permute-start.27 = (bf16[48,4096]{1,0:T(8,128)(2,1)S(1)}, bf16[48,4096]{1,0:T(8,128)(2,1)S(1)}, u32[]{:S(2)}, u32[]{:S(2)}) collective-permute-start(bf16[48,4096]{1,0:T(8,128)(2,1)S(1)} %add_convert_fusion.5), channel_id=1, source_target_pairs={{0,1},{3,2},{4,5},{7,6},{8,9},{11,10},{12,13},{15,14},{16,17},{19,... | collective-permute-start | bytes 1179656 | tf_op jit(solution)/shard_map/ppermute | solution.py:372
  57.4 2.4 %attend.5 = (bf16[2,48,512]{2,1,0:T(8,128)(2,1)S(1)}, bf16[2,48,512]{2,1,0:T(8,128)(2,1)S(1)}) custom-call(f32[8,1,768]{2,1,0:T(1,128)S(1)} %reshape.61.key_doc, bf16[576,128]{1,0:T(8,128)(2,1)S(1)} %get-tuple-element.63.refs_0_.refs_8_, bf16[576,128]{1,0:T(8,128)(2,1)S(1)} %collective-permute-done.refs_1_.refs_9_, ...), custom_call_target="tpu_custom_call" | custom-call | flops 966000000 | tf_op jit(solution)/shard_map/attend/pallas_call | solution.py:190
  59.9 1.6 %collective-permute-start.16 = (bf16[48,4096]{1,0:T(8,128)(2,1)S(1)}, bf16[48,4096]{1,0:T(8,128)(2,1)S(1)}, u32[]{:S(2)}, u32[]{:S(2)}) collective-permute-start(bf16[48,4096]{1,0:T(8,128)(2,1)S(1)} %get-tuple-element.109), channel_id=1, source_target_pairs={{0,8},{4,12},{8,0},{12,4},{1,9},{5,13},{9,1},{13,5},{2,10},{6,14},... | collective-permute-start | bytes 1179656 | tf_op jit(solution)/shard_map/ppermute | solution.py:354
  61.6 1.3 %collective-permute-start.19 = (bf16[48,4096]{1,0:T(8,128)(2,1)S(1)}, bf16[48,4096]{1,0:T(8,128)(2,1)S(1)}, u32[]{:S(2)}, u32[]{:S(2)}) collective-permute-start(bf16[48,4096]{1,0:T(8,128)(2,1)S(1)} %add_convert_fusion.13), channel_id=1, source_target_pairs={{0,1},{3,2},{4,5},{7,6},{8,9},{11,10},{12,13},{15,14},{16,17},{19,... | collective-permute-start | bytes 1179656 | tf_op jit(solution)/shard_map/ppermute | solution.py:372
  62.9 5.8 %first_half.5 = (f32[96,8192]{1,0:T(8,128)S(1)}, bf16[512,8192]{1,0:T(8,128)(2,1)S(1)}) custom-call(bf16[96,512]{1,0:T(8,128)(2,1)S(1)} %bitcast.20, bf16[512,8192]{1,0:T(8,128)(2,1)} %near.3, bf16[512,8192]{1,0:T(8,128)(2,1)} %collective-permute-done.11.far), custom_call_target="tpu_custom_call" | custom-call | flops 2000999936 | tf_op jit(solution)/shard_map/first_half/pallas_call | solution.py:220
  68.7 1.5 %project.5 = (bf16[48,4096]{1,0:T(8,128)(2,1)S(1)}, bf16[48,4096]{1,0:T(8,128)(2,1)S(1)}, bf16[48,4096]{1,0:T(8,128)(2,1)S(1)}, bf16[48,4096]{1,0:T(8,128)(2,1)S(1)}) custom-call(bf16[96,512]{1,0:T(8,128)(2,1)S(1)} %bitcast.21, bf16[512,8192]{1,0:T(8,128)(2,1)S(1)} %get-tuple-element.102.refs_1_, f32[96,8192]{1,0:T(8,128)S(1)} %get-tuple-element.103.refs_2_), custom_call_target="tpu_custom_call" | custom-call | flops 517500000 | tf_op jit(solution)/shard_map/project/pallas_call | solution.py:258
  70.3 1.3 %collective-permute-start.30 = (bf16[48,4096]{1,0:T(8,128)(2,1)S(1)}, bf16[48,4096]{1,0:T(8,128)(2,1)S(1)}, u32[]{:S(2)}, u32[]{:S(2)}) collective-permute-start(bf16[48,4096]{1,0:T(8,128)(2,1)S(1)} %add_convert_fusion.2), channel_id=1, source_target_pairs={{0,1},{3,2},{4,5},{7,6},{8,9},{11,10},{12,13},{15,14},{16,17},{19,... | collective-permute-start | bytes 1179656 | tf_op jit(solution)/shard_map/ppermute | solution.py:372
  71.7 0.7 collective-permute-start.28
  72.4 0.6 collective-permute-start.25
  73.2 3.3 %collective-permute-start.22 = (bf16[48,4096]{1,0:T(8,128)(2,1)S(1)}, bf16[48,4096]{1,0:T(8,128)(2,1)S(1)}, u32[]{:S(2)}, u32[]{:S(2)}) collective-permute-start(bf16[48,4096]{1,0:T(8,128)(2,1)S(1)} %add_convert_fusion.10), channel_id=1, source_target_pairs={{0,1},{3,2},{4,5},{7,6},{8,9},{11,10},{12,13},{15,14},{16,17},{19,... | collective-permute-start | bytes 1179656 | tf_op jit(solution)/shard_map/ppermute | solution.py:372
  76.6 0.7 collective-permute-start.20
  77.2 6.5 %collective-permute-done.30 = bf16[48,4096]{1,0:T(8,128)(2,1)S(1)} collective-permute-done((bf16[48,4096]{1,0:T(8,128)(2,1)S(1)}, bf16[48,4096]{1,0:T(8,128)(2,1)S(1)}, u32[]{:S(2)}, u32[]{:S(2)}) %collective-permute-start.30) | collective-permute-done | bytes 393248 | tf_op jit(solution)/shard_map/ppermute | solution.py:372
  83.7 1.5 %collective-permute-start.17 = (bf16[48,4096]{1,0:T(8,128)(2,1)S(1)}, bf16[48,4096]{1,0:T(8,128)(2,1)S(1)}, u32[]{:S(2)}, u32[]{:S(2)}) collective-permute-start(bf16[48,4096]{1,0:T(8,128)(2,1)S(1)} %get-tuple-element.110), channel_id=1, source_target_pairs={{0,8},{4,12},{8,0},{12,4},{1,9},{5,13},{9,1},{13,5},{2,10},{6,14},... | collective-permute-start | bytes 1179656 | tf_op jit(solution)/shard_map/ppermute | solution.py:354
  85.3 0.7 collective-permute-start.31
  86.2 3.8 %collective-permute-start.29 = (bf16[48,4096]{1,0:T(8,128)(2,1)S(1)}, bf16[48,4096]{1,0:T(8,128)(2,1)S(1)}, u32[]{:S(2)}, u32[]{:S(2)}) collective-permute-start(bf16[48,4096]{1,0:T(8,128)(2,1)S(1)} %fusion.1), channel_id=1, source_target_pairs={{0,1},{3,2},{1,0},{2,3},{4,5},{7,6},{5,4},{6,7},{8,9},{11,10},{9,8... | collective-permute-start | bytes 1179656 | tf_op jit(solution)/shard_map/ppermute | solution.py:372
  90.0 2.2 %collective-permute-done.22 = bf16[48,4096]{1,0:T(8,128)(2,1)S(1)} collective-permute-done((bf16[48,4096]{1,0:T(8,128)(2,1)S(1)}, bf16[48,4096]{1,0:T(8,128)(2,1)S(1)}, u32[]{:S(2)}, u32[]{:S(2)}) %collective-permute-start.22) | collective-permute-done | bytes 393248 | tf_op jit(solution)/shard_map/ppermute | solution.py:372
  92.1 1.5 %collective-permute-start.26 = (bf16[48,4096]{1,0:T(8,128)(2,1)S(1)}, bf16[48,4096]{1,0:T(8,128)(2,1)S(1)}, u32[]{:S(2)}, u32[]{:S(2)}) collective-permute-start(bf16[48,4096]{1,0:T(8,128)(2,1)S(1)} %get-tuple-element.119), channel_id=1, source_target_pairs={{0,8},{4,12},{8,0},{12,4},{1,9},{5,13},{9,1},{13,5},{2,10},{6,14},... | collective-permute-start | bytes 1179656 | tf_op jit(solution)/shard_map/ppermute | solution.py:354
  93.7 0.7 collective-permute-start.23
  94.6 3.8 %collective-permute-start.21 = (bf16[48,4096]{1,0:T(8,128)(2,1)S(1)}, bf16[48,4096]{1,0:T(8,128)(2,1)S(1)}, u32[]{:S(2)}, u32[]{:S(2)}) collective-permute-start(bf16[48,4096]{1,0:T(8,128)(2,1)S(1)} %fusion), channel_id=1, source_target_pairs={{0,1},{3,2},{1,0},{2,3},{4,5},{7,6},{5,4},{6,7},{8,9},{11,10},{9,8... | collective-permute-start | bytes 1179656 | tf_op jit(solution)/shard_map/ppermute | solution.py:372
  98.4 0.5 collective-permute-start.18
  98.9 1.6 %collective-permute-done.29 = bf16[48,4096]{1,0:T(8,128)(2,1)S(1)} collective-permute-done((bf16[48,4096]{1,0:T(8,128)(2,1)S(1)}, bf16[48,4096]{1,0:T(8,128)(2,1)S(1)}, u32[]{:S(2)}, u32[]{:S(2)}) %collective-permute-start.29) | collective-permute-done | bytes 393248 | tf_op jit(solution)/shard_map/ppermute | solution.py:372
  100.6 3.1 %collective-permute-done.26 = bf16[48,4096]{1,0:T(8,128)(2,1)S(1)} collective-permute-done((bf16[48,4096]{1,0:T(8,128)(2,1)S(1)}, bf16[48,4096]{1,0:T(8,128)(2,1)S(1)}, u32[]{:S(2)}, u32[]{:S(2)}) %collective-permute-start.26) | collective-permute-done | bytes 393248 | tf_op jit(solution)/shard_map/ppermute | solution.py:354
  103.9 4.0 %collective-permute-done.21 = bf16[48,4096]{1,0:T(8,128)(2,1)S(1)} collective-permute-done((bf16[48,4096]{1,0:T(8,128)(2,1)S(1)}, bf16[48,4096]{1,0:T(8,128)(2,1)S(1)}, u32[]{:S(2)}, u32[]{:S(2)}) %collective-permute-start.21) | collective-permute-done | bytes 393248 | tf_op jit(solution)/shard_map/ppermute | solution.py:372
  107.9 1.6 %collective-permute-done.18 = bf16[48,4096]{1,0:T(8,128)(2,1)S(1)} collective-permute-done((bf16[48,4096]{1,0:T(8,128)(2,1)S(1)}, bf16[48,4096]{1,0:T(8,128)(2,1)S(1)}, u32[]{:S(2)}, u32[]{:S(2)}) %collective-permute-start.18) | collective-permute-done | bytes 393248 | tf_op jit(solution)/shard_map/ppermute | solution.py:354
  109.7 0.9 pad_maximum_fusion
  (62 shorter events, 3.8 us)
Async XLA Ops:
  0.0 31.3 %collective-permute-start.11 = (bf16[512,8192]{1,0:T(8,128)(2,1)}, bf16[512,8192]{1,0:T(8,128)(2,1)}, u32[]{:S(2)}, u32[]{:S(2)}) collective-permute-start(bf16[512,8192]{1,0:T(8,128)(2,1)} %near.3), channel_id=1, source_target_pairs={{0,4},{4,0},{8,12},{12,8},{1,5},{5,1},{9,13},{13,9},{2,6},{6,2},{1... | collective-permute-start | bytes 25165832 | tf_op jit(solution)/shard_map/ppermute | solution.py:316
  1.9 9.5 %collective-permute-start = (bf16[576,128]{1,0:T(8,128)(2,1)S(1)}, bf16[576,128]{1,0:T(8,128)(2,1)S(1)}, u32[]{:S(2)}, u32[]{:S(2)}) collective-permute-start(bf16[576,128]{1,0:T(8,128)(2,1)S(1)} %get-tuple-element.64), channel_id=1, source_target_pairs={{0,1},{1,2},{2,3},{3,0},{4,5},{5,6},{6,7},{7,4},{8,9},{9,10},{10,1... | collective-permute-start | bytes 442376 | tf_op jit(solution)/shard_map/ppermute | solution.py:299
  4.6 12.9 %collective-permute-start.1 = (bf16[576,128]{1,0:T(8,128)(2,1)S(1)}, bf16[576,128]{1,0:T(8,128)(2,1)S(1)}, u32[]{:S(2)}, u32[]{:S(2)}) collective-permute-start(bf16[576,128]{1,0:T(8,128)(2,1)S(1)} %get-tuple-element.65), channel_id=1, source_target_pairs={{0,2},{1,3},{2,0},{3,1},{4,6},{5,7},{6,4},{7,5},{8,10},{9,11},{10,... | collective-permute-start | bytes 442376 | tf_op jit(solution)/shard_map/ppermute | solution.py:299
  7.1 13.8 %collective-permute-start.2 = (bf16[576,128]{1,0:T(8,128)(2,1)S(1)}, bf16[576,128]{1,0:T(8,128)(2,1)S(1)}, u32[]{:S(2)}, u32[]{:S(2)}) collective-permute-start(bf16[576,128]{1,0:T(8,128)(2,1)S(1)} %get-tuple-element.66), channel_id=1, source_target_pairs={{0,3},{1,0},{2,1},{3,2},{4,7},{5,4},{6,5},{7,6},{8,11},{9,8},{10,9... | collective-permute-start | bytes 442376 | tf_op jit(solution)/shard_map/ppermute | solution.py:299
  8.5 13.9 %collective-permute-start.3 = (bf16[384,128]{1,0:T(8,128)(2,1)S(1)}, bf16[384,128]{1,0:T(8,128)(2,1)S(1)}, u32[]{:S(2)}, u32[]{:S(2)}) collective-permute-start(bf16[384,128]{1,0:T(8,128)(2,1)S(1)} %slice.40), channel_id=1, source_target_pairs={{1,17},{2,18},{3,19},{5,21},{6,22},{7,23},{9,25},{10,26},{11,27},{... | collective-permute-start | bytes 294920 | tf_op jit(solution)/shard_map/ppermute | solution.py:314
  11.4 13.4 %collective-permute-start.4 = (bf16[384,128]{1,0:T(8,128)(2,1)S(1)}, bf16[384,128]{1,0:T(8,128)(2,1)S(1)}, u32[]{:S(2)}, u32[]{:S(2)}) collective-permute-start(bf16[384,128]{1,0:T(8,128)(2,1)S(1)} %slice.44), channel_id=1, source_target_pairs={{0,16},{2,18},{3,19},{4,20},{6,22},{7,23},{8,24},{10,26},{11,27},{... | collective-permute-start | bytes 294920 | tf_op jit(solution)/shard_map/ppermute | solution.py:314
  17.5 9.6 %collective-permute-start.5 = (bf16[384,128]{1,0:T(8,128)(2,1)S(1)}, bf16[384,128]{1,0:T(8,128)(2,1)S(1)}, u32[]{:S(2)}, u32[]{:S(2)}) collective-permute-start(bf16[384,128]{1,0:T(8,128)(2,1)S(1)} %slice.45), channel_id=1, source_target_pairs={{0,16},{1,17},{3,19},{4,20},{5,21},{7,23},{8,24},{9,25},{11,27},{1... | collective-permute-start | bytes 294920 | tf_op jit(solution)/shard_map/ppermute | solution.py:314
  21.0 6.9 %collective-permute-start.6 = (bf16[384,128]{1,0:T(8,128)(2,1)S(1)}, bf16[384,128]{1,0:T(8,128)(2,1)S(1)}, u32[]{:S(2)}, u32[]{:S(2)}) collective-permute-start(bf16[384,128]{1,0:T(8,128)(2,1)S(1)} %slice.46), channel_id=1, source_target_pairs={{0,16},{1,17},{2,18},{4,20},{5,21},{6,22},{8,24},{9,25},{10,26},{1... | collective-permute-start | bytes 294920 | tf_op jit(solution)/shard_map/ppermute | solution.py:314
  22.4 15.4 %collective-permute-start.7 = (bf16[576,128]{1,0:T(8,128)(2,1)S(1)}, bf16[576,128]{1,0:T(8,128)(2,1)S(1)}, u32[]{:S(2)}, u32[]{:S(2)}) collective-permute-start(bf16[576,128]{1,0:T(8,128)(2,1)S(1)} %get-tuple-element.69), channel_id=1, source_target_pairs={{0,1},{1,2},{2,3},{3,0},{4,5},{5,6},{6,7},{7,4},{8,9},{9,10},{10,1... | collective-permute-start | bytes 442376 | tf_op jit(solution)/shard_map/ppermute | solution.py:299
  24.8 13.0 %collective-permute-start.8 = (bf16[576,128]{1,0:T(8,128)(2,1)S(1)}, bf16[576,128]{1,0:T(8,128)(2,1)S(1)}, u32[]{:S(2)}, u32[]{:S(2)}) collective-permute-start(bf16[576,128]{1,0:T(8,128)(2,1)S(1)} %get-tuple-element.71), channel_id=1, source_target_pairs={{0,2},{1,3},{2,0},{3,1},{4,6},{5,7},{6,4},{7,5},{8,10},{9,11},{10,... | collective-permute-start | bytes 442376 | tf_op jit(solution)/shard_map/ppermute | solution.py:299
  27.1 10.6 %collective-permute-start.9 = (bf16[576,128]{1,0:T(8,128)(2,1)S(1)}, bf16[576,128]{1,0:T(8,128)(2,1)S(1)}, u32[]{:S(2)}, u32[]{:S(2)}) collective-permute-start(bf16[576,128]{1,0:T(8,128)(2,1)S(1)} %get-tuple-element.73), channel_id=1, source_target_pairs={{0,3},{1,0},{2,1},{3,2},{4,7},{5,4},{6,5},{7,6},{8,11},{9,8},{10,9... | collective-permute-start | bytes 442376 | tf_op jit(solution)/shard_map/ppermute | solution.py:299
  31.2 3.5 %collective-permute-start.10 = (bf16[2,48,512]{2,1,0:T(8,128)(2,1)S(1)}, bf16[2,48,512]{2,1,0:T(8,128)(2,1)S(1)}, u32[]{:S(2)}, u32[]{:S(2)}) collective-permute-start(bf16[2,48,512]{2,1,0:T(8,128)(2,1)S(1)} %get-tuple-element.74), channel_id=1, source_target_pairs={{0,4},{4,0},{8,12},{12,8},{1,5},{5,1},{9,13},{13,9},{2,6},{6,2},{1... | collective-permute-start | bytes 294920 | tf_op jit(solution)/shard_map/ppermute | solution.py:415
  36.2 14.4 %collective-permute-start.13 = (bf16[48,4096]{1,0:T(8,128)(2,1)S(1)}, bf16[48,4096]{1,0:T(8,128)(2,1)}, u32[]{:S(2)}, u32[]{:S(2)}) collective-permute-start(bf16[48,4096]{1,0:T(8,128)(2,1)S(1)} %get-tuple-element.95), channel_id=1, source_target_pairs={{0,8},{4,12},{8,0},{12,4},{1,9},{5,13},{9,1},{13,5},{2,10},{6,14},... | collective-permute-start | bytes 1179656 | tf_op jit(solution)/shard_map/ppermute | solution.py:354
  37.8 4.7 %copy-start = (bf16[576,128]{1,0:T(8,128)(2,1)}, bf16[576,128]{1,0:T(8,128)(2,1)S(1)}, u32[]{:S(2)}) copy-start(bf16[576,128]{1,0:T(8,128)(2,1)S(1)} %collective-permute-done.8.refs_10_) | copy-start | bytes 442372
  37.8 4.6 %copy-start.2 = (bf16[576,128]{1,0:T(8,128)(2,1)}, bf16[576,128]{1,0:T(8,128)(2,1)S(1)}, u32[]{:S(2)}) copy-start(bf16[576,128]{1,0:T(8,128)(2,1)S(1)} %collective-permute-done.9.refs_11_) | copy-start | bytes 442372
  42.2 6.6 %collective-permute-start.12 = (bf16[2,96,512]{2,1,0:T(8,128)(2,1)S(1)}, bf16[2,96,512]{2,1,0:T(8,128)(2,1)S(1)}, u32[]{:S(2)}, u32[]{:S(2)}) collective-permute-start(bf16[2,96,512]{2,1,0:T(8,128)(2,1)S(1)} %get-tuple-element.85), channel_id=1, source_target_pairs={{0,4},{4,0},{8,12},{12,8},{1,5},{5,1},{9,13},{13,9},{2,6},{6,2},{1... | collective-permute-start | bytes 589832 | tf_op jit(solution)/shard_map/ppermute | solution.py:415
  42.4 17.5 %collective-permute-start.15 = (bf16[48,4096]{1,0:T(8,128)(2,1)S(1)}, bf16[48,4096]{1,0:T(8,128)(2,1)S(1)}, u32[]{:S(2)}, u32[]{:S(2)}) collective-permute-start(bf16[48,4096]{1,0:T(8,128)(2,1)S(1)} %get-tuple-element.108), channel_id=1, source_target_pairs={{0,8},{4,12},{8,0},{12,4},{1,9},{5,13},{9,1},{13,5},{2,10},{6,14},... | collective-permute-start | bytes 1179656 | tf_op jit(solution)/shard_map/ppermute | solution.py:354
  48.8 8.6 %copy-start.1 = (bf16[576,128]{1,0:T(8,128)(2,1)S(1)}, bf16[576,128]{1,0:T(8,128)(2,1)}, u32[]{:S(2)}) copy-start(bf16[576,128]{1,0:T(8,128)(2,1)} %copy-done) | copy-start | bytes 442372
  48.8 8.6 %copy-start.3 = (bf16[576,128]{1,0:T(8,128)(2,1)S(1)}, bf16[576,128]{1,0:T(8,128)(2,1)}, u32[]{:S(2)}) copy-start(bf16[576,128]{1,0:T(8,128)(2,1)} %copy-done.2) | copy-start | bytes 442372
  50.6 19.5 %collective-permute-start.24 = (bf16[48,4096]{1,0:T(8,128)(2,1)S(1)}, bf16[48,4096]{1,0:T(8,128)(2,1)S(1)}, u32[]{:S(2)}, u32[]{:S(2)}) collective-permute-start(bf16[48,4096]{1,0:T(8,128)(2,1)S(1)} %get-tuple-element.117), channel_id=1, source_target_pairs={{0,8},{4,12},{8,0},{12,4},{1,9},{5,13},{9,1},{13,5},{2,10},{6,14},... | collective-permute-start | bytes 1179656 | tf_op jit(solution)/shard_map/ppermute | solution.py:354
  53.3 18.3 %collective-permute-start.27 = (bf16[48,4096]{1,0:T(8,128)(2,1)S(1)}, bf16[48,4096]{1,0:T(8,128)(2,1)S(1)}, u32[]{:S(2)}, u32[]{:S(2)}) collective-permute-start(bf16[48,4096]{1,0:T(8,128)(2,1)S(1)} %add_convert_fusion.5), channel_id=1, source_target_pairs={{0,1},{3,2},{4,5},{7,6},{8,9},{11,10},{12,13},{15,14},{16,17},{19,... | collective-permute-start | bytes 1179656 | tf_op jit(solution)/shard_map/ppermute | solution.py:372
  59.9 8.9 %collective-permute-start.14 = (bf16[2,48,512]{2,1,0:T(8,128)(2,1)S(1)}, bf16[2,48,512]{2,1,0:T(8,128)(2,1)S(1)}, u32[]{:S(2)}, u32[]{:S(2)}) collective-permute-start(bf16[2,48,512]{2,1,0:T(8,128)(2,1)S(1)} %get-tuple-element.100), channel_id=1, source_target_pairs={{0,4},{4,0},{8,12},{12,8},{1,5},{5,1},{9,13},{13,9},{2,6},{6,2},{1... | collective-permute-start | bytes 294920 | tf_op jit(solution)/shard_map/ppermute | solution.py:415
  59.9 13.1 %collective-permute-start.16 = (bf16[48,4096]{1,0:T(8,128)(2,1)S(1)}, bf16[48,4096]{1,0:T(8,128)(2,1)S(1)}, u32[]{:S(2)}, u32[]{:S(2)}) collective-permute-start(bf16[48,4096]{1,0:T(8,128)(2,1)S(1)} %get-tuple-element.109), channel_id=1, source_target_pairs={{0,8},{4,12},{8,0},{12,4},{1,9},{5,13},{9,1},{13,5},{2,10},{6,14},... | collective-permute-start | bytes 1179656 | tf_op jit(solution)/shard_map/ppermute | solution.py:354
  61.6 14.9 %collective-permute-start.19 = (bf16[48,4096]{1,0:T(8,128)(2,1)S(1)}, bf16[48,4096]{1,0:T(8,128)(2,1)S(1)}, u32[]{:S(2)}, u32[]{:S(2)}) collective-permute-start(bf16[48,4096]{1,0:T(8,128)(2,1)S(1)} %add_convert_fusion.13), channel_id=1, source_target_pairs={{0,1},{3,2},{4,5},{7,6},{8,9},{11,10},{12,13},{15,14},{16,17},{19,... | collective-permute-start | bytes 1179656 | tf_op jit(solution)/shard_map/ppermute | solution.py:372
  70.3 13.4 %collective-permute-start.30 = (bf16[48,4096]{1,0:T(8,128)(2,1)S(1)}, bf16[48,4096]{1,0:T(8,128)(2,1)S(1)}, u32[]{:S(2)}, u32[]{:S(2)}) collective-permute-start(bf16[48,4096]{1,0:T(8,128)(2,1)S(1)} %add_convert_fusion.2), channel_id=1, source_target_pairs={{0,1},{3,2},{4,5},{7,6},{8,9},{11,10},{12,13},{15,14},{16,17},{19,... | collective-permute-start | bytes 1179656 | tf_op jit(solution)/shard_map/ppermute | solution.py:372
  71.7 13.6 %collective-permute-start.28 = (bf16[48,4096]{1,0:T(8,128)(2,1)S(1)}, bf16[48,4096]{1,0:T(8,128)(2,1)S(1)}, u32[]{:S(2)}, u32[]{:S(2)}) collective-permute-start(bf16[48,4096]{1,0:T(8,128)(2,1)S(1)} %add_convert_fusion.4), channel_id=1, source_target_pairs={{1,2},{2,1},{5,6},{6,5},{9,10},{10,9},{13,14},{14,13},{17,18},{18,... | collective-permute-start | bytes 1179656 | tf_op jit(solution)/shard_map/ppermute | solution.py:372
  72.4 13.6 %collective-permute-start.25 = (bf16[48,4096]{1,0:T(8,128)(2,1)S(1)}, bf16[48,4096]{1,0:T(8,128)(2,1)S(1)}, u32[]{:S(2)}, u32[]{:S(2)}) collective-permute-start(bf16[48,4096]{1,0:T(8,128)(2,1)S(1)} %get-tuple-element.118), channel_id=1, source_target_pairs={{0,8},{4,12},{8,0},{12,4},{1,9},{5,13},{9,1},{13,5},{2,10},{6,14},... | collective-permute-start | bytes 1179656 | tf_op jit(solution)/shard_map/ppermute | solution.py:354
  73.2 19.0 %collective-permute-start.22 = (bf16[48,4096]{1,0:T(8,128)(2,1)S(1)}, bf16[48,4096]{1,0:T(8,128)(2,1)S(1)}, u32[]{:S(2)}, u32[]{:S(2)}) collective-permute-start(bf16[48,4096]{1,0:T(8,128)(2,1)S(1)} %add_convert_fusion.10), channel_id=1, source_target_pairs={{0,1},{3,2},{4,5},{7,6},{8,9},{11,10},{12,13},{15,14},{16,17},{19,... | collective-permute-start | bytes 1179656 | tf_op jit(solution)/shard_map/ppermute | solution.py:372
  76.6 17.2 %collective-permute-start.20 = (bf16[48,4096]{1,0:T(8,128)(2,1)S(1)}, bf16[48,4096]{1,0:T(8,128)(2,1)S(1)}, u32[]{:S(2)}, u32[]{:S(2)}) collective-permute-start(bf16[48,4096]{1,0:T(8,128)(2,1)S(1)} %add_convert_fusion.12), channel_id=1, source_target_pairs={{1,2},{2,1},{5,6},{6,5},{9,10},{10,9},{13,14},{14,13},{17,18},{18,... | collective-permute-start | bytes 1179656 | tf_op jit(solution)/shard_map/ppermute | solution.py:372
  83.7 10.7 %collective-permute-start.17 = (bf16[48,4096]{1,0:T(8,128)(2,1)S(1)}, bf16[48,4096]{1,0:T(8,128)(2,1)S(1)}, u32[]{:S(2)}, u32[]{:S(2)}) collective-permute-start(bf16[48,4096]{1,0:T(8,128)(2,1)S(1)} %get-tuple-element.110), channel_id=1, source_target_pairs={{0,8},{4,12},{8,0},{12,4},{1,9},{5,13},{9,1},{13,5},{2,10},{6,14},... | collective-permute-start | bytes 1179656 | tf_op jit(solution)/shard_map/ppermute | solution.py:354
  85.3 13.1 %collective-permute-start.31 = (bf16[48,4096]{1,0:T(8,128)(2,1)S(1)}, bf16[48,4096]{1,0:T(8,128)(2,1)S(1)}, u32[]{:S(2)}, u32[]{:S(2)}) collective-permute-start(bf16[48,4096]{1,0:T(8,128)(2,1)S(1)} %add_convert_fusion.1), channel_id=1, source_target_pairs={{1,2},{2,1},{5,6},{6,5},{9,10},{10,9},{13,14},{14,13},{17,18},{18,... | collective-permute-start | bytes 1179656 | tf_op jit(solution)/shard_map/ppermute | solution.py:372
  86.2 14.4 %collective-permute-start.29 = (bf16[48,4096]{1,0:T(8,128)(2,1)S(1)}, bf16[48,4096]{1,0:T(8,128)(2,1)S(1)}, u32[]{:S(2)}, u32[]{:S(2)}) collective-permute-start(bf16[48,4096]{1,0:T(8,128)(2,1)S(1)} %fusion.1), channel_id=1, source_target_pairs={{0,1},{3,2},{1,0},{2,3},{4,5},{7,6},{5,4},{6,7},{8,9},{11,10},{9,8... | collective-permute-start | bytes 1179656 | tf_op jit(solution)/shard_map/ppermute | solution.py:372
  92.1 11.5 %collective-permute-start.26 = (bf16[48,4096]{1,0:T(8,128)(2,1)S(1)}, bf16[48,4096]{1,0:T(8,128)(2,1)S(1)}, u32[]{:S(2)}, u32[]{:S(2)}) collective-permute-start(bf16[48,4096]{1,0:T(8,128)(2,1)S(1)} %get-tuple-element.119), channel_id=1, source_target_pairs={{0,8},{4,12},{8,0},{12,4},{1,9},{5,13},{9,1},{13,5},{2,10},{6,14},... | collective-permute-start | bytes 1179656 | tf_op jit(solution)/shard_map/ppermute | solution.py:354
  93.7 10.1 %collective-permute-start.23 = (bf16[48,4096]{1,0:T(8,128)(2,1)S(1)}, bf16[48,4096]{1,0:T(8,128)(2,1)S(1)}, u32[]{:S(2)}, u32[]{:S(2)}) collective-permute-start(bf16[48,4096]{1,0:T(8,128)(2,1)S(1)} %add_convert_fusion.9), channel_id=1, source_target_pairs={{1,2},{2,1},{5,6},{6,5},{9,10},{10,9},{13,14},{14,13},{17,18},{18,... | collective-permute-start | bytes 1179656 | tf_op jit(solution)/shard_map/ppermute | solution.py:372
  94.6 13.3 %collective-permute-start.21 = (bf16[48,4096]{1,0:T(8,128)(2,1)S(1)}, bf16[48,4096]{1,0:T(8,128)(2,1)S(1)}, u32[]{:S(2)}, u32[]{:S(2)}) collective-permute-start(bf16[48,4096]{1,0:T(8,128)(2,1)S(1)} %fusion), channel_id=1, source_target_pairs={{0,1},{3,2},{1,0},{2,3},{4,5},{7,6},{5,4},{6,7},{8,9},{11,10},{9,8... | collective-permute-start | bytes 1179656 | tf_op jit(solution)/shard_map/ppermute | solution.py:372
  98.4 11.1 %collective-permute-start.18 = (bf16[48,4096]{1,0:T(8,128)(2,1)S(1)}, bf16[48,4096]{1,0:T(8,128)(2,1)S(1)}, u32[]{:S(2)}, u32[]{:S(2)}) collective-permute-start(bf16[48,4096]{1,0:T(8,128)(2,1)S(1)} %get-tuple-element.111), channel_id=1, source_target_pairs={{0,8},{4,12},{8,0},{12,4},{1,9},{5,13},{9,1},{13,5},{2,10},{6,14},... | collective-permute-start | bytes 1179656 | tf_op jit(solution)/shard_map/ppermute | solution.py:354

commit v12 on v11

--- a/solution.py
+++ b/solution.py
@@ -20,7 +20,7 @@
 VMEM = pl.BlockSpec(memory_space=pltpu.VMEM)
 SMEM = pl.BlockSpec(memory_space=pltpu.SMEM)
 HBM = pl.BlockSpec(memory_space=pltpu.HBM)
-LIMIT = pltpu.CompilerParams(vmem_limit_bytes=18 << 20)
+LIMIT = pltpu.CompilerParams(vmem_limit_bytes=12 << 20)
 TILE = 1024
 HALVES = 2
 UNDER_WAY = 2

time: 111 us -> 111 us (level)
  no operation moved by 1% of the time
where the time goes in v12:
time: 111 us
  starting transfers between devices  51.4 us (46%)
  Pallas kernels  31.4 us (28%)
  waiting for transfers between devices  21.9 us (20%)
  other arithmetic  5.15 us (5%)
    ppermute x10, starting transfers between devices, step(): now.setdefault(c, {})[n] = lax.ppermute(message, 'wsh', route)  20.3 us
    pallas_call x3, Pallas kernels, first_half(): pl.pallas_call(first_half_kernel, out_shape=[pltpu.VMEM((rows_here.shape[...  15 us
    ppermute x10, waiting for transfers between devices, step(): now.setdefault(c, {})[n] = lax.ppermute(message, 'wsh', route)  14.3 us
    ppermute x6, starting transfers between devices, around(): lax.ppermute(array, 'wsh', [(i, (i + k) % slabs) for i in range(slabs)])  12 us
    pallas_call x3, Pallas kernels, attend(): pl.pallas_call(partial(attend_kernel, slabs=slabs, heads=heads, share=sha...  10.2 us
    ppermute x8, starting transfers between devices, cross(): lax.ppermute(a, 'head', r)  9.31 us
    ppermute x4, starting transfers between devices, on_device(): lax.ppermute(a[:2 * block], ('srv', 'wsh'), within_reach(k))  8.94 us
    ppermute x8, waiting for transfers between devices, cross(): lax.ppermute(a, 'head', r)  4.76 us
  transfers between devices with their start and end apart: 32, of which 8 were waited for; matrix products, arithmetic and copies ran while one was open for 4% of the time, Pallas kernels for 28%

profile of v12, /device:TPU:0, one launch (start us, length us, event | category | flops | bytes accessed | tf_op | source)
XLA Modules:
  0.0 110.6 jit_solution(3961142376794089091)
XLA Ops:
  0.5 1.5 %pack.1 = (bf16[576,128]{1,0:T(8,128)(2,1)S(1)}, bf16[576,128]{1,0:T(8,128)(2,1)S(1)}, bf16[576,128]{1,0:T(8,128)(2,1)S(1)}, bf16[576,128]{1,0:T(8,128)(2,1)S(1)...) custom-call(bf16[192,2048]{1,0:T(8,128)(2,1)} %queries.1, ...), custom_call_target="tpu_custom_call" | custom-call | tf_op jit(solution)/shard_map/pack/pallas_call | solution.py:101
  1.9 2.6 %collective-permute-start = (bf16[576,128]{1,0:T(8,128)(2,1)S(1)}, bf16[576,128]{1,0:T(8,128)(2,1)S(1)}, u32[]{:S(2)}, u32[]{:S(2)}) collective-permute-start(bf16[576,128]{1,0:T(8,128)(2,1)S(1)} %get-tuple-element.64), channel_id=1, source_target_pairs={{0,1},{1,2},{2,3},{3,0},{4,5},{5,6},{6,7},{7,4},{8,9},{9,10},{10,1... | collective-permute-start | bytes 442376 | tf_op jit(solution)/shard_map/ppermute | solution.py:299
  4.6 2.6 %collective-permute-start.1 = (bf16[576,128]{1,0:T(8,128)(2,1)S(1)}, bf16[576,128]{1,0:T(8,128)(2,1)S(1)}, u32[]{:S(2)}, u32[]{:S(2)}) collective-permute-start(bf16[576,128]{1,0:T(8,128)(2,1)S(1)} %get-tuple-element.65), channel_id=1, source_target_pairs={{0,2},{1,3},{2,0},{3,1},{4,6},{5,7},{6,4},{7,5},{8,10},{9,11},{10,... | collective-permute-start | bytes 442376 | tf_op jit(solution)/shard_map/ppermute | solution.py:299
  7.1 1.3 %collective-permute-start.2 = (bf16[576,128]{1,0:T(8,128)(2,1)S(1)}, bf16[576,128]{1,0:T(8,128)(2,1)S(1)}, u32[]{:S(2)}, u32[]{:S(2)}) collective-permute-start(bf16[576,128]{1,0:T(8,128)(2,1)S(1)} %get-tuple-element.66), channel_id=1, source_target_pairs={{0,3},{1,0},{2,1},{3,2},{4,7},{5,4},{6,5},{7,6},{8,11},{9,8},{10,9... | collective-permute-start | bytes 442376 | tf_op jit(solution)/shard_map/ppermute | solution.py:299
  8.5 0.7 collective-permute-start.3
  9.2 0.7 convert_element_type.166
  10.0 0.8 compare_bitcast_fusion.3
  11.4 3.6 %collective-permute-start.4 = (bf16[384,128]{1,0:T(8,128)(2,1)S(1)}, bf16[384,128]{1,0:T(8,128)(2,1)S(1)}, u32[]{:S(2)}, u32[]{:S(2)}) collective-permute-start(bf16[384,128]{1,0:T(8,128)(2,1)S(1)} %slice.44), channel_id=1, source_target_pairs={{0,16},{2,18},{3,19},{4,20},{6,22},{7,23},{8,24},{10,26},{11,27},{... | collective-permute-start | bytes 294920 | tf_op jit(solution)/shard_map/ppermute | solution.py:314
  15.0 2.5 %collective-permute-done.1.refs_2_.refs_10_ = bf16[576,128]{1,0:T(8,128)(2,1)S(1)} collective-permute-done((bf16[576,128]{1,0:T(8,128)(2,1)S(1)}, bf16[576,128]{1,0:T(8,128)(2,1)S(1)}, u32[]{:S(2)}, u32[]{:S(2)}) %collective-permute-start.1) | collective-permute-done | bytes 147488 | tf_op jit(solution)/shard_map/ppermute | solution.py:299
  17.5 3.4 %collective-permute-start.5 = (bf16[384,128]{1,0:T(8,128)(2,1)S(1)}, bf16[384,128]{1,0:T(8,128)(2,1)S(1)}, u32[]{:S(2)}, u32[]{:S(2)}) collective-permute-start(bf16[384,128]{1,0:T(8,128)(2,1)S(1)} %slice.45), channel_id=1, source_target_pairs={{0,16},{1,17},{3,19},{4,20},{5,21},{7,23},{8,24},{9,25},{11,27},{1... | collective-permute-start | bytes 294920 | tf_op jit(solution)/shard_map/ppermute | solution.py:314
  21.0 1.3 %collective-permute-start.6 = (bf16[384,128]{1,0:T(8,128)(2,1)S(1)}, bf16[384,128]{1,0:T(8,128)(2,1)S(1)}, u32[]{:S(2)}, u32[]{:S(2)}) collective-permute-start(bf16[384,128]{1,0:T(8,128)(2,1)S(1)} %slice.46), channel_id=1, source_target_pairs={{0,16},{1,17},{2,18},{4,20},{5,21},{6,22},{8,24},{9,25},{10,26},{1... | collective-permute-start | bytes 294920 | tf_op jit(solution)/shard_map/ppermute | solution.py:314
  22.4 2.4 %collective-permute-start.7 = (bf16[576,128]{1,0:T(8,128)(2,1)S(1)}, bf16[576,128]{1,0:T(8,128)(2,1)S(1)}, u32[]{:S(2)}, u32[]{:S(2)}) collective-permute-start(bf16[576,128]{1,0:T(8,128)(2,1)S(1)} %get-tuple-element.69), channel_id=1, source_target_pairs={{0,1},{1,2},{2,3},{3,0},{4,5},{5,6},{6,7},{7,4},{8,9},{9,10},{10,1... | collective-permute-start | bytes 442376 | tf_op jit(solution)/shard_map/ppermute | solution.py:299
  24.8 2.3 %collective-permute-start.8 = (bf16[576,128]{1,0:T(8,128)(2,1)S(1)}, bf16[576,128]{1,0:T(8,128)(2,1)S(1)}, u32[]{:S(2)}, u32[]{:S(2)}) collective-permute-start(bf16[576,128]{1,0:T(8,128)(2,1)S(1)} %get-tuple-element.71), channel_id=1, source_target_pairs={{0,2},{1,3},{2,0},{3,1},{4,6},{5,7},{6,4},{7,5},{8,10},{9,11},{10,... | collective-permute-start | bytes 442376 | tf_op jit(solution)/shard_map/ppermute | solution.py:299
  27.1 0.7 collective-permute-start.9
  27.9 3.4 %attend.3 = (bf16[2,48,512]{2,1,0:T(8,128)(2,1)S(1)}, bf16[2,48,512]{2,1,0:T(8,128)(2,1)S(1)}, bf16[512,8192]{1,0:T(8,128)(2,1)S(1)}) custom-call(f32[8,1,768]{2,1,0:T(1,128)S(1)} %reshape.61.key_doc, bf16[576,128]{1,0:T(8,128)(2,1)S(1)} %get-tuple-element.63.refs_0_.refs_8_, bf16[576,128]{1,0:T(8,128)(2,1)S(1)} %collective-permute-done.refs_1_.refs_9_, ...), custom_call_target="tpu_custom_call" | custom-call | flops 1150000000 | tf_op jit(solution)/shard_map/attend/pallas_call | solution.py:190
  31.3 3.4 %first_half.3 = (f32[96,8192]{1,0:T(8,128)S(1)}, bf16[512,8192]{1,0:T(8,128)(2,1)S(1)}) custom-call(bf16[96,512]{1,0:T(8,128)(2,1)S(1)} %bitcast.23, bf16[512,8192]{1,0:T(8,128)(2,1)S(1)} %get-tuple-element.76.near, bf16[512,8192]{1,0:T(8,128)(2,1)} %collective-permute-done.11.far), custom_call_target="tpu_custom_call" | custom-call | flops 1172999936 | tf_op jit(solution)/shard_map/first_half/pallas_call | solution.py:220
  34.8 1.5 %project.3 = (bf16[48,4096]{1,0:T(8,128)(2,1)S(1)}, bf16[48,4096]{1,0:T(8,128)(2,1)S(1)}, bf16[48,4096]{1,0:T(8,128)(2,1)S(1)}, bf16[48,4096]{1,0:T(8,128)(2,1)S(1)}) custom-call(bf16[96,512]{1,0:T(8,128)(2,1)S(1)} %bitcast.22, bf16[512,8192]{1,0:T(8,128)(2,1)S(1)} %get-tuple-element.77.refs_1_, f32[96,8192]{1,0:T(8,128)S(1)} %get-tuple-element.78.refs_2_), custom_call_target="tpu_custom_call" | custom-call | flops 517500000 | tf_op jit(solution)/shard_map/project/pallas_call | solution.py:258
  36.2 1.6 %collective-permute-start.13 = (bf16[48,4096]{1,0:T(8,128)(2,1)S(1)}, bf16[48,4096]{1,0:T(8,128)(2,1)}, u32[]{:S(2)}, u32[]{:S(2)}) collective-permute-start(bf16[48,4096]{1,0:T(8,128)(2,1)S(1)} %get-tuple-element.95), channel_id=1, source_target_pairs={{0,8},{4,12},{8,0},{12,4},{1,9},{5,13},{9,1},{13,5},{2,10},{6,14},... | collective-permute-start | bytes 1179656 | tf_op jit(solution)/shard_map/ppermute | solution.py:354
  37.8 4.3 %attend.4 = (bf16[2,96,512]{2,1,0:T(8,128)(2,1)S(1)}, bf16[2,96,512]{2,1,0:T(8,128)(2,1)S(1)}) custom-call(f32[8,1,768]{2,1,0:T(1,128)S(1)} %reshape.61.key_doc, bf16[576,128]{1,0:T(8,128)(2,1)S(1)} %get-tuple-element.63.refs_0_.refs_8_, bf16[576,128]{1,0:T(8,128)(2,1)S(1)} %collective-permute-done.refs_1_.refs_9_, ...), custom_call_target="tpu_custom_call" | custom-call | flops 1207500032 | tf_op jit(solution)/shard_map/attend/pallas_call | solution.py:190
  43.0 5.8 %first_half.4 = (f32[192,8192]{1,0:T(8,128)S(1)}, bf16[512,8192]{1,0:T(8,128)(2,1)S(1)}) custom-call(bf16[192,512]{1,0:T(8,128)(2,1)S(1)} %bitcast.19, bf16[512,8192]{1,0:T(8,128)(2,1)} %near.3, bf16[512,8192]{1,0:T(8,128)(2,1)} %collective-permute-done.11.far), custom_call_target="tpu_custom_call" | custom-call | flops 2000999936 | tf_op jit(solution)/shard_map/first_half/pallas_call | solution.py:220
  48.8 1.8 %project.4 = (bf16[48,4096]{1,0:T(8,128)(2,1)S(1)}, bf16[48,4096]{1,0:T(8,128)(2,1)S(1)}, bf16[48,4096]{1,0:T(8,128)(2,1)S(1)}, bf16[48,4096]{1,0:T(8,128)(2,1)S...) custom-call(bf16[192,512]{1,0:T(8,128)(2,1)S(1)} %bitcast.18, ...), custom_call_target="tpu_custom_call" | custom-call | flops 517500000 | tf_op jit(solution)/shard_map/project/pallas_call | solution.py:258
  50.6 1.6 %collective-permute-start.24 = (bf16[48,4096]{1,0:T(8,128)(2,1)S(1)}, bf16[48,4096]{1,0:T(8,128)(2,1)S(1)}, u32[]{:S(2)}, u32[]{:S(2)}) collective-permute-start(bf16[48,4096]{1,0:T(8,128)(2,1)S(1)} %get-tuple-element.117), channel_id=1, source_target_pairs={{0,8},{4,12},{8,0},{12,4},{1,9},{5,13},{9,1},{13,5},{2,10},{6,14},... | collective-permute-start | bytes 1179656 | tf_op jit(solution)/shard_map/ppermute | solution.py:354
  52.2 1.1 add_convert_fusion.5
  53.3 4.1 %collective-permute-start.27 = (bf16[48,4096]{1,0:T(8,128)(2,1)S(1)}, bf16[48,4096]{1,0:T(8,128)(2,1)S(1)}, u32[]{:S(2)}, u32[]{:S(2)}) collective-permute-start(bf16[48,4096]{1,0:T(8,128)(2,1)S(1)} %add_convert_fusion.5), channel_id=1, source_target_pairs={{0,1},{3,2},{4,5},{7,6},{8,9},{11,10},{12,13},{15,14},{16,17},{19,... | collective-permute-start | bytes 1179656 | tf_op jit(solution)/shard_map/ppermute | solution.py:372
  57.4 2.4 %attend.5 = (bf16[2,48,512]{2,1,0:T(8,128)(2,1)S(1)}, bf16[2,48,512]{2,1,0:T(8,128)(2,1)S(1)}) custom-call(f32[8,1,768]{2,1,0:T(1,128)S(1)} %reshape.61.key_doc, bf16[576,128]{1,0:T(8,128)(2,1)S(1)} %get-tuple-element.63.refs_0_.refs_8_, bf16[576,128]{1,0:T(8,128)(2,1)S(1)} %collective-permute-done.refs_1_.refs_9_, ...), custom_call_target="tpu_custom_call" | custom-call | flops 966000000 | tf_op jit(solution)/shard_map/attend/pallas_call | solution.py:190
  59.9 1.6 %collective-permute-start.16 = (bf16[48,4096]{1,0:T(8,128)(2,1)S(1)}, bf16[48,4096]{1,0:T(8,128)(2,1)S(1)}, u32[]{:S(2)}, u32[]{:S(2)}) collective-permute-start(bf16[48,4096]{1,0:T(8,128)(2,1)S(1)} %get-tuple-element.109), channel_id=1, source_target_pairs={{0,8},{4,12},{8,0},{12,4},{1,9},{5,13},{9,1},{13,5},{2,10},{6,14},... | collective-permute-start | bytes 1179656 | tf_op jit(solution)/shard_map/ppermute | solution.py:354
  61.6 1.3 %collective-permute-start.19 = (bf16[48,4096]{1,0:T(8,128)(2,1)S(1)}, bf16[48,4096]{1,0:T(8,128)(2,1)S(1)}, u32[]{:S(2)}, u32[]{:S(2)}) collective-permute-start(bf16[48,4096]{1,0:T(8,128)(2,1)S(1)} %add_convert_fusion.13), channel_id=1, source_target_pairs={{0,1},{3,2},{4,5},{7,6},{8,9},{11,10},{12,13},{15,14},{16,17},{19,... | collective-permute-start | bytes 1179656 | tf_op jit(solution)/shard_map/ppermute | solution.py:372
  62.9 5.8 %first_half.5 = (f32[96,8192]{1,0:T(8,128)S(1)}, bf16[512,8192]{1,0:T(8,128)(2,1)S(1)}) custom-call(bf16[96,512]{1,0:T(8,128)(2,1)S(1)} %bitcast.20, bf16[512,8192]{1,0:T(8,128)(2,1)} %near.3, bf16[512,8192]{1,0:T(8,128)(2,1)} %collective-permute-done.11.far), custom_call_target="tpu_custom_call" | custom-call | flops 2000999936 | tf_op jit(solution)/shard_map/first_half/pallas_call | solution.py:220
  68.7 1.5 %project.5 = (bf16[48,4096]{1,0:T(8,128)(2,1)S(1)}, bf16[48,4096]{1,0:T(8,128)(2,1)S(1)}, bf16[48,4096]{1,0:T(8,128)(2,1)S(1)}, bf16[48,4096]{1,0:T(8,128)(2,1)S(1)}) custom-call(bf16[96,512]{1,0:T(8,128)(2,1)S(1)} %bitcast.21, bf16[512,8192]{1,0:T(8,128)(2,1)S(1)} %get-tuple-element.102.refs_1_, f32[96,8192]{1,0:T(8,128)S(1)} %get-tuple-element.103.refs_2_), custom_call_target="tpu_custom_call" | custom-call | flops 517500000 | tf_op jit(solution)/shard_map/project/pallas_call | solution.py:258
  70.3 1.3 %collective-permute-start.30 = (bf16[48,4096]{1,0:T(8,128)(2,1)S(1)}, bf16[48,4096]{1,0:T(8,128)(2,1)S(1)}, u32[]{:S(2)}, u32[]{:S(2)}) collective-permute-start(bf16[48,4096]{1,0:T(8,128)(2,1)S(1)} %add_convert_fusion.2), channel_id=1, source_target_pairs={{0,1},{3,2},{4,5},{7,6},{8,9},{11,10},{12,13},{15,14},{16,17},{19,... | collective-permute-start | bytes 1179656 | tf_op jit(solution)/shard_map/ppermute | solution.py:372
  71.7 0.7 collective-permute-start.28
  72.4 0.6 collective-permute-start.25
  73.2 3.3 %collective-permute-start.22 = (bf16[48,4096]{1,0:T(8,128)(2,1)S(1)}, bf16[48,4096]{1,0:T(8,128)(2,1)S(1)}, u32[]{:S(2)}, u32[]{:S(2)}) collective-permute-start(bf16[48,4096]{1,0:T(8,128)(2,1)S(1)} %add_convert_fusion.10), channel_id=1, source_target_pairs={{0,1},{3,2},{4,5},{7,6},{8,9},{11,10},{12,13},{15,14},{16,17},{19,... | collective-permute-start | bytes 1179656 | tf_op jit(solution)/shard_map/ppermute | solution.py:372
  76.6 0.7 collective-permute-start.20
  77.2 6.5 %collective-permute-done.30 = bf16[48,4096]{1,0:T(8,128)(2,1)S(1)} collective-permute-done((bf16[48,4096]{1,0:T(8,128)(2,1)S(1)}, bf16[48,4096]{1,0:T(8,128)(2,1)S(1)}, u32[]{:S(2)}, u32[]{:S(2)}) %collective-permute-start.30) | collective-permute-done | bytes 393248 | tf_op jit(solution)/shard_map/ppermute | solution.py:372
  83.7 1.5 %collective-permute-start.17 = (bf16[48,4096]{1,0:T(8,128)(2,1)S(1)}, bf16[48,4096]{1,0:T(8,128)(2,1)S(1)}, u32[]{:S(2)}, u32[]{:S(2)}) collective-permute-start(bf16[48,4096]{1,0:T(8,128)(2,1)S(1)} %get-tuple-element.110), channel_id=1, source_target_pairs={{0,8},{4,12},{8,0},{12,4},{1,9},{5,13},{9,1},{13,5},{2,10},{6,14},... | collective-permute-start | bytes 1179656 | tf_op jit(solution)/shard_map/ppermute | solution.py:354
  85.3 0.7 collective-permute-start.31
  86.2 3.8 %collective-permute-start.29 = (bf16[48,4096]{1,0:T(8,128)(2,1)S(1)}, bf16[48,4096]{1,0:T(8,128)(2,1)S(1)}, u32[]{:S(2)}, u32[]{:S(2)}) collective-permute-start(bf16[48,4096]{1,0:T(8,128)(2,1)S(1)} %fusion.1), channel_id=1, source_target_pairs={{0,1},{3,2},{1,0},{2,3},{4,5},{7,6},{5,4},{6,7},{8,9},{11,10},{9,8... | collective-permute-start | bytes 1179656 | tf_op jit(solution)/shard_map/ppermute | solution.py:372
  90.0 2.2 %collective-permute-done.22 = bf16[48,4096]{1,0:T(8,128)(2,1)S(1)} collective-permute-done((bf16[48,4096]{1,0:T(8,128)(2,1)S(1)}, bf16[48,4096]{1,0:T(8,128)(2,1)S(1)}, u32[]{:S(2)}, u32[]{:S(2)}) %collective-permute-start.22) | collective-permute-done | bytes 393248 | tf_op jit(solution)/shard_map/ppermute | solution.py:372
  92.1 1.5 %collective-permute-start.26 = (bf16[48,4096]{1,0:T(8,128)(2,1)S(1)}, bf16[48,4096]{1,0:T(8,128)(2,1)S(1)}, u32[]{:S(2)}, u32[]{:S(2)}) collective-permute-start(bf16[48,4096]{1,0:T(8,128)(2,1)S(1)} %get-tuple-element.119), channel_id=1, source_target_pairs={{0,8},{4,12},{8,0},{12,4},{1,9},{5,13},{9,1},{13,5},{2,10},{6,14},... | collective-permute-start | bytes 1179656 | tf_op jit(solution)/shard_map/ppermute | solution.py:354
  93.7 0.7 collective-permute-start.23
  94.6 3.8 %collective-permute-start.21 = (bf16[48,4096]{1,0:T(8,128)(2,1)S(1)}, bf16[48,4096]{1,0:T(8,128)(2,1)S(1)}, u32[]{:S(2)}, u32[]{:S(2)}) collective-permute-start(bf16[48,4096]{1,0:T(8,128)(2,1)S(1)} %fusion), channel_id=1, source_target_pairs={{0,1},{3,2},{1,0},{2,3},{4,5},{7,6},{5,4},{6,7},{8,9},{11,10},{9,8... | collective-permute-start | bytes 1179656 | tf_op jit(solution)/shard_map/ppermute | solution.py:372
  98.4 0.5 collective-permute-start.18
  98.9 1.6 %collective-permute-done.29 = bf16[48,4096]{1,0:T(8,128)(2,1)S(1)} collective-permute-done((bf16[48,4096]{1,0:T(8,128)(2,1)S(1)}, bf16[48,4096]{1,0:T(8,128)(2,1)S(1)}, u32[]{:S(2)}, u32[]{:S(2)}) %collective-permute-start.29) | collective-permute-done | bytes 393248 | tf_op jit(solution)/shard_map/ppermute | solution.py:372
  100.6 3.1 %collective-permute-done.26 = bf16[48,4096]{1,0:T(8,128)(2,1)S(1)} collective-permute-done((bf16[48,4096]{1,0:T(8,128)(2,1)S(1)}, bf16[48,4096]{1,0:T(8,128)(2,1)S(1)}, u32[]{:S(2)}, u32[]{:S(2)}) %collective-permute-start.26) | collective-permute-done | bytes 393248 | tf_op jit(solution)/shard_map/ppermute | solution.py:354
  103.9 4.0 %collective-permute-done.21 = bf16[48,4096]{1,0:T(8,128)(2,1)S(1)} collective-permute-done((bf16[48,4096]{1,0:T(8,128)(2,1)S(1)}, bf16[48,4096]{1,0:T(8,128)(2,1)S(1)}, u32[]{:S(2)}, u32[]{:S(2)}) %collective-permute-start.21) | collective-permute-done | bytes 393248 | tf_op jit(solution)/shard_map/ppermute | solution.py:372
  107.9 1.6 %collective-permute-done.18 = bf16[48,4096]{1,0:T(8,128)(2,1)S(1)} collective-permute-done((bf16[48,4096]{1,0:T(8,128)(2,1)S(1)}, bf16[48,4096]{1,0:T(8,128)(2,1)S(1)}, u32[]{:S(2)}, u32[]{:S(2)}) %collective-permute-start.18) | collective-permute-done | bytes 393248 | tf_op jit(solution)/shard_map/ppermute | solution.py:354
  109.7 0.9 pad_maximum_fusion
  (62 shorter events, 3.8 us)
Async XLA Ops:
  0.0 31.3 %collective-permute-start.11 = (bf16[512,8192]{1,0:T(8,128)(2,1)}, bf16[512,8192]{1,0:T(8,128)(2,1)}, u32[]{:S(2)}, u32[]{:S(2)}) collective-permute-start(bf16[512,8192]{1,0:T(8,128)(2,1)} %near.3), channel_id=1, source_target_pairs={{0,4},{4,0},{8,12},{12,8},{1,5},{5,1},{9,13},{13,9},{2,6},{6,2},{1... | collective-permute-start | bytes 25165832 | tf_op jit(solution)/shard_map/ppermute | solution.py:316
  1.9 9.5 %collective-permute-start = (bf16[576,128]{1,0:T(8,128)(2,1)S(1)}, bf16[576,128]{1,0:T(8,128)(2,1)S(1)}, u32[]{:S(2)}, u32[]{:S(2)}) collective-permute-start(bf16[576,128]{1,0:T(8,128)(2,1)S(1)} %get-tuple-element.64), channel_id=1, source_target_pairs={{0,1},{1,2},{2,3},{3,0},{4,5},{5,6},{6,7},{7,4},{8,9},{9,10},{10,1... | collective-permute-start | bytes 442376 | tf_op jit(solution)/shard_map/ppermute | solution.py:299
  4.6 12.9 %collective-permute-start.1 = (bf16[576,128]{1,0:T(8,128)(2,1)S(1)}, bf16[576,128]{1,0:T(8,128)(2,1)S(1)}, u32[]{:S(2)}, u32[]{:S(2)}) collective-permute-start(bf16[576,128]{1,0:T(8,128)(2,1)S(1)} %get-tuple-element.65), channel_id=1, source_target_pairs={{0,2},{1,3},{2,0},{3,1},{4,6},{5,7},{6,4},{7,5},{8,10},{9,11},{10,... | collective-permute-start | bytes 442376 | tf_op jit(solution)/shard_map/ppermute | solution.py:299
  7.1 13.8 %collective-permute-start.2 = (bf16[576,128]{1,0:T(8,128)(2,1)S(1)}, bf16[576,128]{1,0:T(8,128)(2,1)S(1)}, u32[]{:S(2)}, u32[]{:S(2)}) collective-permute-start(bf16[576,128]{1,0:T(8,128)(2,1)S(1)} %get-tuple-element.66), channel_id=1, source_target_pairs={{0,3},{1,0},{2,1},{3,2},{4,7},{5,4},{6,5},{7,6},{8,11},{9,8},{10,9... | collective-permute-start | bytes 442376 | tf_op jit(solution)/shard_map/ppermute | solution.py:299
  8.5 13.9 %collective-permute-start.3 = (bf16[384,128]{1,0:T(8,128)(2,1)S(1)}, bf16[384,128]{1,0:T(8,128)(2,1)S(1)}, u32[]{:S(2)}, u32[]{:S(2)}) collective-permute-start(bf16[384,128]{1,0:T(8,128)(2,1)S(1)} %slice.40), channel_id=1, source_target_pairs={{1,17},{2,18},{3,19},{5,21},{6,22},{7,23},{9,25},{10,26},{11,27},{... | collective-permute-start | bytes 294920 | tf_op jit(solution)/shard_map/ppermute | solution.py:314
  11.4 13.4 %collective-permute-start.4 = (bf16[384,128]{1,0:T(8,128)(2,1)S(1)}, bf16[384,128]{1,0:T(8,128)(2,1)S(1)}, u32[]{:S(2)}, u32[]{:S(2)}) collective-permute-start(bf16[384,128]{1,0:T(8,128)(2,1)S(1)} %slice.44), channel_id=1, source_target_pairs={{0,16},{2,18},{3,19},{4,20},{6,22},{7,23},{8,24},{10,26},{11,27},{... | collective-permute-start | bytes 294920 | tf_op jit(solution)/shard_map/ppermute | solution.py:314
  17.5 9.6 %collective-permute-start.5 = (bf16[384,128]{1,0:T(8,128)(2,1)S(1)}, bf16[384,128]{1,0:T(8,128)(2,1)S(1)}, u32[]{:S(2)}, u32[]{:S(2)}) collective-permute-start(bf16[384,128]{1,0:T(8,128)(2,1)S(1)} %slice.45), channel_id=1, source_target_pairs={{0,16},{1,17},{3,19},{4,20},{5,21},{7,23},{8,24},{9,25},{11,27},{1... | collective-permute-start | bytes 294920 | tf_op jit(solution)/shard_map/ppermute | solution.py:314
  21.0 6.9 %collective-permute-start.6 = (bf16[384,128]{1,0:T(8,128)(2,1)S(1)}, bf16[384,128]{1,0:T(8,128)(2,1)S(1)}, u32[]{:S(2)}, u32[]{:S(2)}) collective-permute-start(bf16[384,128]{1,0:T(8,128)(2,1)S(1)} %slice.46), channel_id=1, source_target_pairs={{0,16},{1,17},{2,18},{4,20},{5,21},{6,22},{8,24},{9,25},{10,26},{1... | collective-permute-start | bytes 294920 | tf_op jit(solution)/shard_map/ppermute | solution.py:314
  22.4 15.4 %collective-permute-start.7 = (bf16[576,128]{1,0:T(8,128)(2,1)S(1)}, bf16[576,128]{1,0:T(8,128)(2,1)S(1)}, u32[]{:S(2)}, u32[]{:S(2)}) collective-permute-start(bf16[576,128]{1,0:T(8,128)(2,1)S(1)} %get-tuple-element.69), channel_id=1, source_target_pairs={{0,1},{1,2},{2,3},{3,0},{4,5},{5,6},{6,7},{7,4},{8,9},{9,10},{10,1... | collective-permute-start | bytes 442376 | tf_op jit(solution)/shard_map/ppermute | solution.py:299
  24.8 13.0 %collective-permute-start.8 = (bf16[576,128]{1,0:T(8,128)(2,1)S(1)}, bf16[576,128]{1,0:T(8,128)(2,1)S(1)}, u32[]{:S(2)}, u32[]{:S(2)}) collective-permute-start(bf16[576,128]{1,0:T(8,128)(2,1)S(1)} %get-tuple-element.71), channel_id=1, source_target_pairs={{0,2},{1,3},{2,0},{3,1},{4,6},{5,7},{6,4},{7,5},{8,10},{9,11},{10,... | collective-permute-start | bytes 442376 | tf_op jit(solution)/shard_map/ppermute | solution.py:299
  27.1 10.6 %collective-permute-start.9 = (bf16[576,128]{1,0:T(8,128)(2,1)S(1)}, bf16[576,128]{1,0:T(8,128)(2,1)S(1)}, u32[]{:S(2)}, u32[]{:S(2)}) collective-permute-start(bf16[576,128]{1,0:T(8,128)(2,1)S(1)} %get-tuple-element.73), channel_id=1, source_target_pairs={{0,3},{1,0},{2,1},{3,2},{4,7},{5,4},{6,5},{7,6},{8,11},{9,8},{10,9... | collective-permute-start | bytes 442376 | tf_op jit(solution)/shard_map/ppermute | solution.py:299
  31.2 3.5 %collective-permute-start.10 = (bf16[2,48,512]{2,1,0:T(8,128)(2,1)S(1)}, bf16[2,48,512]{2,1,0:T(8,128)(2,1)S(1)}, u32[]{:S(2)}, u32[]{:S(2)}) collective-permute-start(bf16[2,48,512]{2,1,0:T(8,128)(2,1)S(1)} %get-tuple-element.74), channel_id=1, source_target_pairs={{0,4},{4,0},{8,12},{12,8},{1,5},{5,1},{9,13},{13,9},{2,6},{6,2},{1... | collective-permute-start | bytes 294920 | tf_op jit(solution)/shard_map/ppermute | solution.py:415
  36.2 14.4 %collective-permute-start.13 = (bf16[48,4096]{1,0:T(8,128)(2,1)S(1)}, bf16[48,4096]{1,0:T(8,128)(2,1)}, u32[]{:S(2)}, u32[]{:S(2)}) collective-permute-start(bf16[48,4096]{1,0:T(8,128)(2,1)S(1)} %get-tuple-element.95), channel_id=1, source_target_pairs={{0,8},{4,12},{8,0},{12,4},{1,9},{5,13},{9,1},{13,5},{2,10},{6,14},... | collective-permute-start | bytes 1179656 | tf_op jit(solution)/shard_map/ppermute | solution.py:354
  37.8 4.7 %copy-start = (bf16[576,128]{1,0:T(8,128)(2,1)}, bf16[576,128]{1,0:T(8,128)(2,1)S(1)}, u32[]{:S(2)}) copy-start(bf16[576,128]{1,0:T(8,128)(2,1)S(1)} %collective-permute-done.8.refs_10_) | copy-start | bytes 442372
  37.8 4.6 %copy-start.2 = (bf16[576,128]{1,0:T(8,128)(2,1)}, bf16[576,128]{1,0:T(8,128)(2,1)S(1)}, u32[]{:S(2)}) copy-start(bf16[576,128]{1,0:T(8,128)(2,1)S(1)} %collective-permute-done.9.refs_11_) | copy-start | bytes 442372
  42.2 6.6 %collective-permute-start.12 = (bf16[2,96,512]{2,1,0:T(8,128)(2,1)S(1)}, bf16[2,96,512]{2,1,0:T(8,128)(2,1)S(1)}, u32[]{:S(2)}, u32[]{:S(2)}) collective-permute-start(bf16[2,96,512]{2,1,0:T(8,128)(2,1)S(1)} %get-tuple-element.85), channel_id=1, source_target_pairs={{0,4},{4,0},{8,12},{12,8},{1,5},{5,1},{9,13},{13,9},{2,6},{6,2},{1... | collective-permute-start | bytes 589832 | tf_op jit(solution)/shard_map/ppermute | solution.py:415
  42.4 17.5 %collective-permute-start.15 = (bf16[48,4096]{1,0:T(8,128)(2,1)S(1)}, bf16[48,4096]{1,0:T(8,128)(2,1)S(1)}, u32[]{:S(2)}, u32[]{:S(2)}) collective-permute-start(bf16[48,4096]{1,0:T(8,128)(2,1)S(1)} %get-tuple-element.108), channel_id=1, source_target_pairs={{0,8},{4,12},{8,0},{12,4},{1,9},{5,13},{9,1},{13,5},{2,10},{6,14},... | collective-permute-start | bytes 1179656 | tf_op jit(solution)/shard_map/ppermute | solution.py:354
  48.8 8.6 %copy-start.1 = (bf16[576,128]{1,0:T(8,128)(2,1)S(1)}, bf16[576,128]{1,0:T(8,128)(2,1)}, u32[]{:S(2)}) copy-start(bf16[576,128]{1,0:T(8,128)(2,1)} %copy-done) | copy-start | bytes 442372
  48.8 8.6 %copy-start.3 = (bf16[576,128]{1,0:T(8,128)(2,1)S(1)}, bf16[576,128]{1,0:T(8,128)(2,1)}, u32[]{:S(2)}) copy-start(bf16[576,128]{1,0:T(8,128)(2,1)} %copy-done.2) | copy-start | bytes 442372
  50.6 19.5 %collective-permute-start.24 = (bf16[48,4096]{1,0:T(8,128)(2,1)S(1)}, bf16[48,4096]{1,0:T(8,128)(2,1)S(1)}, u32[]{:S(2)}, u32[]{:S(2)}) collective-permute-start(bf16[48,4096]{1,0:T(8,128)(2,1)S(1)} %get-tuple-element.117), channel_id=1, source_target_pairs={{0,8},{4,12},{8,0},{12,4},{1,9},{5,13},{9,1},{13,5},{2,10},{6,14},... | collective-permute-start | bytes 1179656 | tf_op jit(solution)/shard_map/ppermute | solution.py:354
  53.3 18.3 %collective-permute-start.27 = (bf16[48,4096]{1,0:T(8,128)(2,1)S(1)}, bf16[48,4096]{1,0:T(8,128)(2,1)S(1)}, u32[]{:S(2)}, u32[]{:S(2)}) collective-permute-start(bf16[48,4096]{1,0:T(8,128)(2,1)S(1)} %add_convert_fusion.5), channel_id=1, source_target_pairs={{0,1},{3,2},{4,5},{7,6},{8,9},{11,10},{12,13},{15,14},{16,17},{19,... | collective-permute-start | bytes 1179656 | tf_op jit(solution)/shard_map/ppermute | solution.py:372
  59.9 8.9 %collective-permute-start.14 = (bf16[2,48,512]{2,1,0:T(8,128)(2,1)S(1)}, bf16[2,48,512]{2,1,0:T(8,128)(2,1)S(1)}, u32[]{:S(2)}, u32[]{:S(2)}) collective-permute-start(bf16[2,48,512]{2,1,0:T(8,128)(2,1)S(1)} %get-tuple-element.100), channel_id=1, source_target_pairs={{0,4},{4,0},{8,12},{12,8},{1,5},{5,1},{9,13},{13,9},{2,6},{6,2},{1... | collective-permute-start | bytes 294920 | tf_op jit(solution)/shard_map/ppermute | solution.py:415
  59.9 13.1 %collective-permute-start.16 = (bf16[48,4096]{1,0:T(8,128)(2,1)S(1)}, bf16[48,4096]{1,0:T(8,128)(2,1)S(1)}, u32[]{:S(2)}, u32[]{:S(2)}) collective-permute-start(bf16[48,4096]{1,0:T(8,128)(2,1)S(1)} %get-tuple-element.109), channel_id=1, source_target_pairs={{0,8},{4,12},{8,0},{12,4},{1,9},{5,13},{9,1},{13,5},{2,10},{6,14},... | collective-permute-start | bytes 1179656 | tf_op jit(solution)/shard_map/ppermute | solution.py:354
  61.6 14.9 %collective-permute-start.19 = (bf16[48,4096]{1,0:T(8,128)(2,1)S(1)}, bf16[48,4096]{1,0:T(8,128)(2,1)S(1)}, u32[]{:S(2)}, u32[]{:S(2)}) collective-permute-start(bf16[48,4096]{1,0:T(8,128)(2,1)S(1)} %add_convert_fusion.13), channel_id=1, source_target_pairs={{0,1},{3,2},{4,5},{7,6},{8,9},{11,10},{12,13},{15,14},{16,17},{19,... | collective-permute-start | bytes 1179656 | tf_op jit(solution)/shard_map/ppermute | solution.py:372
  70.3 13.4 %collective-permute-start.30 = (bf16[48,4096]{1,0:T(8,128)(2,1)S(1)}, bf16[48,4096]{1,0:T(8,128)(2,1)S(1)}, u32[]{:S(2)}, u32[]{:S(2)}) collective-permute-start(bf16[48,4096]{1,0:T(8,128)(2,1)S(1)} %add_convert_fusion.2), channel_id=1, source_target_pairs={{0,1},{3,2},{4,5},{7,6},{8,9},{11,10},{12,13},{15,14},{16,17},{19,... | collective-permute-start | bytes 1179656 | tf_op jit(solution)/shard_map/ppermute | solution.py:372
  71.7 13.6 %collective-permute-start.28 = (bf16[48,4096]{1,0:T(8,128)(2,1)S(1)}, bf16[48,4096]{1,0:T(8,128)(2,1)S(1)}, u32[]{:S(2)}, u32[]{:S(2)}) collective-permute-start(bf16[48,4096]{1,0:T(8,128)(2,1)S(1)} %add_convert_fusion.4), channel_id=1, source_target_pairs={{1,2},{2,1},{5,6},{6,5},{9,10},{10,9},{13,14},{14,13},{17,18},{18,... | collective-permute-start | bytes 1179656 | tf_op jit(solution)/shard_map/ppermute | solution.py:372
  72.4 13.6 %collective-permute-start.25 = (bf16[48,4096]{1,0:T(8,128)(2,1)S(1)}, bf16[48,4096]{1,0:T(8,128)(2,1)S(1)}, u32[]{:S(2)}, u32[]{:S(2)}) collective-permute-start(bf16[48,4096]{1,0:T(8,128)(2,1)S(1)} %get-tuple-element.118), channel_id=1, source_target_pairs={{0,8},{4,12},{8,0},{12,4},{1,9},{5,13},{9,1},{13,5},{2,10},{6,14},... | collective-permute-start | bytes 1179656 | tf_op jit(solution)/shard_map/ppermute | solution.py:354
  73.2 19.0 %collective-permute-start.22 = (bf16[48,4096]{1,0:T(8,128)(2,1)S(1)}, bf16[48,4096]{1,0:T(8,128)(2,1)S(1)}, u32[]{:S(2)}, u32[]{:S(2)}) collective-permute-start(bf16[48,4096]{1,0:T(8,128)(2,1)S(1)} %add_convert_fusion.10), channel_id=1, source_target_pairs={{0,1},{3,2},{4,5},{7,6},{8,9},{11,10},{12,13},{15,14},{16,17},{19,... | collective-permute-start | bytes 1179656 | tf_op jit(solution)/shard_map/ppermute | solution.py:372
  76.6 17.2 %collective-permute-start.20 = (bf16[48,4096]{1,0:T(8,128)(2,1)S(1)}, bf16[48,4096]{1,0:T(8,128)(2,1)S(1)}, u32[]{:S(2)}, u32[]{:S(2)}) collective-permute-start(bf16[48,4096]{1,0:T(8,128)(2,1)S(1)} %add_convert_fusion.12), channel_id=1, source_target_pairs={{1,2},{2,1},{5,6},{6,5},{9,10},{10,9},{13,14},{14,13},{17,18},{18,... | collective-permute-start | bytes 1179656 | tf_op jit(solution)/shard_map/ppermute | solution.py:372
  83.7 10.7 %collective-permute-start.17 = (bf16[48,4096]{1,0:T(8,128)(2,1)S(1)}, bf16[48,4096]{1,0:T(8,128)(2,1)S(1)}, u32[]{:S(2)}, u32[]{:S(2)}) collective-permute-start(bf16[48,4096]{1,0:T(8,128)(2,1)S(1)} %get-tuple-element.110), channel_id=1, source_target_pairs={{0,8},{4,12},{8,0},{12,4},{1,9},{5,13},{9,1},{13,5},{2,10},{6,14},... | collective-permute-start | bytes 1179656 | tf_op jit(solution)/shard_map/ppermute | solution.py:354
  85.3 13.1 %collective-permute-start.31 = (bf16[48,4096]{1,0:T(8,128)(2,1)S(1)}, bf16[48,4096]{1,0:T(8,128)(2,1)S(1)}, u32[]{:S(2)}, u32[]{:S(2)}) collective-permute-start(bf16[48,4096]{1,0:T(8,128)(2,1)S(1)} %add_convert_fusion.1), channel_id=1, source_target_pairs={{1,2},{2,1},{5,6},{6,5},{9,10},{10,9},{13,14},{14,13},{17,18},{18,... | collective-permute-start | bytes 1179656 | tf_op jit(solution)/shard_map/ppermute | solution.py:372
  86.2 14.4 %collective-permute-start.29 = (bf16[48,4096]{1,0:T(8,128)(2,1)S(1)}, bf16[48,4096]{1,0:T(8,128)(2,1)S(1)}, u32[]{:S(2)}, u32[]{:S(2)}) collective-permute-start(bf16[48,4096]{1,0:T(8,128)(2,1)S(1)} %fusion.1), channel_id=1, source_target_pairs={{0,1},{3,2},{1,0},{2,3},{4,5},{7,6},{5,4},{6,7},{8,9},{11,10},{9,8... | collective-permute-start | bytes 1179656 | tf_op jit(solution)/shard_map/ppermute | solution.py:372
  92.1 11.5 %collective-permute-start.26 = (bf16[48,4096]{1,0:T(8,128)(2,1)S(1)}, bf16[48,4096]{1,0:T(8,128)(2,1)S(1)}, u32[]{:S(2)}, u32[]{:S(2)}) collective-permute-start(bf16[48,4096]{1,0:T(8,128)(2,1)S(1)} %get-tuple-element.119), channel_id=1, source_target_pairs={{0,8},{4,12},{8,0},{12,4},{1,9},{5,13},{9,1},{13,5},{2,10},{6,14},... | collective-permute-start | bytes 1179656 | tf_op jit(solution)/shard_map/ppermute | solution.py:354
  93.7 10.1 %collective-permute-start.23 = (bf16[48,4096]{1,0:T(8,128)(2,1)S(1)}, bf16[48,4096]{1,0:T(8,128)(2,1)S(1)}, u32[]{:S(2)}, u32[]{:S(2)}) collective-permute-start(bf16[48,4096]{1,0:T(8,128)(2,1)S(1)} %add_convert_fusion.9), channel_id=1, source_target_pairs={{1,2},{2,1},{5,6},{6,5},{9,10},{10,9},{13,14},{14,13},{17,18},{18,... | collective-permute-start | bytes 1179656 | tf_op jit(solution)/shard_map/ppermute | solution.py:372
  94.6 13.3 %collective-permute-start.21 = (bf16[48,4096]{1,0:T(8,128)(2,1)S(1)}, bf16[48,4096]{1,0:T(8,128)(2,1)S(1)}, u32[]{:S(2)}, u32[]{:S(2)}) collective-permute-start(bf16[48,4096]{1,0:T(8,128)(2,1)S(1)} %fusion), channel_id=1, source_target_pairs={{0,1},{3,2},{1,0},{2,3},{4,5},{7,6},{5,4},{6,7},{8,9},{11,10},{9,8... | collective-permute-start | bytes 1179656 | tf_op jit(solution)/shard_map/ppermute | solution.py:372
  98.4 11.1 %collective-permute-start.18 = (bf16[48,4096]{1,0:T(8,128)(2,1)S(1)}, bf16[48,4096]{1,0:T(8,128)(2,1)S(1)}, u32[]{:S(2)}, u32[]{:S(2)}) collective-permute-start(bf16[48,4096]{1,0:T(8,128)(2,1)S(1)} %get-tuple-element.111), channel_id=1, source_target_pairs={{0,8},{4,12},{8,0},{12,4},{1,9},{5,13},{9,1},{13,5},{2,10},{6,14},... | collective-permute-start | bytes 1179656 | tf_op jit(solution)/shard_map/ppermute | solution.py:354
